TPU v7x, 32 devices: a whole 2x2x4 slice. The times are simulated.
32 devices in a mesh: seq: 16 (over z, x, core), row: 2 (over y).
Axes of the slice: x: 2, y: 2, z: 4, core: 2. Of those that a mesh axis runs over, the one named last changes fastest.
Arguments:
- hidden_in: bfloat16 [6, 1024, 1024], P('row', 'seq'), may hold values from -6 to 6
- grad_out: bfloat16 [6, 1024, 1024], P('row', 'seq'), may hold values from -6 to 6
- doc_starts: int32 [6, 8], P('row'), may hold values from 0 to 1023, as said below
- norm_gain: bfloat16 [1024], P(('seq', 'row')), may hold values from 0.5 to 1.5
- in_proj: bfloat16 [4096, 1024], P(('seq', 'row')), may hold values from -0.1875 to 0.1875
- out_proj: bfloat16 [1024, 2048], P(('seq', 'row')), may hold values from -0.25 to 0.25
- conv_weight: bfloat16 [4, 2048], P(None, 'seq'), may hold values from -3 to 3
- conv_bias: bfloat16 [2048], P('seq'), may hold values from -3 to 3
- x_proj: bfloat16 [2048, 96], P('seq'), may hold values from -0.125 to 0.125
- dt_proj: bfloat16 [64, 2048], P(None, 'seq'), may hold values from -0.75 to 0.75
- dt_bias: bfloat16 [2048], P('seq'), may hold values from -6.875 to -2.25
- decay_log: bfloat16 [16, 2048], P(None, 'seq'), may hold values from 0 to 2.765625
- skip_scale: bfloat16 [2048], P('seq'), may hold values from 0.5 to 1.5
Outputs:
- hidden_out: bfloat16 [6, 1024, 1024], P('row', 'seq')
- grad_hidden: float32 [6, 1024, 1024], P('row', 'seq')
- grad_norm_gain: float32 [1024], P(('seq', 'row'))
- grad_in_proj: float32 [4096, 1024], P(('seq', 'row'))
- grad_out_proj: float32 [1024, 2048], P(('seq', 'row'))
- grad_conv_weight: float32 [4, 2048], P(None, 'seq')
- grad_conv_bias: float32 [2048], P('seq')
- grad_x_proj: float32 [2048, 96], P('seq')
- grad_dt_proj: float32 [64, 2048], P(None, 'seq')
- grad_dt_bias: float32 [2048], P('seq')
- grad_decay_log: float32 [16, 2048], P(None, 'seq')
- grad_skip_scale: float32 [2048], P('seq')
- dt_stats: float32 [2, 2048], P(None, 'seq')
Inputs may be any that keep to these rules, and one draw needn't show every extreme that they name: doc_starts[r, 0] is 0 and each row's 8 starts rise strictly; in each group of 3 rows that one index of row holds, one row's first document covers every position before its last 64, and that row's last start is 1023.
All inputs are finite; a program needn't handle non-finite values.
Results may differ from a plain program's by a relative error of at most 0.012.
The roundings to bfloat16 on the way count: a program that leaves them out, or rounds other values in their place, can miss the bound.
Values may be sent and summed in bfloat16 or wider, within the bound.
No kernel may reach another device: no remote copies, remote signals or barrier semaphores. Data moves between devices by JAX's collectives and lax.ppermute only.
A program may use at most 512 MiB of HBM per device.

v0:
```python
from functools import partial

import jax
import jax.numpy as jnp
from jax import lax
from jax.sharding import PartitionSpec as P

E = 2048
NSTATE = 16
CONV = 4
DT_RANK = 64


eps_norm = 1e-05
eps_spread = 1e-06
block_len = 16


def lagged(values, offset, filler):
    if offset == 0:
        return values
    widths = [(0, 0)] * values.ndim
    widths[1] = (offset, 0)
    return jnp.pad(values, widths, constant_values=filler)[:, : values.shape[1]]


def leading(values, offset):
    if offset == 0:
        return values
    widths = [(0, 0)] * values.ndim
    widths[1] = (0, offset)
    return jnp.pad(values, widths)[:, offset:]


def silu_slope(values):
    logistic = jax.nn.sigmoid(values)
    return logistic * (1.0 + values * (1.0 - logistic))


def block_scan(decay_rates, dt_row, x_row, b_row, c_row, keep_row):
    length, channels = dt_row.shape
    blocks = length // block_len

    def regroup(values):
        grouped = values.reshape((blocks, block_len) + values.shape[1:])
        return jnp.moveaxis(grouped, 0, -1)

    dt_q, x_q, b_q, c_q, keep_q = (regroup(v) for v in (dt_row, x_row, b_row, c_row, keep_row))

    def decay_at(dt_now, keep_now):
        return jnp.exp(dt_now[None, :, :] * decay_rates[:, :, None]) * keep_now[None, None, :]

    def local_pass(running, inputs):
        state_now, product = running
        dt_now, x_now, b_now, keep_now = inputs
        decay_now = decay_at(dt_now, keep_now)
        state_now = decay_now * state_now + b_now[:, None, :] * (dt_now * x_now)[None, :, :]
        return ((state_now, decay_now * product), None)

    empty_state = jnp.zeros((NSTATE, channels, blocks), jnp.float32)
    (block_ends, block_decay), _ = lax.scan(
        local_pass, (empty_state, jnp.ones_like(empty_state)), (dt_q, x_q, b_q, keep_q)
    )

    def combine(earlier, later):
        return (earlier[0] * later[0], later[0] * earlier[1] + later[1])

    _, reached = lax.associative_scan(combine, (block_decay, block_ends), axis=2)
    starting = jnp.concatenate([jnp.zeros_like(reached[:, :, :1]), reached[:, :, :-1]], axis=2)

    def full_pass(state_now, inputs):
        dt_now, x_now, b_now, c_now, keep_now = inputs
        state_now = (
            decay_at(dt_now, keep_now) * state_now
            + b_now[:, None, :] * (dt_now * x_now)[None, :, :]
        )
        return (state_now, jnp.sum(c_now[:, None, :] * state_now, axis=0))

    _, outputs = lax.scan(full_pass, starting, (dt_q, x_q, b_q, c_q, keep_q))
    return jnp.moveaxis(outputs, 2, 0).reshape(length, channels)


def scan_all(dt_vals, x_vals, b_vals, c_vals, decay_full, skip_full, keep_mask):
    decay_rates = -jnp.exp(decay_full)
    per_row = jax.checkpoint(block_scan)

    def one_row(row_items):
        return per_row(decay_rates, *row_items)

    outputs = lax.map(one_row, (dt_vals, x_vals, b_vals, c_vals, keep_mask))
    return outputs + skip_full * x_vals


def local(
    hidden_in,
    grad_out,
    doc_starts,
    norm_gain,
    in_proj,
    out_proj,
    conv_weight,
    conv_bias,
    x_proj,
    dt_proj,
    dt_bias,
    decay_log,
    skip_scale,
):
    row_count, seg_len, model_width = hidden_in.shape
    full_len = seg_len * lax.axis_size("seq")
    gain_whole, in_whole, out_whole = (
        lax.all_gather(norm_gain, ("seq", "row"), axis=0, tiled=True),
        lax.all_gather(in_proj, ("seq", "row"), axis=0, tiled=True),
        lax.all_gather(out_proj, ("seq", "row"), axis=0, tiled=True),
    )
    residual = hidden_in.astype(jnp.float32)
    inv_rms = lax.rsqrt(jnp.mean(residual * residual, axis=-1, keepdims=True) + eps_norm)
    scaled = residual * inv_rms
    gain_full = gain_whole.astype(jnp.float32)
    normed = (scaled * gain_full).astype(jnp.bfloat16)
    proj_in = jnp.einsum("rtd,fd->rtf", normed, in_whole, preferred_element_type=jnp.float32)
    x_tokens = proj_in[..., :E].astype(jnp.bfloat16)
    gate_z = proj_in[..., E:]
    x_chan = lax.all_to_all(x_tokens, "seq", split_axis=2, concat_axis=1, tiled=True)
    positions = lax.broadcasted_iota(jnp.int32, (1, full_len, 1), 1)
    doc_ids = jnp.sum((doc_starts[:, None, :] <= positions).astype(jnp.int32), axis=2) - 1
    same_docs = [
        (lagged(doc_ids, offset, -1) == doc_ids).astype(jnp.float32)[..., None]
        for offset in range(CONV)
    ]
    keep_mask = same_docs[1][..., 0]
    x_vals = x_chan.astype(jnp.float32)
    conv_full = conv_weight.astype(jnp.float32)
    pre_conv = conv_bias.astype(jnp.float32) + jnp.zeros_like(x_vals)
    for offset in range(CONV):
        pre_conv = (
            pre_conv
            + conv_full[CONV - 1 - offset] * lagged(x_vals, offset, 0.0) * same_docs[offset]
        )
    conv_low = jax.nn.silu(pre_conv).astype(jnp.bfloat16)
    part_sums = jnp.einsum("rtc,cm->rtm", conv_low, x_proj, preferred_element_type=jnp.float32)
    dtbc = lax.psum(part_sums, "seq").astype(jnp.bfloat16)
    dt_low = dtbc[..., :DT_RANK]
    b_vals = dtbc[..., DT_RANK : DT_RANK + NSTATE].astype(jnp.float32)
    c_vals = dtbc[..., DT_RANK + NSTATE :].astype(jnp.float32)
    pre_dt = jnp.einsum(
        "rtk,kc->rtc", dt_low, dt_proj, preferred_element_type=jnp.float32
    ) + dt_bias.astype(jnp.float32)
    dt_vals = jax.nn.softplus(pre_dt)
    y_vals, pullback = jax.vjp(
        partial(scan_all, keep_mask=keep_mask),
        dt_vals,
        conv_low.astype(jnp.float32),
        b_vals,
        c_vals,
        decay_log.astype(jnp.float32),
        skip_scale.astype(jnp.float32),
    )
    y_tokens = lax.all_to_all(
        y_vals.astype(jnp.bfloat16), "seq", split_axis=1, concat_axis=2, tiled=True
    )
    y_token_vals = y_tokens.astype(jnp.float32)
    gate_act = jax.nn.silu(gate_z)
    gated = (y_token_vals * gate_act).astype(jnp.bfloat16)
    mixed = jnp.einsum("rte,de->rtd", gated, out_whole, preferred_element_type=jnp.float32)
    hidden_out = (residual + mixed).astype(jnp.bfloat16)
    grad_out_proj = jnp.einsum("rtd,rte->de", grad_out, gated, preferred_element_type=jnp.float32)
    grad_gated = jnp.einsum("rtd,de->rte", grad_out, out_whole, preferred_element_type=jnp.float32)
    grad_y = (grad_gated * gate_act).astype(jnp.bfloat16)
    grad_gate = (grad_gated * y_token_vals * silu_slope(gate_z)).astype(jnp.bfloat16)
    grad_y_chan = lax.all_to_all(grad_y, "seq", split_axis=2, concat_axis=1, tiled=True)
    grad_dt_scan, grad_x_scan, grad_b, grad_c, grad_decay, grad_skip = pullback(
        grad_y_chan.astype(jnp.float32)
    )
    grad_pre_dt = (grad_dt_scan * jax.nn.sigmoid(pre_dt)).astype(jnp.bfloat16)
    grad_dt_low = jnp.einsum(
        "rtc,kc->rtk", grad_pre_dt, dt_proj, preferred_element_type=jnp.float32
    )
    grad_dt_proj = jnp.einsum(
        "rtk,rtc->kc", dt_low, grad_pre_dt, preferred_element_type=jnp.float32
    )
    grad_dt_bias = jnp.sum(grad_pre_dt.astype(jnp.float32), axis=(0, 1))
    grad_parts = jnp.concatenate([grad_dt_low, grad_b, grad_c], axis=-1)
    grad_share = lax.psum_scatter(grad_parts, "seq", scatter_dimension=1, tiled=True)
    grad_dtbc = lax.all_gather(grad_share.astype(jnp.bfloat16), "seq", axis=1, tiled=True)
    grad_x_proj = jnp.einsum("rtc,rtm->cm", conv_low, grad_dtbc, preferred_element_type=jnp.float32)
    grad_conv_out = grad_x_scan + jnp.einsum(
        "rtm,cm->rtc", grad_dtbc, x_proj, preferred_element_type=jnp.float32
    )
    grad_pre_conv = grad_conv_out * silu_slope(pre_conv)
    grad_conv_bias = jnp.sum(grad_pre_conv, axis=(0, 1))
    conv_rows = [None] * CONV
    grad_x = jnp.zeros_like(grad_pre_conv)
    for offset in range(CONV):
        masked = grad_pre_conv * same_docs[offset]
        conv_rows[CONV - 1 - offset] = jnp.sum(masked * lagged(x_vals, offset, 0.0), axis=(0, 1))
        grad_x = grad_x + conv_full[CONV - 1 - offset] * leading(masked, offset)
    grad_conv_weight = jnp.stack(conv_rows)
    grad_x_tokens = lax.all_to_all(
        grad_x.astype(jnp.bfloat16), "seq", split_axis=1, concat_axis=2, tiled=True
    )
    grad_proj = jnp.concatenate([grad_x_tokens, grad_gate], axis=-1)
    grad_in_proj = jnp.einsum("rtf,rtd->fd", grad_proj, normed, preferred_element_type=jnp.float32)
    grad_normed = jnp.einsum("rtf,fd->rtd", grad_proj, in_whole, preferred_element_type=jnp.float32)
    grad_gain = jnp.sum(grad_normed * scaled, axis=(0, 1))
    grad_scaled = grad_normed * gain_full
    grad_hidden = grad_out.astype(jnp.float32) + inv_rms * (
        grad_scaled - scaled * jnp.mean(grad_scaled * scaled, axis=-1, keepdims=True)
    )
    gain_share, in_share, out_share = (
        lax.psum_scatter(grad_gain, ("seq", "row"), scatter_dimension=0, tiled=True),
        lax.psum_scatter(grad_in_proj, ("seq", "row"), scatter_dimension=0, tiled=True),
        lax.psum_scatter(grad_out_proj, ("seq", "row"), scatter_dimension=0, tiled=True),
    )
    centre = jnp.log(jax.nn.softplus(dt_bias.astype(jnp.float32)))
    offset_dt = jnp.log(dt_vals) - centre
    first_sum = jnp.sum(offset_dt, axis=(0, 1))
    second_sum = jnp.sum(offset_dt * offset_dt, axis=(0, 1))
    summed = lax.psum(
        (
            grad_conv_weight,
            grad_conv_bias,
            grad_x_proj,
            grad_dt_proj,
            grad_dt_bias,
            grad_decay,
            grad_skip,
            first_sum,
            second_sum,
        ),
        "row",
    )
    token_count = full_len * row_count * lax.axis_size("row")
    mean_off = summed[7] / token_count
    spread = jnp.sqrt(summed[8] / token_count - mean_off * mean_off + eps_spread)
    dt_stats = jnp.stack([centre + mean_off, spread])
    return (
        hidden_out,
        grad_hidden,
        gain_share,
        in_share,
        out_share,
        summed[0],
        summed[1],
        summed[2],
        summed[3],
        summed[4],
        summed[5],
        summed[6],
        dt_stats,
    )


def solution(mesh):
    return jax.shard_map(
        local,
        mesh=mesh,
        in_specs=(
            P("row", "seq", None),
            P("row", "seq", None),
            P("row", None),
            P(("seq", "row")),
            P(("seq", "row"), None),
            P(("seq", "row"), None),
            P(None, "seq"),
            P("seq"),
            P("seq", None),
            P(None, "seq"),
            P("seq"),
            P(None, "seq"),
            P("seq"),
        ),
        out_specs=(
            P("row", "seq", None),
            P("row", "seq", None),
            P(("seq", "row")),
            P(("seq", "row"), None),
            P(("seq", "row"), None),
            P(None, "seq"),
            P("seq"),
            P("seq", None),
            P(None, "seq"),
            P("seq"),
            P(None, "seq"),
            P("seq"),
            P(None, "seq"),
        ),
        check_vma=False,
    )
```

profile of v0, /device:TPU:18, one launch (start us, length us, event | category | flops | bytes accessed | tf_op | source)
XLA Modules:
  0.0 3286.8 jit_solution(13502404749414010140)
XLA Ops:
  9.5 41.4 %all-reduce.79 = bf16[1024]{0:T(1024)(128)(2,1)S(1)} all-reduce(bf16[1024]{0:T(1024)(128)(2,1)S(1)} %dynamic-update-slice), channel_id=1, replica_groups=mesh['seq'=16,'row'=2] {'seq','row'}, use_global_device_ids=true, to_apply=%add.79 | all-reduce | flops 1024 | bytes 4096
  52.2 37.8 %all-gather.3.cloned.1.call-done = bf16[4096,1024]{1,0:T(8,128)(2,1)} async-done(((bf16[128,1024]{1,0:T(8,128)(2,1)}), bf16[4096,1024]{1,0:T(8,128)(2,1)}) %all-gather.3.cloned.1.call-update) | async-done | bytes 8388624 | tf_op jit(solution)/shard_map/all_gather | solution.py:113
  96.3 56.7 %all-gather.5.cloned.1.call-done = bf16[1024,2048]{1,0:T(8,128)(2,1)} async-done(((bf16[32,2048]{1,0:T(8,128)(2,1)}), bf16[1024,2048]{1,0:T(8,128)(2,1)}) %all-gather.5.cloned.1.call-update) | async-done | bytes 4194320 | tf_op jit(solution)/shard_map/all_gather | solution.py:114
  178.2 11.3 all-to-all-done.2
  229.5 61.8 %all-reduce.88 = bf16[3,1024,96]{1,2,0:T(8,128)(2,1)S(1)} all-reduce(f32[3,1024,96]{1,2,0:T(8,128)} %fusion.79), channel_id=1, replica_groups=mesh['seq'=16,'row'=2] {'seq'}, use_global_device_ids=true, to_apply=%region_2.3 | all-reduce | flops 294912 | bytes 1769472 | tf_op jit(solution)/shard_map/psum | solution.py:142
  299.6 2058.2 %while.326 = (s32[]{:T(128)}, f32[16,128]{1,0:T(8,128)}, f32[3,1024,128]{2,1,0:T(8,128)}, f32[3,1024,128]{2,1,0:T(8,128)}, f32[3,1024,16]{1,2,0:T(8,128)}, /*ind...) while((s32[]{:T(128)}, f32[16,128]{1,0:T(8,128)}, ...), condition=%wide.region_28.29_spmd.clone, body=%wide.region_10.0_spmd.clone.sunk | while | flops 10540049 | bytes 199177776 | solution.py:90
  324.2 8.1 broadcast.507.clone
  332.3 8.0 broadcast.507.clone.1
  358.3 103.2 %while.329 = (s32[]{:T(128)}, f32[16,128,64]{2,1,0:T(8,128)S(1)}, f32[16,128,64]{2,1,0:T(8,128)S(1)}, f32[16,1,128,64]{3,2,1,0:T(8,128)}, f32[16,16,128,64]{3,2,...) while((s32[]{:T(128)}, f32[16,128,64]{2,1,0:T(8,128)S(1)}, ...), condition=%wide.region_12.12_spmd.clone, body=%wide.region_11.11_spmd.clone.sunk | while | flops 1589251 | bytes 7847620 | solution.py:61
  466.4 10.4 pad.1161
  483.8 8.0 broadcast.507
  519.0 151.3 %while.330 = (s32[]{:T(128)}, f32[16,128,64]{2,1,0:T(8,128)S(1)}, f32[16,16,128,64]{3,2,1,0:T(8,128)}, f32[16,16,1,64]{3,2,1,0:T(1,128)}, f32[16,1,128,64]{3,2,1...) while((s32[]{:T(128)}, f32[16,128,64]{2,1,0:T(8,128)S(1)}, ...), condition=%wide.region_14.14_spmd, body=%wide.region_13.13_spmd.sunk | while | flops 933890 | bytes 6431925 | solution.py:79
  673.9 176.2 %while.331 = (s32[]{:T(128)}, f32[16,128]{1,0:T(8,128)}, f32[16,128,64]{2,1,0:T(8,128)S(1)}, f32[16,128,64]{2,1,0:T(8,128)}, f32[16,128,64]{2,1,0:T(8,128)}, /*i...) while((s32[]{:T(128)}, f32[16,128]{1,0:T(8,128)}, ...), condition=%wide.region_21.21_spmd.clone, body=%wide.region_15.20_spmd.clone.sunk | while | flops 2236420 | bytes 5112892 | solution.py:79
  863.6 124.2 %while.332 = (s32[]{:T(128)}, f32[16,128]{1,0:T(8,128)S(1)}, f32[16,128,64]{2,1,0:T(8,128)S(1)}, f32[16,128,64]{2,1,0:T(8,128)S(1)}, f32[16,128,64]{2,1,0:T(8,12...) while((s32[]{:T(128)}, f32[16,128]{1,0:T(8,128)S(1)}, ...), condition=%wide.region_27.27_spmd.clone, body=%wide.region_22.26_spmd.clone.sunk | while | flops 1975300 | bytes 5907435 | solution.py:61
  1005.0 8.1 broadcast.507.clone
  1013.1 8.0 broadcast.507.clone.1
  1039.1 103.2 %while.329 = (s32[]{:T(128)}, f32[16,128,64]{2,1,0:T(8,128)S(1)}, f32[16,128,64]{2,1,0:T(8,128)S(1)}, f32[16,1,128,64]{3,2,1,0:T(8,128)}, f32[16,16,128,64]{3,2,...) while((s32[]{:T(128)}, f32[16,128,64]{2,1,0:T(8,128)S(1)}, ...), condition=%wide.region_12.12_spmd.clone, body=%wide.region_11.11_spmd.clone.sunk | while | flops 1589251 | bytes 7847620 | solution.py:61
  1147.2 10.4 pad.1161
  1164.6 8.0 broadcast.507
  1180.5 7.9 broadcast.507.clone.5
  1199.8 151.3 %while.330 = (s32[]{:T(128)}, f32[16,128,64]{2,1,0:T(8,128)S(1)}, f32[16,16,128,64]{3,2,1,0:T(8,128)}, f32[16,16,1,64]{3,2,1,0:T(1,128)}, f32[16,1,128,64]{3,2,1...) while((s32[]{:T(128)}, f32[16,128,64]{2,1,0:T(8,128)S(1)}, ...), condition=%wide.region_14.14_spmd, body=%wide.region_13.13_spmd.sunk | while | flops 933890 | bytes 6431925 | solution.py:79
  1354.7 176.2 %while.331 = (s32[]{:T(128)}, f32[16,128]{1,0:T(8,128)}, f32[16,128,64]{2,1,0:T(8,128)S(1)}, f32[16,128,64]{2,1,0:T(8,128)}, f32[16,128,64]{2,1,0:T(8,128)}, /*i...) while((s32[]{:T(128)}, f32[16,128]{1,0:T(8,128)}, ...), condition=%wide.region_21.21_spmd.clone, body=%wide.region_15.20_spmd.clone.sunk | while | flops 2236420 | bytes 5112892 | solution.py:79
  1544.4 124.2 %while.332 = (s32[]{:T(128)}, f32[16,128]{1,0:T(8,128)S(1)}, f32[16,128,64]{2,1,0:T(8,128)S(1)}, f32[16,128,64]{2,1,0:T(8,128)S(1)}, f32[16,128,64]{2,1,0:T(8,12...) while((s32[]{:T(128)}, f32[16,128]{1,0:T(8,128)S(1)}, ...), condition=%wide.region_27.27_spmd.clone, body=%wide.region_22.26_spmd.clone.sunk | while | flops 1975300 | bytes 5907435 | solution.py:61
  1685.8 8.1 broadcast.507.clone
  1693.8 8.0 broadcast.507.clone.1
  1719.8 103.2 %while.329 = (s32[]{:T(128)}, f32[16,128,64]{2,1,0:T(8,128)S(1)}, f32[16,128,64]{2,1,0:T(8,128)S(1)}, f32[16,1,128,64]{3,2,1,0:T(8,128)}, f32[16,16,128,64]{3,2,...) while((s32[]{:T(128)}, f32[16,128,64]{2,1,0:T(8,128)S(1)}, ...), condition=%wide.region_12.12_spmd.clone, body=%wide.region_11.11_spmd.clone.sunk | while | flops 1589251 | bytes 7847620 | solution.py:61
  1828.0 10.4 pad.1161
  1845.4 8.0 broadcast.507
  1861.2 7.9 broadcast.507.clone.5
  1880.6 151.3 %while.330 = (s32[]{:T(128)}, f32[16,128,64]{2,1,0:T(8,128)S(1)}, f32[16,16,128,64]{3,2,1,0:T(8,128)}, f32[16,16,1,64]{3,2,1,0:T(1,128)}, f32[16,1,128,64]{3,2,1...) while((s32[]{:T(128)}, f32[16,128,64]{2,1,0:T(8,128)S(1)}, ...), condition=%wide.region_14.14_spmd, body=%wide.region_13.13_spmd.sunk | while | flops 933890 | bytes 6431925 | solution.py:79
  2035.4 176.2 %while.331 = (s32[]{:T(128)}, f32[16,128]{1,0:T(8,128)}, f32[16,128,64]{2,1,0:T(8,128)S(1)}, f32[16,128,64]{2,1,0:T(8,128)}, f32[16,128,64]{2,1,0:T(8,128)}, /*i...) while((s32[]{:T(128)}, f32[16,128]{1,0:T(8,128)}, ...), condition=%wide.region_21.21_spmd.clone, body=%wide.region_15.20_spmd.clone.sunk | while | flops 2236420 | bytes 5112892 | solution.py:79
  2225.1 124.2 %while.332 = (s32[]{:T(128)}, f32[16,128]{1,0:T(8,128)S(1)}, f32[16,128,64]{2,1,0:T(8,128)S(1)}, f32[16,128,64]{2,1,0:T(8,128)S(1)}, f32[16,128,64]{2,1,0:T(8,12...) while((s32[]{:T(128)}, f32[16,128]{1,0:T(8,128)S(1)}, ...), condition=%wide.region_27.27_spmd.clone, body=%wide.region_22.26_spmd.clone.sunk | while | flops 1975300 | bytes 5907435 | solution.py:61
  2363.6 72.7 %all-reduce.89 = bf16[3,1024,96]{2,0,1:T(4,128)(2,1)} all-reduce(f32[3,1024,96]{2,0,1:T(4,128)S(1)} %copy.268), channel_id=2, replica_groups=mesh['seq'=16,'row'=2] {'seq'}, use_global_device_ids=true, to_apply=%region_29.30.clone | all-reduce | flops 294912 | bytes 1769472
  2438.2 200.2 %while.321 = (s32[]{:T(128)}, f32[3,1024,128]{2,1,0:T(8,128)}, f32[3,1024,128]{2,1,0:T(8,128)}, f32[3,1024,128]{2,1,0:T(8,128)}, f32[3,1024,16]{1,2,0:T(8,128)},...) while((s32[]{:T(128)}, f32[3,1024,128]{2,1,0:T(8,128)}, ...), condition=%wide.region_9.10_spmd, body=%wide.region_3.9_spmd.sunk | while | flops 3090439 | bytes 29768312 | solution.py:90
  2443.4 28.1 while.327
  2476.2 27.5 while.328
  2510.1 28.1 while.327
  2543.0 27.5 while.328
  2576.8 28.1 while.327
  2609.7 27.5 while.328
  2641.9 17.1 all-to-all-start.1
  2660.0 35.9 %all_gather.15 = bf16[3,1024,96]{2,1,0:T(8,128)(2,1)S(1)} all-gather(bf16[3,64,96]{2,1,0:T(8,128)(2,1)S(1)} %copy.281), channel_id=1, replica_groups=mesh['seq'=16,'row'=2] {'seq'}, dimensions={1}, use_global_device_ids=true | all-gather | bytes 626688 | tf_op jit(solution)/shard_map/all_gather | solution.py:185
  2720.3 9.2 copy.273
  2734.9 34.2 %all_to_all.45 = bf16[3,1024,128]{2,0,1:T(4,128)(2,1)S(1)} all-to-all(bf16[3,1024,128]{2,0,1:T(4,128)(2,1)S(1)} %copy.270), channel_id=1, replica_groups=mesh['seq'=16,'row'=2] {'seq'}, dimensions={1} | all-to-all | bytes 1572864 | tf_op jit(solution)/shard_map/all_to_all | solution.py:199
  2770.3 8.3 convolution_bitcast_fusion
  2786.0 44.0 %all-reduce.81 = f32[1024]{0:T(1024)S(1)} all-reduce(f32[1024]{0:T(1024)S(1)} %get-tuple-element.2319), channel_id=3, replica_groups=mesh['seq'=16,'row'=2] {'seq','row'}, use_global_device_ids=true, to_apply=%region_32.33.clone | all-reduce | flops 1024 | bytes 8192
  2836.3 78.8 %reduce-scatter.7.cloned.1.call-done = f32[32,2048]{1,0:T(8,128)} async-done(((f32[1024,2048]{1,0:T(8,128)}), f32[32,2048]{1,0:T(8,128)}) %reduce-scatter.7.cloned.1.call-update) | async-done | bytes 262160
  2915.1 360.9 %reduce-scatter.5.cloned.1.call-done = f32[128,1024]{1,0:T(8,128)} async-done(((f32[4096,1024]{1,0:T(8,128)}), f32[128,1024]{1,0:T(8,128)}) %reduce-scatter.5.cloned.1.call-update) | async-done | bytes 524304 | tf_op jit(solution)/shard_map/reduce_scatter | solution.py:212
  (3568 shorter events, 2252.3 us)
Async XLA Ops:
  7.2 220.9 %copy-start = (bf16[128,96]{0,1:T(8,128)(2,1)S(1)}, bf16[128,96]{0,1:T(8,128)(2,1)}, u32[]{:S(2)}) copy-start(bf16[128,96]{0,1:T(8,128)(2,1)} %param.37) | copy-start | bytes 73732
  7.2 82.7 %all-gather.3.cloned.1.call-start = ((), (), s32[]{:S(2)}) async-start(), calls=%async_computation.6 | async-start | bytes 8650752 | tf_op jit(solution)/shard_map/all_gather | solution.py:113
  7.9 145.1 %all-gather.5.cloned.1.call-start = ((), (), s32[]{:S(2)}) async-start(), calls=%async_computation.7 | async-start | bytes 4325376 | tf_op jit(solution)/shard_map/all_gather | solution.py:114
  51.0 45.3 %copy-start.77 = (f32[1024]{0:T(1024)}, f32[1024]{0:T(1024)S(1)}, u32[]{:S(2)}) copy-start(f32[1024]{0:T(1024)S(1)} %convert_element_type.128) | copy-start | bytes 12292
  52.2 44.1 %copy-start.85 = (f32[3,64]{1,0:T(4,128)}, f32[3,64]{1,0:T(4,128)S(1)}, u32[]{:S(2)}) copy-start(f32[3,64]{1,0:T(4,128)S(1)} %add_rsqrt_fusion) | copy-start | bytes 2308
  96.3 75.5 %copy-start.38 = (f32[3,64,4096]{2,1,0:T(8,128)}, f32[3,64,4096]{2,1,0:T(8,128)S(1)}, u32[]{:S(2)}) copy-start(f32[3,64,4096]{2,1,0:T(8,128)S(1)} %fusion.41) | copy-start | bytes 9437188
  166.2 23.4 all-to-all-start.2
  175.6 20.4 copy-start.103
  175.7 20.4 copy-start.107
  175.7 20.4 copy-start.104
  175.7 20.5 copy-start.108
  175.7 21.0 copy-start.112
  175.7 22.3 copy-start.101
  175.7 22.4 copy-start.89
  189.5 24.3 all-to-all-start
  198.1 22.5 copy-start.93
  198.1 22.4 copy-start.95
  198.2 22.4 copy-start.97
  198.2 22.4 copy-start.99
  198.9 21.7 copy-start.81
  198.9 21.7 copy-start.83
  229.5 62.7 %copy-start.79 = (bf16[64,128]{1,0:T(8,128)(2,1)S(1)}, bf16[64,128]{1,0:T(8,128)(2,1)}, u32[]{:S(2)}) copy-start(bf16[64,128]{1,0:T(8,128)(2,1)} %param.38) | copy-start | bytes 49156
  863.6 124.3 %copy-start.31 = (f32[16,16,64]{2,1,0:T(8,128)S(1)}, f32[16,16,64]{2,1,0:T(8,128)}, u32[]{:S(2)}) copy-start(f32[16,16,64]{2,1,0:T(8,128)} %get-tuple-element.3700) | copy-start | bytes 196612 | tf_op jit(solution)/shard_map/transpose(jvp())/while
  1544.4 124.3 %copy-start.31 = (f32[16,16,64]{2,1,0:T(8,128)S(1)}, f32[16,16,64]{2,1,0:T(8,128)}, u32[]{:S(2)}) copy-start(f32[16,16,64]{2,1,0:T(8,128)} %get-tuple-element.3700) | copy-start | bytes 196612 | tf_op jit(solution)/shard_map/transpose(jvp())/while
  2225.1 124.3 %copy-start.31 = (f32[16,16,64]{2,1,0:T(8,128)S(1)}, f32[16,16,64]{2,1,0:T(8,128)}, u32[]{:S(2)}) copy-start(f32[16,16,64]{2,1,0:T(8,128)} %get-tuple-element.3700) | copy-start | bytes 196612 | tf_op jit(solution)/shard_map/transpose(jvp())/while
  2363.6 72.7 %copy-start.74 = (f32[16,128]{1,0:T(8,128)S(1)}, f32[16,128]{1,0:T(8,128)}, u32[]{:S(2)}) copy-start(f32[16,128]{1,0:T(8,128)} %get-tuple-element.1515) | copy-start | bytes 24580
  2363.6 72.7 %copy-start.90 = (bf16[16,128]{1,0:T(8,128)(2,1)S(1)}, bf16[16,128]{1,0:T(8,128)(2,1)}, u32[]{:S(2)}) copy-start(bf16[16,128]{1,0:T(8,128)(2,1)} %param.40) | copy-start | bytes 12292
  2438.2 200.2 %copy-start.106 = (f32[128]{0:T(128)S(1)}, f32[128]{0:T(128)}, u32[]{:S(2)}) copy-start(f32[128]{0:T(128)} %convert_element_type.145) | copy-start | bytes 1540
  2641.9 54.0 %copy-start.24 = (f32[3,1024,128]{2,1,0:T(8,128)S(1)}, f32[3,1024,128]{2,1,0:T(8,128)}, u32[]{:S(2)}) copy-start(f32[3,1024,128]{2,1,0:T(8,128)} %copy-done.23) | copy-start | bytes 4718596
  2641.9 54.0 %copy-start.49 = (f32[3,64,16,128]{3,1,2,0:T(8,128)S(1)}, f32[3,64,16,128]{3,1,2,0:T(8,128)}, u32[]{:S(2)}) copy-start(f32[3,64,16,128]{3,1,2,0:T(8,128)} %copy.263) | copy-start | bytes 4718596
  2641.9 54.0 %copy-start.82 = (f32[3,1024]{1,0:T(4,128)S(1)}, f32[3,1024]{1,0:T(4,128)}, u32[]{:S(2)}) copy-start(f32[3,1024]{1,0:T(4,128)} %copy-done.81) | copy-start | bytes 36868
  2641.9 54.0 %copy-start.84 = (f32[3,1024]{1,0:T(4,128)S(1)}, f32[3,1024]{1,0:T(4,128)}, u32[]{:S(2)}) copy-start(f32[3,1024]{1,0:T(4,128)} %copy-done.83) | copy-start | bytes 36868
  2641.9 63.2 %all-to-all-start.1 = ((bf16[3,1024,128]{2,0,1:T(4,128)(2,1)}), bf16[3,1024,128]{2,0,1:T(4,128)(2,1)}, u32[]{:S(2)}, u32[]{:S(2)}) async-start(bf16[3,1024,128]{2,0,1:T(4,128)(2,1)} %copy.264), calls=%async_computation.1 | async-start | bytes 2097152 | tf_op jit(solution)/shard_map/all_to_all | solution.py:159
  2659.1 119.6 %all-reduce.87.cloned.1.call-start = ((), (), s32[]{:S(2)}) async-start(), calls=%async_computation.10 | async-start | bytes 189440 | tf_op jit(solution)/shard_map/psum | solution.py:219
  2696.0 7.1 copy-start.46
  2696.0 7.1 copy-start.52
  2696.0 8.0 copy-start.26
  2705.1 210.0 %reduce-scatter.7.cloned.1.call-start = ((), (), s32[]{:S(2)}) async-start(), calls=%async_computation.9 | async-start | bytes 8650752
  2729.6 546.4 %reduce-scatter.5.cloned.1.call-start = ((), (), s32[]{:S(2)}) async-start(), calls=%async_computation.8 | async-start | bytes 17301504 | tf_op jit(solution)/shard_map/reduce_scatter | solution.py:212
  2780.5 50.1 %copy-start.71 = (bf16[3,64,1024]{2,1,0:T(8,128)(2,1)S(1)}, bf16[3,64,1024]{2,1,0:T(8,128)(2,1)}, u32[]{:S(2)}) copy-start(bf16[3,64,1024]{2,1,0:T(8,128)(2,1)} %param.30) | copy-start | bytes 1179652
  2786.0 45.8 %copy-start.67 = (bf16[3,64,2048]{2,1,0:T(8,128)(2,1)S(1)}, bf16[3,64,2048]{2,1,0:T(8,128)(2,1)}, u32[]{:S(2)}) copy-start(bf16[3,64,2048]{2,1,0:T(8,128)(2,1)} %copy-done.66) | copy-start | bytes 2359300
  2831.8 444.3 %copy-start.102 = (f32[4,128]{1,0:T(4,128)S(1)}, f32[4,128]{1,0:T(4,128)}, u32[]{:S(2)}) copy-start(f32[4,128]{1,0:T(4,128)} %get-tuple-element.4322) | copy-start | bytes 6148
  2831.8 444.9 %copy-start.111 = (f32[128]{0:T(128)S(1)}, f32[128]{0:T(128)}, u32[]{:S(2)}) copy-start(f32[128]{0:T(128)} %get-tuple-element.4323) | copy-start | bytes 1540
  2831.8 445.4 %copy-start.87 = (f32[128,96]{0,1:T(8,128)S(1)}, f32[128,96]{0,1:T(8,128)}, u32[]{:S(2)}) copy-start(f32[128,96]{0,1:T(8,128)} %get-tuple-element.4324) | copy-start | bytes 147460
  2831.8 446.0 %copy-start.88 = (f32[64,128]{1,0:T(8,128)S(1)}, f32[64,128]{1,0:T(8,128)}, u32[]{:S(2)}) copy-start(f32[64,128]{1,0:T(8,128)} %get-tuple-element.4325) | copy-start | bytes 98308
  2831.8 446.6 %copy-start.110 = (f32[128]{0:T(128)S(1)}, f32[128]{0:T(128)}, u32[]{:S(2)}) copy-start(f32[128]{0:T(128)} %get-tuple-element.4326) | copy-start | bytes 1540
  2831.8 447.1 %copy-start.92 = (f32[16,128]{1,0:T(8,128)S(1)}, f32[16,128]{1,0:T(8,128)}, u32[]{:S(2)}) copy-start(f32[16,128]{1,0:T(8,128)} %get-tuple-element.4327) | copy-start | bytes 24580
  2831.8 447.7 %copy-start.109 = (f32[128]{0:T(128)S(1)}, f32[128]{0:T(128)}, u32[]{:S(2)}) copy-start(f32[128]{0:T(128)} %get-tuple-element.4328) | copy-start | bytes 1540
  (274 other events, 439.8 us)
Sparse Core Ops, SparseCore 0:
  11.1 78.7 all-gather.2
  92.8 60.1 all-gather.4
  2705.2 22.6 all-reduce.86
  2730.6 184.4 reduce-scatter.6
  2917.8 358.1 reduce-scatter.4
where the time goes:
time: 3340 us; the launch traced here: 3290 us
  other arithmetic  1270 us (38%)
  local copies, waits for them, and re-layouts  1050 us (31%)
  waiting for transfers between devices  555 us (17%)
  blocking collectives  290 us (9%)
  matrix products  44.9 us (1%)
    dynamic_update_slice x240, other arithmetic, block_scan(): lax.scan(local_pass, (empty_state, jnp.ones_like(empty_state)), (dt_q, x_...  420 us
    reduce_scatter x1, waiting for transfers between devices, local(): lax.psum_scatter(grad_in_proj, ('seq', 'row'), scatter_dimension=0, tiled...  361 us
    mul x144, other arithmetic, local_pass(): return ((state_now, decay_now * product), None)  240 us
    another operation x77, local copies, waits for them, and re-layouts  232 us
    mul x192, other arithmetic, decay_at(): dt_now[None, :, :] * decay_rates[:, :, None]  167 us
    unnamed x3, blocking collectives  158 us
    reduce_sum x48, other arithmetic, full_pass(): b_now[:, None, :] * (dt_now * x_now)[None, :, :]  152 us
    dynamic_update_slice x240, local copies, waits for them, and re-layouts, block_scan(): lax.scan(local_pass, (empty_state, jnp.ones_like(empty_state)), (dt_q, x_...  150 us
  transfers between devices with their start and end apart: 8, of which 6 were waited for; matrix products, arithmetic and copies ran while one was open for 3% of the time, Pallas kernels for 0%

commit v1 on v0

--- a/solution.py
+++ b/solution.py
@@ -3,16 +3,963 @@
 import jax
 import jax.numpy as jnp
 from jax import lax
+from jax.experimental import pallas as pl
+from jax.experimental.pallas import tpu as pltpu
 from jax.sharding import PartitionSpec as P
 
 E = 2048
 NSTATE = 16
 CONV = 4
 DT_RANK = 64
-
+MAPS = DT_RANK + 2 * NSTATE
 
 eps_norm = 1e-05
 eps_spread = 1e-06
+BF = jnp.bfloat16
+F32 = jnp.float32
+LOG2E = 1.4426950408889634
+FAR = 1e4
+LANES = 128
+VMEM = 40 << 20
+
+
+def params():
+    return pltpu.CompilerParams(
+        dimension_semantics=("arbitrary", "arbitrary"), vmem_limit_bytes=VMEM
+    )
+
+
+def place_in_doc(starts_ref, row, first, count):
+    pos = lax.broadcasted_iota(jnp.int32, (count, LANES), 0) + first
+    base = jnp.zeros_like(pos)
+    for j in range(1, starts_ref.shape[1]):
+        start = starts_ref[row, j]
+        base = jnp.where(pos >= start, start, base)
+    return pos - base
+
+
+def large(shape, dtype):
+    return pltpu.HBM(shape, dtype)
+
+
+def still(*values):
+    return [pltpu.with_memory_space_constraint(v, pltpu.HBM) for v in values]
+
+
+def sigmoid(v):
+    return 1.0 / (1.0 + jnp.exp2(v * -LOG2E))
+
+
+def silu_slope(v):
+    s = sigmoid(v)
+    return s * (1.0 + v * (1.0 - s))
+
+
+def softplus(v):
+    return jnp.maximum(v, 0.0) + jnp.log1p(jnp.exp2(jnp.abs(v) * -LOG2E))
+
+
+def dot(a, b, dims):
+    return lax.dot_general(a, b, (dims, ((), ())), preferred_element_type=F32)
+
+
+def whole(shape):
+    return pl.BlockSpec(shape, lambda r, c, s, o: (0,) * len(shape))
+
+
+def own_place():
+    s = lax.axis_index("seq")
+    return jnp.stack([s // 4, s // 2 % 2, s % 2]).astype(jnp.int32)
+
+
+def pieces_spec(seg, n, at, row):
+    return pl.BlockSpec(
+        (2, 1, 1, seg, n), lambda r, c, s, o: (0, at(c) ^ o[0], r + row, 0, 0)
+    )
+
+
+def put_pieces(own, value, keep, send):
+    seg = keep.shape[3]
+    first = own[2] == 0
+    for x in range(2):
+        even = value[2 * x * seg : (2 * x + 1) * seg]
+        odd = value[(2 * x + 1) * seg : (2 * x + 2) * seg]
+        keep[x ^ own[1], 0, 0] = jnp.where(first, even, odd).astype(keep.dtype)
+        send[x ^ own[1], 0, 0] = jnp.where(first, odd, even).astype(send.dtype)
+
+
+def take_pieces(own, near, far, out):
+    seg = near.shape[3]
+    first = own[2] == 0
+    for x in range(2):
+        a = near[x ^ own[1], 0, 0].astype(F32)
+        b = far[x ^ own[1], 0, 0].astype(F32)
+        out[2 * x * seg : (2 * x + 1) * seg, :] = jnp.where(first, a, b)
+        out[(2 * x + 1) * seg : (2 * x + 2) * seg, :] = jnp.where(first, b, a)
+
+
+def gate_kernel(*refs):
+    pass
+
+
+def gate(values, others):
+    place = pl.BlockSpec(memory_space=pl.ANY)
+    return pl.pallas_call(
+        gate_kernel,
+        in_specs=[place] * (len(values) + len(others)),
+        out_specs=[place] * len(values),
+        out_shape=[jax.ShapeDtypeStruct(v.shape, v.dtype) for v in values],
+        input_output_aliases={i: i for i in range(len(values))},
+        compiler_params=pltpu.CompilerParams(vmem_limit_bytes=1 << 16),
+        cost_estimate=pl.CostEstimate(flops=1, bytes_accessed=1, transcendentals=0),
+        name="gate",
+    )(*values, *others)
+
+
+PARTS = 6
+
+
+def row_copies(own, parts, slots, sems, row):
+    place = own[0] * 4 + own[1] * 2 + own[2]
+    head = parts[0].shape[1]
+    seg = parts[0].shape[2]
+    copies = []
+    for d in range(16):
+        z, x, core = d >> 2, d >> 1 & 1, d & 1
+        if row < head:
+            piece = parts[core * 2 + x].at[z, row]
+        else:
+            piece = parts[4 + core].at[z, x, row - head]
+        copies.append(
+            pltpu.make_async_copy(
+                piece,
+                slots.at[row, pl.ds(pl.multiple_of((place ^ d) * seg, seg), seg)],
+                sems.at[row, d],
+            )
+        )
+    return copies
+
+
+def bring_row(own, pieces, slots, sems):
+    r, c = pl.program_id(0), pl.program_id(1)
+
+    @pl.when((c == 0) & (r == 0))
+    def _():
+        for row in range(slots.shape[0]):
+            for copy in row_copies(own, pieces, slots, sems, row):
+                copy.start()
+
+    for row in range(slots.shape[0]):
+
+        @pl.when((c == 0) & (r == row))
+        def _(row=row):
+            for copy in row_copies(own, pieces, slots, sems, row):
+                copy.wait()
+
+
+def front_kernel(starts, own, *refs):
+    pieces, refs = refs[:PARTS], refs[PARTS:]
+    gain, weight, conv_w, conv_b, xproj = refs[:5]
+    normed_o, x_o, z_o, conv_o, keep_o, send_o, xs, slots, sems = refs[-9:]
+    r, c = pl.program_id(0), pl.program_id(1)
+    t = x_o.shape[1]
+    ch = conv_w.shape[1]
+    bring_row(own, pieces, slots, sems)
+    res = slots[r, pl.ds(pl.multiple_of(c * t, t), t), :].astype(F32)
+    inv = lax.rsqrt(jnp.mean(res * res, axis=-1, keepdims=True) + eps_norm)
+    normed = (res * inv * gain[...]).astype(BF)
+    normed_o[0] = normed
+    proj = dot(normed, weight[...], ((1,), (1,)))
+    z_o[0] = proj[:, ch:]
+    x_low = proj[:, :ch].astype(BF)
+    x_o[0] = x_low
+
+    @pl.when(c == 0)
+    def _():
+        xs[0:8, :] = jnp.zeros((8, ch), F32)
+
+    @pl.when(c > 0)
+    def _():
+        xs[0:8, :] = xs[t : t + 8, :]
+
+    xs[8 : 8 + t, :] = x_low.astype(F32)
+    place = place_in_doc(starts, r, c * t, t)
+    pre = conv_b[...] + conv_w[CONV - 1 : CONV, :] * xs[8 : 8 + t, :]
+    for k in range(1, CONV):
+        lag = conv_w[CONV - 1 - k : CONV - k, :] * xs[8 - k : 8 - k + t, :]
+        pre = pre + jnp.where(place >= k, lag, 0.0)
+    conv = (pre * sigmoid(pre)).astype(BF)
+    conv_o[0] = conv
+    put_pieces(own, dot(conv, xproj[...], ((1,), (0,))), keep_o, send_o)
+
+
+def front(after, starts, own, pieces, gain, weight, conv_w, conv_b, xproj):
+    _, _, seg, width = pieces[0].shape
+    rows = starts.shape[0]
+    ch = conv_w.shape[1]
+    length = 16 * seg
+    t = 4 * seg
+    tok = lambda n: pl.BlockSpec((1, t, n), lambda r, c, s, o: (r, c, 0))
+    piece = pieces_spec(seg, MAPS, lambda c: c, 0)
+    return pl.pallas_call(
+        front_kernel,
+        grid_spec=pltpu.PrefetchScalarGridSpec(
+            num_scalar_prefetch=2,
+            grid=(rows, length // t),
+            in_specs=[
+                *[pl.BlockSpec(memory_space=pl.ANY)] * PARTS,
+                whole(gain.shape),
+                whole(weight.shape),
+                whole(conv_w.shape),
+                whole(conv_b.shape),
+                whole(xproj.shape),
+                *[pl.BlockSpec(memory_space=pl.ANY)] * len(after),
+            ],
+            out_specs=[tok(width), tok(ch), tok(ch), tok(ch), piece, piece],
+            scratch_shapes=[
+                pltpu.VMEM((t + 8, ch), F32),
+                pltpu.VMEM((rows, length, width), BF),
+                pltpu.SemaphoreType.DMA((rows, 16)),
+            ],
+        ),
+        out_shape=[
+            large((rows, length, width), BF),
+            large((rows, length, ch), BF),
+            large((rows, length, ch), F32),
+            large((rows, length, ch), BF),
+            jax.ShapeDtypeStruct((2, 4, rows, seg, MAPS), F32),
+            jax.ShapeDtypeStruct((2, 4, rows, seg, MAPS), F32),
+        ],
+        compiler_params=params(),
+        cost_estimate=pl.CostEstimate(flops=1, bytes_accessed=1, transcendentals=0),
+        name="front",
+    )(starts, own, *pieces, gain, weight, conv_w, conv_b, xproj, *after)
+
+
+def maps_across(dtbc):
+    pick = lax.broadcasted_iota(jnp.int32, (2 * NSTATE, MAPS), 0) + DT_RANK
+    pick = (pick == lax.broadcasted_iota(jnp.int32, (2 * NSTATE, MAPS), 1)).astype(BF)
+    return dot(pick, dtbc, ((1,), (1,)))
+
+
+def forward_kernel(
+    starts, own, near, far, dtproj, dtbias, decay, skip, conv, z, stats_i, *refs, row,
+):
+    (
+        gated_o, y_o, states_o, last_o, stats_o,
+        state, dtk_s, dtx_s, y_s, across_s, low_s,
+    ) = refs[-11:]
+    r, c = pl.program_id(0), pl.program_id(1)
+    t, ch = conv.shape[1], conv.shape[2]
+
+    @pl.when(c == 0)
+    def _():
+        state[...] = jnp.zeros_like(state)
+
+    @pl.when((c == 0) & (r == 0))
+    def _():
+        stats_o[...] = stats_i[...]
+
+    rate = -LOG2E * jnp.exp(decay[...])
+    take_pieces(own, near, far, low_s)
+    low = low_s[...].astype(BF)
+    dt = softplus(dot(low[:, :DT_RANK], dtproj[...], ((1,), (0,))) + dtbias[...])
+    off = jnp.log(dt) - jnp.log(softplus(dtbias[...]))
+    stats_o[0:1, :] += jnp.sum(off, axis=0, keepdims=True)
+    stats_o[1:2, :] += jnp.sum(off * off, axis=0, keepdims=True)
+    x = conv[0].astype(F32)
+    place = place_in_doc(starts, r + row, c * t, t)
+    dtk_s[...] = jnp.where(place >= 1, dt, FAR)
+    dtx_s[...] = dt * x
+    across_s[...] = maps_across(low)
+
+    def some(block, s):
+        base = pl.multiple_of(block * LANES, LANES)
+        both = across_s[:, pl.ds(base, LANES)]
+        b, cm = both[:NSTATE], both[NSTATE:]
+        for i in range(LANES):
+            a = jnp.exp2(dtk_s[pl.ds(base + i, 1), :] * rate)
+            states_o[0, base + i] = s
+            u = dtx_s[pl.ds(base + i, 1), :] * jnp.broadcast_to(b[:, i : i + 1], (NSTATE, ch))
+            s = a * s + u
+            ys = s * jnp.broadcast_to(cm[:, i : i + 1], (NSTATE, ch))
+            y_s[pl.ds(base * 8 + i * 8, 8), :] = ys[:8] + ys[8:]
+        return s
+
+    s = lax.fori_loop(0, t // LANES, some, state[...])
+    state[...] = s
+    last_o[0] = s
+    y = y_s[pl.ds(0, t, stride=8), :]
+    for j in range(1, 8):
+        y = y + y_s[pl.ds(j, t, stride=8), :]
+    y_low = (y + skip[...] * x).astype(BF)
+    y_o[0] = y_low
+    zz = z[0]
+    gated_o[0] = (y_low.astype(F32) * (zz * sigmoid(zz))).astype(BF)
+
+
+def forward_scan(
+    row, rows, after, so_far, starts, own, near, far, dtproj, dtbias, decay, skip, conv, z
+):
+    conv, z = still(conv, z)
+    rows_all, length, ch = conv.shape
+    done, sums_so_far = so_far
+    fixed = 11
+    t = length // 4
+    seg = t // 4
+    tok = lambda n: pl.BlockSpec((1, t, n), lambda r, c, s, o: (r + row, c, 0))
+    piece = pieces_spec(seg, MAPS, lambda c: c, row)
+    return pl.pallas_call(
+        partial(forward_kernel, row=row),
+        grid_spec=pltpu.PrefetchScalarGridSpec(
+            num_scalar_prefetch=2,
+            grid=(rows, length // t),
+            in_specs=[
+                piece,
+                piece,
+                whole(dtproj.shape),
+                whole(dtbias.shape),
+                whole(decay.shape),
+                whole(skip.shape),
+                tok(ch),
+                tok(ch),
+                whole((8, ch)),
+                *[pl.BlockSpec(memory_space=pl.ANY)] * (len(done) + len(after)),
+            ],
+            out_specs=[
+                tok(ch),
+                tok(ch),
+                pl.BlockSpec((1, t, NSTATE, ch), lambda r, c, s, o: (r + row, c, 0, 0)),
+                pl.BlockSpec((1, NSTATE, ch), lambda r, c, s, o: (r + row, 0, 0)),
+                whole((8, ch)),
+            ],
+            scratch_shapes=[
+                pltpu.VMEM((NSTATE, ch), F32),
+                pltpu.VMEM((t, ch), F32),
+                pltpu.VMEM((t, ch), F32),
+                pltpu.VMEM((t * 8, ch), F32),
+                pltpu.VMEM((2 * NSTATE, t), F32),
+                pltpu.VMEM((t, MAPS), F32),
+            ],
+        ),
+        out_shape=[
+            large((rows_all, length, ch), BF),
+            large((rows_all, length, ch), BF),
+            large((rows_all, length, NSTATE, ch), F32),
+            jax.ShapeDtypeStruct((rows_all, NSTATE, ch), F32),
+            jax.ShapeDtypeStruct((8, ch), F32),
+        ],
+        input_output_aliases={fixed + i: i for i in range(len(done))},
+        compiler_params=params(),
+        cost_estimate=pl.CostEstimate(flops=1, bytes_accessed=1, transcendentals=0),
+        name="forward_scan",
+    )(
+        starts, own, near, far, dtproj, dtbias, decay, skip, conv, z, *sums_so_far, *done, *after
+    )
+
+
+def backward_kernel(
+    starts, own, near, far, dtproj, dtbias, decay, skip, conv, z, y, gg, states, last, sums,
+    gdtproj_i, misc_i, *refs, row,
+):
+    (
+        ggate_o, gxs_o, keep_o, send_o, gdtproj_o, misc_o,
+        back, after, dtk_s, dt_s, dtx_s, gy_s, p1_s, p2_s, gb_s, gc_s, across_s, low_s,
+    ) = refs[-18:]
+    r, c = pl.program_id(0), pl.program_id(1)
+    chunks = pl.num_programs(1)
+    t, ch = conv.shape[1], conv.shape[2]
+
+    @pl.when(c == 0)
+    def _():
+        back[...] = jnp.zeros_like(back)
+        after[...] = last[0]
+
+    @pl.when((c == 0) & (r == 0))
+    def _():
+        gdtproj_o[...] = gdtproj_i[...]
+        misc_o[...] = misc_i[...]
+
+    neg = -jnp.exp(decay[...])
+    rate = LOG2E * neg
+    take_pieces(own, near, far, low_s)
+    low = low_s[...].astype(BF)
+    pre = dot(low[:, :DT_RANK], dtproj[...], ((1,), (0,))) + dtbias[...]
+    dt = softplus(pre)
+    x = conv[0].astype(F32)
+    place = place_in_doc(starts, r + row, (chunks - 1 - c) * t, t)
+    dtk_s[...] = jnp.where(place >= 1, dt, FAR)
+    dt_s[...] = dt
+    dtx_s[...] = dt * x
+    zz = z[0]
+    ggv = gg[0]
+    sg = sigmoid(zz)
+    gy = (ggv * (zz * sg)).astype(BF).astype(F32)
+    ggate_o[0] = (ggv * y[0].astype(F32) * (sg * (1.0 + zz * (1.0 - sg)))).astype(BF)
+    gy_s[...] = gy
+    across_s[...] = maps_across(low)
+
+    def some(block, carry):
+        h, s_next, acc = carry
+        base = pl.multiple_of(t - LANES - block * LANES, LANES)
+        both = across_s[:, pl.ds(base, LANES)]
+        b, cm = both[:NSTATE], both[NSTATE:]
+        for i in range(LANES - 1, -1, -1):
+            at = base + i
+            gyr = gy_s[pl.ds(at, 1), :]
+            g = gyr * jnp.broadcast_to(cm[:, i : i + 1], (NSTATE, ch)) + h
+            h = jnp.exp2(dtk_s[pl.ds(at, 1), :] * rate) * g
+            s_prev = states[0, at]
+            q = h * s_prev
+            acc = acc + q * dt_s[pl.ds(at, 1), :]
+            aq = q * neg
+            bg = g * jnp.broadcast_to(b[:, i : i + 1], (NSTATE, ch))
+            p2_s[pl.ds(base * 8 + i * 8, 8), :] = aq[:8] + aq[8:]
+            p1_s[pl.ds(base * 8 + i * 8, 8), :] = bg[:8] + bg[8:]
+            gb_s[pl.ds(base * NSTATE + i * NSTATE, NSTATE), :] = g * dtx_s[pl.ds(at, 1), :]
+            gc_s[pl.ds(base * NSTATE + i * NSTATE, NSTATE), :] = gyr * s_next
+            s_next = s_prev
+        return h, s_next, acc
+
+    h, s_next, acc = lax.fori_loop(
+        0, t // LANES, some, (back[...], after[...], jnp.zeros((NSTATE, ch), F32))
+    )
+    back[...] = h
+    after[...] = s_next
+    p1 = p1_s[pl.ds(0, t, stride=8), :]
+    p2 = p2_s[pl.ds(0, t, stride=8), :]
+    for j in range(1, 8):
+        p1 = p1 + p1_s[pl.ds(j, t, stride=8), :]
+        p2 = p2 + p2_s[pl.ds(j, t, stride=8), :]
+    gxs_o[0] = dt * p1 + skip[...] * gy
+    gpre = ((p2 + x * p1) * sigmoid(pre)).astype(BF)
+    gdtproj_o[...] += dot(low[:, :DT_RANK], gpre, ((0,), (0,)))
+    misc_o[0:NSTATE, :] += neg * acc
+    misc_o[NSTATE : NSTATE + 1, :] += jnp.sum(gpre.astype(F32), axis=0, keepdims=True)
+    misc_o[NSTATE + 1 : NSTATE + 2, :] += jnp.sum(gy * x, axis=0, keepdims=True)
+    total = dot(gpre, sums[0:ch, :], ((1,), (0,)))
+    for n in range(NSTATE):
+        one = gb_s[pl.ds(n, t, stride=NSTATE), :].astype(BF)
+        two = gc_s[pl.ds(n, t, stride=NSTATE), :].astype(BF)
+        total = total + dot(one, sums[(1 + n) * ch : (2 + n) * ch, :], ((1,), (0,)))
+        total = total + dot(
+            two, sums[(1 + NSTATE + n) * ch : (2 + NSTATE + n) * ch, :], ((1,), (0,))
+        )
+    put_pieces(own, total, keep_o, send_o)
+
+
+def sum_columns(dtproj):
+    ch = dtproj.shape[1]
+    which = jnp.arange(2 * NSTATE * ch) // ch + DT_RANK
+    ones = (which[:, None] == jnp.arange(MAPS)[None, :]).astype(BF)
+    wide = jnp.pad(dtproj.T, ((0, 0), (0, 2 * NSTATE)))
+    return jnp.concatenate([wide, ones], axis=0)
+
+
+def backward_scan(
+    row, rows, after, so_far, starts, own, near, far, dtproj, dtbias, decay, skip, conv, z, y, gg,
+    states, last, sums,
+):
+    conv, z, y, gg, states = still(conv, z, y, gg, states)
+    rows_all, length, ch = conv.shape
+    done, sums_so_far = so_far
+    t = length // 4
+    seg = t // 4
+    chunks = length // t
+    tok = lambda n: pl.BlockSpec((1, t, n), lambda r, c, s, o: (r + row, chunks - 1 - c, 0))
+    piece = pieces_spec(seg, MAPS, lambda c: chunks - 1 - c, row)
+    fixed = 17
+    return pl.pallas_call(
+        partial(backward_kernel, row=row),
+        grid_spec=pltpu.PrefetchScalarGridSpec(
+            num_scalar_prefetch=2,
+            grid=(rows, chunks),
+            in_specs=[
+                piece,
+                piece,
+                whole(dtproj.shape),
+                whole(dtbias.shape),
+                whole(decay.shape),
+                whole(skip.shape),
+                tok(ch),
+                tok(ch),
+                tok(ch),
+                tok(ch),
+                pl.BlockSpec((1, t, NSTATE, ch), lambda r, c, s, o: (r + row, chunks - 1 - c, 0, 0)),
+                pl.BlockSpec((1, NSTATE, ch), lambda r, c, s, o: (r + row, 0, 0)),
+                whole(sums.shape),
+                whole((DT_RANK, ch)),
+                whole((24, ch)),
+                *[pl.BlockSpec(memory_space=pl.ANY)] * (len(done) + len(after)),
+            ],
+            out_specs=[
+                tok(ch),
+                tok(ch),
+                piece,
+                piece,
+                whole((DT_RANK, ch)),
+                whole((24, ch)),
+            ],
+            scratch_shapes=[
+                pltpu.VMEM((NSTATE, ch), F32),
+                pltpu.VMEM((NSTATE, ch), F32),
+                pltpu.VMEM((t, ch), F32),
+                pltpu.VMEM((t, ch), F32),
+                pltpu.VMEM((t, ch), F32),
+                pltpu.VMEM((t, ch), F32),
+                pltpu.VMEM((t * 8, ch), F32),
+                pltpu.VMEM((t * 8, ch), F32),
+                pltpu.VMEM((t * NSTATE, ch), F32),
+                pltpu.VMEM((t * NSTATE, ch), F32),
+                pltpu.VMEM((2 * NSTATE, t), F32),
+                pltpu.VMEM((t, MAPS), F32),
+            ],
+        ),
+        out_shape=[
+            large((rows_all, length, ch), BF),
+            large((rows_all, length, ch), F32),
+            jax.ShapeDtypeStruct((2, 4, rows_all, seg, MAPS), F32),
+            jax.ShapeDtypeStruct((2, 4, rows_all, seg, MAPS), F32),
+            jax.ShapeDtypeStruct((DT_RANK, ch), F32),
+            jax.ShapeDtypeStruct((24, ch), F32),
+        ],
+        input_output_aliases={fixed + i: i for i in range(len(done))},
+        compiler_params=params(),
+        cost_estimate=pl.CostEstimate(flops=1, bytes_accessed=1, transcendentals=0),
+        name="backward_scan",
+    )(
+        starts, own, near, far, dtproj, dtbias, decay, skip, conv, z, y, gg, states, last, sums, *sums_so_far, *done, *after,
+    )
+
+
+def tail_kernel(
+    starts, own, near, far, conv, gxs, ggate, x, before, normed, weight, conv_w, conv_b, xproj,
+    gin_i, gxproj_i, misc_i, *refs, row,
+):
+    keep_o, send_o, gin_o, gxproj_o, misc_o, xs, gm_s, low_s = refs[-8:]
+    r, c = pl.program_id(0), pl.program_id(1)
+    chunks = pl.num_programs(1)
+    t, ch = conv.shape[1], conv.shape[2]
+
+    @pl.when((c == 0) & (r == 0))
+    def _():
+        gin_o[...] = gin_i[...]
+        gxproj_o[...] = gxproj_i[...]
+        misc_o[...] = misc_i[...]
+
+    @pl.when(c == 0)
+    def _():
+        gm_s[:, t : t + 8, :] = jnp.zeros((CONV - 1, 8, ch), F32)
+
+    @pl.when(c > 0)
+    def _():
+        gm_s[:, t : t + 8, :] = gm_s[:, 0:8, :]
+
+    xs[0:16, :] = before[0].astype(F32)
+    xs[16 : 16 + t, :] = x[0].astype(F32)
+    place = place_in_doc(starts, r + row, (chunks - 1 - c) * t, t)
+    lags = [xs[16 : 16 + t, :]]
+    pre = conv_b[...] + conv_w[CONV - 1 : CONV, :] * lags[0]
+    for k in range(1, CONV):
+        lags.append(jnp.where(place >= k, xs[16 - k : 16 - k + t, :], 0.0))
+        pre = pre + conv_w[CONV - 1 - k : CONV - k, :] * lags[k]
+    take_pieces(own, near, far, low_s)
+    low = low_s[...].astype(BF)
+    gpre = (gxs[0] + dot(low, xproj[...], ((1,), (1,)))) * silu_slope(pre)
+    gxproj_o[...] += dot(conv[0], low, ((0,), (0,)))
+    gx = conv_w[CONV - 1 : CONV, :] * gpre
+    for k in range(CONV):
+        misc_o[CONV - 1 - k : CONV - k, :] += jnp.sum(gpre * lags[k], axis=0, keepdims=True)
+        if k:
+            gm_s[k - 1, 0:t, :] = jnp.where(place >= k, gpre, 0.0)
+            gx = gx + conv_w[CONV - 1 - k : CONV - k, :] * gm_s[k - 1, k : k + t, :]
+    misc_o[CONV : CONV + 1, :] += jnp.sum(gpre, axis=0, keepdims=True)
+    gproj = jnp.concatenate([gx.astype(BF), ggate[0]], axis=1)
+    gin_o[...] += dot(gproj, normed[0], ((0,), (0,)))
+    put_pieces(own, dot(gproj, weight[...], ((1,), (0,))), keep_o, send_o)
+
+
+def tail(
+    row, rows, after, so_far, starts, own, near, far, conv, gxs, ggate, x, normed, weight, conv_w, conv_b, xproj
+):
+    conv, gxs, ggate, x, normed = still(conv, gxs, ggate, x, normed)
+    _, length, width = normed.shape
+    ch = conv.shape[2]
+    t = length // 4
+    seg = t // 4
+    chunks = length // t
+    tok = lambda n: pl.BlockSpec((1, t, n), lambda r, c, s, o: (r + row, chunks - 1 - c, 0))
+    piece = lambda n, row: pieces_spec(seg, n, lambda c: chunks - 1 - c, row)
+    before = pl.BlockSpec(
+        (1, 16, ch),
+        lambda r, c, s, o: (r + row, jnp.maximum((chunks - 1 - c) * (t // 16) - 1, 0), 0),
+    )
+    return pl.pallas_call(
+        partial(tail_kernel, row=row),
+        grid_spec=pltpu.PrefetchScalarGridSpec(
+            num_scalar_prefetch=2,
+            grid=(rows, chunks),
+            in_specs=[
+                piece(MAPS, row),
+                piece(MAPS, row),
+                tok(ch),
+                tok(ch),
+                tok(ch),
+                tok(ch),
+                before,
+                tok(width),
+                whole(weight.shape),
+                whole(conv_w.shape),
+                whole(conv_b.shape),
+                whole(xproj.shape),
+                whole(weight.shape),
+                whole((ch, MAPS)),
+                whole((8, ch)),
+                *[pl.BlockSpec(memory_space=pl.ANY)] * len(after),
+            ],
+            out_specs=[
+                piece(width, 0),
+                piece(width, 0),
+                whole(weight.shape),
+                whole((ch, MAPS)),
+                whole((8, ch)),
+            ],
+            scratch_shapes=[
+                pltpu.VMEM((t + 16, ch), F32),
+                pltpu.VMEM((CONV - 1, t + 8, ch), F32),
+                pltpu.VMEM((t, MAPS), F32),
+            ],
+        ),
+        out_shape=[
+            large((2, 4, rows, seg, width), BF),
+            large((2, 4, rows, seg, width), BF),
+            jax.ShapeDtypeStruct(weight.shape, F32),
+            jax.ShapeDtypeStruct((ch, MAPS), F32),
+            jax.ShapeDtypeStruct((8, ch), F32),
+        ],
+        compiler_params=params(),
+        cost_estimate=pl.CostEstimate(flops=1, bytes_accessed=1, transcendentals=0),
+        name="tail",
+    )(
+        starts, own, near, far, conv, gxs, ggate, x, x, normed, weight, conv_w, conv_b, xproj, *so_far, *after,
+    )
+
+
+def mix_kernel(own, gated, cols, *refs):
+    keep_o, send_o = refs[-2:]
+    put_pieces(own, dot(gated[0], cols[...], ((1,), (1,))), keep_o, send_o)
+
+
+def mix(row, rows, after, own, gated, cols):
+    (gated,) = still(gated)
+    _, length, ch = gated.shape
+    width = cols.shape[0]
+    t = length // 4
+    seg = t // 4
+    piece = pl.BlockSpec((2, 1, 1, seg, width), lambda r, c, o: (0, c ^ o[0], r, 0, 0))
+    return pl.pallas_call(
+        mix_kernel,
+        grid_spec=pltpu.PrefetchScalarGridSpec(
+            num_scalar_prefetch=1,
+            grid=(rows, length // t),
+            in_specs=[
+                pl.BlockSpec((1, t, ch), lambda r, c, o: (r + row, c, 0)),
+                pl.BlockSpec(cols.shape, lambda r, c, o: (0, 0)),
+                *[pl.BlockSpec(memory_space=pl.ANY)] * len(after),
+            ],
+            out_specs=[piece, piece],
+        ),
+        out_shape=[
+            large((2, 4, rows, seg, width), BF),
+            large((2, 4, rows, seg, width), BF),
+        ],
+        compiler_params=params(),
+        cost_estimate=pl.CostEstimate(flops=1, bytes_accessed=1, transcendentals=0),
+        name="mix",
+    )(own, gated, cols, *after)
+
+
+def turn_kernel(own, *refs):
+    pieces = refs[:PARTS]
+    cols = refs[PARTS]
+    gg_o, gout_o, slots, sems = refs[-4:]
+    r, c = pl.program_id(0), pl.program_id(1)
+    t = gg_o.shape[1]
+    bring_row(own, pieces, slots, sems)
+    part = slots[r, pl.ds(pl.multiple_of(c * t, t), t), :]
+    gout_o[0] = part
+    gg_o[0] = dot(part, cols[...], ((1,), (0,)))
+
+
+def turn(rows, after, own, pieces, cols):
+    _, _, seg, width = pieces[0].shape
+    ch = cols.shape[1]
+    length = 16 * seg
+    t = 4 * seg
+    tok = lambda n: pl.BlockSpec((1, t, n), lambda r, c, o: (r, c, 0))
+    return pl.pallas_call(
+        turn_kernel,
+        grid_spec=pltpu.PrefetchScalarGridSpec(
+            num_scalar_prefetch=1,
+            grid=(rows, length // t),
+            in_specs=[
+                *[pl.BlockSpec(memory_space=pl.ANY)] * PARTS,
+                pl.BlockSpec(cols.shape, lambda r, c, o: (0, 0)),
+                *[pl.BlockSpec(memory_space=pl.ANY)] * len(after),
+            ],
+            out_specs=[tok(ch), tok(width)],
+            scratch_shapes=[
+                pltpu.VMEM((rows, length, width), BF),
+                pltpu.SemaphoreType.DMA((rows, 16)),
+            ],
+        ),
+        out_shape=[
+            large((rows, length, ch), F32),
+            large((rows, length, width), BF),
+        ],
+        compiler_params=params(),
+        cost_estimate=pl.CostEstimate(flops=1, bytes_accessed=1, transcendentals=0),
+        name="turn",
+    )(own, *pieces, cols, *after)
+
+
+def cross(v, bits):
+    return lax.ppermute(v, "seq", [(s, s ^ bits) for s in range(16)])
+
+
+def swap_row(v):
+    return lax.ppermute(v, "row", [(0, 1), (1, 0)])
+
+
+def total_of_all(v):
+    v = v + swap_row(v)
+    for bits in (1, 2, 4, 8):
+        v = v + cross(v, bits)
+    return v
+
+
+def sum_pieces(keep, send, sent, others):
+    (acc,) = gate([keep.astype(F32) + cross(send, 1).astype(F32)], others)
+    acc = acc[0] + cross(acc[1].astype(sent), 2).astype(F32)
+    total = acc[0]
+    for k in (1, 2, 3):
+        total = total + cross(acc[k].astype(sent), 4 * k).astype(F32)
+    return total
+
+
+def spread_pieces(own_piece):
+    line = jnp.stack([own_piece] + [cross(own_piece, 4 * k) for k in (1, 2, 3)])
+    near = jnp.stack([line, cross(line, 2)])
+    return near, cross(near, 1)
+
+
+def gather_start(v, after):
+    head = v.shape[0] - v.shape[0] // 3
+    return gate([v[:head], v[head:]], after)
+
+
+def gather_first(a, b):
+    return a, b, cross_z([a] * 3), cross(b, 2)
+
+
+def gather_pause(a, b, line, across):
+    return jnp.stack([a, *line]), jnp.stack([b, across])
+
+
+def gather_second(a, b):
+    return a, b, cross(a, 2), cross_z([b] * 3)
+
+
+def gather_third(a, b, across, line):
+    a, b = [a, across], jnp.stack([b, *line])
+    return [*a, *[cross(p, 1) for p in a], b, cross(b, 1)]
+
+
+def up(v):
+    return v.astype(F32)
+
+
+class Sum:
+    def __init__(self, keep, send):
+        self.keep, self.near = keep, cross(send, 1)
+        self.head = keep.shape[2] - keep.shape[2] // 3
+
+    def part(self, *at):
+        return up(self.keep[at]) + up(self.near[at])
+
+    def first(self, others):
+        (self.near,) = gate([self.near], others)
+        a, b = slice(0, self.head), slice(self.head, None)
+        sent = [self.part(1, slice(None), a).astype(BF)]
+        sent += [self.part(slice(None), k, b).astype(BF) for k in (1, 2, 3)]
+        self.second_of = [cross(sent[0], 2), *cross_z(sent[1:])]
+        return sent
+
+    def second(self, others):
+        across, *line = gate(self.second_of, others)
+        a, b = slice(0, self.head), slice(self.head, None)
+        sent = [(self.part(0, k, a) + up(across[k])).astype(BF) for k in (1, 2, 3)]
+        sent.append((self.part(1, 0, b) + sum(up(v[1]) for v in line)).astype(BF))
+        self.third_of = [*cross_z(sent[:3]), cross(sent[3], 2)]
+        self.a = self.part(0, 0, a) + up(across[0])
+        self.b = self.part(0, 0, b) + sum(up(v[0]) for v in line)
+        return sent
+
+    def third(self, others):
+        *line, across = gate(self.third_of, others)
+        return jnp.concatenate([self.a + sum(up(v) for v in line), self.b + up(across)])
+
+
+def cross_z(pieces):
+    return [cross(v, 4 * k) for k, v in zip((1, 2, 3), pieces)]
+
+
+def channel_plan(
+    hidden_in, grad_out, doc_starts, norm_gain, in_proj, out_proj, conv_weight, conv_bias,
+    x_proj, dt_proj, dt_bias, decay_log, skip_scale,
+):
+    row_count, seg_len, width = hidden_in.shape
+    shards = lax.axis_size("seq")
+    full_len = seg_len * shards
+    ch = conv_weight.shape[1]
+    first = lax.axis_index("row") == 0
+    both = ("seq", "row")
+    place = 2 * lax.axis_index("seq") + lax.axis_index("row")
+    own = own_place()
+    gain_len = norm_gain.shape[0]
+
+    to_shard = [(i, 2 * (i % shards) + i // shards) for i in range(2 * shards)]
+    mine = lax.ppermute(in_proj, both, to_shard)
+    head = row_count - row_count // 3
+    hid = gather_first(*gate([hidden_in[:head], hidden_in[head:]], []))
+    spot = jnp.zeros((2 * shards, gain_len), F32)
+    spot = lax.dynamic_update_slice(spot, norm_gain.astype(F32)[None], (place, 0))
+    spot = spot + swap_row(spot)
+    *hid, mine, spot = gate([*hid[:2], *hid[2], hid[3], mine, spot + sum(cross_z([spot] * 3))], [])
+    hid = gather_second(*gather_pause(*hid[:2], hid[2:5], hid[5]))
+    other = swap_row(mine)
+    weight = jnp.concatenate([jnp.where(first, mine, other), jnp.where(first, other, mine)])
+    other = swap_row(out_proj)
+    pair = jnp.concatenate([jnp.where(first, out_proj, other), jnp.where(first, other, out_proj)])
+    spot = spot + cross(spot, 1)
+    sent = [grad_out[:head], grad_out[head:]]
+    vectors = [
+        conv_weight.astype(F32),
+        conv_bias.astype(F32)[None],
+        dt_bias.astype(F32)[None],
+        decay_log.astype(F32),
+        skip_scale.astype(F32)[None],
+        sum_columns(dt_proj),
+        x_proj,
+    ]
+    held = gate([*hid[:3], *hid[3], weight, pair, spot, *sent, *vectors], [])
+    hid, (weight, pair, spot, *sent), vectors = held[:6], held[6:11], held[11:]
+    gain_whole = (spot + cross(spot, 2)).reshape(1, width)
+    conv_w, conv_b, dtb, decay, skip, sums, x_proj = vectors
+    hid = gather_third(*hid[:3], hid[3:6])
+    sent = gate(sent, [*hid, gain_whole])
+    gout = gather_first(*sent)
+
+    normed, x, z, conv, keep, send = front(
+        sent, doc_starts, own, hid, gain_whole, weight, conv_w, conv_b, x_proj
+    )
+    keep, send, *gout = gate([keep, send, *gout[:2], *gout[2], gout[3]], [])
+    gout = gather_pause(*gout[:2], gout[2:5], gout[5])
+    low = sum_pieces(keep, send, F32, []).astype(BF)
+    near, far = spread_pieces(low)
+    pair, *gout = gate([pair, *gout], [far])
+    gout = gather_second(*gout)
+    out_cols = lax.all_to_all(pair, "seq", split_axis=1, concat_axis=0, tiled=True)
+
+    gated, y, states, last, stats = forward_scan(
+        0, row_count, [gout[0], gout[1], pair], ([], (jnp.zeros((8, ch), F32),)), doc_starts, own, near, far, dt_proj,
+        dtb, decay, skip, conv, z,
+    )
+    gated, out_cols, *gout = gate([gated, out_cols, *gout[:3], *gout[3]], [])
+    gout = gather_third(*gout[:3], gout[3:])
+    keep, send = mix(0, row_count, [], own, gated, out_cols)
+    keep, send, *gout = gate([keep, send, *gout], [])
+    mixed = Sum(keep, send)
+    gg, gout = turn(row_count, [], own, gout, out_cols)
+    after = mixed.first([gg])
+    back = [], (jnp.zeros((DT_RANK, ch), F32), jnp.zeros((24, ch), F32))
+    for r in range(row_count):
+        out = backward_scan(
+            r, 1, after, back, doc_starts, own, near, far, dt_proj, dtb, decay, skip,
+            conv, z, y, gg, states, last, sums,
+        )
+        back = out[:4], out[4:]
+        after = mixed.second([out[0]]) if r == row_count - 2 else []
+    ggate, gxs, keep, send = back[0]
+    gdtproj, misc = back[1]
+    mixed = mixed.third([gxs])
+    keep, send, gout, gated = gate([keep, send, gout, gated], [mixed])
+    low = sum_pieces(keep, send, BF, []).astype(BF)
+    gout_cols = jnp.einsum("rtd,rtc->dc", gout, gated, preferred_element_type=F32)
+    parts = gout_cols.reshape(shards, 2, width // (2 * shards), ch)
+    keep = jnp.where(first, parts[:, 0], parts[:, 1])
+    send = jnp.where(first, parts[:, 1], parts[:, 0])
+    out_half = (keep + swap_row(send)).astype(BF)
+    near, far = spread_pieces(low)
+    tail_sums = (jnp.zeros(weight.shape, F32), jnp.zeros((ch, MAPS), F32), jnp.zeros((8, ch), F32))
+    keep, send, gin, gxproj, cmisc = tail(
+        0, row_count, [out_half], tail_sums, doc_starts, own, near, far, conv, gxs, ggate, x, normed,
+        weight, conv_w, conv_b, x_proj,
+    )
+    gnormed = Sum(keep, send)
+    grad_gain = jnp.sum(weight.astype(F32) * gin, axis=0) / gain_whole[0]
+    grad_gain = grad_gain.reshape(2 * shards, gain_len)
+    grad_gain = grad_gain + swap_row(grad_gain)
+    grad_gain = grad_gain + cross(grad_gain, 1)
+    keep = jnp.where(first, gin[:ch], gin[ch:])
+    send = jnp.where(first, gin[ch:], gin[:ch])
+    in_half = (keep + swap_row(send.astype(BF)).astype(F32)).astype(BF)
+    small = jnp.concatenate([gdtproj, misc, stats, cmisc, jnp.transpose(gxproj)])
+    small = small + swap_row(small)
+    gnormed.first([])
+    gnormed.second([in_half, small, grad_gain])
+    gnormed = gnormed.third([])
+    grad_gain, in_half, out_half = gate([grad_gain, in_half, out_half], [gnormed])
+    grad_gain = grad_gain + cross(grad_gain, 2)
+    grad_gain = grad_gain + sum(cross_z([grad_gain] * 3))
+    out_share = lax.all_to_all(out_half, "seq", split_axis=0, concat_axis=0, tiled=True)
+    to_owner = [(b, a) for a, b in to_shard]
+    in_share = lax.ppermute(in_half, both, to_owner).astype(F32)
+    out_share = jnp.transpose(out_share.astype(F32), (1, 0, 2)).reshape(width // (2 * shards), E)
+
+    residual = hidden_in.astype(F32)
+    hidden_out = (residual + mixed).astype(BF)
+    inv_rms = lax.rsqrt(jnp.mean(residual * residual, axis=-1, keepdims=True) + eps_norm)
+    scaled = residual * inv_rms
+    grad_scaled = gnormed * gain_whole
+    grad_hidden = grad_out.astype(F32) + inv_rms * (
+        grad_scaled - scaled * jnp.mean(grad_scaled * scaled, axis=-1, keepdims=True)
+    )
+    grad_gain = lax.dynamic_slice(grad_gain, (place, 0), (1, gain_len))[0]
+    gdtproj, misc, stats, cmisc, gxproj = jnp.split(
+        small, [DT_RANK, DT_RANK + 24, DT_RANK + 32, DT_RANK + 40]
+    )
+    token_count = full_len * row_count * 2
+    mean_off = stats[0] / token_count
+    spread = jnp.sqrt(stats[1] / token_count - mean_off * mean_off + eps_spread)
+    centre = jnp.log(jax.nn.softplus(dt_bias.astype(F32)))
+    return (
+        hidden_out,
+        grad_hidden,
+        grad_gain,
+        in_share,
+        out_share,
+        cmisc[:CONV],
+        cmisc[CONV],
+        jnp.transpose(gxproj),
+        gdtproj,
+        misc[NSTATE],
+        misc[:NSTATE],
+        misc[NSTATE + 1],
+        jnp.stack([centre + mean_off, spread]),
+    )
+
+
 block_len = 16
 
 
@@ -32,7 +979,7 @@
     return jnp.pad(values, widths)[:, offset:]
 
 
-def silu_slope(values):
+def slope_of_silu(values):
     logistic = jax.nn.sigmoid(values)
     return logistic * (1.0 + values * (1.0 - logistic))
 
@@ -91,7 +1038,7 @@
     return outputs + skip_full * x_vals
 
 
-def local(
+def token_plan(
     hidden_in,
     grad_out,
     doc_starts,
@@ -167,7 +1114,7 @@
     grad_out_proj = jnp.einsum("rtd,rte->de", grad_out, gated, preferred_element_type=jnp.float32)
     grad_gated = jnp.einsum("rtd,de->rte", grad_out, out_whole, preferred_element_type=jnp.float32)
     grad_y = (grad_gated * gate_act).astype(jnp.bfloat16)
-    grad_gate = (grad_gated * y_token_vals * silu_slope(gate_z)).astype(jnp.bfloat16)
+    grad_gate = (grad_gated * y_token_vals * slope_of_silu(gate_z)).astype(jnp.bfloat16)
     grad_y_chan = lax.all_to_all(grad_y, "seq", split_axis=2, concat_axis=1, tiled=True)
     grad_dt_scan, grad_x_scan, grad_b, grad_c, grad_decay, grad_skip = pullback(
         grad_y_chan.astype(jnp.float32)
@@ -187,7 +1134,7 @@
     grad_conv_out = grad_x_scan + jnp.einsum(
         "rtm,cm->rtc", grad_dtbc, x_proj, preferred_element_type=jnp.float32
     )
-    grad_pre_conv = grad_conv_out * silu_slope(pre_conv)
+    grad_pre_conv = grad_conv_out * slope_of_silu(pre_conv)
     grad_conv_bias = jnp.sum(grad_pre_conv, axis=(0, 1))
     conv_rows = [None] * CONV
     grad_x = jnp.zeros_like(grad_pre_conv)
@@ -252,8 +1199,10 @@
 
 
 def solution(mesh):
+    fits = mesh.shape["seq"] == 16 and mesh.shape["row"] == 2
+    plan = channel_plan if fits else token_plan
     return jax.shard_map(
-        local,
+        plan,
         mesh=mesh,
         in_specs=(
             P("row", "seq", None),

time: 3340 us -> 459 us (0.14); the launches traced: 3290 us -> 453 us
  other arithmetic: 1270 us -> 27.7 us
  local copies, waits for them, and re-layouts: 1050 us -> 34.2 us
  waiting for transfers between devices: 555 us -> 155 us
  blocking collectives: 290 us -> 0 us
  Pallas kernels: 0 us -> 138 us
  starting transfers between devices: 29.5 us -> 94.6 us
  matrix products: 44.9 us -> 1.83 us
    dynamic_update_slice x336 -> x1, other arithmetic: 569 us -> 0.01 us  [channel_plan(): lax.dynamic_update_slice(spot, norm_gain.astype(F32)[None], (place, 0))]
    mul x379 -> x0, other arithmetic: 411 us -> none  [the longest x144 240 us: local_pass(): return ((state_now, decay_now * product), None)]
    reduce_scatter x1 -> x0, waiting for transfers between devices: 361 us -> none  [local(): lax.psum_scatter(grad_in_proj, ('seq', 'row'), scatter_dimension=0, tiled...]
    mul x673 -> x1, local copies, waits for them, and re-layouts: 310 us -> 0.07 us  [channel_plan(): grad_scaled = gnormed * gain_whole]
    reduce_sum x197 -> x1, other arithmetic: 262 us -> 0.16 us  [channel_plan(): grad_gain = jnp.sum(weight.astype(F32) * gin, axis=0) / gain_whole[0]]
    another operation x77 -> x1, local copies, waits for them, and re-layouts: 232 us -> 0.01 us
    dynamic_update_slice x441 -> x1, local copies, waits for them, and re-layouts: 216 us -> 0.03 us  [channel_plan(): lax.dynamic_update_slice(spot, norm_gain.astype(F32)[None], (place, 0))]
    unnamed x3 -> x0, blocking collectives: 158 us -> none
  transfers between devices with their start and end apart: 8 -> 81, of which waited for: 6 -> 46; matrix products, arithmetic and copies ran while one was open for 3% -> 6% of each run, Pallas kernels for 0% -> 27%
where the time goes in v1:
time: 459 us; the launch traced here: 453 us
  waiting for transfers between devices  155 us (34%)
  Pallas kernels  138 us (30%)
  starting transfers between devices  94.6 us (21%)
  local copies, waits for them, and re-layouts  34.2 us (7%)
  other arithmetic  27.7 us (6%)
    ppermute x70, waiting for transfers between devices, cross(): return lax.ppermute(v, 'seq', [(s, s ^ bits) for s in range(16)])  150 us
    ppermute x70, starting transfers between devices, cross(): return lax.ppermute(v, 'seq', [(s, s ^ bits) for s in range(16)])  68.5 us
    pallas_call x3, Pallas kernels, backward_scan(): pl.pallas_call(partial(backward_kernel, row=row), grid_spec=pltpu.Prefetc...  53.4 us
    pallas_call x1, Pallas kernels, forward_scan(): pl.pallas_call(partial(forward_kernel, row=row), grid_spec=pltpu.Prefetch...  29.1 us
    unnamed x108, local copies, waits for them, and re-layouts  27.6 us
    pallas_call x1, Pallas kernels, turn(): pl.pallas_call(turn_kernel, grid_spec=pltpu.PrefetchScalarGridSpec(num_sc...  16.3 us
    pallas_call x1, Pallas kernels, tail(): pl.pallas_call(partial(tail_kernel, row=row), grid_spec=pltpu.PrefetchSca...  15.8 us
    pallas_call x1, Pallas kernels, front(): pl.pallas_call(front_kernel, grid_spec=pltpu.PrefetchScalarGridSpec(num_s...  13.8 us
  transfers between devices with their start and end apart: 81, of which 46 were waited for; matrix products, arithmetic and copies ran while one was open for 6% of the time, Pallas kernels for 27%

profile of v1, /device:TPU:18, one launch (start us, length us, event | category | flops | bytes accessed | tf_op | source)
XLA Modules:
  0.0 453.1 jit_solution(5489688690136690399)
XLA Ops:
  8.5 2.7 fusion.1
  13.5 2.5 collective-permute-start.6
  16.1 6.5 %collective-permute-done.6 = f32[32,32]{1,0:T(8,128)S(1)} collective-permute-done((f32[32,32]{1,0:T(8,128)S(1)}, f32[32,32]{1,0:T(8,128)S(1)}, u32[]{:S(2)}, u32[]{:S(2)}) %collective-permute-start.6) | collective-permute-done | bytes 4128 | tf_op jit(solution)/shard_map/ppermute | solution.py:727
  22.6 3.3 collective-permute-start.4
  25.9 2.5 collective-permute-done.7
  28.4 2.2 collective-permute-start.8
  31.7 4.1 collective-permute-done.8
  36.3 4.4 collective-permute-done.3.refs_5_
  48.5 3.4 collective-permute-start.10
  54.0 7.4 %collective-permute-done.10.refs_3_ = bf16[2,1,64,1024]{3,2,1,0:T(8,128)(2,1)S(1)} collective-permute-done((bf16[2,1,64,1024]{3,2,1,0:T(8,128)(2,1)S(1)}, bf16[2,1,64,1024]{3,2,1,0:T(8,128)(2,1)S(1)}, u32[]{:S(2)}, u32[]{:S(2)}) %collective-permute-start.10) | collective-permute-done | bytes 262176 | tf_op jit(solution)/shard_map/ppermute | solution.py:727
  61.4 8.3 %collective-permute-done.11.refs_4_ = bf16[2,1,64,1024]{3,2,1,0:T(8,128)(2,1)S(1)} collective-permute-done((bf16[2,1,64,1024]{3,2,1,0:T(8,128)(2,1)S(1)}, bf16[2,1,64,1024]{3,2,1,0:T(8,128)(2,1)S(1)}, u32[]{:S(2)}, u32[]{:S(2)}) %collective-permute-start.11) | collective-permute-done | bytes 262176 | tf_op jit(solution)/shard_map/ppermute | solution.py:727
  69.7 7.4 %collective-permute-done.12.refs_5_ = bf16[2,1,64,1024]{3,2,1,0:T(8,128)(2,1)S(1)} collective-permute-done((bf16[2,1,64,1024]{3,2,1,0:T(8,128)(2,1)S(1)}, bf16[2,1,64,1024]{3,2,1,0:T(8,128)(2,1)S(1)}, u32[]{:S(2)}, u32[]{:S(2)}) %collective-permute-start.12) | collective-permute-done | bytes 262176 | tf_op jit(solution)/shard_map/ppermute | solution.py:727
  79.9 3.1 collective-permute-done.19
  89.0 13.8 %front.1 = (bf16[3,1024,1024]{2,1,0:T(8,128)(2,1)}, bf16[3,1024,128]{2,1,0:T(8,128)(2,1)}, f32[3,1024,128]{2,1,0:T(8,128)}, bf16[3,1024,128]{2,1,0:T(8,128)(2,1)...) custom-call(s32[3,8]{1,0:T(4,128)S(1)} %copy-done.34, s32[3]{0:T(128)S(1)} %pad_add_fusion.own, ...), custom_call_target="tpu_custom_call" | custom-call | flops 1 | bytes 1 | tf_op jit(solution)/shard_map/front/pallas_call | solution.py:204
  102.8 1.9 collective-permute-done.21.refs_5_
  104.7 6.6 %collective-permute-done.22.refs_6_ = bf16[2,64,1024]{2,1,0:T(8,128)(2,1)} collective-permute-done((bf16[2,64,1024]{2,1,0:T(8,128)(2,1)S(1)}, bf16[2,64,1024]{2,1,0:T(8,128)(2,1)}, u32[]{:S(2)}, u32[]{:S(2)}) %collective-permute-start.22) | collective-permute-done | bytes 262176 | tf_op jit(solution)/shard_map/ppermute | solution.py:727
  111.4 2.3 collective-permute-done.24
  114.5 10.6 %collective-permute-done.25 = f32[4,3,64,96]{3,2,1,0:T(8,128)S(1)} collective-permute-done((f32[4,3,64,96]{3,2,1,0:T(8,128)S(1)}, f32[4,3,64,96]{3,2,1,0:T(8,128)S(1)}, u32[]{:S(2)}, u32[]{:S(2)}) %collective-permute-start.25) | collective-permute-done | bytes 294944 | tf_op jit(solution)/shard_map/ppermute | solution.py:727
  128.7 2.2 collective-permute-done.26
  130.9 2.7 collective-permute-done.27
  133.7 2.8 collective-permute-done.28
  143.8 5.1 %collective-permute-done.32 = bf16[4,3,64,96]{3,2,1,0:T(8,128)(2,1)S(1)} collective-permute-done((bf16[4,3,64,96]{3,2,1,0:T(8,128)(2,1)S(1)}, bf16[4,3,64,96]{3,2,1,0:T(8,128)(2,1)S(1)}, u32[]{:S(2)}, u32[]{:S(2)}) %collective-permute-start.32) | collective-permute-done | bytes 147488 | tf_op jit(solution)/shard_map/ppermute | solution.py:727
  153.6 7.4 %all-to-all-start = ((bf16[64,16,128]{2,0,1:T(8,128)(2,1)}), bf16[64,16,128]{2,0,1:T(8,128)(2,1)}, u32[]{:S(2)}, u32[]{:S(2)}) async-start(bf16[64,16,128]{2,0,1:T(8,128)(2,1)} %copy_bitcast_fusion.1), calls=%async_computation | async-start | bytes 524288 | tf_op jit(solution)/shard_map/all_to_all | solution.py:872
  166.4 29.1 %forward_scan.1 = (bf16[3,1024,128]{2,1,0:T(8,128)(2,1)}, bf16[3,1024,128]{2,1,0:T(8,128)(2,1)}, f32[3,1024,16,128]{3,2,1,0:T(8,128)}, f32[3,16,128]{2,1,0:T(8,128)S(1)}, f32[8,128]{1,0:T(8,128)S(1)}) custom-call(s32[3,8]{1,0:T(4,128)S(1)} %copy-done.34, s32[3]{0:T(128)S(1)} %pad_add_fusion.own, bf16[2,4,3,64,96]{4,3,2,1,0:T(8,128)(2,1)S(1)} %pad_maximum_fusion.7.near, ...), custom_call_target="tpu_custom_call" | custom-call | flops 1 | bytes 1 | tf_op jit(solution)/shard_map/forward_scan/pallas_call | solution.py:312
  208.3 10.0 %mix.1 = (bf16[2,4,3,64,1024]{4,3,2,1,0:T(8,128)(2,1)}, bf16[2,4,3,64,1024]{4,3,2,1,0:T(8,128)(2,1)}) custom-call(s32[3]{0:T(128)S(1)} %pad_add_fusion.own, bf16[3,1024,128]{2,1,0:T(8,128)(2,1)} %copy-done.8, bf16[1024,128]{1,0:T(8,128)(2,1)} %get-tuple-element.177.cols.refs_6_), custom_call_target="tpu_custom_call" | custom-call | flops 1 | bytes 1 | tf_op jit(solution)/shard_map/mix/pallas_call | solution.py:660
  222.3 16.3 %turn.1 = (f32[3,1024,128]{2,1,0:T(8,128)}, bf16[3,1024,1024]{2,1,0:T(8,128)(2,1)}) custom-call(s32[3]{0:T(128)S(1)} %pad_add_fusion.own, bf16[4,2,64,1024]{3,2,1,0:T(8,128)(2,1)S(1)} %get-tuple-element.188.refs_0_, bf16[4,2,64,1024]{3,2,1,0:T(8,128)(2,1)} %get-tuple-element.189.refs_1_, bf16[4,2,64,1024]{3,2,1,0:T(8,128)(2,1)S(1)} %get-tuple-element.190.refs_2_, ...), custom_call_target="tpu_custom_call" | custom-call | flops 1 | bytes 1 | tf_op jit(solution)/shard_map/turn/pallas_call | solution.py:700
  243.2 2.4 collective-permute-start.43
  247.2 17.6 %backward_scan.3 = (bf16[3,1024,128]{2,1,0:T(8,128)(2,1)}, f32[3,1024,128]{2,1,0:T(8,128)}, f32[2,4,3,64,96]{4,3,2,1,0:T(8,128)S(1)}, f32[2,4,3,64,96]{4,3,2,1,0...) custom-call(s32[3,8]{1,0:T(4,128)S(1)} %copy-done.34, s32[3]{0:T(128)S(1)} %pad_add_fusion.own, ...), custom_call_target="tpu_custom_call" | custom-call | flops 1 | bytes 1 | tf_op jit(solution)/shard_map/backward_scan/pallas_call | solution.py:472
  264.7 17.6 %backward_scan.4 = (bf16[3,1024,128]{2,1,0:T(8,128)(2,1)}, f32[3,1024,128]{2,1,0:T(8,128)}, f32[2,4,3,64,96]{4,3,2,1,0:T(8,128)S(1)}, f32[2,4,3,64,96]{4,3,2,1,0...) custom-call(s32[3,8]{1,0:T(4,128)S(1)} %copy-done.34, ...), custom_call_target="tpu_custom_call", output_to_operand_aliasing={{0}: (17, {}), {1}: (18, {}), {2}: (19, {}), {3}: (20, {})} | custom-call | flops 1 | bytes 1 | tf_op jit(solution)/shard_map/backward_scan/pallas_call | solution.py:472
  283.9 2.9 collective-permute-start.46
  290.0 18.2 %backward_scan.5 = (bf16[3,1024,128]{2,1,0:T(8,128)(2,1)}, f32[3,1024,128]{2,1,0:T(8,128)}, f32[2,4,3,64,96]{4,3,2,1,0:T(8,128)S(1)}, f32[2,4,3,64,96]{4,3,2,1,0...) custom-call(s32[3,8]{1,0:T(4,128)S(1)} %copy-done.34, ...), custom_call_target="tpu_custom_call", output_to_operand_aliasing={{0}: (17, {}), {1}: (18, {}), {2}: (19, {}), {3}: (20, {})} | custom-call | flops 1 | bytes 1 | tf_op jit(solution)/shard_map/backward_scan/pallas_call | solution.py:472
  308.2 2.2 collective-permute-done.48.refs_2_
  313.2 2.3 collective-permute-done.50
  317.2 5.5 %collective-permute-done.51 = bf16[4,3,64,96]{3,2,1,0:T(8,128)(2,1)S(1)} collective-permute-done((bf16[4,3,64,96]{3,2,1,0:T(8,128)(2,1)S(1)}, bf16[4,3,64,96]{3,2,1,0:T(8,128)(2,1)S(1)}, u32[]{:S(2)}, u32[]{:S(2)}) %collective-permute-start.51) | collective-permute-done | bytes 147488 | tf_op jit(solution)/shard_map/ppermute | solution.py:727
  338.4 4.2 collective-permute-done.58
  342.8 2.0 collective-permute-done.60
  345.7 15.8 %tail.1 = (bf16[2,4,3,64,1024]{4,3,2,1,0:T(8,128)(2,1)}, bf16[2,4,3,64,1024]{4,3,2,1,0:T(8,128)(2,1)}, f32[256,1024]{1,0:T(8,128)S(1)}, f32[128,96]{1,0:T(8,128)S(1)}, f32[8,128]{1,0:T(8,128)S(1)}) custom-call(s32[3,8]{1,0:T(4,128)S(1)} %copy-done.34, s32[3]{0:T(128)S(1)} %pad_add_fusion.own, bf16[2,4,3,64,96]{4,3,2,1,0:T(8,128)(2,1)S(1)} %pad_maximum_fusion.8.near, ...), custom_call_target="tpu_custom_call" | custom-call | flops 1 | bytes 1 | tf_op jit(solution)/shard_map/tail/pallas_call | solution.py:597
  362.0 2.0 collective-permute-start.67
  372.3 3.5 collective-permute-start.63
  378.1 7.1 %collective-permute-done.63.refs_1_ = bf16[2,1,64,1024]{3,2,1,0:T(8,128)(2,1)S(1)} collective-permute-done((bf16[2,1,64,1024]{3,2,1,0:T(8,128)(2,1)S(1)}, bf16[2,1,64,1024]{3,2,1,0:T(8,128)(2,1)S(1)}, u32[]{:S(2)}, u32[]{:S(2)}) %collective-permute-start.63) | collective-permute-done | bytes 262176 | tf_op jit(solution)/shard_map/ppermute | solution.py:727
  385.3 8.5 %collective-permute-done.64.refs_2_ = bf16[2,1,64,1024]{3,2,1,0:T(8,128)(2,1)S(1)} collective-permute-done((bf16[2,1,64,1024]{3,2,1,0:T(8,128)(2,1)S(1)}, bf16[2,1,64,1024]{3,2,1,0:T(8,128)(2,1)S(1)}, u32[]{:S(2)}, u32[]{:S(2)}) %collective-permute-start.64) | collective-permute-done | bytes 262176 | tf_op jit(solution)/shard_map/ppermute | solution.py:727
  393.8 6.3 %collective-permute-done.65.refs_3_ = bf16[2,1,64,1024]{3,2,1,0:T(8,128)(2,1)S(1)} collective-permute-done((bf16[2,1,64,1024]{3,2,1,0:T(8,128)(2,1)S(1)}, bf16[2,1,64,1024]{3,2,1,0:T(8,128)(2,1)S(1)}, u32[]{:S(2)}, u32[]{:S(2)}) %collective-permute-start.65) | collective-permute-done | bytes 262176 | tf_op jit(solution)/shard_map/ppermute | solution.py:727
  403.7 2.0 collective-permute-start.71
  410.1 2.9 collective-permute-done.70.refs_0_
  413.0 10.7 %collective-permute-done.71.refs_1_ = bf16[2,64,1024]{2,1,0:T(8,128)(2,1)S(1)} collective-permute-done((bf16[2,64,1024]{2,1,0:T(8,128)(2,1)S(1)}, bf16[2,64,1024]{2,1,0:T(8,128)(2,1)S(1)}, u32[]{:S(2)}, u32[]{:S(2)}) %collective-permute-start.71) | collective-permute-done | bytes 262176 | tf_op jit(solution)/shard_map/ppermute | solution.py:727
  423.7 4.8 %collective-permute-done.72.refs_2_ = bf16[2,64,1024]{2,1,0:T(8,128)(2,1)S(1)} collective-permute-done((bf16[2,64,1024]{2,1,0:T(8,128)(2,1)S(1)}, bf16[2,64,1024]{2,1,0:T(8,128)(2,1)S(1)}, u32[]{:S(2)}, u32[]{:S(2)}) %collective-permute-start.72) | collective-permute-done | bytes 262176 | tf_op jit(solution)/shard_map/ppermute | solution.py:727
  433.0 7.1 %all-to-all-start.1 = ((bf16[16,32,128]{2,1,0:T(8,128)(2,1)}), bf16[16,32,128]{2,1,0:T(8,128)(2,1)S(1)}, u32[]{:S(2)}, u32[]{:S(2)}) async-start(bf16[16,32,128]{2,1,0:T(8,128)(2,1)} %get-tuple-element.248), calls=%async_computation.1 | async-start | bytes 262144 | tf_op jit(solution)/shard_map/all_to_all | solution.py:925
  440.7 3.2 collective-permute-done.74
  (342 shorter events, 134.2 us)
Async XLA Ops:
  2.7 39.5 %collective-permute-start = (bf16[2,64,1024]{2,1,0:T(8,128)(2,1)S(1)}, bf16[2,64,1024]{2,1,0:T(8,128)(2,1)S(1)}, u32[]{:S(2)}, u32[]{:S(2)}) collective-permute-start(bf16[2,64,1024]{2,1,0:T(8,128)(2,1)S(1)} %get-tuple-element.131.refs_0_), channel_id=1, source_target_pairs={{0,8},{2,10},{4,12},{6,14},{8,0},{10,2},{12,4},{14,6},{16,24},{18,... | collective-permute-start | bytes 786440 | tf_op jit(solution)/shard_map/ppermute | solution.py:727
  4.3 37.9 %collective-permute-start.1 = (bf16[2,64,1024]{2,1,0:T(8,128)(2,1)S(1)}, bf16[2,64,1024]{2,1,0:T(8,128)(2,1)S(1)}, u32[]{:S(2)}, u32[]{:S(2)}) collective-permute-start(bf16[2,64,1024]{2,1,0:T(8,128)(2,1)S(1)} %get-tuple-element.131.refs_0_), channel_id=1, source_target_pairs={{0,16},{2,18},{4,20},{6,22},{8,24},{10,26},{12,28},{14,30},{16,0},... | collective-permute-start | bytes 786440 | tf_op jit(solution)/shard_map/ppermute | solution.py:727
  4.7 37.6 %collective-permute-start.2 = (bf16[2,64,1024]{2,1,0:T(8,128)(2,1)S(1)}, bf16[2,64,1024]{2,1,0:T(8,128)(2,1)S(1)}, u32[]{:S(2)}, u32[]{:S(2)}) collective-permute-start(bf16[2,64,1024]{2,1,0:T(8,128)(2,1)S(1)} %get-tuple-element.131.refs_0_), channel_id=1, source_target_pairs={{0,24},{2,26},{4,28},{6,30},{8,16},{10,18},{12,20},{14,22},{16,8},... | collective-permute-start | bytes 786440 | tf_op jit(solution)/shard_map/ppermute | solution.py:727
  13.5 9.1 %collective-permute-start.6 = (f32[32,32]{1,0:T(8,128)S(1)}, f32[32,32]{1,0:T(8,128)S(1)}, u32[]{:S(2)}, u32[]{:S(2)}) collective-permute-start(f32[32,32]{1,0:T(8,128)S(1)} %add.524), channel_id=1, source_target_pairs={{0,8},{2,10},{4,12},{6,14},{8,0},{10,2},{12,4},{14,6},{16,24},{18,... | collective-permute-start | bytes 12296 | tf_op jit(solution)/shard_map/ppermute | solution.py:727
  16.1 12.3 %collective-permute-start.7 = (f32[32,32]{1,0:T(8,128)S(1)}, f32[32,32]{1,0:T(8,128)S(1)}, u32[]{:S(2)}, u32[]{:S(2)}) collective-permute-start(f32[32,32]{1,0:T(8,128)S(1)} %add.524), channel_id=1, source_target_pairs={{0,16},{2,18},{4,20},{6,22},{8,24},{10,26},{12,28},{14,30},{16,0},... | collective-permute-start | bytes 12296 | tf_op jit(solution)/shard_map/ppermute | solution.py:727
  22.6 19.6 %collective-permute-start.4 = (bf16[128,1024]{1,0:T(8,128)(2,1)}, bf16[128,1024]{1,0:T(8,128)(2,1)S(1)}, u32[]{:S(2)}, u32[]{:S(2)}) collective-permute-start(bf16[128,1024]{1,0:T(8,128)(2,1)} %param.17), channel_id=1, source_target_pairs={{0,0},{1,2},{2,4},{3,6},{4,8},{5,10},{6,12},{7,14},{8,16},{9,18},{... | collective-permute-start | bytes 786440 | tf_op jit(solution)/shard_map/ppermute | solution.py:832
  28.4 7.3 %collective-permute-start.8 = (f32[32,32]{1,0:T(8,128)S(1)}, f32[32,32]{1,0:T(8,128)S(1)}, u32[]{:S(2)}, u32[]{:S(2)}) collective-permute-start(f32[32,32]{1,0:T(8,128)S(1)} %add.524), channel_id=1, source_target_pairs={{0,24},{2,26},{4,28},{6,30},{8,16},{10,18},{12,20},{14,22},{16,8},... | collective-permute-start | bytes 12296 | tf_op jit(solution)/shard_map/ppermute | solution.py:727
  45.7 31.3 %collective-permute-start.9 = (bf16[4,2,64,1024]{3,2,1,0:T(8,128)(2,1)S(1)}, bf16[4,2,64,1024]{3,2,1,0:T(8,128)(2,1)}, u32[]{:S(2)}, u32[]{:S(2)}) collective-permute-start(bf16[4,2,64,1024]{3,2,1,0:T(8,128)(2,1)S(1)} %pad_maximum_fusion.refs_0_), channel_id=1, source_target_pairs={{0,4},{2,6},{4,0},{6,2},{8,12},{10,14},{12,8},{14,10},{16,20},{18,... | collective-permute-start | bytes 3145736 | tf_op jit(solution)/shard_map/ppermute | solution.py:727
  48.5 12.9 %collective-permute-start.10 = (bf16[2,1,64,1024]{3,2,1,0:T(8,128)(2,1)S(1)}, bf16[2,1,64,1024]{3,2,1,0:T(8,128)(2,1)S(1)}, u32[]{:S(2)}, u32[]{:S(2)}) collective-permute-start(bf16[2,1,64,1024]{3,2,1,0:T(8,128)(2,1)S(1)} %pad_maximum_fusion.9.refs_1_), channel_id=1, source_target_pairs={{0,8},{2,10},{4,12},{6,14},{8,0},{10,2},{12,4},{14,6},{16,24},{18,... | collective-permute-start | bytes 786440 | tf_op jit(solution)/shard_map/ppermute | solution.py:727
  51.9 17.8 %collective-permute-start.11 = (bf16[2,1,64,1024]{3,2,1,0:T(8,128)(2,1)S(1)}, bf16[2,1,64,1024]{3,2,1,0:T(8,128)(2,1)S(1)}, u32[]{:S(2)}, u32[]{:S(2)}) collective-permute-start(bf16[2,1,64,1024]{3,2,1,0:T(8,128)(2,1)S(1)} %pad_maximum_fusion.9.refs_1_), channel_id=1, source_target_pairs={{0,16},{2,18},{4,20},{6,22},{8,24},{10,26},{12,28},{14,30},{16,0},... | collective-permute-start | bytes 786440 | tf_op jit(solution)/shard_map/ppermute | solution.py:727
  51.9 25.1 %collective-permute-start.12 = (bf16[2,1,64,1024]{3,2,1,0:T(8,128)(2,1)S(1)}, bf16[2,1,64,1024]{3,2,1,0:T(8,128)(2,1)S(1)}, u32[]{:S(2)}, u32[]{:S(2)}) collective-permute-start(bf16[2,1,64,1024]{3,2,1,0:T(8,128)(2,1)S(1)} %pad_maximum_fusion.9.refs_1_), channel_id=1, source_target_pairs={{0,24},{2,26},{4,28},{6,30},{8,16},{10,18},{12,20},{14,22},{16,8},... | collective-permute-start | bytes 786440 | tf_op jit(solution)/shard_map/ppermute | solution.py:727
  84.8 17.9 %collective-permute-start.20 = (bf16[2,64,1024]{2,1,0:T(8,128)(2,1)S(1)}, bf16[2,64,1024]{2,1,0:T(8,128)(2,1)S(1)}, u32[]{:S(2)}, u32[]{:S(2)}) collective-permute-start(bf16[2,64,1024]{2,1,0:T(8,128)(2,1)S(1)} %get-tuple-element.154.refs_11_.refs_2_), channel_id=1, source_target_pairs={{0,8},{2,10},{4,12},{6,14},{8,0},{10,2},{12,4},{14,6},{16,24},{18,... | collective-permute-start | bytes 786440 | tf_op jit(solution)/shard_map/ppermute | solution.py:727
  84.9 19.9 %collective-permute-start.21 = (bf16[2,64,1024]{2,1,0:T(8,128)(2,1)S(1)}, bf16[2,64,1024]{2,1,0:T(8,128)(2,1)}, u32[]{:S(2)}, u32[]{:S(2)}) collective-permute-start(bf16[2,64,1024]{2,1,0:T(8,128)(2,1)S(1)} %get-tuple-element.154.refs_11_.refs_2_), channel_id=1, source_target_pairs={{0,16},{2,18},{4,20},{6,22},{8,24},{10,26},{12,28},{14,30},{16,0},... | collective-permute-start | bytes 786440 | tf_op jit(solution)/shard_map/ppermute | solution.py:727
  86.8 24.6 %collective-permute-start.22 = (bf16[2,64,1024]{2,1,0:T(8,128)(2,1)S(1)}, bf16[2,64,1024]{2,1,0:T(8,128)(2,1)}, u32[]{:S(2)}, u32[]{:S(2)}) collective-permute-start(bf16[2,64,1024]{2,1,0:T(8,128)(2,1)S(1)} %get-tuple-element.154.refs_11_.refs_2_), channel_id=1, source_target_pairs={{0,24},{2,26},{4,28},{6,30},{8,16},{10,18},{12,20},{14,22},{16,8},... | collective-permute-start | bytes 786440 | tf_op jit(solution)/shard_map/ppermute | solution.py:727
  88.3 14.4 %collective-permute-start.23 = (bf16[1,64,1024]{2,1,0:T(8,128)(2,1)S(1)}, bf16[1,64,1024]{2,1,0:T(8,128)(2,1)S(1)}, u32[]{:S(2)}, u32[]{:S(2)}) collective-permute-start(bf16[1,64,1024]{2,1,0:T(8,128)(2,1)S(1)} %get-tuple-element.155.refs_12_.refs_3_), channel_id=1, source_target_pairs={{0,4},{2,6},{4,0},{6,2},{8,12},{10,14},{12,8},{14,10},{16,20},{18,... | collective-permute-start | bytes 393224 | tf_op jit(solution)/shard_map/ppermute | solution.py:727
  113.8 11.2 %collective-permute-start.25 = (f32[4,3,64,96]{3,2,1,0:T(8,128)S(1)}, f32[4,3,64,96]{3,2,1,0:T(8,128)S(1)}, u32[]{:S(2)}, u32[]{:S(2)}) collective-permute-start(f32[4,3,64,96]{3,2,1,0:T(8,128)S(1)} %slice_bitcast_fusion.1), channel_id=1, source_target_pairs={{0,4},{2,6},{4,0},{6,2},{8,12},{10,14},{12,8},{14,10},{16,20},{18,... | collective-permute-start | bytes 884744 | tf_op jit(solution)/shard_map/ppermute | solution.py:727
  125.2 8.5 %collective-permute-start.27 = (f32[3,64,96]{2,1,0:T(8,128)S(1)}, f32[3,64,96]{2,1,0:T(8,128)S(1)}, u32[]{:S(2)}, u32[]{:S(2)}) collective-permute-start(f32[3,64,96]{2,1,0:T(8,128)S(1)} %get-tuple-element.272), channel_id=1, source_target_pairs={{0,16},{2,18},{4,20},{6,22},{8,24},{10,26},{12,28},{14,30},{16,0},... | collective-permute-start | bytes 221192 | tf_op jit(solution)/shard_map/ppermute | solution.py:727
  127.2 9.4 %collective-permute-start.28 = (f32[3,64,96]{2,1,0:T(8,128)S(1)}, f32[3,64,96]{2,1,0:T(8,128)S(1)}, u32[]{:S(2)}, u32[]{:S(2)}) collective-permute-start(f32[3,64,96]{2,1,0:T(8,128)S(1)} %get-tuple-element.271), channel_id=1, source_target_pairs={{0,24},{2,26},{4,28},{6,30},{8,16},{10,18},{12,20},{14,22},{16,8},... | collective-permute-start | bytes 221192 | tf_op jit(solution)/shard_map/ppermute | solution.py:727
  151.5 46.2 %collective-permute-start.34 = (bf16[4,2,64,1024]{3,2,1,0:T(8,128)(2,1)S(1)}, bf16[4,2,64,1024]{3,2,1,0:T(8,128)(2,1)}, u32[]{:S(2)}, u32[]{:S(2)}) collective-permute-start(bf16[4,2,64,1024]{3,2,1,0:T(8,128)(2,1)S(1)} %get-tuple-element.172.refs_0_.refs_2_), channel_id=1, source_target_pairs={{0,4},{2,6},{4,0},{6,2},{8,12},{10,14},{12,8},{14,10},{16,20},{18,... | collective-permute-start | bytes 3145736 | tf_op jit(solution)/shard_map/ppermute | solution.py:727
  153.6 44.1 %all-to-all-start = ((bf16[64,16,128]{2,0,1:T(8,128)(2,1)}), bf16[64,16,128]{2,0,1:T(8,128)(2,1)}, u32[]{:S(2)}, u32[]{:S(2)}) async-start(bf16[64,16,128]{2,0,1:T(8,128)(2,1)} %copy_bitcast_fusion.1), calls=%async_computation | async-start | bytes 524288 | tf_op jit(solution)/shard_map/all_to_all | solution.py:872
  161.0 34.5 %collective-permute-start.35 = (bf16[2,1,64,1024]{3,2,1,0:T(8,128)(2,1)}, bf16[2,1,64,1024]{3,2,1,0:T(8,128)(2,1)S(1)}, u32[]{:S(2)}, u32[]{:S(2)}) collective-permute-start(bf16[2,1,64,1024]{3,2,1,0:T(8,128)(2,1)} %copy-done.14), channel_id=1, source_target_pairs={{0,8},{2,10},{4,12},{6,14},{8,0},{10,2},{12,4},{14,6},{16,24},{18,... | collective-permute-start | bytes 786440 | tf_op jit(solution)/shard_map/ppermute | solution.py:727
  162.5 33.7 %collective-permute-start.36 = (bf16[2,1,64,1024]{3,2,1,0:T(8,128)(2,1)}, bf16[2,1,64,1024]{3,2,1,0:T(8,128)(2,1)S(1)}, u32[]{:S(2)}, u32[]{:S(2)}) collective-permute-start(bf16[2,1,64,1024]{3,2,1,0:T(8,128)(2,1)} %copy-done.14), channel_id=1, source_target_pairs={{0,16},{2,18},{4,20},{6,22},{8,24},{10,26},{12,28},{14,30},{16,0},... | collective-permute-start | bytes 786440 | tf_op jit(solution)/shard_map/ppermute | solution.py:727
  163.1 33.9 %collective-permute-start.37 = (bf16[2,1,64,1024]{3,2,1,0:T(8,128)(2,1)}, bf16[2,1,64,1024]{3,2,1,0:T(8,128)(2,1)S(1)}, u32[]{:S(2)}, u32[]{:S(2)}) collective-permute-start(bf16[2,1,64,1024]{3,2,1,0:T(8,128)(2,1)} %copy-done.14), channel_id=1, source_target_pairs={{0,24},{2,26},{4,28},{6,30},{8,16},{10,18},{12,20},{14,22},{16,8},... | collective-permute-start | bytes 786440 | tf_op jit(solution)/shard_map/ppermute | solution.py:727
  207.6 10.6 %collective-permute-start.40 = (bf16[4,2,1,64,1024]{4,3,2,1,0:T(8,128)(2,1)S(1)}, bf16[4,2,1,64,1024]{4,3,2,1,0:T(8,128)(2,1)S(1)}, u32[]{:S(2)}, u32[]{:S(2)}) collective-permute-start(bf16[4,2,1,64,1024]{4,3,2,1,0:T(8,128)(2,1)S(1)} %pad_maximum_fusion.3.refs_6_), channel_id=1, source_target_pairs={{0,2},{2,0},{4,6},{6,4},{8,10},{10,8},{12,14},{14,12},{16,18},{18,... | collective-permute-start | bytes 3145736 | tf_op jit(solution)/shard_map/ppermute | solution.py:727
  207.7 10.6 %collective-permute-start.38 = (bf16[4,2,64,1024]{3,2,1,0:T(8,128)(2,1)S(1)}, bf16[4,2,64,1024]{3,2,1,0:T(8,128)(2,1)S(1)}, u32[]{:S(2)}, u32[]{:S(2)}) collective-permute-start(bf16[4,2,64,1024]{3,2,1,0:T(8,128)(2,1)S(1)} %get-tuple-element.180.refs_2_), channel_id=1, source_target_pairs={{0,2},{2,0},{4,6},{6,4},{8,10},{10,8},{12,14},{14,12},{16,18},{18,... | collective-permute-start | bytes 3145736 | tf_op jit(solution)/shard_map/ppermute | solution.py:727
  208.2 10.1 %collective-permute-start.39 = (bf16[4,2,64,1024]{3,2,1,0:T(8,128)(2,1)}, bf16[4,2,64,1024]{3,2,1,0:T(8,128)(2,1)S(1)}, u32[]{:S(2)}, u32[]{:S(2)}) collective-permute-start(bf16[4,2,64,1024]{3,2,1,0:T(8,128)(2,1)} %get-tuple-element.181.refs_3_), channel_id=1, source_target_pairs={{0,2},{2,0},{4,6},{6,4},{8,10},{10,8},{12,14},{14,12},{16,18},{18,... | collective-permute-start | bytes 3145736 | tf_op jit(solution)/shard_map/ppermute | solution.py:727
  221.8 16.8 %collective-permute-start.41 = (bf16[2,4,3,64,1024]{4,3,2,1,0:T(8,128)(2,1)}, bf16[2,4,3,64,1024]{4,3,2,1,0:T(8,128)(2,1)S(1)}, u32[]{:S(2)}, u32[]{:S(2)}) collective-permute-start(bf16[2,4,3,64,1024]{4,3,2,1,0:T(8,128)(2,1)} %get-tuple-element.187), channel_id=1, source_target_pairs={{0,2},{2,0},{4,6},{6,4},{8,10},{10,8},{12,14},{14,12},{16,18},{18,... | collective-permute-start | bytes 9437192 | tf_op jit(solution)/shard_map/ppermute | solution.py:727
  242.3 40.1 %collective-permute-start.42 = (bf16[4,2,64,1024]{3,2,1,0:T(8,128)(2,1)S(1)}, bf16[4,2,64,1024]{3,2,1,0:T(8,128)(2,1)S(1)}, u32[]{:S(2)}, u32[]{:S(2)}) collective-permute-start(bf16[4,2,64,1024]{3,2,1,0:T(8,128)(2,1)S(1)} %fusion.3.refs_0_), channel_id=1, source_target_pairs={{0,4},{2,6},{4,0},{6,2},{8,12},{10,14},{12,8},{14,10},{16,20},{18,... | collective-permute-start | bytes 3145736 | tf_op jit(solution)/shard_map/ppermute | solution.py:727
  243.2 39.1 %collective-permute-start.43 = (bf16[2,1,64,1024]{3,2,1,0:T(8,128)(2,1)S(1)}, bf16[2,1,64,1024]{3,2,1,0:T(8,128)(2,1)S(1)}, u32[]{:S(2)}, u32[]{:S(2)}) collective-permute-start(bf16[2,1,64,1024]{3,2,1,0:T(8,128)(2,1)S(1)} %get-tuple-element.262.refs_1_), channel_id=1, source_target_pairs={{0,8},{2,10},{4,12},{6,14},{8,0},{10,2},{12,4},{14,6},{16,24},{18,... | collective-permute-start | bytes 786440 | tf_op jit(solution)/shard_map/ppermute | solution.py:727
  245.6 36.7 %collective-permute-start.44 = (bf16[2,1,64,1024]{3,2,1,0:T(8,128)(2,1)S(1)}, bf16[2,1,64,1024]{3,2,1,0:T(8,128)(2,1)S(1)}, u32[]{:S(2)}, u32[]{:S(2)}) collective-permute-start(bf16[2,1,64,1024]{3,2,1,0:T(8,128)(2,1)S(1)} %get-tuple-element.261.refs_2_), channel_id=1, source_target_pairs={{0,16},{2,18},{4,20},{6,22},{8,24},{10,26},{12,28},{14,30},{16,0},... | collective-permute-start | bytes 786440 | tf_op jit(solution)/shard_map/ppermute | solution.py:727
  245.6 36.7 %collective-permute-start.45 = (bf16[2,1,64,1024]{3,2,1,0:T(8,128)(2,1)S(1)}, bf16[2,1,64,1024]{3,2,1,0:T(8,128)(2,1)S(1)}, u32[]{:S(2)}, u32[]{:S(2)}) collective-permute-start(bf16[2,1,64,1024]{3,2,1,0:T(8,128)(2,1)S(1)} %get-tuple-element.260.refs_3_), channel_id=1, source_target_pairs={{0,24},{2,26},{4,28},{6,30},{8,16},{10,18},{12,20},{14,22},{16,8},... | collective-permute-start | bytes 786440 | tf_op jit(solution)/shard_map/ppermute | solution.py:727
  283.9 24.3 %collective-permute-start.46 = (bf16[2,64,1024]{2,1,0:T(8,128)(2,1)S(1)}, bf16[2,64,1024]{2,1,0:T(8,128)(2,1)S(1)}, u32[]{:S(2)}, u32[]{:S(2)}) collective-permute-start(bf16[2,64,1024]{2,1,0:T(8,128)(2,1)S(1)} %get-tuple-element.256.refs_4_), channel_id=1, source_target_pairs={{0,8},{2,10},{4,12},{6,14},{8,0},{10,2},{12,4},{14,6},{16,24},{18,... | collective-permute-start | bytes 786440 | tf_op jit(solution)/shard_map/ppermute | solution.py:727
  286.9 21.4 %collective-permute-start.47 = (bf16[2,64,1024]{2,1,0:T(8,128)(2,1)S(1)}, bf16[2,64,1024]{2,1,0:T(8,128)(2,1)S(1)}, u32[]{:S(2)}, u32[]{:S(2)}) collective-permute-start(bf16[2,64,1024]{2,1,0:T(8,128)(2,1)S(1)} %get-tuple-element.255.refs_5_), channel_id=1, source_target_pairs={{0,16},{2,18},{4,20},{6,22},{8,24},{10,26},{12,28},{14,30},{16,0},... | collective-permute-start | bytes 786440 | tf_op jit(solution)/shard_map/ppermute | solution.py:727
  286.9 23.6 %collective-permute-start.48 = (bf16[2,64,1024]{2,1,0:T(8,128)(2,1)S(1)}, bf16[2,64,1024]{2,1,0:T(8,128)(2,1)S(1)}, u32[]{:S(2)}, u32[]{:S(2)}) collective-permute-start(bf16[2,64,1024]{2,1,0:T(8,128)(2,1)S(1)} %get-tuple-element.254.refs_6_), channel_id=1, source_target_pairs={{0,24},{2,26},{4,28},{6,30},{8,16},{10,18},{12,20},{14,22},{16,8},... | collective-permute-start | bytes 786440 | tf_op jit(solution)/shard_map/ppermute | solution.py:727
  288.5 19.7 %collective-permute-start.49 = (bf16[1,64,1024]{2,1,0:T(8,128)(2,1)S(1)}, bf16[1,64,1024]{2,1,0:T(8,128)(2,1)S(1)}, u32[]{:S(2)}, u32[]{:S(2)}) collective-permute-start(bf16[1,64,1024]{2,1,0:T(8,128)(2,1)S(1)} %fusion.33.refs_7_), channel_id=1, source_target_pairs={{0,4},{2,6},{4,0},{6,2},{8,12},{10,14},{12,8},{14,10},{16,20},{18,... | collective-permute-start | bytes 393224 | tf_op jit(solution)/shard_map/ppermute | solution.py:727
  315.7 7.0 %collective-permute-start.51 = (bf16[4,3,64,96]{3,2,1,0:T(8,128)(2,1)S(1)}, bf16[4,3,64,96]{3,2,1,0:T(8,128)(2,1)S(1)}, u32[]{:S(2)}, u32[]{:S(2)}) collective-permute-start(bf16[4,3,64,96]{3,2,1,0:T(8,128)(2,1)S(1)} %fusion.34), channel_id=1, source_target_pairs={{0,4},{2,6},{4,0},{6,2},{8,12},{10,14},{12,8},{14,10},{16,20},{18,... | collective-permute-start | bytes 442376 | tf_op jit(solution)/shard_map/ppermute | solution.py:727
  362.0 8.3 %collective-permute-start.67 = (f32[200,128]{1,0:T(8,128)S(1)}, f32[200,128]{1,0:T(8,128)S(1)}, u32[]{:S(2)}, u32[]{:S(2)}) collective-permute-start(f32[200,128]{1,0:T(8,128)S(1)} %bitcast_dynamic-update-slice_fusion), channel_id=1, source_target_pairs={{0,1},{1,0},{2,3},{3,2},{4,5},{5,4},{6,7},{7,6},{8,9},{9,8},{10,11... | collective-permute-start | bytes 307208 | tf_op jit(solution)/shard_map/ppermute | solution.py:731
  369.3 30.7 %collective-permute-start.62 = (bf16[4,2,64,1024]{3,2,1,0:T(8,128)(2,1)S(1)}, bf16[4,2,64,1024]{3,2,1,0:T(8,128)(2,1)S(1)}, u32[]{:S(2)}, u32[]{:S(2)}) collective-permute-start(bf16[4,2,64,1024]{3,2,1,0:T(8,128)(2,1)S(1)} %fusion.4), channel_id=1, source_target_pairs={{0,4},{2,6},{4,0},{6,2},{8,12},{10,14},{12,8},{14,10},{16,20},{18,... | collective-permute-start | bytes 3145736 | tf_op jit(solution)/shard_map/ppermute | solution.py:727
  370.1 7.9 %collective-permute-start.66 = (bf16[128,1024]{1,0:T(8,128)(2,1)S(1)}, bf16[128,1024]{1,0:T(8,128)(2,1)S(1)}, u32[]{:S(2)}, u32[]{:S(2)}) collective-permute-start(bf16[128,1024]{1,0:T(8,128)(2,1)S(1)} %select_convert_fusion), channel_id=1, source_target_pairs={{0,1},{1,0},{2,3},{3,2},{4,5},{5,4},{6,7},{7,6},{8,9},{9,8},{10,11... | collective-permute-start | bytes 786440 | tf_op jit(solution)/shard_map/ppermute | solution.py:731
  372.3 12.9 %collective-permute-start.63 = (bf16[2,1,64,1024]{3,2,1,0:T(8,128)(2,1)S(1)}, bf16[2,1,64,1024]{3,2,1,0:T(8,128)(2,1)S(1)}, u32[]{:S(2)}, u32[]{:S(2)}) collective-permute-start(bf16[2,1,64,1024]{3,2,1,0:T(8,128)(2,1)S(1)} %get-tuple-element.259), channel_id=1, source_target_pairs={{0,8},{2,10},{4,12},{6,14},{8,0},{10,2},{12,4},{14,6},{16,24},{18,... | collective-permute-start | bytes 786440 | tf_op jit(solution)/shard_map/ppermute | solution.py:727
  375.8 18.0 %collective-permute-start.64 = (bf16[2,1,64,1024]{3,2,1,0:T(8,128)(2,1)S(1)}, bf16[2,1,64,1024]{3,2,1,0:T(8,128)(2,1)S(1)}, u32[]{:S(2)}, u32[]{:S(2)}) collective-permute-start(bf16[2,1,64,1024]{3,2,1,0:T(8,128)(2,1)S(1)} %get-tuple-element.258), channel_id=1, source_target_pairs={{0,16},{2,18},{4,20},{6,22},{8,24},{10,26},{12,28},{14,30},{16,0},... | collective-permute-start | bytes 786440 | tf_op jit(solution)/shard_map/ppermute | solution.py:727
  375.8 24.2 %collective-permute-start.65 = (bf16[2,1,64,1024]{3,2,1,0:T(8,128)(2,1)S(1)}, bf16[2,1,64,1024]{3,2,1,0:T(8,128)(2,1)S(1)}, u32[]{:S(2)}, u32[]{:S(2)}) collective-permute-start(bf16[2,1,64,1024]{3,2,1,0:T(8,128)(2,1)S(1)} %get-tuple-element.257), channel_id=1, source_target_pairs={{0,24},{2,26},{4,28},{6,30},{8,16},{10,18},{12,20},{14,22},{16,8},... | collective-permute-start | bytes 786440 | tf_op jit(solution)/shard_map/ppermute | solution.py:727
  401.1 9.0 %collective-permute-start.73 = (bf16[1,64,1024]{2,1,0:T(8,128)(2,1)S(1)}, bf16[1,64,1024]{2,1,0:T(8,128)(2,1)S(1)}, u32[]{:S(2)}, u32[]{:S(2)}) collective-permute-start(bf16[1,64,1024]{2,1,0:T(8,128)(2,1)S(1)} %fusion.30), channel_id=1, source_target_pairs={{0,4},{2,6},{4,0},{6,2},{8,12},{10,14},{12,8},{14,10},{16,20},{18,... | collective-permute-start | bytes 393224 | tf_op jit(solution)/shard_map/ppermute | solution.py:727
  403.7 9.3 %collective-permute-start.70 = (bf16[2,64,1024]{2,1,0:T(8,128)(2,1)S(1)}, bf16[2,64,1024]{2,1,0:T(8,128)(2,1)S(1)}, u32[]{:S(2)}, u32[]{:S(2)}) collective-permute-start(bf16[2,64,1024]{2,1,0:T(8,128)(2,1)S(1)} %get-tuple-element.253), channel_id=1, source_target_pairs={{0,8},{2,10},{4,12},{6,14},{8,0},{10,2},{12,4},{14,6},{16,24},{18,... | collective-permute-start | bytes 786440 | tf_op jit(solution)/shard_map/ppermute | solution.py:727
  403.7 20.0 %collective-permute-start.71 = (bf16[2,64,1024]{2,1,0:T(8,128)(2,1)S(1)}, bf16[2,64,1024]{2,1,0:T(8,128)(2,1)S(1)}, u32[]{:S(2)}, u32[]{:S(2)}) collective-permute-start(bf16[2,64,1024]{2,1,0:T(8,128)(2,1)S(1)} %get-tuple-element.252), channel_id=1, source_target_pairs={{0,16},{2,18},{4,20},{6,22},{8,24},{10,26},{12,28},{14,30},{16,0},... | collective-permute-start | bytes 786440 | tf_op jit(solution)/shard_map/ppermute | solution.py:727
  405.7 22.8 %collective-permute-start.72 = (bf16[2,64,1024]{2,1,0:T(8,128)(2,1)S(1)}, bf16[2,64,1024]{2,1,0:T(8,128)(2,1)S(1)}, u32[]{:S(2)}, u32[]{:S(2)}) collective-permute-start(bf16[2,64,1024]{2,1,0:T(8,128)(2,1)S(1)} %get-tuple-element.251), channel_id=1, source_target_pairs={{0,24},{2,26},{4,28},{6,30},{8,16},{10,18},{12,20},{14,22},{16,8},... | collective-permute-start | bytes 786440 | tf_op jit(solution)/shard_map/ppermute | solution.py:727
  431.1 21.2 %collective-permute-start.78 = (bf16[128,1024]{1,0:T(8,128)(2,1)S(1)}, bf16[128,1024]{1,0:T(8,128)(2,1)S(1)}, u32[]{:S(2)}, u32[]{:S(2)}) collective-permute-start(bf16[128,1024]{1,0:T(8,128)(2,1)S(1)} %get-tuple-element.247), channel_id=1, source_target_pairs={{0,0},{2,1},{4,2},{6,3},{8,4},{10,5},{12,6},{14,7},{16,8},{18,9},{... | collective-permute-start | bytes 786440 | tf_op jit(solution)/shard_map/ppermute | solution.py:927
  433.0 18.5 %all-to-all-start.1 = ((bf16[16,32,128]{2,1,0:T(8,128)(2,1)}), bf16[16,32,128]{2,1,0:T(8,128)(2,1)S(1)}, u32[]{:S(2)}, u32[]{:S(2)}) async-start(bf16[16,32,128]{2,1,0:T(8,128)(2,1)} %get-tuple-element.248), calls=%async_computation.1 | async-start | bytes 262144 | tf_op jit(solution)/shard_map/all_to_all | solution.py:925
  (84 other events, 588.4 us)

commit v2 on v0

--- a/solution.py
+++ b/solution.py
@@ -3,16 +3,843 @@
 import jax
 import jax.numpy as jnp
 from jax import lax
+from jax.experimental import pallas as pl
+from jax.experimental.pallas import tpu as pltpu
 from jax.sharding import PartitionSpec as P
 
 E = 2048
 NSTATE = 16
 CONV = 4
 DT_RANK = 64
-
+MAPS = DT_RANK + 2 * NSTATE
 
 eps_norm = 1e-05
 eps_spread = 1e-06
+BF = jnp.bfloat16
+F32 = jnp.float32
+LOG2E = 1.4426950408889634
+FAR = 1e4
+LANES = 128
+VMEM = 28 << 20
+
+
+def params(dims=2):
+    return pltpu.CompilerParams(
+        dimension_semantics=("arbitrary",) * dims, vmem_limit_bytes=VMEM
+    )
+
+
+def place_in_doc(starts_ref, row, first, count):
+    pos = lax.broadcasted_iota(jnp.int32, (count, LANES), 0) + first
+    base = jnp.zeros_like(pos)
+    for j in range(1, starts_ref.shape[1]):
+        start = starts_ref[row, j]
+        base = jnp.where(pos >= start, start, base)
+    return pos - base
+
+
+def large(shape, dtype):
+    return pltpu.HBM(shape, dtype)
+
+
+def still(*values):
+    return [pltpu.with_memory_space_constraint(v, pltpu.HBM) for v in values]
+
+
+def sigmoid(v):
+    return 1.0 / (1.0 + jnp.exp2(v * -LOG2E))
+
+
+def silu_slope(v):
+    s = sigmoid(v)
+    return s * (1.0 + v * (1.0 - s))
+
+
+def softplus(v):
+    return jnp.maximum(v, 0.0) + jnp.log1p(jnp.exp2(jnp.abs(v) * -LOG2E))
+
+
+def dot(a, b, dims):
+    return lax.dot_general(a, b, (dims, ((), ())), preferred_element_type=F32)
+
+
+def own_place():
+    s = lax.axis_index("seq")
+    return jnp.stack([s // 4, s // 2 % 2, s % 2]).astype(jnp.int32)
+
+
+def gate_kernel(*refs):
+    pass
+
+
+def gate(values, others):
+    place = pl.BlockSpec(memory_space=pl.ANY)
+    return pl.pallas_call(
+        gate_kernel,
+        in_specs=[place] * (len(values) + len(others)),
+        out_specs=[place] * len(values),
+        out_shape=[jax.ShapeDtypeStruct(v.shape, v.dtype) for v in values],
+        input_output_aliases={i: i for i in range(len(values))},
+        compiler_params=pltpu.CompilerParams(vmem_limit_bytes=1 << 16),
+        cost_estimate=pl.CostEstimate(flops=1, bytes_accessed=1, transcendentals=0),
+        name="gate",
+    )(*values, *others)
+
+
+def put_pieces(own, value, keep, send):
+    rows, seg = keep.shape[2], keep.shape[3]
+    first = own[2] == 0
+    for r in range(rows):
+        for x in range(2):
+            at = (r * 4 + 2 * x) * seg
+            even, odd = value[at : at + seg], value[at + seg : at + 2 * seg]
+            keep[x ^ own[1], 0, r] = jnp.where(first, even, odd).astype(keep.dtype)
+            send[x ^ own[1], 0, r] = jnp.where(first, odd, even).astype(send.dtype)
+
+
+def take_pieces(own, near, far, out):
+    rows, seg = near.shape[2], near.shape[3]
+    first = own[2] == 0
+    for r in range(rows):
+        for x in range(2):
+            at = (r * 4 + 2 * x) * seg
+            a = near[x ^ own[1], 0, r].astype(F32)
+            b = far[x ^ own[1], 0, r].astype(F32)
+            out[at : at + seg, :] = jnp.where(first, a, b)
+            out[at + seg : at + 2 * seg, :] = jnp.where(first, b, a)
+
+
+def pieces_spec(rows, seg, n, at):
+    return pl.BlockSpec((2, 1, rows, seg, n), lambda c, s, o: (0, at(c) ^ o[0], 0, 0, 0))
+
+
+def fixed_block(shape):
+    return pl.BlockSpec(shape, lambda c, s, o: (0,) * len(shape))
+
+
+def front_kernel(
+    starts, own, hid, gain, weight, conv_w, conv_b, xproj,
+    normed_o, x_o, z_o, conv_o, keep_o, send_o,
+    xs,
+):
+    c = pl.program_id(0)
+    rows, t, ch = x_o.shape
+    width = normed_o.shape[2]
+
+    @pl.when(c == 0)
+    def _():
+        xs[:, 0:8, :] = jnp.zeros((rows, 8, ch), F32)
+
+    @pl.when(c > 0)
+    def _():
+        xs[:, 0:8, :] = xs[:, t : t + 8, :]
+
+    res = hid[...].reshape(rows * t, width).astype(F32)
+    inv = lax.rsqrt(jnp.mean(res * res, axis=-1, keepdims=True) + eps_norm)
+    normed = (res * inv * gain[...]).astype(BF)
+    normed_o[...] = normed.reshape(rows, t, width)
+    proj = dot(normed, weight[...], ((1,), (1,)))
+    z_o[...] = proj[:, ch:].reshape(rows, t, ch)
+    x_low = proj[:, :ch].astype(BF).reshape(rows, t, ch)
+    x_o[...] = x_low
+    xs[:, 8 : 8 + t, :] = x_low.astype(F32)
+    for r in range(rows):
+        place = place_in_doc(starts, r, c * t, t)
+        pre = conv_b[...] + conv_w[CONV - 1 : CONV, :] * xs[r, 8 : 8 + t, :]
+        for k in range(1, CONV):
+            lag = conv_w[CONV - 1 - k : CONV - k, :] * xs[r, 8 - k : 8 - k + t, :]
+            pre = pre + jnp.where(place >= k, lag, 0.0)
+        conv_o[r] = (pre * sigmoid(pre)).astype(BF)
+    conv = conv_o[...].reshape(rows * t, ch)
+    put_pieces(own, dot(conv, xproj[...], ((1,), (0,))), keep_o, send_o)
+
+
+def front(starts, own, hid, gain, weight, conv_w, conv_b, xproj):
+    (hid,) = still(hid)
+    rows, length, width = hid.shape
+    ch = conv_w.shape[1]
+    t = length // 4
+    seg = t // 4
+    tok = lambda n: pl.BlockSpec((rows, t, n), lambda c, s, o: (0, c, 0))
+    piece = pieces_spec(rows, seg, MAPS, lambda c: c)
+    return pl.pallas_call(
+        front_kernel,
+        grid_spec=pltpu.PrefetchScalarGridSpec(
+            num_scalar_prefetch=2,
+            grid=(length // t,),
+            in_specs=[
+                tok(width),
+                fixed_block(gain.shape),
+                fixed_block(weight.shape),
+                fixed_block(conv_w.shape),
+                fixed_block(conv_b.shape),
+                fixed_block(xproj.shape),
+            ],
+            out_specs=[tok(width), tok(ch), tok(ch), tok(ch), piece, piece],
+            scratch_shapes=[pltpu.VMEM((rows, t + 8, ch), F32)],
+        ),
+        out_shape=[
+            large((rows, length, width), BF),
+            large((rows, length, ch), BF),
+            large((rows, length, ch), F32),
+            large((rows, length, ch), BF),
+            jax.ShapeDtypeStruct((2, 4, rows, seg, MAPS), F32),
+            jax.ShapeDtypeStruct((2, 4, rows, seg, MAPS), F32),
+        ],
+        compiler_params=params(1),
+        cost_estimate=pl.CostEstimate(flops=1, bytes_accessed=1, transcendentals=0),
+        name="front",
+    )(starts, own, hid, gain, weight, conv_w, conv_b, xproj)
+
+
+def maps_across(low):
+    pick = lax.broadcasted_iota(jnp.int32, (2 * NSTATE, MAPS), 0) + DT_RANK
+    pick = (pick == lax.broadcasted_iota(jnp.int32, (2 * NSTATE, MAPS), 1)).astype(BF)
+    return dot(pick, low, ((1,), (1,)))
+
+
+def half_spec(rows, seg, n, at):
+    return pl.BlockSpec(
+        (1, 1, rows, seg, n),
+        lambda c, s, o: (at(c) % 2 ^ o[1], at(c) // 2 ^ o[0], 0, 0, 0),
+    )
+
+
+def put_halves(own, value, keep, send):
+    rows, seg = keep.shape[2], keep.shape[3]
+    first = own[2] == 0
+    for r in range(rows):
+        even = value[2 * r * seg : (2 * r + 1) * seg]
+        odd = value[(2 * r + 1) * seg : (2 * r + 2) * seg]
+        keep[0, 0, r] = jnp.where(first, even, odd).astype(keep.dtype)
+        send[0, 0, r] = jnp.where(first, odd, even).astype(send.dtype)
+
+
+def take_halves(own, near, far, out):
+    rows, seg = near.shape[2], near.shape[3]
+    first = own[2] == 0
+    for r in range(rows):
+        a = near[0, 0, r].astype(F32)
+        b = far[0, 0, r].astype(F32)
+        out[2 * r * seg : (2 * r + 1) * seg, :] = jnp.where(first, a, b)
+        out[(2 * r + 1) * seg : (2 * r + 2) * seg, :] = jnp.where(first, b, a)
+
+
+def fold(parts):
+    row = lax.broadcasted_iota(jnp.int32, parts[0].shape, 0)
+    upper = row < 4
+    parts = [
+        jnp.where(upper, a, b) + pltpu.roll(jnp.where(upper, b, a), 4, 0)
+        for a, b in zip(parts[:4], parts[4:])
+    ]
+    for step in (2, 1):
+        half = len(parts) // 2
+        upper = row & step == 0
+        parts = [
+            jnp.where(upper, a + pltpu.roll(a, 8 - step, 0), b + pltpu.roll(b, step, 0))
+            for a, b in zip(parts[:half], parts[half:])
+        ]
+    return parts[0]
+
+
+def spread_maps(low, first, out):
+    count, ch = low.shape[0], out.shape[1]
+    pick = lax.broadcasted_iota(jnp.int32, (MAPS, NSTATE * ch), 1) // ch + first
+    pick = (pick == lax.broadcasted_iota(jnp.int32, (MAPS, NSTATE * ch), 0)).astype(BF)
+    wide = dot(low, pick, ((1,), (0,)))
+    for b in range(count // 8):
+        for n in range(NSTATE):
+            row = (b * NSTATE + n) * 8
+            out[row : row + 8, :] = wide[b * 8 : b * 8 + 8, n * ch : (n + 1) * ch]
+
+
+def forward_kernel(starts, own, near, far, dtproj, dtbias, decay, skip, conv, z, *refs):
+    (
+        gated_o, y_o, states_o, last_o, stats_o,
+        state, dtk_s, dtx_s, y_s, across_s, low_s, cm_s,
+    ) = refs[-12:]
+    c = pl.program_id(0)
+    rows, t, ch = conv.shape
+
+    @pl.when(c == 0)
+    def _():
+        state[...] = jnp.zeros_like(state)
+        stats_o[...] = jnp.zeros_like(stats_o)
+
+    rate = -LOG2E * jnp.exp(decay[...])
+    take_halves(own, near, far, low_s)
+    low = low_s[...].astype(BF)
+    dt = softplus(dot(low[:, :DT_RANK], dtproj[...], ((1,), (0,))) + dtbias[...])
+    off = jnp.log(dt) - jnp.log(softplus(dtbias[...]))
+    stats_o[0:1, :] += jnp.sum(off, axis=0, keepdims=True)
+    stats_o[1:2, :] += jnp.sum(off * off, axis=0, keepdims=True)
+    x = conv[...].astype(F32).reshape(rows * t, ch)
+    for r in range(rows):
+        place = place_in_doc(starts, r, c * t, t)
+        dtk_s[r * t : (r + 1) * t, :] = jnp.where(place >= 1, dt[r * t : (r + 1) * t], FAR)
+    dtx_s[...] = dt * x
+    across_s[...] = maps_across(low)
+    spread_maps(low, DT_RANK + NSTATE, cm_s)
+
+    def every_step(states):
+        states, sums = list(states), [None] * rows
+        maps = [across_s[:, r * t : (r + 1) * t] for r in range(rows)]
+        for i in range(t):
+            for r in range(rows):
+                if i % 8 == 0:
+                    sums[r] = []
+                at = r * t + i
+                s = states[r]
+                a = jnp.exp2(dtk_s[pl.ds(at, 1), :] * rate)
+                states_o[r, i] = s
+                b = jnp.broadcast_to(maps[r][:NSTATE, i : i + 1], (NSTATE, ch))
+                s = a * s + dtx_s[pl.ds(at, 1), :] * b
+                ys = s * cm_s[pl.ds(at // 8 * 8 * NSTATE + at % 8, NSTATE, stride=8), :]
+                sums[r].append(ys[:8] + ys[8:])
+                if i % 8 == 7:
+                    y_s[pl.ds(r * t + i - 7, 8), :] = fold(sums[r])
+                states[r] = s
+        return tuple(states)
+
+    states = every_step(tuple(state[r] for r in range(rows)))
+    for r in range(rows):
+        state[r] = states[r]
+        last_o[r] = states[r]
+    y_low = (y_s[...] + skip[...] * x).astype(BF)
+    y_o[...] = y_low.reshape(rows, t, ch)
+    zz = z[...].reshape(rows * t, ch)
+    gated_o[...] = (y_low.astype(F32) * (zz * sigmoid(zz))).astype(BF).reshape(rows, t, ch)
+
+
+def forward_scan(after, starts, own, near, far, dtproj, dtbias, decay, skip, conv, z):
+    conv, z = still(conv, z)
+    rows, length, ch = conv.shape
+    t = length // 8
+    seg = t // 2
+    tok = lambda n: pl.BlockSpec((rows, t, n), lambda c, s, o: (0, c, 0))
+    half = half_spec(rows, seg, MAPS, lambda c: c)
+    return pl.pallas_call(
+        forward_kernel,
+        grid_spec=pltpu.PrefetchScalarGridSpec(
+            num_scalar_prefetch=2,
+            grid=(length // t,),
+            in_specs=[
+                half,
+                half,
+                fixed_block(dtproj.shape),
+                fixed_block(dtbias.shape),
+                fixed_block(decay.shape),
+                fixed_block(skip.shape),
+                tok(ch),
+                tok(ch),
+                *[pl.BlockSpec(memory_space=pl.ANY)] * len(after),
+            ],
+            out_specs=[
+                tok(ch),
+                tok(ch),
+                pl.BlockSpec((rows, t, NSTATE, ch), lambda c, s, o: (0, c, 0, 0)),
+                fixed_block((rows, NSTATE, ch)),
+                fixed_block((8, ch)),
+            ],
+            scratch_shapes=[
+                pltpu.VMEM((rows, NSTATE, ch), F32),
+                pltpu.VMEM((rows * t, ch), F32),
+                pltpu.VMEM((rows * t, ch), F32),
+                pltpu.VMEM((rows * t, ch), F32),
+                pltpu.VMEM((2 * NSTATE, rows * t), F32),
+                pltpu.VMEM((rows * t, MAPS), F32),
+                pltpu.VMEM((rows * t * NSTATE, ch), F32),
+            ],
+        ),
+        out_shape=[
+            large((rows, length, ch), BF),
+            large((rows, length, ch), BF),
+            large((rows, length, NSTATE, ch), F32),
+            jax.ShapeDtypeStruct((rows, NSTATE, ch), F32),
+            jax.ShapeDtypeStruct((8, ch), F32),
+        ],
+        compiler_params=params(1),
+        cost_estimate=pl.CostEstimate(flops=1, bytes_accessed=1, transcendentals=0),
+        name="forward_scan",
+    )(starts, own, near, far, dtproj, dtbias, decay, skip, conv, z, *after)
+
+
+def backward_kernel(
+    starts, own, near, far, dtproj, dtbias, decay, skip, conv, z, y, gg, states, wide,
+    gdtproj_i, misc_i, back_i, next_i, *refs, top,
+):
+    (
+        ggate_o, gxs_o, keep_o, send_o, gdtproj_o, misc_o, back_o, next_o,
+        dtk_s, dt_s, dtx_s, gy_s, p1_s, p2_s, gb_s, gc_s, fold_s, across_s, low_s,
+    ) = refs[-19:]
+    c = pl.program_id(0)
+    rows, t, ch = conv.shape
+    count = rows * t
+
+    @pl.when(c == 0)
+    def _():
+        back_o[...] = back_i[...]
+        next_o[...] = next_i[...]
+        gdtproj_o[...] = gdtproj_i[...]
+        misc_o[...] = misc_i[...]
+
+    neg = -jnp.exp(decay[...])
+    rate = LOG2E * neg
+    take_halves(own, near, far, low_s)
+    low = low_s[...].astype(BF)
+    pre = dot(low[:, :DT_RANK], dtproj[...], ((1,), (0,))) + dtbias[...]
+    dt = softplus(pre)
+    x = conv[...].astype(F32).reshape(count, ch)
+    for r in range(rows):
+        place = place_in_doc(starts, r, (top - c) * t, t)
+        dtk_s[r * t : (r + 1) * t, :] = jnp.where(place >= 1, dt[r * t : (r + 1) * t], FAR)
+    dt_s[...] = dt
+    dtx_s[...] = dt * x
+    zz = z[...].reshape(count, ch)
+    ggv = gg[...].reshape(count, ch)
+    sg = sigmoid(zz)
+    gy = (ggv * (zz * sg)).astype(BF).astype(F32)
+    yv = y[...].astype(F32).reshape(count, ch)
+    ggate = (ggv * yv * (sg * (1.0 + zz * (1.0 - sg)))).astype(BF)
+    ggate_o[...] = ggate.reshape(rows, t, ch)
+    gy_s[...] = gy
+    across_s[...] = maps_across(low)
+
+    def every_step(carry):
+        hs, s_nexts, acc = list(carry[0]), list(carry[1]), carry[2]
+        p1s, p2s = [None] * rows, [None] * rows
+        maps = [across_s[:, r * t : (r + 1) * t] for r in range(rows)]
+        for i in range(t - 1, -1, -1):
+            for r in range(rows):
+                at = r * t + i
+                gyr = gy_s[pl.ds(at, 1), :]
+                g = gyr * jnp.broadcast_to(maps[r][NSTATE:, i : i + 1], (NSTATE, ch)) + hs[r]
+                h = jnp.exp2(dtk_s[pl.ds(at, 1), :] * rate) * g
+                s_prev = states[r, i]
+                q = h * s_prev
+                acc = acc + q * dt_s[pl.ds(at, 1), :]
+                aq = q * neg
+                bg = g * jnp.broadcast_to(maps[r][:NSTATE, i : i + 1], (NSTATE, ch))
+                if i % 8 == 7:
+                    p1s[r], p2s[r] = [], []
+                p1s[r].insert(0, bg[:8] + bg[8:])
+                p2s[r].insert(0, aq[:8] + aq[8:])
+                if i % 8 == 0:
+                    whole8 = pl.ds(at, 8)
+                    p1_s[whole8, :] = fold(p1s[r])
+                    p2_s[whole8, :] = fold(p2s[r])
+                tile = pl.ds(at * NSTATE, NSTATE)
+                gb_s[tile, :] = (g * dtx_s[pl.ds(at, 1), :]).astype(BF)
+                gc_s[tile, :] = (gyr * s_nexts[r]).astype(BF)
+                hs[r], s_nexts[r] = h, s_prev
+        return tuple(hs), tuple(s_nexts), acc
+
+    hs, s_nexts, acc = every_step(
+        (
+            tuple(back_o[r] for r in range(rows)),
+            tuple(next_o[r] for r in range(rows)),
+            jnp.zeros((NSTATE, ch), F32),
+        ),
+    )
+    for r in range(rows):
+        back_o[r] = hs[r]
+        next_o[r] = s_nexts[r]
+    p1, p2 = p1_s[...], p2_s[...]
+    gxs_o[...] = (dt * p1 + skip[...] * gy).reshape(rows, t, ch)
+    gpre = ((p2 + x * p1) * sigmoid(pre)).astype(BF)
+    gdtproj_o[...] += dot(low[:, :DT_RANK], gpre, ((0,), (0,)))
+    misc_o[0:NSTATE, :] += neg * acc
+    misc_o[NSTATE : NSTATE + 1, :] += jnp.sum(gpre.astype(F32), axis=0, keepdims=True)
+    misc_o[NSTATE + 1 : NSTATE + 2, :] += jnp.sum(gy * x, axis=0, keepdims=True)
+    ones = jnp.ones((ch, ch), BF)
+    entry = lax.broadcasted_iota(jnp.int32, (1, NSTATE, ch), 1) + DT_RANK
+    lane = lax.broadcasted_iota(jnp.int32, (1, NSTATE, ch), 2)
+    maps = jnp.zeros((count, NSTATE, ch), F32)
+    for ref in (gb_s, gc_s):
+        every = dot(ref[...], ones, ((1,), (0,))).reshape(count, NSTATE, ch)
+        maps = jnp.where(lane == entry, every, maps)
+        entry = entry + NSTATE
+    fold_s[...] = (maps[:, :8] + maps[:, 8:]).reshape(count * 8, ch)
+    total = dot(gpre, wide[...], ((1,), (0,)))
+    for j in range(8):
+        total = total + fold_s[pl.ds(j, count, stride=8), :][:, :MAPS]
+    put_halves(own, total, keep_o, send_o)
+
+
+def widened(dtproj):
+    return jnp.pad(dtproj.T, ((0, 0), (0, 2 * NSTATE)))
+
+
+def backward_scan(
+    top, chunks, after, so_far, starts, own, near, far, dtproj, dtbias, decay, skip, conv, z, y,
+    gg, states, wide,
+):
+    conv, z, y, gg, states = still(conv, z, y, gg, states)
+    rows, length, ch = conv.shape
+    t = length // 8
+    seg = t // 2
+    done, passed = so_far
+    fixed = 18
+    tok = lambda n: pl.BlockSpec((rows, t, n), lambda c, s, o: (0, top - c, 0))
+    half = half_spec(rows, seg, MAPS, lambda c: top - c)
+    small = [(DT_RANK, ch), (24, ch), (rows, NSTATE, ch), (rows, NSTATE, ch)]
+    return pl.pallas_call(
+        partial(backward_kernel, top=top),
+        grid_spec=pltpu.PrefetchScalarGridSpec(
+            num_scalar_prefetch=2,
+            grid=(chunks,),
+            in_specs=[
+                half,
+                half,
+                fixed_block(dtproj.shape),
+                fixed_block(dtbias.shape),
+                fixed_block(decay.shape),
+                fixed_block(skip.shape),
+                tok(ch),
+                tok(ch),
+                tok(ch),
+                tok(ch),
+                pl.BlockSpec((rows, t, NSTATE, ch), lambda c, s, o: (0, top - c, 0, 0)),
+                fixed_block(wide.shape),
+                *[fixed_block(s) for s in small],
+                *[pl.BlockSpec(memory_space=pl.ANY)] * (len(done) + len(after)),
+            ],
+            out_specs=[tok(ch), tok(ch), half, half, *[fixed_block(s) for s in small]],
+            scratch_shapes=[
+                pltpu.VMEM((rows * t, ch), F32),
+                pltpu.VMEM((rows * t, ch), F32),
+                pltpu.VMEM((rows * t, ch), F32),
+                pltpu.VMEM((rows * t, ch), F32),
+                pltpu.VMEM((rows * t, ch), F32),
+                pltpu.VMEM((rows * t, ch), F32),
+                pltpu.VMEM((rows * t * NSTATE, ch), BF),
+                pltpu.VMEM((rows * t * NSTATE, ch), BF),
+                pltpu.VMEM((rows * t * 8, ch), F32),
+                pltpu.VMEM((2 * NSTATE, rows * t), F32),
+                pltpu.VMEM((rows * t, MAPS), F32),
+            ],
+        ),
+        out_shape=[
+            large((rows, length, ch), BF),
+            large((rows, length, ch), F32),
+            jax.ShapeDtypeStruct((2, 4, rows, seg, MAPS), F32),
+            jax.ShapeDtypeStruct((2, 4, rows, seg, MAPS), F32),
+            *[jax.ShapeDtypeStruct(s, F32) for s in small],
+        ],
+        input_output_aliases={fixed + i: i for i in range(len(done))},
+        compiler_params=params(1),
+        cost_estimate=pl.CostEstimate(flops=1, bytes_accessed=1, transcendentals=0),
+        name="backward_scan",
+    )(
+        starts, own, near, far, dtproj, dtbias, decay, skip, conv, z, y, gg, states, wide,
+        *passed, *done, *after,
+    )
+
+
+def tail_kernel(
+    starts, own, near, far, conv, gxs, ggate, x, before, normed, weight, conv_w, conv_b, xproj, *refs
+):
+    keep_o, send_o, gin_o, gxproj_o, misc_o, xs, gm_s, low_s, gx_s = refs[-9:]
+    c = pl.program_id(0)
+    chunks = pl.num_programs(0)
+    rows, t, ch = conv.shape
+    count = rows * t
+
+    @pl.when(c == 0)
+    def _():
+        gin_o[...] = jnp.zeros_like(gin_o)
+        gxproj_o[...] = jnp.zeros_like(gxproj_o)
+        misc_o[...] = jnp.zeros_like(misc_o)
+        gm_s[:, :, t : t + 8, :] = jnp.zeros((CONV - 1, rows, 8, ch), F32)
+
+    @pl.when(c > 0)
+    def _():
+        gm_s[:, :, t : t + 8, :] = gm_s[:, :, 0:8, :]
+
+    xs[:, 0:16, :] = before[...].astype(F32)
+    xs[:, 16 : 16 + t, :] = x[...].astype(F32)
+    take_pieces(own, near, far, low_s)
+    low = low_s[...].astype(BF)
+    gconv = gxs[...].reshape(count, ch) + dot(low, xproj[...], ((1,), (1,)))
+    gxproj_o[...] += dot(conv[...].reshape(count, ch), low, ((0,), (0,)))
+    for r in range(rows):
+        place = place_in_doc(starts, r, (chunks - 1 - c) * t, t)
+        lags = [xs[r, 16 : 16 + t, :]]
+        pre = conv_b[...] + conv_w[CONV - 1 : CONV, :] * lags[0]
+        for k in range(1, CONV):
+            lags.append(jnp.where(place >= k, xs[r, 16 - k : 16 - k + t, :], 0.0))
+            pre = pre + conv_w[CONV - 1 - k : CONV - k, :] * lags[k]
+        gpre = gconv[r * t : (r + 1) * t] * silu_slope(pre)
+        gx = conv_w[CONV - 1 : CONV, :] * gpre
+        for k in range(CONV):
+            misc_o[CONV - 1 - k : CONV - k, :] += jnp.sum(gpre * lags[k], axis=0, keepdims=True)
+            if k:
+                gm_s[k - 1, r, 0:t, :] = jnp.where(place >= k, gpre, 0.0)
+                gx = gx + conv_w[CONV - 1 - k : CONV - k, :] * gm_s[k - 1, r, k : k + t, :]
+        misc_o[CONV : CONV + 1, :] += jnp.sum(gpre, axis=0, keepdims=True)
+        gx_s[r * t : (r + 1) * t, :] = gx.astype(BF)
+    gproj = jnp.concatenate([gx_s[...], ggate[...].reshape(count, ch)], axis=1)
+    gin_o[...] += dot(gproj, normed[...].reshape(count, normed.shape[2]), ((0,), (0,)))
+    put_pieces(own, dot(gproj, weight[...], ((1,), (0,))), keep_o, send_o)
+
+
+def tail(after, starts, own, near, far, conv, gxs, ggate, x, normed, weight, conv_w, conv_b, xproj):
+    conv, gxs, ggate, x, normed = still(conv, gxs, ggate, x, normed)
+    rows, length, width = normed.shape
+    ch = conv.shape[2]
+    t = length // 4
+    seg = t // 4
+    last = length // t - 1
+    tok = lambda n: pl.BlockSpec((rows, t, n), lambda c, s, o: (0, last - c, 0))
+    piece = lambda n: pieces_spec(rows, seg, n, lambda c: last - c)
+    before = pl.BlockSpec(
+        (rows, 16, ch), lambda c, s, o: (0, jnp.maximum((last - c) * (t // 16) - 1, 0), 0)
+    )
+    return pl.pallas_call(
+        tail_kernel,
+        grid_spec=pltpu.PrefetchScalarGridSpec(
+            num_scalar_prefetch=2,
+            grid=(length // t,),
+            in_specs=[
+                piece(MAPS),
+                piece(MAPS),
+                tok(ch),
+                tok(ch),
+                tok(ch),
+                tok(ch),
+                before,
+                tok(width),
+                fixed_block(weight.shape),
+                fixed_block(conv_w.shape),
+                fixed_block(conv_b.shape),
+                fixed_block(xproj.shape),
+                *[pl.BlockSpec(memory_space=pl.ANY)] * len(after),
+            ],
+            out_specs=[
+                piece(width),
+                piece(width),
+                fixed_block(weight.shape),
+                fixed_block((ch, MAPS)),
+                fixed_block((8, ch)),
+            ],
+            scratch_shapes=[
+                pltpu.VMEM((rows, t + 16, ch), F32),
+                pltpu.VMEM((CONV - 1, rows, t + 8, ch), F32),
+                pltpu.VMEM((rows * t, MAPS), F32),
+                pltpu.VMEM((rows * t, ch), BF),
+            ],
+        ),
+        out_shape=[
+            large((2, 4, rows, seg, width), BF),
+            large((2, 4, rows, seg, width), BF),
+            jax.ShapeDtypeStruct(weight.shape, F32),
+            jax.ShapeDtypeStruct((ch, MAPS), F32),
+            jax.ShapeDtypeStruct((8, ch), F32),
+        ],
+        compiler_params=params(1),
+        cost_estimate=pl.CostEstimate(flops=1, bytes_accessed=1, transcendentals=0),
+        name="tail",
+    )(starts, own, near, far, conv, gxs, ggate, x, x, normed, weight, conv_w, conv_b, xproj, *after)
+
+
+def cross(v, bits):
+    return lax.ppermute(v, "seq", [(s, s ^ bits) for s in range(16)])
+
+
+def swap_row(v):
+    return lax.ppermute(v, "row", [(0, 1), (1, 0)])
+
+
+def total_of_all(v):
+    v = v + swap_row(v)
+    for bits in (1, 2, 4, 8):
+        v = v + cross(v, bits)
+    return v
+
+
+def sum_pieces(keep, send, sent, others):
+    (acc,) = gate([keep.astype(F32) + cross(send, 1).astype(F32)], others)
+    acc = acc[0] + cross(acc[1].astype(sent), 2).astype(F32)
+    total = acc[0]
+    for k in (1, 2, 3):
+        total = total + cross(acc[k].astype(sent), 4 * k).astype(F32)
+    return total
+
+
+def spread_pieces(own_piece):
+    line = jnp.stack([own_piece] + [cross(own_piece, 4 * k) for k in (1, 2, 3)])
+    near = jnp.stack([line, cross(line, 2)])
+    return near, cross(near, 1)
+
+
+def gather_tokens(v):
+    return lax.all_gather(v, "seq", axis=1, tiled=True)
+
+
+def up(v):
+    return v.astype(F32)
+
+
+class Sum:
+    def __init__(self, keep, send):
+        self.keep, self.near = keep, cross(send, 1)
+        self.head = keep.shape[2] - keep.shape[2] // 3
+
+    def part(self, *at):
+        return up(self.keep[at]) + up(self.near[at])
+
+    def first(self, others):
+        (self.near,) = gate([self.near], others)
+        a, b = slice(0, self.head), slice(self.head, None)
+        sent = [self.part(1, slice(None), a).astype(BF)]
+        sent += [self.part(slice(None), k, b).astype(BF) for k in (1, 2, 3)]
+        self.second_of = [cross(sent[0], 2), *cross_z(sent[1:])]
+        return sent
+
+    def second(self, others):
+        across, *line = gate(self.second_of, others)
+        a, b = slice(0, self.head), slice(self.head, None)
+        sent = [(self.part(0, k, a) + up(across[k])).astype(BF) for k in (1, 2, 3)]
+        sent.append((self.part(1, 0, b) + sum(up(v[1]) for v in line)).astype(BF))
+        self.third_of = [*cross_z(sent[:3]), cross(sent[3], 2)]
+        self.a = self.part(0, 0, a) + up(across[0])
+        self.b = self.part(0, 0, b) + sum(up(v[0]) for v in line)
+        return sent
+
+    def third(self, others):
+        *line, across = gate(self.third_of, others)
+        return jnp.concatenate([self.a + sum(up(v) for v in line), self.b + up(across)])
+
+
+def cross_z(pieces):
+    return [cross(v, 4 * k) for k, v in zip((1, 2, 3), pieces)]
+
+
+def channel_plan(
+    hidden_in, grad_out, doc_starts, norm_gain, in_proj, out_proj, conv_weight, conv_bias,
+    x_proj, dt_proj, dt_bias, decay_log, skip_scale,
+):
+    row_count, seg_len, width = hidden_in.shape
+    shards = lax.axis_size("seq")
+    full_len = seg_len * shards
+    ch = conv_weight.shape[1]
+    first = lax.axis_index("row") == 0
+    both = ("seq", "row")
+    place = 2 * lax.axis_index("seq") + lax.axis_index("row")
+    own = own_place()
+    gain_len = norm_gain.shape[0]
+
+    hid = gather_tokens(hidden_in)
+    gout = gather_tokens(grad_out)
+    to_shard = [(i, 2 * (i % shards) + i // shards) for i in range(2 * shards)]
+    mine = lax.ppermute(in_proj, both, to_shard)
+    other = swap_row(mine)
+    weight = jnp.concatenate([jnp.where(first, mine, other), jnp.where(first, other, mine)])
+    other = swap_row(out_proj)
+    pair = jnp.concatenate([jnp.where(first, out_proj, other), jnp.where(first, other, out_proj)])
+    out_cols = lax.all_to_all(pair, "seq", split_axis=1, concat_axis=0, tiled=True)
+    spot = jnp.zeros((2 * shards, gain_len), F32)
+    spot = lax.dynamic_update_slice(spot, norm_gain.astype(F32)[None], (place, 0))
+    gain_whole = total_of_all(spot).reshape(1, width)
+    vectors = [
+        conv_weight.astype(F32),
+        conv_bias.astype(F32)[None],
+        dt_bias.astype(F32)[None],
+        decay_log.astype(F32),
+        skip_scale.astype(F32)[None],
+        widened(dt_proj),
+        x_proj,
+    ]
+    weight, gain_whole, out_cols, *vectors = gate([weight, gain_whole, out_cols, *vectors], [])
+    conv_w, conv_b, dtb, decay, skip, wide, x_proj = vectors
+
+    normed, x, z, conv, keep, send = front(
+        doc_starts, own, hid, gain_whole, weight, conv_w, conv_b, x_proj
+    )
+    low = sum_pieces(keep, send, F32, []).astype(BF)
+    near, far = spread_pieces(low)
+    gated, y, states, last, stats = forward_scan(
+        [], doc_starts, own, near, far, dt_proj, dtb, decay, skip, conv, z
+    )
+    mixed = jnp.einsum("rtc,dc->rtd", gated, out_cols, preferred_element_type=F32).astype(BF)
+    (cols,) = gate([out_cols], [mixed])
+    mixed = lax.psum_scatter(mixed, "seq", scatter_dimension=1, tiled=True)
+    gg = jnp.einsum("rtd,dc->rtc", gout, cols, preferred_element_type=F32)
+    passed = [jnp.zeros((DT_RANK, ch), F32), jnp.zeros((24, ch), F32), jnp.zeros_like(last), last]
+    ggate, gxs, keep, send, gdtproj, misc, _, _ = backward_scan(
+        7, 8, [], ([], passed), doc_starts, own, near, far, dt_proj, dtb, decay, skip, conv, z, y,
+        gg, states, wide,
+    )
+    keep, send, gated = gate([keep, send, gated], [])
+    low = sum_pieces(keep, send, BF, []).astype(BF)
+    gout_cols = jnp.einsum("rtd,rtc->dc", gout, gated, preferred_element_type=F32)
+    parts = gout_cols.reshape(shards, 2, width // (2 * shards), ch)
+    keep = jnp.where(first, parts[:, 0], parts[:, 1])
+    send = jnp.where(first, parts[:, 1], parts[:, 0])
+    out_half = (keep + swap_row(send)).astype(BF)
+    near, far = spread_pieces(low)
+    keep, send, gin, gxproj, cmisc = tail(
+        [out_half], doc_starts, own, near, far, conv, gxs, ggate, x, normed, weight, conv_w, conv_b,
+        x_proj,
+    )
+    gnormed = Sum(keep, send)
+    gnormed.first([])
+    held = [gin, gdtproj, misc, stats, cmisc, gxproj]
+    gin, gdtproj, misc, stats, cmisc, gxproj = gate(held, [gnormed.second_of[1]])
+    grad_gain = jnp.sum(weight.astype(F32) * gin, axis=0) / gain_whole[0]
+    grad_gain = grad_gain.reshape(2 * shards, gain_len)
+    grad_gain = grad_gain + swap_row(grad_gain)
+    grad_gain = grad_gain + cross(grad_gain, 1)
+    keep = jnp.where(first, gin[:ch], gin[ch:])
+    send = jnp.where(first, gin[ch:], gin[:ch])
+    in_half = (keep + swap_row(send.astype(BF)).astype(F32)).astype(BF)
+    small = jnp.concatenate([gdtproj, misc, stats, cmisc, jnp.transpose(gxproj)])
+    small = small + swap_row(small)
+    gnormed.second([in_half, small, grad_gain])
+    grad_gain, out_half = gate([grad_gain, out_half], [gnormed.third_of[0]])
+    out_share = lax.all_to_all(out_half, "seq", split_axis=0, concat_axis=0, tiled=True)
+    grad_gain = grad_gain + cross(grad_gain, 2)
+    *gnormed.third_of, grad_gain = gate([*gnormed.third_of, grad_gain], [])
+    gnormed = gnormed.third([])
+    in_half, grad_gain = gate([in_half, grad_gain], [gnormed])
+    to_owner = [(b, a) for a, b in to_shard]
+    in_share = lax.ppermute(in_half, both, to_owner).astype(F32)
+    grad_gain = grad_gain + sum(cross_z([grad_gain] * 3))
+    out_share = jnp.transpose(out_share.astype(F32), (1, 0, 2)).reshape(width // (2 * shards), E)
+
+    residual = hidden_in.astype(F32)
+    hidden_out = (residual + mixed.astype(F32)).astype(BF)
+    inv_rms = lax.rsqrt(jnp.mean(residual * residual, axis=-1, keepdims=True) + eps_norm)
+    scaled = residual * inv_rms
+    grad_scaled = gnormed * gain_whole
+    grad_hidden = grad_out.astype(F32) + inv_rms * (
+        grad_scaled - scaled * jnp.mean(grad_scaled * scaled, axis=-1, keepdims=True)
+    )
+    grad_gain = lax.dynamic_slice(grad_gain, (place, 0), (1, gain_len))[0]
+    gdtproj, misc, stats, cmisc, gxproj = jnp.split(
+        small, [DT_RANK, DT_RANK + 24, DT_RANK + 32, DT_RANK + 40]
+    )
+    token_count = full_len * row_count * 2
+    mean_off = stats[0] / token_count
+    spread = jnp.sqrt(stats[1] / token_count - mean_off * mean_off + eps_spread)
+    centre = jnp.log(jax.nn.softplus(dt_bias.astype(F32)))
+    return (
+        hidden_out,
+        grad_hidden,
+        grad_gain,
+        in_share,
+        out_share,
+        cmisc[:CONV],
+        cmisc[CONV],
+        jnp.transpose(gxproj),
+        gdtproj,
+        misc[NSTATE],
+        misc[:NSTATE],
+        misc[NSTATE + 1],
+        jnp.stack([centre + mean_off, spread]),
+    )
+
+
 block_len = 16
 
 
@@ -32,7 +859,7 @@
     return jnp.pad(values, widths)[:, offset:]
 
 
-def silu_slope(values):
+def slope_of_silu(values):
     logistic = jax.nn.sigmoid(values)
     return logistic * (1.0 + values * (1.0 - logistic))
 
@@ -91,7 +918,7 @@
     return outputs + skip_full * x_vals
 
 
-def local(
+def token_plan(
     hidden_in,
     grad_out,
     doc_starts,
@@ -167,7 +994,7 @@
     grad_out_proj = jnp.einsum("rtd,rte->de", grad_out, gated, preferred_element_type=jnp.float32)
     grad_gated = jnp.einsum("rtd,de->rte", grad_out, out_whole, preferred_element_type=jnp.float32)
     grad_y = (grad_gated * gate_act).astype(jnp.bfloat16)
-    grad_gate = (grad_gated * y_token_vals * silu_slope(gate_z)).astype(jnp.bfloat16)
+    grad_gate = (grad_gated * y_token_vals * slope_of_silu(gate_z)).astype(jnp.bfloat16)
     grad_y_chan = lax.all_to_all(grad_y, "seq", split_axis=2, concat_axis=1, tiled=True)
     grad_dt_scan, grad_x_scan, grad_b, grad_c, grad_decay, grad_skip = pullback(
         grad_y_chan.astype(jnp.float32)
@@ -187,7 +1014,7 @@
     grad_conv_out = grad_x_scan + jnp.einsum(
         "rtm,cm->rtc", grad_dtbc, x_proj, preferred_element_type=jnp.float32
     )
-    grad_pre_conv = grad_conv_out * silu_slope(pre_conv)
+    grad_pre_conv = grad_conv_out * slope_of_silu(pre_conv)
     grad_conv_bias = jnp.sum(grad_pre_conv, axis=(0, 1))
     conv_rows = [None] * CONV
     grad_x = jnp.zeros_like(grad_pre_conv)
@@ -252,8 +1079,10 @@
 
 
 def solution(mesh):
+    fits = mesh.shape["seq"] == 16 and mesh.shape["row"] == 2
+    plan = channel_plan if fits else token_plan
     return jax.shard_map(
-        local,
+        plan,
         mesh=mesh,
         in_specs=(
             P("row", "seq", None),

time: 3340 us -> 385 us (0.12); the launches traced: 3290 us -> 383 us
  other arithmetic: 1270 us -> 28.9 us
  local copies, waits for them, and re-layouts: 1050 us -> 8.12 us
  waiting for transfers between devices: 555 us -> 156 us
  blocking collectives: 290 us -> 0 us
  Pallas kernels: 0 us -> 77.3 us
  starting transfers between devices: 29.5 us -> 83 us
    dynamic_update_slice x336 -> x1, other arithmetic: 569 us -> 0.66 us  [channel_plan(): lax.dynamic_update_slice(spot, norm_gain.astype(F32)[None], (place, 0))]
    mul x379 -> x0, other arithmetic: 411 us -> none  [the longest x144 240 us: local_pass(): return ((state_now, decay_now * product), None)]
    reduce_scatter x1, waiting for transfers between devices: 361 us -> 0.01 us  [channel_plan(): mixed = lax.psum_scatter(mixed, 'seq', scatter_dimension=1, tiled=True)]
    mul x673 -> x0, local copies, waits for them, and re-layouts: 310 us -> none  [the longest x288 122 us: decay_at(): jnp.exp(dt_now[None, :, :] * decay_rates[:, :, None])]
    reduce_sum x197 -> x2, other arithmetic: 262 us -> 0.31 us  [the longest x1 0.16 us: channel_plan(): grad_gain = jnp.sum(weight.astype(F32) * gin, axis=0) / gain_whole[0]]
    another operation x77 -> x0, local copies, waits for them, and re-layouts: 232 us -> none
    dynamic_update_slice x441 -> x1, local copies, waits for them, and re-layouts: 216 us -> 0.03 us  [channel_plan(): lax.dynamic_update_slice(spot, norm_gain.astype(F32)[None], (place, 0))]
    unnamed x3 -> x0, blocking collectives: 158 us -> none
  transfers between devices with their start and end apart: 8 -> 52, of which waited for: 6 -> 28; matrix products, arithmetic and copies ran while one was open for 3% -> 11% of each run, Pallas kernels for 0% -> 11%
where the time goes in v2:
time: 385 us; the launch traced here: 383 us
  waiting for transfers between devices  156 us (41%)
  starting transfers between devices  83 us (22%)
  Pallas kernels  77.3 us (20%)
  other arithmetic  28.9 us (8%)
  matrix products  15.6 us (4%)
  between operations  14.3 us (4%)
  local copies, waits for them, and re-layouts  8.12 us (2%)
    ppermute x38, waiting for transfers between devices, cross(): return lax.ppermute(v, 'seq', [(s, s ^ bits) for s in range(16)])  93.2 us
    ppermute x38, starting transfers between devices, cross(): return lax.ppermute(v, 'seq', [(s, s ^ bits) for s in range(16)])  58.5 us
    all_gather x2, waiting for transfers between devices, gather_tokens(): return lax.all_gather(v, 'seq', axis=1, tiled=True)  35.2 us
    pallas_call x1, Pallas kernels, backward_scan(): pl.pallas_call(partial(backward_kernel, top=top), grid_spec=pltpu.Prefetc...  35.1 us
    pallas_call x1, Pallas kernels, forward_scan(): pl.pallas_call(forward_kernel, grid_spec=pltpu.PrefetchScalarGridSpec(num...  19.4 us
    ppermute x1, waiting for transfers between devices, channel_plan(): in_share = lax.ppermute(in_half, both, to_owner).astype(F32)  13.6 us
    ppermute x7, waiting for transfers between devices, swap_row(): return lax.ppermute(v, 'row', [(0, 1), (1, 0)])  12.8 us
    pallas_call x1, Pallas kernels, tail(): pl.pallas_call(tail_kernel, grid_spec=pltpu.PrefetchScalarGridSpec(num_sc...  12.4 us
  transfers between devices with their start and end apart: 52, of which 28 were waited for; matrix products, arithmetic and copies ran while one was open for 11% of the time, Pallas kernels for 11%

profile of v2, /device:TPU:18, one launch (start us, length us, event | category | flops | bytes accessed | tf_op | source)
XLA Modules:
  0.0 383.5 jit_solution(4003184744932392645)
XLA Ops:
  10.9 2.2 collective-permute-done.2
  15.5 2.3 collective-permute-start
  18.7 3.7 collective-permute-done.4
  22.4 7.1 %collective-permute-start.5 = (f32[32,32]{1,0:T(8,128)S(1)}, f32[32,32]{1,0:T(8,128)S(1)}, u32[]{:S(2)}, u32[]{:S(2)}) collective-permute-start(f32[32,32]{1,0:T(8,128)S(1)} %add.320), channel_id=1, source_target_pairs={{0,8},{2,10},{4,12},{6,14},{8,0},{10,2},{12,4},{14,6},{16,24},{18,... | collective-permute-start | bytes 12296 | tf_op jit(solution)/shard_map/ppermute | solution.py:646
  31.2 6.2 %all-to-all-start = ((bf16[64,16,128]{2,0,1:T(8,128)(2,1)}), bf16[64,16,128]{2,0,1:T(8,128)(2,1)S(1)}, u32[]{:S(2)}, u32[]{:S(2)}) async-start(bf16[64,16,128]{2,0,1:T(8,128)(2,1)} %copy_bitcast_fusion.1), calls=%async_computation | async-start | bytes 524288 | tf_op jit(solution)/shard_map/all_to_all | solution.py:740
  42.0 2.5 collective-permute-done.6
  45.9 35.2 %all-gather.3.cloned.1.call-done.hid = bf16[3,1024,1024]{2,1,0:T(8,128)(2,1)} async-done(((bf16[3,64,1024]{2,1,0:T(8,128)(2,1)}), bf16[3,1024,1024]{2,1,0:T(8,128)(2,1)}) %all-gather.3.cloned.1.call-update) | async-done | bytes 6291472 | tf_op jit(solution)/shard_map/all_gather | solution.py:676
  81.2 10.4 %front.1 = (bf16[3,1024,1024]{2,1,0:T(8,128)(2,1)}, bf16[3,1024,128]{2,1,0:T(8,128)(2,1)}, f32[3,1024,128]{2,1,0:T(8,128)}, bf16[3,1024,128]{2,1,0:T(8,128)(2,1)...) custom-call(s32[3,8]{1,0:T(4,128)S(1)} %copy-done.3, s32[3]{0:T(128)S(1)} %pad_add_fusion.own, ...), custom_call_target="tpu_custom_call" | custom-call | flops 1 | bytes 1 | tf_op jit(solution)/shard_map/front/pallas_call | solution.py:165
  91.8 2.0 collective-permute-done.8
  95.5 10.3 %collective-permute-done.9 = f32[4,3,64,96]{3,2,1,0:T(8,128)S(1)} collective-permute-done((f32[4,3,64,96]{3,2,1,0:T(8,128)S(1)}, f32[4,3,64,96]{3,2,1,0:T(8,128)S(1)}, u32[]{:S(2)}, u32[]{:S(2)}) %collective-permute-start.9) | collective-permute-done | bytes 294944 | tf_op jit(solution)/shard_map/ppermute | solution.py:646
  107.5 2.9 collective-permute-start.11
  111.7 11.6 %collective-permute-done.12 = f32[3,64,96]{2,1,0:T(8,128)S(1)} collective-permute-done((f32[3,64,96]{2,1,0:T(8,128)S(1)}, f32[3,64,96]{2,1,0:T(8,128)S(1)}, u32[]{:S(2)}, u32[]{:S(2)}) %collective-permute-start.12) | collective-permute-done | bytes 73760 | tf_op jit(solution)/shard_map/ppermute | solution.py:646
  123.3 6.7 %collective-permute-start.15 = (bf16[3,64,96]{2,1,0:T(8,128)(2,1)S(1)}, bf16[3,64,96]{2,1,0:T(8,128)(2,1)S(1)}, u32[]{:S(2)}, u32[]{:S(2)}) collective-permute-start(bf16[3,64,96]{2,1,0:T(8,128)(2,1)S(1)} %fusion.31), channel_id=1, source_target_pairs={{0,24},{2,26},{4,28},{6,30},{8,16},{10,18},{12,20},{14,22},{16,8},... | collective-permute-start | bytes 110600 | tf_op jit(solution)/shard_map/ppermute | solution.py:646
  130.1 5.2 %collective-permute-start.14 = (bf16[3,64,96]{2,1,0:T(8,128)(2,1)S(1)}, bf16[3,64,96]{2,1,0:T(8,128)(2,1)S(1)}, u32[]{:S(2)}, u32[]{:S(2)}) collective-permute-start(bf16[3,64,96]{2,1,0:T(8,128)(2,1)S(1)} %fusion.31), channel_id=1, source_target_pairs={{0,16},{2,18},{4,20},{6,22},{8,24},{10,26},{12,28},{14,30},{16,0},... | collective-permute-start | bytes 110600 | tf_op jit(solution)/shard_map/ppermute | solution.py:646
  135.2 4.7 %collective-permute-done.14 = bf16[3,64,96]{2,1,0:T(8,128)(2,1)S(1)} collective-permute-done((bf16[3,64,96]{2,1,0:T(8,128)(2,1)S(1)}, bf16[3,64,96]{2,1,0:T(8,128)(2,1)S(1)}, u32[]{:S(2)}, u32[]{:S(2)}) %collective-permute-start.14) | collective-permute-done | bytes 36896 | tf_op jit(solution)/shard_map/ppermute | solution.py:646
  140.0 2.4 collective-permute-start.16
  142.4 3.6 collective-permute-done.16
  146.2 2.0 collective-permute-done.17.far
  148.2 19.4 %forward_scan.1 = (bf16[3,1024,128]{2,1,0:T(8,128)(2,1)}, bf16[3,1024,128]{2,1,0:T(8,128)(2,1)}, f32[3,1024,16,128]{3,2,1,0:T(8,128)}, f32[3,16,128]{2,1,0:T(8,128)S(1)}, f32[8,128]{1,0:T(8,128)S(1)}) custom-call(s32[3,8]{1,0:T(4,128)S(1)} %copy-done.3, s32[3]{0:T(128)S(1)} %pad_add_fusion.own, bf16[2,4,3,64,96]{4,3,2,1,0:T(8,128)(2,1)S(1)} %pad_maximum_fusion.2.near, ...), custom_call_target="tpu_custom_call" | custom-call | flops 1 | bytes 1 | tf_op jit(solution)/shard_map/forward_scan/pallas_call | solution.py:321
  167.7 5.6 %convolution_convert_fusion.refs_1_ = bf16[3,1024,1024]{2,1,0:T(8,128)(2,1)} fusion(bf16[3,1024,128]{2,1,0:T(8,128)(2,1)} %get-tuple-element.83.refs_2_, bf16[1024,128]{1,0:T(8,128)(2,1)S(1)} %get-tuple-element.84.refs_0_), kind=kOutput, calls=%fused_computation | convolution fusion | flops 808452096 | bytes 7340032 | tf_op jit(solution)/shard_map/rtc,dc->rtd/dot_general | solution.py:764
  173.3 2.8 copy-done
  176.1 5.7 %convolution_bitcast_fusion.gg = f32[3,1024,128]{2,1,0:T(8,128)} fusion(bf16[3,1024,1024]{2,1,0:T(8,128)(2,1)} %all-gather.5.cloned.1.call-done, bf16[1024,128]{1,0:T(8,128)(2,1)S(1)} %gate.14), kind=kOutput, calls=%fused_computation.2 | convolution fusion | flops 805306368 | bytes 8126464 | tf_op jit(solution)/shard_map/rtd,dc->rtc/dot_general | solution.py:767
  181.8 35.1 %backward_scan.1 = (bf16[3,1024,128]{2,1,0:T(8,128)(2,1)}, f32[3,1024,128]{2,1,0:T(8,128)}, f32[2,4,3,64,96]{4,3,2,1,0:T(8,128)S(1)}, f32[2,4,3,64,96]{4,3,2,1,0...) custom-call(s32[3,8]{1,0:T(4,128)S(1)} %copy-done.3, ...), custom_call_target="tpu_custom_call" | custom-call | flops 1 | bytes 1 | tf_op jit(solution)/shard_map/backward_scan/pallas_call | solution.py:486
  217.2 2.1 collective-permute-done.18
  221.3 5.4 %collective-permute-done.19 = bf16[4,3,64,96]{3,2,1,0:T(8,128)(2,1)S(1)} collective-permute-done((bf16[4,3,64,96]{3,2,1,0:T(8,128)(2,1)S(1)}, bf16[4,3,64,96]{3,2,1,0:T(8,128)(2,1)S(1)}, u32[]{:S(2)}, u32[]{:S(2)}) %collective-permute-start.19) | collective-permute-done | bytes 147488 | tf_op jit(solution)/shard_map/ppermute | solution.py:646
  231.2 2.5 collective-permute-done.22
  235.8 3.1 collective-permute-start.24
  238.9 4.2 %convolution_bitcast_fusion.1 = f32[1024,128]{0,1:T(8,128)S(1)} fusion(bf16[3,1024,128]{2,1,0:T(8,128)(2,1)S(1)} %get-tuple-element.97, bf16[3,1024,1024]{2,1,0:T(8,128)(2,1)} %all-gather.5.cloned.1.call-done), kind=kOutput, calls=%fused_computation.3 | convolution fusion | flops 805306368 | bytes 7602176 | tf_op jit(solution)/shard_map/rtd,rtc->dc/dot_general | solution.py:775
  246.9 2.2 collective-permute-done.26
  249.3 2.3 collective-permute-done.28
  252.4 12.4 %tail.1 = (bf16[2,4,3,64,1024]{4,3,2,1,0:T(8,128)(2,1)}, bf16[2,4,3,64,1024]{4,3,2,1,0:T(8,128)(2,1)}, f32[256,1024]{1,0:T(8,128)S(1)}, f32[128,96]{1,0:T(8,128)S(1)}, f32[8,128]{1,0:T(8,128)S(1)}) custom-call(s32[3,8]{1,0:T(4,128)S(1)} %copy-done.3, s32[3]{0:T(128)S(1)} %pad_add_fusion.own, bf16[2,4,3,64,96]{4,3,2,1,0:T(8,128)(2,1)S(1)} %pad_maximum_fusion.3.near, ...), custom_call_target="tpu_custom_call" | custom-call | flops 1 | bytes 1 | tf_op jit(solution)/shard_map/tail/pallas_call | solution.py:598
  266.2 4.6 %collective-permute-done.29.refs_0_ = bf16[2,4,3,64,1024]{4,3,2,1,0:T(8,128)(2,1)} collective-permute-done((bf16[2,4,3,64,1024]{4,3,2,1,0:T(8,128)(2,1)}, bf16[2,4,3,64,1024]{4,3,2,1,0:T(8,128)(2,1)}, u32[]{:S(2)}, u32[]{:S(2)}) %collective-permute-start.29) | collective-permute-done | bytes 3145760 | tf_op jit(solution)/shard_map/ppermute | solution.py:646
  270.7 2.2 fusion.17
  273.9 3.1 collective-permute-start.32
  277.1 2.6 fusion
  280.1 21.0 %collective-permute-done.31.refs_6_.refs_1_ = bf16[2,1,64,1024]{3,2,1,0:T(8,128)(2,1)S(1)} collective-permute-done((bf16[2,1,64,1024]{3,2,1,0:T(8,128)(2,1)S(1)}, bf16[2,1,64,1024]{3,2,1,0:T(8,128)(2,1)S(1)}, u32[]{:S(2)}, u32[]{:S(2)}) %collective-permute-start.31) | collective-permute-done | bytes 262176 | tf_op jit(solution)/shard_map/ppermute | solution.py:646
  309.3 5.4 %collective-permute-done.34 = bf16[128,1024]{1,0:T(8,128)(2,1)S(1)} collective-permute-done((bf16[128,1024]{1,0:T(8,128)(2,1)S(1)}, bf16[128,1024]{1,0:T(8,128)(2,1)S(1)}, u32[]{:S(2)}, u32[]{:S(2)}) %collective-permute-start.34) | collective-permute-done | bytes 262176 | tf_op jit(solution)/shard_map/ppermute | solution.py:650
  314.9 2.5 fusion.9
  320.5 4.4 %collective-permute-start.39 = (bf16[2,64,1024]{2,1,0:T(8,128)(2,1)S(1)}, bf16[2,64,1024]{2,1,0:T(8,128)(2,1)S(1)}, u32[]{:S(2)}, u32[]{:S(2)}) collective-permute-start(bf16[2,64,1024]{2,1,0:T(8,128)(2,1)S(1)} %get-tuple-element.132), channel_id=1, source_target_pairs={{0,16},{2,18},{4,20},{6,22},{8,24},{10,26},{12,28},{14,30},{16,0},... | collective-permute-start | bytes 786440 | tf_op jit(solution)/shard_map/ppermute | solution.py:646
  325.4 2.0 collective-permute-done.38.refs_2_.refs_0_
  330.5 5.4 %all-to-all-start.1 = ((bf16[16,32,128]{2,1,0:T(8,128)(2,1)}), bf16[16,32,128]{2,1,0:T(8,128)(2,1)}, u32[]{:S(2)}, u32[]{:S(2)}) async-start(bf16[16,32,128]{2,1,0:T(8,128)(2,1)} %get-tuple-element.128), calls=%async_computation.2 | async-start | bytes 262144 | tf_op jit(solution)/shard_map/all_to_all | solution.py:800
  336.0 6.6 %collective-permute-done.40.refs_2_ = bf16[2,64,1024]{2,1,0:T(8,128)(2,1)S(1)} collective-permute-done((bf16[2,64,1024]{2,1,0:T(8,128)(2,1)}, bf16[2,64,1024]{2,1,0:T(8,128)(2,1)S(1)}, u32[]{:S(2)}, u32[]{:S(2)}) %collective-permute-start.40) | collective-permute-done | bytes 262176 | tf_op jit(solution)/shard_map/ppermute | solution.py:646
  342.6 2.3 collective-permute-done.39.refs_1_
  345.0 2.1 fusion.12
  349.8 2.3 pad_maximum_fusion
  353.8 4.3 %collective-permute-start.44 = (f32[32,32]{1,0:T(8,128)S(1)}, f32[32,32]{1,0:T(8,128)S(1)}, u32[]{:S(2)}, u32[]{:S(2)}) collective-permute-start(f32[32,32]{1,0:T(8,128)S(1)} %get-tuple-element.126), channel_id=1, source_target_pairs={{0,16},{2,18},{4,20},{6,22},{8,24},{10,26},{12,28},{14,30},{16,0},... | collective-permute-start | bytes 12296 | tf_op jit(solution)/shard_map/ppermute | solution.py:646
  358.1 1.9 collective-permute-start.46
  362.5 13.6 %collective-permute-done.46 = bf16[128,1024]{1,0:T(8,128)(2,1)S(1)} collective-permute-done((bf16[128,1024]{1,0:T(8,128)(2,1)S(1)}, bf16[128,1024]{1,0:T(8,128)(2,1)S(1)}, u32[]{:S(2)}, u32[]{:S(2)}) %collective-permute-start.46) | collective-permute-done | bytes 262176 | tf_op jit(solution)/shard_map/ppermute | solution.py:806
  (177 shorter events, 59.0 us)
Async XLA Ops:
  7.2 74.0 %all-gather.3.cloned.1.call-start = ((), (), s32[]{:S(2)}) async-start(), calls=%async_computation.3 | async-start | bytes 6684672 | tf_op jit(solution)/shard_map/all_gather | solution.py:676
  7.9 168.2 %all-gather.5.cloned.1.call-start = ((), (), s32[]{:S(2)}) async-start(), calls=%async_computation.5 | async-start | bytes 6684672 | tf_op jit(solution)/shard_map/all_gather | solution.py:676
  9.4 3.8 collective-permute-start.2
  13.9 3.9 %collective-permute-start.3 = (f32[32,32]{1,0:T(8,128)S(1)}, f32[32,32]{1,0:T(8,128)S(1)}, u32[]{:S(2)}, u32[]{:S(2)}) collective-permute-start(f32[32,32]{1,0:T(8,128)S(1)} %add.318), channel_id=1, source_target_pairs={{0,2},{2,0},{4,6},{6,4},{8,10},{10,8},{12,14},{14,12},{16,18},{18,... | collective-permute-start | bytes 12296 | tf_op jit(solution)/shard_map/ppermute | solution.py:646
  13.9 15.6 %collective-permute-start.7 = (bf16[32,2048]{1,0:T(8,128)(2,1)}, bf16[32,2048]{1,0:T(8,128)(2,1)S(1)}, u32[]{:S(2)}, u32[]{:S(2)}) collective-permute-start(bf16[32,2048]{1,0:T(8,128)(2,1)} %param.18), channel_id=1, source_target_pairs={{0,1},{1,0},{2,3},{3,2},{4,5},{5,4},{6,7},{7,6},{8,9},{9,8},{10,11... | collective-permute-start | bytes 393224 | tf_op jit(solution)/shard_map/ppermute | solution.py:650
  15.5 21.9 %collective-permute-start = (bf16[128,1024]{1,0:T(8,128)(2,1)}, bf16[128,1024]{1,0:T(8,128)(2,1)S(1)}, u32[]{:S(2)}, u32[]{:S(2)}) collective-permute-start(bf16[128,1024]{1,0:T(8,128)(2,1)} %param.17), channel_id=1, source_target_pairs={{0,0},{1,2},{2,4},{3,6},{4,8},{5,10},{6,12},{7,14},{8,16},{9,18},{... | collective-permute-start | bytes 786440 | tf_op jit(solution)/shard_map/ppermute | solution.py:735
  17.8 4.6 %collective-permute-start.4 = (f32[32,32]{1,0:T(8,128)S(1)}, f32[32,32]{1,0:T(8,128)S(1)}, u32[]{:S(2)}, u32[]{:S(2)}) collective-permute-start(f32[32,32]{1,0:T(8,128)S(1)} %add.319), channel_id=1, source_target_pairs={{0,4},{2,6},{4,0},{6,2},{8,12},{10,14},{12,8},{14,10},{16,20},{18,... | collective-permute-start | bytes 12296 | tf_op jit(solution)/shard_map/ppermute | solution.py:646
  22.4 15.8 %collective-permute-start.5 = (f32[32,32]{1,0:T(8,128)S(1)}, f32[32,32]{1,0:T(8,128)S(1)}, u32[]{:S(2)}, u32[]{:S(2)}) collective-permute-start(f32[32,32]{1,0:T(8,128)S(1)} %add.320), channel_id=1, source_target_pairs={{0,8},{2,10},{4,12},{6,14},{8,0},{10,2},{12,4},{14,6},{16,24},{18,... | collective-permute-start | bytes 12296 | tf_op jit(solution)/shard_map/ppermute | solution.py:646
  31.2 14.7 %all-to-all-start = ((bf16[64,16,128]{2,0,1:T(8,128)(2,1)}), bf16[64,16,128]{2,0,1:T(8,128)(2,1)S(1)}, u32[]{:S(2)}, u32[]{:S(2)}) async-start(bf16[64,16,128]{2,0,1:T(8,128)(2,1)} %copy_bitcast_fusion.1), calls=%async_computation | async-start | bytes 524288 | tf_op jit(solution)/shard_map/all_to_all | solution.py:740
  37.4 312.5 %reduce-scatter.2.cloned.1.call-start = ((), (), s32[]{:S(2)}) async-start(), calls=%async_computation.4 | async-start | bytes 6684672 | tf_op jit(solution)/shard_map/reduce_scatter | solution.py:766
  37.4 8.4 %collective-permute-start.1 = (bf16[128,1024]{1,0:T(8,128)(2,1)S(1)}, bf16[128,1024]{1,0:T(8,128)(2,1)S(1)}, u32[]{:S(2)}, u32[]{:S(2)}) collective-permute-start(bf16[128,1024]{1,0:T(8,128)(2,1)S(1)} %collective-permute-done), channel_id=1, source_target_pairs={{0,1},{1,0},{2,3},{3,2},{4,5},{5,4},{6,7},{7,6},{8,9},{9,8},{10,11... | collective-permute-start | bytes 786440 | tf_op jit(solution)/shard_map/ppermute | solution.py:650
  38.2 6.2 %collective-permute-start.6 = (f32[32,32]{1,0:T(8,128)S(1)}, f32[32,32]{1,0:T(8,128)S(1)}, u32[]{:S(2)}, u32[]{:S(2)}) collective-permute-start(f32[32,32]{1,0:T(8,128)S(1)} %add.321), channel_id=1, source_target_pairs={{0,16},{2,18},{4,20},{6,22},{8,24},{10,26},{12,28},{14,30},{16,0},... | collective-permute-start | bytes 12296 | tf_op jit(solution)/shard_map/ppermute | solution.py:646
  94.0 11.8 %collective-permute-start.9 = (f32[4,3,64,96]{3,2,1,0:T(8,128)S(1)}, f32[4,3,64,96]{3,2,1,0:T(8,128)S(1)}, u32[]{:S(2)}, u32[]{:S(2)}) collective-permute-start(f32[4,3,64,96]{3,2,1,0:T(8,128)S(1)} %slice_bitcast_fusion.1), channel_id=1, source_target_pairs={{0,4},{2,6},{4,0},{6,2},{8,12},{10,14},{12,8},{14,10},{16,20},{18,... | collective-permute-start | bytes 884744 | tf_op jit(solution)/shard_map/ppermute | solution.py:646
  105.9 5.7 %collective-permute-start.10 = (f32[3,64,96]{2,1,0:T(8,128)S(1)}, f32[3,64,96]{2,1,0:T(8,128)S(1)}, u32[]{:S(2)}, u32[]{:S(2)}) collective-permute-start(f32[3,64,96]{2,1,0:T(8,128)S(1)} %get-tuple-element.142), channel_id=1, source_target_pairs={{0,8},{2,10},{4,12},{6,14},{8,0},{10,2},{12,4},{14,6},{16,24},{18,... | collective-permute-start | bytes 221192 | tf_op jit(solution)/shard_map/ppermute | solution.py:646
  107.5 15.8 %collective-permute-start.12 = (f32[3,64,96]{2,1,0:T(8,128)S(1)}, f32[3,64,96]{2,1,0:T(8,128)S(1)}, u32[]{:S(2)}, u32[]{:S(2)}) collective-permute-start(f32[3,64,96]{2,1,0:T(8,128)S(1)} %get-tuple-element.143), channel_id=1, source_target_pairs={{0,24},{2,26},{4,28},{6,30},{8,16},{10,18},{12,20},{14,22},{16,8},... | collective-permute-start | bytes 221192 | tf_op jit(solution)/shard_map/ppermute | solution.py:646
  107.5 15.8 %collective-permute-start.11 = (f32[3,64,96]{2,1,0:T(8,128)S(1)}, f32[3,64,96]{2,1,0:T(8,128)S(1)}, u32[]{:S(2)}, u32[]{:S(2)}) collective-permute-start(f32[3,64,96]{2,1,0:T(8,128)S(1)} %get-tuple-element.144), channel_id=1, source_target_pairs={{0,16},{2,18},{4,20},{6,22},{8,24},{10,26},{12,28},{14,30},{16,0},... | collective-permute-start | bytes 221192 | tf_op jit(solution)/shard_map/ppermute | solution.py:646
  123.3 11.9 %collective-permute-start.15 = (bf16[3,64,96]{2,1,0:T(8,128)(2,1)S(1)}, bf16[3,64,96]{2,1,0:T(8,128)(2,1)S(1)}, u32[]{:S(2)}, u32[]{:S(2)}) collective-permute-start(bf16[3,64,96]{2,1,0:T(8,128)(2,1)S(1)} %fusion.31), channel_id=1, source_target_pairs={{0,24},{2,26},{4,28},{6,30},{8,16},{10,18},{12,20},{14,22},{16,8},... | collective-permute-start | bytes 110600 | tf_op jit(solution)/shard_map/ppermute | solution.py:646
  130.1 9.8 %collective-permute-start.14 = (bf16[3,64,96]{2,1,0:T(8,128)(2,1)S(1)}, bf16[3,64,96]{2,1,0:T(8,128)(2,1)S(1)}, u32[]{:S(2)}, u32[]{:S(2)}) collective-permute-start(bf16[3,64,96]{2,1,0:T(8,128)(2,1)S(1)} %fusion.31), channel_id=1, source_target_pairs={{0,16},{2,18},{4,20},{6,22},{8,24},{10,26},{12,28},{14,30},{16,0},... | collective-permute-start | bytes 110600 | tf_op jit(solution)/shard_map/ppermute | solution.py:646
  135.2 4.7 %collective-permute-start.13 = (bf16[3,64,96]{2,1,0:T(8,128)(2,1)S(1)}, bf16[3,64,96]{2,1,0:T(8,128)(2,1)S(1)}, u32[]{:S(2)}, u32[]{:S(2)}) collective-permute-start(bf16[3,64,96]{2,1,0:T(8,128)(2,1)S(1)} %fusion.31), channel_id=1, source_target_pairs={{0,8},{2,10},{4,12},{6,14},{8,0},{10,2},{12,4},{14,6},{16,24},{18,... | collective-permute-start | bytes 110600 | tf_op jit(solution)/shard_map/ppermute | solution.py:646
  140.0 6.1 %collective-permute-start.16 = (bf16[4,3,64,96]{3,2,1,0:T(8,128)(2,1)S(1)}, bf16[4,3,64,96]{3,2,1,0:T(8,128)(2,1)S(1)}, u32[]{:S(2)}, u32[]{:S(2)}) collective-permute-start(bf16[4,3,64,96]{3,2,1,0:T(8,128)(2,1)S(1)} %get-tuple-element.153), channel_id=1, source_target_pairs={{0,4},{2,6},{4,0},{6,2},{8,12},{10,14},{12,8},{14,10},{16,20},{18,... | collective-permute-start | bytes 442376 | tf_op jit(solution)/shard_map/ppermute | solution.py:646
  219.5 7.1 %collective-permute-start.19 = (bf16[4,3,64,96]{3,2,1,0:T(8,128)(2,1)S(1)}, bf16[4,3,64,96]{3,2,1,0:T(8,128)(2,1)S(1)}, u32[]{:S(2)}, u32[]{:S(2)}) collective-permute-start(bf16[4,3,64,96]{3,2,1,0:T(8,128)(2,1)S(1)} %fusion.23), channel_id=1, source_target_pairs={{0,4},{2,6},{4,0},{6,2},{8,12},{10,14},{12,8},{14,10},{16,20},{18,... | collective-permute-start | bytes 442376 | tf_op jit(solution)/shard_map/ppermute | solution.py:646
  226.7 4.5 %collective-permute-start.20 = (bf16[3,64,96]{2,1,0:T(8,128)(2,1)S(1)}, bf16[3,64,96]{2,1,0:T(8,128)(2,1)S(1)}, u32[]{:S(2)}, u32[]{:S(2)}) collective-permute-start(bf16[3,64,96]{2,1,0:T(8,128)(2,1)S(1)} %get-tuple-element.149), channel_id=1, source_target_pairs={{0,8},{2,10},{4,12},{6,14},{8,0},{10,2},{12,4},{14,6},{16,24},{18,... | collective-permute-start | bytes 110600 | tf_op jit(solution)/shard_map/ppermute | solution.py:646
  228.2 5.4 %collective-permute-start.22 = (bf16[3,64,96]{2,1,0:T(8,128)(2,1)S(1)}, bf16[3,64,96]{2,1,0:T(8,128)(2,1)S(1)}, u32[]{:S(2)}, u32[]{:S(2)}) collective-permute-start(bf16[3,64,96]{2,1,0:T(8,128)(2,1)S(1)} %get-tuple-element.150), channel_id=1, source_target_pairs={{0,24},{2,26},{4,28},{6,30},{8,16},{10,18},{12,20},{14,22},{16,8},... | collective-permute-start | bytes 110600 | tf_op jit(solution)/shard_map/ppermute | solution.py:646
  229.4 5.0 %collective-permute-start.21 = (bf16[3,64,96]{2,1,0:T(8,128)(2,1)S(1)}, bf16[3,64,96]{2,1,0:T(8,128)(2,1)S(1)}, u32[]{:S(2)}, u32[]{:S(2)}) collective-permute-start(bf16[3,64,96]{2,1,0:T(8,128)(2,1)S(1)} %get-tuple-element.151), channel_id=1, source_target_pairs={{0,16},{2,18},{4,20},{6,22},{8,24},{10,26},{12,28},{14,30},{16,0},... | collective-permute-start | bytes 110600 | tf_op jit(solution)/shard_map/ppermute | solution.py:646
  234.5 8.8 %collective-permute-start.25 = (bf16[3,64,96]{2,1,0:T(8,128)(2,1)S(1)}, bf16[3,64,96]{2,1,0:T(8,128)(2,1)S(1)}, u32[]{:S(2)}, u32[]{:S(2)}) collective-permute-start(bf16[3,64,96]{2,1,0:T(8,128)(2,1)S(1)} %fusion.27), channel_id=1, source_target_pairs={{0,24},{2,26},{4,28},{6,30},{8,16},{10,18},{12,20},{14,22},{16,8},... | collective-permute-start | bytes 110600 | tf_op jit(solution)/shard_map/ppermute | solution.py:646
  235.8 7.6 %collective-permute-start.24 = (bf16[3,64,96]{2,1,0:T(8,128)(2,1)S(1)}, bf16[3,64,96]{2,1,0:T(8,128)(2,1)S(1)}, u32[]{:S(2)}, u32[]{:S(2)}) collective-permute-start(bf16[3,64,96]{2,1,0:T(8,128)(2,1)S(1)} %fusion.27), channel_id=1, source_target_pairs={{0,16},{2,18},{4,20},{6,22},{8,24},{10,26},{12,28},{14,30},{16,0},... | collective-permute-start | bytes 110600 | tf_op jit(solution)/shard_map/ppermute | solution.py:646
  238.9 4.5 %collective-permute-start.23 = (bf16[3,64,96]{2,1,0:T(8,128)(2,1)S(1)}, bf16[3,64,96]{2,1,0:T(8,128)(2,1)S(1)}, u32[]{:S(2)}, u32[]{:S(2)}) collective-permute-start(bf16[3,64,96]{2,1,0:T(8,128)(2,1)S(1)} %fusion.27), channel_id=1, source_target_pairs={{0,8},{2,10},{4,12},{6,14},{8,0},{10,2},{12,4},{14,6},{16,24},{18,... | collective-permute-start | bytes 110600 | tf_op jit(solution)/shard_map/ppermute | solution.py:646
  243.4 5.7 %collective-permute-start.26 = (bf16[4,3,64,96]{3,2,1,0:T(8,128)(2,1)S(1)}, bf16[4,3,64,96]{3,2,1,0:T(8,128)(2,1)S(1)}, u32[]{:S(2)}, u32[]{:S(2)}) collective-permute-start(bf16[4,3,64,96]{3,2,1,0:T(8,128)(2,1)S(1)} %get-tuple-element.148), channel_id=1, source_target_pairs={{0,4},{2,6},{4,0},{6,2},{8,12},{10,14},{12,8},{14,10},{16,20},{18,... | collective-permute-start | bytes 442376 | tf_op jit(solution)/shard_map/ppermute | solution.py:646
  245.2 6.4 %collective-permute-start.28 = (f32[16,32,128]{2,1,0:T(8,128)S(1)}, f32[16,32,128]{2,1,0:T(8,128)S(1)}, u32[]{:S(2)}, u32[]{:S(2)}) collective-permute-start(f32[16,32,128]{2,1,0:T(8,128)S(1)} %select_bitcast_fusion), channel_id=1, source_target_pairs={{0,1},{1,0},{2,3},{3,2},{4,5},{5,4},{6,7},{7,6},{8,9},{9,8},{10,11... | collective-permute-start | bytes 786440 | tf_op jit(solution)/shard_map/ppermute | solution.py:650
  249.3 3.1 collective-permute-start.27
  264.7 6.0 %collective-permute-start.29 = (bf16[2,4,3,64,1024]{4,3,2,1,0:T(8,128)(2,1)}, bf16[2,4,3,64,1024]{4,3,2,1,0:T(8,128)(2,1)}, u32[]{:S(2)}, u32[]{:S(2)}) collective-permute-start(bf16[2,4,3,64,1024]{4,3,2,1,0:T(8,128)(2,1)} %get-tuple-element.99), channel_id=1, source_target_pairs={{0,2},{2,0},{4,6},{6,4},{8,10},{10,8},{12,14},{14,12},{16,18},{18,... | collective-permute-start | bytes 9437192 | tf_op jit(solution)/shard_map/ppermute | solution.py:646
  272.9 41.9 %collective-permute-start.33 = (bf16[2,1,64,1024]{3,2,1,0:T(8,128)(2,1)}, bf16[2,1,64,1024]{3,2,1,0:T(8,128)(2,1)S(1)}, u32[]{:S(2)}, u32[]{:S(2)}) collective-permute-start(bf16[2,1,64,1024]{3,2,1,0:T(8,128)(2,1)} %get-tuple-element.134), channel_id=1, source_target_pairs={{0,24},{2,26},{4,28},{6,30},{8,16},{10,18},{12,20},{14,22},{16,8},... | collective-permute-start | bytes 786440 | tf_op jit(solution)/shard_map/ppermute | solution.py:646
  273.9 40.9 %collective-permute-start.32 = (bf16[2,1,64,1024]{3,2,1,0:T(8,128)(2,1)}, bf16[2,1,64,1024]{3,2,1,0:T(8,128)(2,1)S(1)}, u32[]{:S(2)}, u32[]{:S(2)}) collective-permute-start(bf16[2,1,64,1024]{3,2,1,0:T(8,128)(2,1)} %get-tuple-element.135), channel_id=1, source_target_pairs={{0,16},{2,18},{4,20},{6,22},{8,24},{10,26},{12,28},{14,30},{16,0},... | collective-permute-start | bytes 786440 | tf_op jit(solution)/shard_map/ppermute | solution.py:646
  277.1 24.0 %collective-permute-start.31 = (bf16[2,1,64,1024]{3,2,1,0:T(8,128)(2,1)S(1)}, bf16[2,1,64,1024]{3,2,1,0:T(8,128)(2,1)S(1)}, u32[]{:S(2)}, u32[]{:S(2)}) collective-permute-start(bf16[2,1,64,1024]{3,2,1,0:T(8,128)(2,1)S(1)} %get-tuple-element.136), channel_id=1, source_target_pairs={{0,8},{2,10},{4,12},{6,14},{8,0},{10,2},{12,4},{14,6},{16,24},{18,... | collective-permute-start | bytes 786440 | tf_op jit(solution)/shard_map/ppermute | solution.py:646
  279.7 35.1 %collective-permute-start.30 = (bf16[4,2,64,1024]{3,2,1,0:T(8,128)(2,1)}, bf16[4,2,64,1024]{3,2,1,0:T(8,128)(2,1)S(1)}, u32[]{:S(2)}, u32[]{:S(2)}) collective-permute-start(bf16[4,2,64,1024]{3,2,1,0:T(8,128)(2,1)} %fusion), channel_id=1, source_target_pairs={{0,4},{2,6},{4,0},{6,2},{8,12},{10,14},{12,8},{14,10},{16,20},{18,... | collective-permute-start | bytes 3145736 | tf_op jit(solution)/shard_map/ppermute | solution.py:646
  301.3 3.8 collective-permute-start.36
  303.0 4.9 %collective-permute-start.35 = (f32[200,128]{1,0:T(8,128)S(1)}, f32[200,128]{1,0:T(8,128)S(1)}, u32[]{:S(2)}, u32[]{:S(2)}) collective-permute-start(f32[200,128]{1,0:T(8,128)S(1)} %bitcast_dynamic-update-slice_fusion), channel_id=1, source_target_pairs={{0,1},{1,0},{2,3},{3,2},{4,5},{5,4},{6,7},{7,6},{8,9},{9,8},{10,11... | collective-permute-start | bytes 307208 | tf_op jit(solution)/shard_map/ppermute | solution.py:650
  306.3 8.4 %collective-permute-start.34 = (bf16[128,1024]{1,0:T(8,128)(2,1)S(1)}, bf16[128,1024]{1,0:T(8,128)(2,1)S(1)}, u32[]{:S(2)}, u32[]{:S(2)}) collective-permute-start(bf16[128,1024]{1,0:T(8,128)(2,1)S(1)} %select_convert_fusion), channel_id=1, source_target_pairs={{0,1},{1,0},{2,3},{3,2},{4,5},{5,4},{6,7},{7,6},{8,9},{9,8},{10,11... | collective-permute-start | bytes 786440 | tf_op jit(solution)/shard_map/ppermute | solution.py:650
  317.3 10.1 %collective-permute-start.38 = (bf16[2,64,1024]{2,1,0:T(8,128)(2,1)S(1)}, bf16[2,64,1024]{2,1,0:T(8,128)(2,1)S(1)}, u32[]{:S(2)}, u32[]{:S(2)}) collective-permute-start(bf16[2,64,1024]{2,1,0:T(8,128)(2,1)S(1)} %get-tuple-element.133), channel_id=1, source_target_pairs={{0,8},{2,10},{4,12},{6,14},{8,0},{10,2},{12,4},{14,6},{16,24},{18,... | collective-permute-start | bytes 786440 | tf_op jit(solution)/shard_map/ppermute | solution.py:646
  319.1 16.9 %collective-permute-start.41 = (bf16[1,64,1024]{2,1,0:T(8,128)(2,1)}, bf16[1,64,1024]{2,1,0:T(8,128)(2,1)S(1)}, u32[]{:S(2)}, u32[]{:S(2)}) collective-permute-start(bf16[1,64,1024]{2,1,0:T(8,128)(2,1)} %fusion.19), channel_id=1, source_target_pairs={{0,4},{2,6},{4,0},{6,2},{8,12},{10,14},{12,8},{14,10},{16,20},{18,... | collective-permute-start | bytes 393224 | tf_op jit(solution)/shard_map/ppermute | solution.py:646
  320.5 22.1 %collective-permute-start.40 = (bf16[2,64,1024]{2,1,0:T(8,128)(2,1)}, bf16[2,64,1024]{2,1,0:T(8,128)(2,1)S(1)}, u32[]{:S(2)}, u32[]{:S(2)}) collective-permute-start(bf16[2,64,1024]{2,1,0:T(8,128)(2,1)} %get-tuple-element.131), channel_id=1, source_target_pairs={{0,24},{2,26},{4,28},{6,30},{8,16},{10,18},{12,20},{14,22},{16,8},... | collective-permute-start | bytes 786440 | tf_op jit(solution)/shard_map/ppermute | solution.py:646
  320.5 24.4 %collective-permute-start.39 = (bf16[2,64,1024]{2,1,0:T(8,128)(2,1)S(1)}, bf16[2,64,1024]{2,1,0:T(8,128)(2,1)S(1)}, u32[]{:S(2)}, u32[]{:S(2)}) collective-permute-start(bf16[2,64,1024]{2,1,0:T(8,128)(2,1)S(1)} %get-tuple-element.132), channel_id=1, source_target_pairs={{0,16},{2,18},{4,20},{6,22},{8,24},{10,26},{12,28},{14,30},{16,0},... | collective-permute-start | bytes 786440 | tf_op jit(solution)/shard_map/ppermute | solution.py:646
  327.4 8.5 %collective-permute-start.42 = (f32[32,32]{1,0:T(8,128)S(1)}, f32[32,32]{1,0:T(8,128)S(1)}, u32[]{:S(2)}, u32[]{:S(2)}) collective-permute-start(f32[32,32]{1,0:T(8,128)S(1)} %get-tuple-element.116), channel_id=1, source_target_pairs={{0,4},{2,6},{4,0},{6,2},{8,12},{10,14},{12,8},{14,10},{16,20},{18,... | collective-permute-start | bytes 12296 | tf_op jit(solution)/shard_map/ppermute | solution.py:646
  330.5 17.7 %all-to-all-start.1 = ((bf16[16,32,128]{2,1,0:T(8,128)(2,1)}), bf16[16,32,128]{2,1,0:T(8,128)(2,1)}, u32[]{:S(2)}, u32[]{:S(2)}) async-start(bf16[16,32,128]{2,1,0:T(8,128)(2,1)} %get-tuple-element.128), calls=%async_computation.2 | async-start | bytes 262144 | tf_op jit(solution)/shard_map/all_to_all | solution.py:800
  352.1 9.1 %collective-permute-start.45 = (f32[32,32]{1,0:T(8,128)S(1)}, f32[32,32]{1,0:T(8,128)S(1)}, u32[]{:S(2)}, u32[]{:S(2)}) collective-permute-start(f32[32,32]{1,0:T(8,128)S(1)} %get-tuple-element.126), channel_id=1, source_target_pairs={{0,24},{2,26},{4,28},{6,30},{8,16},{10,18},{12,20},{14,22},{16,8},... | collective-permute-start | bytes 12296 | tf_op jit(solution)/shard_map/ppermute | solution.py:646
  353.8 7.4 %collective-permute-start.44 = (f32[32,32]{1,0:T(8,128)S(1)}, f32[32,32]{1,0:T(8,128)S(1)}, u32[]{:S(2)}, u32[]{:S(2)}) collective-permute-start(f32[32,32]{1,0:T(8,128)S(1)} %get-tuple-element.126), channel_id=1, source_target_pairs={{0,16},{2,18},{4,20},{6,22},{8,24},{10,26},{12,28},{14,30},{16,0},... | collective-permute-start | bytes 12296 | tf_op jit(solution)/shard_map/ppermute | solution.py:646
  358.1 3.9 %collective-permute-start.43 = (f32[32,32]{1,0:T(8,128)S(1)}, f32[32,32]{1,0:T(8,128)S(1)}, u32[]{:S(2)}, u32[]{:S(2)}) collective-permute-start(f32[32,32]{1,0:T(8,128)S(1)} %get-tuple-element.126), channel_id=1, source_target_pairs={{0,8},{2,10},{4,12},{6,14},{8,0},{10,2},{12,4},{14,6},{16,24},{18,... | collective-permute-start | bytes 12296 | tf_op jit(solution)/shard_map/ppermute | solution.py:646
  358.1 18.0 %collective-permute-start.46 = (bf16[128,1024]{1,0:T(8,128)(2,1)S(1)}, bf16[128,1024]{1,0:T(8,128)(2,1)S(1)}, u32[]{:S(2)}, u32[]{:S(2)}) collective-permute-start(bf16[128,1024]{1,0:T(8,128)(2,1)S(1)} %get-tuple-element.127), channel_id=1, source_target_pairs={{0,0},{2,1},{4,2},{6,3},{8,4},{10,5},{12,6},{14,7},{16,8},{18,9},{... | collective-permute-start | bytes 786440 | tf_op jit(solution)/shard_map/ppermute | solution.py:806
  (13 other events, 230.1 us)
Sparse Core Ops, SparseCore 0:
  10.2 70.9 all-gather.2
  83.4 65.0 all-gather.4
  221.4 102.3 reduce-scatter.1

commit v3 on v2

--- a/solution.py
+++ b/solution.py
@@ -253,11 +253,11 @@
             out[row : row + 8, :] = wide[b * 8 : b * 8 + 8, n * ch : (n + 1) * ch]
 
 
-def forward_kernel(starts, own, near, far, dtproj, dtbias, decay, skip, conv, z, *refs):
+def forward_kernel(starts, own, near, far, dtproj, dtbias, decay, skip, conv, z, cols, *refs):
     (
-        gated_o, y_o, states_o, last_o, stats_o,
+        gated_o, y_o, states_o, mixed_o, last_o, stats_o,
         state, dtk_s, dtx_s, y_s, across_s, low_s, cm_s,
-    ) = refs[-12:]
+    ) = refs[-13:]
     c = pl.program_id(0)
     rows, t, ch = conv.shape
 
@@ -308,10 +308,13 @@
     y_low = (y_s[...] + skip[...] * x).astype(BF)
     y_o[...] = y_low.reshape(rows, t, ch)
     zz = z[...].reshape(rows * t, ch)
-    gated_o[...] = (y_low.astype(F32) * (zz * sigmoid(zz))).astype(BF).reshape(rows, t, ch)
-
-
-def forward_scan(after, starts, own, near, far, dtproj, dtbias, decay, skip, conv, z):
+    gated = (y_low.astype(F32) * (zz * sigmoid(zz))).astype(BF)
+    gated_o[...] = gated.reshape(rows, t, ch)
+    mixed = dot(gated, cols[...], ((1,), (1,))).astype(BF)
+    mixed_o[...] = mixed.reshape(rows, t, cols.shape[0])
+
+
+def forward_scan(after, starts, own, near, far, dtproj, dtbias, decay, skip, conv, z, cols):
     conv, z = still(conv, z)
     rows, length, ch = conv.shape
     t = length // 8
@@ -332,12 +335,14 @@
                 fixed_block(skip.shape),
                 tok(ch),
                 tok(ch),
+                fixed_block(cols.shape),
                 *[pl.BlockSpec(memory_space=pl.ANY)] * len(after),
             ],
             out_specs=[
                 tok(ch),
                 tok(ch),
                 pl.BlockSpec((rows, t, NSTATE, ch), lambda c, s, o: (0, c, 0, 0)),
+                tok(cols.shape[0]),
                 fixed_block((rows, NSTATE, ch)),
                 fixed_block((8, ch)),
             ],
@@ -355,17 +360,18 @@
             large((rows, length, ch), BF),
             large((rows, length, ch), BF),
             large((rows, length, NSTATE, ch), F32),
+            large((rows, length, cols.shape[0]), BF),
             jax.ShapeDtypeStruct((rows, NSTATE, ch), F32),
             jax.ShapeDtypeStruct((8, ch), F32),
         ],
         compiler_params=params(1),
         cost_estimate=pl.CostEstimate(flops=1, bytes_accessed=1, transcendentals=0),
         name="forward_scan",
-    )(starts, own, near, far, dtproj, dtbias, decay, skip, conv, z, *after)
+    )(starts, own, near, far, dtproj, dtbias, decay, skip, conv, z, cols, *after)
 
 
 def backward_kernel(
-    starts, own, near, far, dtproj, dtbias, decay, skip, conv, z, y, gg, states, wide,
+    starts, own, near, far, dtproj, dtbias, decay, skip, conv, z, y, gout, cols, states, wide,
     gdtproj_i, misc_i, back_i, next_i, *refs, top,
 ):
     (
@@ -396,7 +402,7 @@
     dt_s[...] = dt
     dtx_s[...] = dt * x
     zz = z[...].reshape(count, ch)
-    ggv = gg[...].reshape(count, ch)
+    ggv = dot(gout[...].reshape(count, gout.shape[2]), cols[...], ((1,), (0,)))
     sg = sigmoid(zz)
     gy = (ggv * (zz * sg)).astype(BF).astype(F32)
     yv = y[...].astype(F32).reshape(count, ch)
@@ -472,14 +478,14 @@
 
 def backward_scan(
     top, chunks, after, so_far, starts, own, near, far, dtproj, dtbias, decay, skip, conv, z, y,
-    gg, states, wide,
+    gout, cols, states, wide,
 ):
-    conv, z, y, gg, states = still(conv, z, y, gg, states)
+    conv, z, y, gout, states = still(conv, z, y, gout, states)
     rows, length, ch = conv.shape
     t = length // 8
     seg = t // 2
     done, passed = so_far
-    fixed = 18
+    fixed = 19
     tok = lambda n: pl.BlockSpec((rows, t, n), lambda c, s, o: (0, top - c, 0))
     half = half_spec(rows, seg, MAPS, lambda c: top - c)
     small = [(DT_RANK, ch), (24, ch), (rows, NSTATE, ch), (rows, NSTATE, ch)]
@@ -498,7 +504,8 @@
                 tok(ch),
                 tok(ch),
                 tok(ch),
-                tok(ch),
+                tok(gout.shape[2]),
+                fixed_block(cols.shape),
                 pl.BlockSpec((rows, t, NSTATE, ch), lambda c, s, o: (0, top - c, 0, 0)),
                 fixed_block(wide.shape),
                 *[fixed_block(s) for s in small],
@@ -531,7 +538,7 @@
         cost_estimate=pl.CostEstimate(flops=1, bytes_accessed=1, transcendentals=0),
         name="backward_scan",
     )(
-        starts, own, near, far, dtproj, dtbias, decay, skip, conv, z, y, gg, states, wide,
+        starts, own, near, far, dtproj, dtbias, decay, skip, conv, z, y, gout, cols, states, wide,
         *passed, *done, *after,
     )
 
@@ -758,17 +765,14 @@
     )
     low = sum_pieces(keep, send, F32, []).astype(BF)
     near, far = spread_pieces(low)
-    gated, y, states, last, stats = forward_scan(
-        [], doc_starts, own, near, far, dt_proj, dtb, decay, skip, conv, z
-    )
-    mixed = jnp.einsum("rtc,dc->rtd", gated, out_cols, preferred_element_type=F32).astype(BF)
-    (cols,) = gate([out_cols], [mixed])
+    gated, y, states, mixed, last, stats = forward_scan(
+        [], doc_starts, own, near, far, dt_proj, dtb, decay, skip, conv, z, out_cols
+    )
     mixed = lax.psum_scatter(mixed, "seq", scatter_dimension=1, tiled=True)
-    gg = jnp.einsum("rtd,dc->rtc", gout, cols, preferred_element_type=F32)
     passed = [jnp.zeros((DT_RANK, ch), F32), jnp.zeros((24, ch), F32), jnp.zeros_like(last), last]
     ggate, gxs, keep, send, gdtproj, misc, _, _ = backward_scan(
         7, 8, [], ([], passed), doc_starts, own, near, far, dt_proj, dtb, decay, skip, conv, z, y,
-        gg, states, wide,
+        gout, out_cols, states, wide,
     )
     keep, send, gated = gate([keep, send, gated], [])
     low = sum_pieces(keep, send, BF, []).astype(BF)

time: 385 us -> 377 us (0.979)
  matrix products: 15.6 us -> 4.22 us
  Pallas kernels: 77.3 us -> 83.5 us
    dot_general x2 -> x0, matrix products: 11.4 us -> none  [the longest x1 5.74 us: channel_plan(): gg = jnp.einsum('rtd,dc->rtc', gout, cols, preferred_element_type=F32)]
    pallas_call x1, Pallas kernels: 35.1 us -> 39.1 us  [backward_scan(): pl.pallas_call(partial(backward_kernel, top=top), grid_spec=pltpu.Prefetc...]
  transfers between devices with their start and end apart: 52 -> 52, of which waited for: 28 -> 29; matrix products, arithmetic and copies ran while one was open for 11% -> 9% of each run, Pallas kernels for 11% -> 12%
where the time goes in v3:
time: 377 us; the launch traced here: 376 us
  waiting for transfers between devices  157 us (42%)
  Pallas kernels  83.5 us (22%)
  starting transfers between devices  82.8 us (22%)
  other arithmetic  28.9 us (8%)
  between operations  14.3 us (4%)
  local copies, waits for them, and re-layouts  5.34 us (1%)
  matrix products  4.22 us (1%)
    ppermute x38, waiting for transfers between devices, cross(): return lax.ppermute(v, 'seq', [(s, s ^ bits) for s in range(16)])  93.3 us
    ppermute x38, starting transfers between devices, cross(): return lax.ppermute(v, 'seq', [(s, s ^ bits) for s in range(16)])  58.6 us
    pallas_call x1, Pallas kernels, backward_scan(): pl.pallas_call(partial(backward_kernel, top=top), grid_spec=pltpu.Prefetc...  39.1 us
    all_gather x2, waiting for transfers between devices, gather_tokens(): return lax.all_gather(v, 'seq', axis=1, tiled=True)  35.2 us
    pallas_call x1, Pallas kernels, forward_scan(): pl.pallas_call(forward_kernel, grid_spec=pltpu.PrefetchScalarGridSpec(num...  21.7 us
    ppermute x1, waiting for transfers between devices, channel_plan(): in_share = lax.ppermute(in_half, both, to_owner).astype(F32)  13.7 us
    ppermute x7, waiting for transfers between devices, swap_row(): return lax.ppermute(v, 'row', [(0, 1), (1, 0)])  12.9 us
    pallas_call x1, Pallas kernels, tail(): pl.pallas_call(tail_kernel, grid_spec=pltpu.PrefetchScalarGridSpec(num_sc...  12.4 us
  transfers between devices with their start and end apart: 52, of which 29 were waited for; matrix products, arithmetic and copies ran while one was open for 9% of the time, Pallas kernels for 12%

profile of v3, /device:TPU:18, one launch (start us, length us, event | category | flops | bytes accessed | tf_op | source)
XLA Modules:
  0.0 375.6 jit_solution(1724070148016184648)
XLA Ops:
  10.9 2.2 collective-permute-done.2
  15.5 2.3 collective-permute-start
  18.7 3.7 collective-permute-done.4
  22.4 7.1 %collective-permute-start.5 = (f32[32,32]{1,0:T(8,128)S(1)}, f32[32,32]{1,0:T(8,128)S(1)}, u32[]{:S(2)}, u32[]{:S(2)}) collective-permute-start(f32[32,32]{1,0:T(8,128)S(1)} %add.320), channel_id=1, source_target_pairs={{0,8},{2,10},{4,12},{6,14},{8,0},{10,2},{12,4},{14,6},{16,24},{18,... | collective-permute-start | bytes 12296 | tf_op jit(solution)/shard_map/ppermute | solution.py:653
  31.2 6.2 %all-to-all-start = ((bf16[64,16,128]{2,0,1:T(8,128)(2,1)}), bf16[64,16,128]{2,0,1:T(8,128)(2,1)S(1)}, u32[]{:S(2)}, u32[]{:S(2)}) async-start(bf16[64,16,128]{2,0,1:T(8,128)(2,1)} %copy_bitcast_fusion.1), calls=%async_computation | async-start | bytes 524288 | tf_op jit(solution)/shard_map/all_to_all | solution.py:747
  42.0 2.5 collective-permute-done.6
  46.0 35.2 %all-gather.3.cloned.1.call-done.hid = bf16[3,1024,1024]{2,1,0:T(8,128)(2,1)} async-done(((bf16[3,64,1024]{2,1,0:T(8,128)(2,1)}), bf16[3,1024,1024]{2,1,0:T(8,128)(2,1)}) %all-gather.3.cloned.1.call-update) | async-done | bytes 6291472 | tf_op jit(solution)/shard_map/all_gather | solution.py:683
  81.2 10.4 %front.1 = (bf16[3,1024,1024]{2,1,0:T(8,128)(2,1)}, bf16[3,1024,128]{2,1,0:T(8,128)(2,1)}, f32[3,1024,128]{2,1,0:T(8,128)}, bf16[3,1024,128]{2,1,0:T(8,128)(2,1)...) custom-call(s32[3,8]{1,0:T(4,128)S(1)} %copy-done.2, s32[3]{0:T(128)S(1)} %pad_add_fusion.own, ...), custom_call_target="tpu_custom_call" | custom-call | flops 1 | bytes 1 | tf_op jit(solution)/shard_map/front/pallas_call | solution.py:165
  91.8 2.0 collective-permute-done.8
  95.5 10.3 %collective-permute-done.9 = f32[4,3,64,96]{3,2,1,0:T(8,128)S(1)} collective-permute-done((f32[4,3,64,96]{3,2,1,0:T(8,128)S(1)}, f32[4,3,64,96]{3,2,1,0:T(8,128)S(1)}, u32[]{:S(2)}, u32[]{:S(2)}) %collective-permute-start.9) | collective-permute-done | bytes 294944 | tf_op jit(solution)/shard_map/ppermute | solution.py:653
  107.5 2.9 collective-permute-start.11
  111.7 11.6 %collective-permute-done.12 = f32[3,64,96]{2,1,0:T(8,128)S(1)} collective-permute-done((f32[3,64,96]{2,1,0:T(8,128)S(1)}, f32[3,64,96]{2,1,0:T(8,128)S(1)}, u32[]{:S(2)}, u32[]{:S(2)}) %collective-permute-start.12) | collective-permute-done | bytes 73760 | tf_op jit(solution)/shard_map/ppermute | solution.py:653
  123.3 6.7 %collective-permute-start.15 = (bf16[3,64,96]{2,1,0:T(8,128)(2,1)S(1)}, bf16[3,64,96]{2,1,0:T(8,128)(2,1)S(1)}, u32[]{:S(2)}, u32[]{:S(2)}) collective-permute-start(bf16[3,64,96]{2,1,0:T(8,128)(2,1)S(1)} %fusion.29), channel_id=1, source_target_pairs={{0,24},{2,26},{4,28},{6,30},{8,16},{10,18},{12,20},{14,22},{16,8},... | collective-permute-start | bytes 110600 | tf_op jit(solution)/shard_map/ppermute | solution.py:653
  130.1 5.2 %collective-permute-start.14 = (bf16[3,64,96]{2,1,0:T(8,128)(2,1)S(1)}, bf16[3,64,96]{2,1,0:T(8,128)(2,1)S(1)}, u32[]{:S(2)}, u32[]{:S(2)}) collective-permute-start(bf16[3,64,96]{2,1,0:T(8,128)(2,1)S(1)} %fusion.29), channel_id=1, source_target_pairs={{0,16},{2,18},{4,20},{6,22},{8,24},{10,26},{12,28},{14,30},{16,0},... | collective-permute-start | bytes 110600 | tf_op jit(solution)/shard_map/ppermute | solution.py:653
  135.3 4.7 %collective-permute-done.14 = bf16[3,64,96]{2,1,0:T(8,128)(2,1)S(1)} collective-permute-done((bf16[3,64,96]{2,1,0:T(8,128)(2,1)S(1)}, bf16[3,64,96]{2,1,0:T(8,128)(2,1)S(1)}, u32[]{:S(2)}, u32[]{:S(2)}) %collective-permute-start.14) | collective-permute-done | bytes 36896 | tf_op jit(solution)/shard_map/ppermute | solution.py:653
  140.0 2.4 collective-permute-start.16
  142.4 3.6 collective-permute-done.16
  146.2 2.0 collective-permute-done.17.far
  148.2 21.7 %forward_scan.1 = (bf16[3,1024,128]{2,1,0:T(8,128)(2,1)}, bf16[3,1024,128]{2,1,0:T(8,128)(2,1)}, f32[3,1024,16,128]{3,2,1,0:T(8,128)}, bf16[3,1024,1024]{2,1,0:T...) custom-call(s32[3,8]{1,0:T(4,128)S(1)} %copy-done.2, s32[3]{0:T(128)S(1)} %pad_add_fusion.own, ...), custom_call_target="tpu_custom_call" | custom-call | flops 1 | bytes 1 | tf_op jit(solution)/shard_map/forward_scan/pallas_call | solution.py:324
  170.0 39.1 %backward_scan.1 = (bf16[3,1024,128]{2,1,0:T(8,128)(2,1)}, f32[3,1024,128]{2,1,0:T(8,128)}, f32[2,4,3,64,96]{4,3,2,1,0:T(8,128)S(1)}, f32[2,4,3,64,96]{4,3,2,1,0...) custom-call(s32[3,8]{1,0:T(4,128)S(1)} %copy-done.2, ...), custom_call_target="tpu_custom_call" | custom-call | flops 1 | bytes 1 | tf_op jit(solution)/shard_map/backward_scan/pallas_call | solution.py:492
  209.3 2.1 collective-permute-done.18
  211.6 1.8 collective-permute-start.19
  213.4 5.3 %collective-permute-done.19 = bf16[4,3,64,96]{3,2,1,0:T(8,128)(2,1)S(1)} collective-permute-done((bf16[4,3,64,96]{3,2,1,0:T(8,128)(2,1)S(1)}, bf16[4,3,64,96]{3,2,1,0:T(8,128)(2,1)S(1)}, u32[]{:S(2)}, u32[]{:S(2)}) %collective-permute-start.19) | collective-permute-done | bytes 147488 | tf_op jit(solution)/shard_map/ppermute | solution.py:653
  223.3 2.5 collective-permute-done.22
  227.8 3.3 collective-permute-start.24
  231.1 4.2 %convolution_bitcast_fusion = f32[1024,128]{0,1:T(8,128)S(1)} fusion(bf16[3,1024,128]{2,1,0:T(8,128)(2,1)S(1)} %get-tuple-element.99, bf16[3,1024,1024]{2,1,0:T(8,128)(2,1)} %all-gather.5.cloned.1.call-done.gout), kind=kOutput, calls=%fused_computation.1 | convolution fusion | flops 805306368 | bytes 7602176 | tf_op jit(solution)/shard_map/rtd,rtc->dc/dot_general | solution.py:779
  235.6 1.8 collective-permute-start.26
  238.9 2.5 collective-permute-done.26
  241.5 2.4 collective-permute-done.28
  244.6 12.4 %tail.1 = (bf16[2,4,3,64,1024]{4,3,2,1,0:T(8,128)(2,1)}, bf16[2,4,3,64,1024]{4,3,2,1,0:T(8,128)(2,1)}, f32[256,1024]{1,0:T(8,128)S(1)}, f32[128,96]{1,0:T(8,128)S(1)}, f32[8,128]{1,0:T(8,128)S(1)}) custom-call(s32[3,8]{1,0:T(4,128)S(1)} %copy-done.2, s32[3]{0:T(128)S(1)} %pad_add_fusion.own, bf16[2,4,3,64,96]{4,3,2,1,0:T(8,128)(2,1)S(1)} %pad_maximum_fusion.3.near, ...), custom_call_target="tpu_custom_call" | custom-call | flops 1 | bytes 1 | tf_op jit(solution)/shard_map/tail/pallas_call | solution.py:605
  258.4 4.6 %collective-permute-done.29.refs_0_ = bf16[2,4,3,64,1024]{4,3,2,1,0:T(8,128)(2,1)} collective-permute-done((bf16[2,4,3,64,1024]{4,3,2,1,0:T(8,128)(2,1)}, bf16[2,4,3,64,1024]{4,3,2,1,0:T(8,128)(2,1)}, u32[]{:S(2)}, u32[]{:S(2)}) %collective-permute-start.29) | collective-permute-done | bytes 3145760 | tf_op jit(solution)/shard_map/ppermute | solution.py:653
  263.0 2.2 fusion.17
  266.2 3.2 collective-permute-start.32
  269.4 2.6 fusion
  272.4 20.8 %collective-permute-done.31.refs_6_.refs_1_ = bf16[2,1,64,1024]{3,2,1,0:T(8,128)(2,1)S(1)} collective-permute-done((bf16[2,1,64,1024]{3,2,1,0:T(8,128)(2,1)S(1)}, bf16[2,1,64,1024]{3,2,1,0:T(8,128)(2,1)S(1)}, u32[]{:S(2)}, u32[]{:S(2)}) %collective-permute-start.31) | collective-permute-done | bytes 262176 | tf_op jit(solution)/shard_map/ppermute | solution.py:653
  301.3 5.4 %collective-permute-done.34 = bf16[128,1024]{1,0:T(8,128)(2,1)S(1)} collective-permute-done((bf16[128,1024]{1,0:T(8,128)(2,1)S(1)}, bf16[128,1024]{1,0:T(8,128)(2,1)S(1)}, u32[]{:S(2)}, u32[]{:S(2)}) %collective-permute-start.34) | collective-permute-done | bytes 262176 | tf_op jit(solution)/shard_map/ppermute | solution.py:657
  306.9 2.5 fusion.9
  309.4 1.7 fusion.19
  312.6 4.4 %collective-permute-start.39 = (bf16[2,64,1024]{2,1,0:T(8,128)(2,1)S(1)}, bf16[2,64,1024]{2,1,0:T(8,128)(2,1)S(1)}, u32[]{:S(2)}, u32[]{:S(2)}) collective-permute-start(bf16[2,64,1024]{2,1,0:T(8,128)(2,1)S(1)} %get-tuple-element.134), channel_id=1, source_target_pairs={{0,16},{2,18},{4,20},{6,22},{8,24},{10,26},{12,28},{14,30},{16,0},... | collective-permute-start | bytes 786440 | tf_op jit(solution)/shard_map/ppermute | solution.py:653
  317.5 1.9 collective-permute-done.38.refs_2_.refs_0_
  322.6 5.4 %all-to-all-start.1 = ((bf16[16,32,128]{2,1,0:T(8,128)(2,1)}), bf16[16,32,128]{2,1,0:T(8,128)(2,1)}, u32[]{:S(2)}, u32[]{:S(2)}) async-start(bf16[16,32,128]{2,1,0:T(8,128)(2,1)} %get-tuple-element.130), calls=%async_computation.2 | async-start | bytes 262144 | tf_op jit(solution)/shard_map/all_to_all | solution.py:804
  328.0 6.7 %collective-permute-done.40.refs_2_ = bf16[2,64,1024]{2,1,0:T(8,128)(2,1)S(1)} collective-permute-done((bf16[2,64,1024]{2,1,0:T(8,128)(2,1)}, bf16[2,64,1024]{2,1,0:T(8,128)(2,1)S(1)}, u32[]{:S(2)}, u32[]{:S(2)}) %collective-permute-start.40) | collective-permute-done | bytes 262176 | tf_op jit(solution)/shard_map/ppermute | solution.py:653
  334.7 2.3 collective-permute-done.39.refs_1_
  337.0 2.1 fusion.12
  341.9 2.3 pad_maximum_fusion
  345.9 4.3 %collective-permute-start.44 = (f32[32,32]{1,0:T(8,128)S(1)}, f32[32,32]{1,0:T(8,128)S(1)}, u32[]{:S(2)}, u32[]{:S(2)}) collective-permute-start(f32[32,32]{1,0:T(8,128)S(1)} %get-tuple-element.128), channel_id=1, source_target_pairs={{0,16},{2,18},{4,20},{6,22},{8,24},{10,26},{12,28},{14,30},{16,0},... | collective-permute-start | bytes 12296 | tf_op jit(solution)/shard_map/ppermute | solution.py:653
  350.1 1.9 collective-permute-start.46
  354.6 13.7 %collective-permute-done.46 = bf16[128,1024]{1,0:T(8,128)(2,1)S(1)} collective-permute-done((bf16[128,1024]{1,0:T(8,128)(2,1)S(1)}, bf16[128,1024]{1,0:T(8,128)(2,1)S(1)}, u32[]{:S(2)}, u32[]{:S(2)}) %collective-permute-start.46) | collective-permute-done | bytes 262176 | tf_op jit(solution)/shard_map/ppermute | solution.py:810
  (172 shorter events, 53.4 us)
Async XLA Ops:
  7.2 74.0 %all-gather.3.cloned.1.call-start = ((), (), s32[]{:S(2)}) async-start(), calls=%async_computation.3 | async-start | bytes 6684672 | tf_op jit(solution)/shard_map/all_gather | solution.py:683
  7.9 162.0 %all-gather.5.cloned.1.call-start = ((), (), s32[]{:S(2)}) async-start(), calls=%async_computation.5 | async-start | bytes 6684672 | tf_op jit(solution)/shard_map/all_gather | solution.py:683
  9.4 3.8 %collective-permute-start.2 = (f32[32,32]{1,0:T(8,128)S(1)}, f32[32,32]{1,0:T(8,128)S(1)}, u32[]{:S(2)}, u32[]{:S(2)}) collective-permute-start(f32[32,32]{1,0:T(8,128)S(1)} %dynamic_update_slice.5), channel_id=1, source_target_pairs={{0,1},{1,0},{2,3},{3,2},{4,5},{5,4},{6,7},{7,6},{8,9},{9,8},{10,11... | collective-permute-start | bytes 12296 | tf_op jit(solution)/shard_map/ppermute | solution.py:657
  13.9 3.9 %collective-permute-start.3 = (f32[32,32]{1,0:T(8,128)S(1)}, f32[32,32]{1,0:T(8,128)S(1)}, u32[]{:S(2)}, u32[]{:S(2)}) collective-permute-start(f32[32,32]{1,0:T(8,128)S(1)} %add.318), channel_id=1, source_target_pairs={{0,2},{2,0},{4,6},{6,4},{8,10},{10,8},{12,14},{14,12},{16,18},{18,... | collective-permute-start | bytes 12296 | tf_op jit(solution)/shard_map/ppermute | solution.py:653
  13.9 15.6 %collective-permute-start.7 = (bf16[32,2048]{1,0:T(8,128)(2,1)}, bf16[32,2048]{1,0:T(8,128)(2,1)S(1)}, u32[]{:S(2)}, u32[]{:S(2)}) collective-permute-start(bf16[32,2048]{1,0:T(8,128)(2,1)} %param.18), channel_id=1, source_target_pairs={{0,1},{1,0},{2,3},{3,2},{4,5},{5,4},{6,7},{7,6},{8,9},{9,8},{10,11... | collective-permute-start | bytes 393224 | tf_op jit(solution)/shard_map/ppermute | solution.py:657
  15.5 21.9 %collective-permute-start = (bf16[128,1024]{1,0:T(8,128)(2,1)}, bf16[128,1024]{1,0:T(8,128)(2,1)S(1)}, u32[]{:S(2)}, u32[]{:S(2)}) collective-permute-start(bf16[128,1024]{1,0:T(8,128)(2,1)} %param.17), channel_id=1, source_target_pairs={{0,0},{1,2},{2,4},{3,6},{4,8},{5,10},{6,12},{7,14},{8,16},{9,18},{... | collective-permute-start | bytes 786440 | tf_op jit(solution)/shard_map/ppermute | solution.py:742
  17.8 4.6 %collective-permute-start.4 = (f32[32,32]{1,0:T(8,128)S(1)}, f32[32,32]{1,0:T(8,128)S(1)}, u32[]{:S(2)}, u32[]{:S(2)}) collective-permute-start(f32[32,32]{1,0:T(8,128)S(1)} %add.319), channel_id=1, source_target_pairs={{0,4},{2,6},{4,0},{6,2},{8,12},{10,14},{12,8},{14,10},{16,20},{18,... | collective-permute-start | bytes 12296 | tf_op jit(solution)/shard_map/ppermute | solution.py:653
  22.4 15.8 %collective-permute-start.5 = (f32[32,32]{1,0:T(8,128)S(1)}, f32[32,32]{1,0:T(8,128)S(1)}, u32[]{:S(2)}, u32[]{:S(2)}) collective-permute-start(f32[32,32]{1,0:T(8,128)S(1)} %add.320), channel_id=1, source_target_pairs={{0,8},{2,10},{4,12},{6,14},{8,0},{10,2},{12,4},{14,6},{16,24},{18,... | collective-permute-start | bytes 12296 | tf_op jit(solution)/shard_map/ppermute | solution.py:653
  31.2 14.7 %all-to-all-start = ((bf16[64,16,128]{2,0,1:T(8,128)(2,1)}), bf16[64,16,128]{2,0,1:T(8,128)(2,1)S(1)}, u32[]{:S(2)}, u32[]{:S(2)}) async-start(bf16[64,16,128]{2,0,1:T(8,128)(2,1)} %copy_bitcast_fusion.1), calls=%async_computation | async-start | bytes 524288 | tf_op jit(solution)/shard_map/all_to_all | solution.py:747
  37.4 304.5 %reduce-scatter.2.cloned.1.call-start = ((), (), s32[]{:S(2)}) async-start(), calls=%async_computation.4 | async-start | bytes 6684672 | tf_op jit(solution)/shard_map/reduce_scatter | solution.py:771
  37.4 8.4 %collective-permute-start.1 = (bf16[128,1024]{1,0:T(8,128)(2,1)S(1)}, bf16[128,1024]{1,0:T(8,128)(2,1)S(1)}, u32[]{:S(2)}, u32[]{:S(2)}) collective-permute-start(bf16[128,1024]{1,0:T(8,128)(2,1)S(1)} %collective-permute-done), channel_id=1, source_target_pairs={{0,1},{1,0},{2,3},{3,2},{4,5},{5,4},{6,7},{7,6},{8,9},{9,8},{10,11... | collective-permute-start | bytes 786440 | tf_op jit(solution)/shard_map/ppermute | solution.py:657
  38.2 6.2 %collective-permute-start.6 = (f32[32,32]{1,0:T(8,128)S(1)}, f32[32,32]{1,0:T(8,128)S(1)}, u32[]{:S(2)}, u32[]{:S(2)}) collective-permute-start(f32[32,32]{1,0:T(8,128)S(1)} %add.321), channel_id=1, source_target_pairs={{0,16},{2,18},{4,20},{6,22},{8,24},{10,26},{12,28},{14,30},{16,0},... | collective-permute-start | bytes 12296 | tf_op jit(solution)/shard_map/ppermute | solution.py:653
  94.0 11.8 %collective-permute-start.9 = (f32[4,3,64,96]{3,2,1,0:T(8,128)S(1)}, f32[4,3,64,96]{3,2,1,0:T(8,128)S(1)}, u32[]{:S(2)}, u32[]{:S(2)}) collective-permute-start(f32[4,3,64,96]{3,2,1,0:T(8,128)S(1)} %slice_bitcast_fusion.1), channel_id=1, source_target_pairs={{0,4},{2,6},{4,0},{6,2},{8,12},{10,14},{12,8},{14,10},{16,20},{18,... | collective-permute-start | bytes 884744 | tf_op jit(solution)/shard_map/ppermute | solution.py:653
  105.9 5.7 %collective-permute-start.10 = (f32[3,64,96]{2,1,0:T(8,128)S(1)}, f32[3,64,96]{2,1,0:T(8,128)S(1)}, u32[]{:S(2)}, u32[]{:S(2)}) collective-permute-start(f32[3,64,96]{2,1,0:T(8,128)S(1)} %get-tuple-element.144), channel_id=1, source_target_pairs={{0,8},{2,10},{4,12},{6,14},{8,0},{10,2},{12,4},{14,6},{16,24},{18,... | collective-permute-start | bytes 221192 | tf_op jit(solution)/shard_map/ppermute | solution.py:653
  107.5 15.8 %collective-permute-start.12 = (f32[3,64,96]{2,1,0:T(8,128)S(1)}, f32[3,64,96]{2,1,0:T(8,128)S(1)}, u32[]{:S(2)}, u32[]{:S(2)}) collective-permute-start(f32[3,64,96]{2,1,0:T(8,128)S(1)} %get-tuple-element.145), channel_id=1, source_target_pairs={{0,24},{2,26},{4,28},{6,30},{8,16},{10,18},{12,20},{14,22},{16,8},... | collective-permute-start | bytes 221192 | tf_op jit(solution)/shard_map/ppermute | solution.py:653
  107.5 15.8 %collective-permute-start.11 = (f32[3,64,96]{2,1,0:T(8,128)S(1)}, f32[3,64,96]{2,1,0:T(8,128)S(1)}, u32[]{:S(2)}, u32[]{:S(2)}) collective-permute-start(f32[3,64,96]{2,1,0:T(8,128)S(1)} %get-tuple-element.146), channel_id=1, source_target_pairs={{0,16},{2,18},{4,20},{6,22},{8,24},{10,26},{12,28},{14,30},{16,0},... | collective-permute-start | bytes 221192 | tf_op jit(solution)/shard_map/ppermute | solution.py:653
  123.3 11.9 %collective-permute-start.15 = (bf16[3,64,96]{2,1,0:T(8,128)(2,1)S(1)}, bf16[3,64,96]{2,1,0:T(8,128)(2,1)S(1)}, u32[]{:S(2)}, u32[]{:S(2)}) collective-permute-start(bf16[3,64,96]{2,1,0:T(8,128)(2,1)S(1)} %fusion.29), channel_id=1, source_target_pairs={{0,24},{2,26},{4,28},{6,30},{8,16},{10,18},{12,20},{14,22},{16,8},... | collective-permute-start | bytes 110600 | tf_op jit(solution)/shard_map/ppermute | solution.py:653
  130.1 9.9 %collective-permute-start.14 = (bf16[3,64,96]{2,1,0:T(8,128)(2,1)S(1)}, bf16[3,64,96]{2,1,0:T(8,128)(2,1)S(1)}, u32[]{:S(2)}, u32[]{:S(2)}) collective-permute-start(bf16[3,64,96]{2,1,0:T(8,128)(2,1)S(1)} %fusion.29), channel_id=1, source_target_pairs={{0,16},{2,18},{4,20},{6,22},{8,24},{10,26},{12,28},{14,30},{16,0},... | collective-permute-start | bytes 110600 | tf_op jit(solution)/shard_map/ppermute | solution.py:653
  135.3 4.7 %collective-permute-start.13 = (bf16[3,64,96]{2,1,0:T(8,128)(2,1)S(1)}, bf16[3,64,96]{2,1,0:T(8,128)(2,1)S(1)}, u32[]{:S(2)}, u32[]{:S(2)}) collective-permute-start(bf16[3,64,96]{2,1,0:T(8,128)(2,1)S(1)} %fusion.29), channel_id=1, source_target_pairs={{0,8},{2,10},{4,12},{6,14},{8,0},{10,2},{12,4},{14,6},{16,24},{18,... | collective-permute-start | bytes 110600 | tf_op jit(solution)/shard_map/ppermute | solution.py:653
  140.0 6.0 %collective-permute-start.16 = (bf16[4,3,64,96]{3,2,1,0:T(8,128)(2,1)S(1)}, bf16[4,3,64,96]{3,2,1,0:T(8,128)(2,1)S(1)}, u32[]{:S(2)}, u32[]{:S(2)}) collective-permute-start(bf16[4,3,64,96]{3,2,1,0:T(8,128)(2,1)S(1)} %get-tuple-element.155), channel_id=1, source_target_pairs={{0,4},{2,6},{4,0},{6,2},{8,12},{10,14},{12,8},{14,10},{16,20},{18,... | collective-permute-start | bytes 442376 | tf_op jit(solution)/shard_map/ppermute | solution.py:653
  211.6 7.1 %collective-permute-start.19 = (bf16[4,3,64,96]{3,2,1,0:T(8,128)(2,1)S(1)}, bf16[4,3,64,96]{3,2,1,0:T(8,128)(2,1)S(1)}, u32[]{:S(2)}, u32[]{:S(2)}) collective-permute-start(bf16[4,3,64,96]{3,2,1,0:T(8,128)(2,1)S(1)} %fusion.21), channel_id=1, source_target_pairs={{0,4},{2,6},{4,0},{6,2},{8,12},{10,14},{12,8},{14,10},{16,20},{18,... | collective-permute-start | bytes 442376 | tf_op jit(solution)/shard_map/ppermute | solution.py:653
  218.8 4.5 %collective-permute-start.20 = (bf16[3,64,96]{2,1,0:T(8,128)(2,1)S(1)}, bf16[3,64,96]{2,1,0:T(8,128)(2,1)S(1)}, u32[]{:S(2)}, u32[]{:S(2)}) collective-permute-start(bf16[3,64,96]{2,1,0:T(8,128)(2,1)S(1)} %get-tuple-element.151), channel_id=1, source_target_pairs={{0,8},{2,10},{4,12},{6,14},{8,0},{10,2},{12,4},{14,6},{16,24},{18,... | collective-permute-start | bytes 110600 | tf_op jit(solution)/shard_map/ppermute | solution.py:653
  220.3 5.4 %collective-permute-start.22 = (bf16[3,64,96]{2,1,0:T(8,128)(2,1)S(1)}, bf16[3,64,96]{2,1,0:T(8,128)(2,1)S(1)}, u32[]{:S(2)}, u32[]{:S(2)}) collective-permute-start(bf16[3,64,96]{2,1,0:T(8,128)(2,1)S(1)} %get-tuple-element.152), channel_id=1, source_target_pairs={{0,24},{2,26},{4,28},{6,30},{8,16},{10,18},{12,20},{14,22},{16,8},... | collective-permute-start | bytes 110600 | tf_op jit(solution)/shard_map/ppermute | solution.py:653
  221.6 5.0 %collective-permute-start.21 = (bf16[3,64,96]{2,1,0:T(8,128)(2,1)S(1)}, bf16[3,64,96]{2,1,0:T(8,128)(2,1)S(1)}, u32[]{:S(2)}, u32[]{:S(2)}) collective-permute-start(bf16[3,64,96]{2,1,0:T(8,128)(2,1)S(1)} %get-tuple-element.153), channel_id=1, source_target_pairs={{0,16},{2,18},{4,20},{6,22},{8,24},{10,26},{12,28},{14,30},{16,0},... | collective-permute-start | bytes 110600 | tf_op jit(solution)/shard_map/ppermute | solution.py:653
  226.7 8.8 %collective-permute-start.25 = (bf16[3,64,96]{2,1,0:T(8,128)(2,1)S(1)}, bf16[3,64,96]{2,1,0:T(8,128)(2,1)S(1)}, u32[]{:S(2)}, u32[]{:S(2)}) collective-permute-start(bf16[3,64,96]{2,1,0:T(8,128)(2,1)S(1)} %fusion.25), channel_id=1, source_target_pairs={{0,24},{2,26},{4,28},{6,30},{8,16},{10,18},{12,20},{14,22},{16,8},... | collective-permute-start | bytes 110600 | tf_op jit(solution)/shard_map/ppermute | solution.py:653
  227.8 7.7 %collective-permute-start.24 = (bf16[3,64,96]{2,1,0:T(8,128)(2,1)S(1)}, bf16[3,64,96]{2,1,0:T(8,128)(2,1)S(1)}, u32[]{:S(2)}, u32[]{:S(2)}) collective-permute-start(bf16[3,64,96]{2,1,0:T(8,128)(2,1)S(1)} %fusion.25), channel_id=1, source_target_pairs={{0,16},{2,18},{4,20},{6,22},{8,24},{10,26},{12,28},{14,30},{16,0},... | collective-permute-start | bytes 110600 | tf_op jit(solution)/shard_map/ppermute | solution.py:653
  231.1 4.5 %collective-permute-start.23 = (bf16[3,64,96]{2,1,0:T(8,128)(2,1)S(1)}, bf16[3,64,96]{2,1,0:T(8,128)(2,1)S(1)}, u32[]{:S(2)}, u32[]{:S(2)}) collective-permute-start(bf16[3,64,96]{2,1,0:T(8,128)(2,1)S(1)} %fusion.25), channel_id=1, source_target_pairs={{0,8},{2,10},{4,12},{6,14},{8,0},{10,2},{12,4},{14,6},{16,24},{18,... | collective-permute-start | bytes 110600 | tf_op jit(solution)/shard_map/ppermute | solution.py:653
  235.6 5.7 %collective-permute-start.26 = (bf16[4,3,64,96]{3,2,1,0:T(8,128)(2,1)S(1)}, bf16[4,3,64,96]{3,2,1,0:T(8,128)(2,1)S(1)}, u32[]{:S(2)}, u32[]{:S(2)}) collective-permute-start(bf16[4,3,64,96]{3,2,1,0:T(8,128)(2,1)S(1)} %get-tuple-element.150), channel_id=1, source_target_pairs={{0,4},{2,6},{4,0},{6,2},{8,12},{10,14},{12,8},{14,10},{16,20},{18,... | collective-permute-start | bytes 442376 | tf_op jit(solution)/shard_map/ppermute | solution.py:653
  237.5 6.4 %collective-permute-start.28 = (f32[16,32,128]{2,1,0:T(8,128)S(1)}, f32[16,32,128]{2,1,0:T(8,128)S(1)}, u32[]{:S(2)}, u32[]{:S(2)}) collective-permute-start(f32[16,32,128]{2,1,0:T(8,128)S(1)} %select_bitcast_fusion), channel_id=1, source_target_pairs={{0,1},{1,0},{2,3},{3,2},{4,5},{5,4},{6,7},{7,6},{8,9},{9,8},{10,11... | collective-permute-start | bytes 786440 | tf_op jit(solution)/shard_map/ppermute | solution.py:657
  241.4 3.2 collective-permute-start.27
  257.0 6.0 %collective-permute-start.29 = (bf16[2,4,3,64,1024]{4,3,2,1,0:T(8,128)(2,1)}, bf16[2,4,3,64,1024]{4,3,2,1,0:T(8,128)(2,1)}, u32[]{:S(2)}, u32[]{:S(2)}) collective-permute-start(bf16[2,4,3,64,1024]{4,3,2,1,0:T(8,128)(2,1)} %get-tuple-element.101), channel_id=1, source_target_pairs={{0,2},{2,0},{4,6},{6,4},{8,10},{10,8},{12,14},{14,12},{16,18},{18,... | collective-permute-start | bytes 9437192 | tf_op jit(solution)/shard_map/ppermute | solution.py:653
  265.2 41.7 %collective-permute-start.33 = (bf16[2,1,64,1024]{3,2,1,0:T(8,128)(2,1)}, bf16[2,1,64,1024]{3,2,1,0:T(8,128)(2,1)S(1)}, u32[]{:S(2)}, u32[]{:S(2)}) collective-permute-start(bf16[2,1,64,1024]{3,2,1,0:T(8,128)(2,1)} %get-tuple-element.136), channel_id=1, source_target_pairs={{0,24},{2,26},{4,28},{6,30},{8,16},{10,18},{12,20},{14,22},{16,8},... | collective-permute-start | bytes 786440 | tf_op jit(solution)/shard_map/ppermute | solution.py:653
  266.2 40.7 %collective-permute-start.32 = (bf16[2,1,64,1024]{3,2,1,0:T(8,128)(2,1)}, bf16[2,1,64,1024]{3,2,1,0:T(8,128)(2,1)S(1)}, u32[]{:S(2)}, u32[]{:S(2)}) collective-permute-start(bf16[2,1,64,1024]{3,2,1,0:T(8,128)(2,1)} %get-tuple-element.137), channel_id=1, source_target_pairs={{0,16},{2,18},{4,20},{6,22},{8,24},{10,26},{12,28},{14,30},{16,0},... | collective-permute-start | bytes 786440 | tf_op jit(solution)/shard_map/ppermute | solution.py:653
  269.4 23.8 %collective-permute-start.31 = (bf16[2,1,64,1024]{3,2,1,0:T(8,128)(2,1)S(1)}, bf16[2,1,64,1024]{3,2,1,0:T(8,128)(2,1)S(1)}, u32[]{:S(2)}, u32[]{:S(2)}) collective-permute-start(bf16[2,1,64,1024]{3,2,1,0:T(8,128)(2,1)S(1)} %get-tuple-element.138), channel_id=1, source_target_pairs={{0,8},{2,10},{4,12},{6,14},{8,0},{10,2},{12,4},{14,6},{16,24},{18,... | collective-permute-start | bytes 786440 | tf_op jit(solution)/shard_map/ppermute | solution.py:653
  272.0 34.9 %collective-permute-start.30 = (bf16[4,2,64,1024]{3,2,1,0:T(8,128)(2,1)}, bf16[4,2,64,1024]{3,2,1,0:T(8,128)(2,1)S(1)}, u32[]{:S(2)}, u32[]{:S(2)}) collective-permute-start(bf16[4,2,64,1024]{3,2,1,0:T(8,128)(2,1)} %fusion), channel_id=1, source_target_pairs={{0,4},{2,6},{4,0},{6,2},{8,12},{10,14},{12,8},{14,10},{16,20},{18,... | collective-permute-start | bytes 3145736 | tf_op jit(solution)/shard_map/ppermute | solution.py:653
  293.4 3.8 %collective-permute-start.36 = (f32[32,32]{1,0:T(8,128)S(1)}, f32[32,32]{1,0:T(8,128)S(1)}, u32[]{:S(2)}, u32[]{:S(2)}) collective-permute-start(f32[32,32]{1,0:T(8,128)S(1)} %div.40), channel_id=1, source_target_pairs={{0,1},{1,0},{2,3},{3,2},{4,5},{5,4},{6,7},{7,6},{8,9},{9,8},{10,11... | collective-permute-start | bytes 12296 | tf_op jit(solution)/shard_map/ppermute | solution.py:657
  295.1 4.9 %collective-permute-start.35 = (f32[200,128]{1,0:T(8,128)S(1)}, f32[200,128]{1,0:T(8,128)S(1)}, u32[]{:S(2)}, u32[]{:S(2)}) collective-permute-start(f32[200,128]{1,0:T(8,128)S(1)} %bitcast_dynamic-update-slice_fusion), channel_id=1, source_target_pairs={{0,1},{1,0},{2,3},{3,2},{4,5},{5,4},{6,7},{7,6},{8,9},{9,8},{10,11... | collective-permute-start | bytes 307208 | tf_op jit(solution)/shard_map/ppermute | solution.py:657
  298.4 8.4 %collective-permute-start.34 = (bf16[128,1024]{1,0:T(8,128)(2,1)S(1)}, bf16[128,1024]{1,0:T(8,128)(2,1)S(1)}, u32[]{:S(2)}, u32[]{:S(2)}) collective-permute-start(bf16[128,1024]{1,0:T(8,128)(2,1)S(1)} %select_convert_fusion), channel_id=1, source_target_pairs={{0,1},{1,0},{2,3},{3,2},{4,5},{5,4},{6,7},{7,6},{8,9},{9,8},{10,11... | collective-permute-start | bytes 786440 | tf_op jit(solution)/shard_map/ppermute | solution.py:657
  309.4 10.0 %collective-permute-start.38 = (bf16[2,64,1024]{2,1,0:T(8,128)(2,1)S(1)}, bf16[2,64,1024]{2,1,0:T(8,128)(2,1)S(1)}, u32[]{:S(2)}, u32[]{:S(2)}) collective-permute-start(bf16[2,64,1024]{2,1,0:T(8,128)(2,1)S(1)} %get-tuple-element.135), channel_id=1, source_target_pairs={{0,8},{2,10},{4,12},{6,14},{8,0},{10,2},{12,4},{14,6},{16,24},{18,... | collective-permute-start | bytes 786440 | tf_op jit(solution)/shard_map/ppermute | solution.py:653
  311.1 16.9 %collective-permute-start.41 = (bf16[1,64,1024]{2,1,0:T(8,128)(2,1)}, bf16[1,64,1024]{2,1,0:T(8,128)(2,1)S(1)}, u32[]{:S(2)}, u32[]{:S(2)}) collective-permute-start(bf16[1,64,1024]{2,1,0:T(8,128)(2,1)} %fusion.19), channel_id=1, source_target_pairs={{0,4},{2,6},{4,0},{6,2},{8,12},{10,14},{12,8},{14,10},{16,20},{18,... | collective-permute-start | bytes 393224 | tf_op jit(solution)/shard_map/ppermute | solution.py:653
  312.6 22.1 %collective-permute-start.40 = (bf16[2,64,1024]{2,1,0:T(8,128)(2,1)}, bf16[2,64,1024]{2,1,0:T(8,128)(2,1)S(1)}, u32[]{:S(2)}, u32[]{:S(2)}) collective-permute-start(bf16[2,64,1024]{2,1,0:T(8,128)(2,1)} %get-tuple-element.133), channel_id=1, source_target_pairs={{0,24},{2,26},{4,28},{6,30},{8,16},{10,18},{12,20},{14,22},{16,8},... | collective-permute-start | bytes 786440 | tf_op jit(solution)/shard_map/ppermute | solution.py:653
  312.6 24.4 %collective-permute-start.39 = (bf16[2,64,1024]{2,1,0:T(8,128)(2,1)S(1)}, bf16[2,64,1024]{2,1,0:T(8,128)(2,1)S(1)}, u32[]{:S(2)}, u32[]{:S(2)}) collective-permute-start(bf16[2,64,1024]{2,1,0:T(8,128)(2,1)S(1)} %get-tuple-element.134), channel_id=1, source_target_pairs={{0,16},{2,18},{4,20},{6,22},{8,24},{10,26},{12,28},{14,30},{16,0},... | collective-permute-start | bytes 786440 | tf_op jit(solution)/shard_map/ppermute | solution.py:653
  319.5 8.5 %collective-permute-start.42 = (f32[32,32]{1,0:T(8,128)S(1)}, f32[32,32]{1,0:T(8,128)S(1)}, u32[]{:S(2)}, u32[]{:S(2)}) collective-permute-start(f32[32,32]{1,0:T(8,128)S(1)} %get-tuple-element.118), channel_id=1, source_target_pairs={{0,4},{2,6},{4,0},{6,2},{8,12},{10,14},{12,8},{14,10},{16,20},{18,... | collective-permute-start | bytes 12296 | tf_op jit(solution)/shard_map/ppermute | solution.py:653
  322.6 17.7 %all-to-all-start.1 = ((bf16[16,32,128]{2,1,0:T(8,128)(2,1)}), bf16[16,32,128]{2,1,0:T(8,128)(2,1)}, u32[]{:S(2)}, u32[]{:S(2)}) async-start(bf16[16,32,128]{2,1,0:T(8,128)(2,1)} %get-tuple-element.130), calls=%async_computation.2 | async-start | bytes 262144 | tf_op jit(solution)/shard_map/all_to_all | solution.py:804
  344.2 9.0 %collective-permute-start.45 = (f32[32,32]{1,0:T(8,128)S(1)}, f32[32,32]{1,0:T(8,128)S(1)}, u32[]{:S(2)}, u32[]{:S(2)}) collective-permute-start(f32[32,32]{1,0:T(8,128)S(1)} %get-tuple-element.128), channel_id=1, source_target_pairs={{0,24},{2,26},{4,28},{6,30},{8,16},{10,18},{12,20},{14,22},{16,8},... | collective-permute-start | bytes 12296 | tf_op jit(solution)/shard_map/ppermute | solution.py:653
  345.9 7.4 %collective-permute-start.44 = (f32[32,32]{1,0:T(8,128)S(1)}, f32[32,32]{1,0:T(8,128)S(1)}, u32[]{:S(2)}, u32[]{:S(2)}) collective-permute-start(f32[32,32]{1,0:T(8,128)S(1)} %get-tuple-element.128), channel_id=1, source_target_pairs={{0,16},{2,18},{4,20},{6,22},{8,24},{10,26},{12,28},{14,30},{16,0},... | collective-permute-start | bytes 12296 | tf_op jit(solution)/shard_map/ppermute | solution.py:653
  350.1 3.9 %collective-permute-start.43 = (f32[32,32]{1,0:T(8,128)S(1)}, f32[32,32]{1,0:T(8,128)S(1)}, u32[]{:S(2)}, u32[]{:S(2)}) collective-permute-start(f32[32,32]{1,0:T(8,128)S(1)} %get-tuple-element.128), channel_id=1, source_target_pairs={{0,8},{2,10},{4,12},{6,14},{8,0},{10,2},{12,4},{14,6},{16,24},{18,... | collective-permute-start | bytes 12296 | tf_op jit(solution)/shard_map/ppermute | solution.py:653
  350.1 18.1 %collective-permute-start.46 = (bf16[128,1024]{1,0:T(8,128)(2,1)S(1)}, bf16[128,1024]{1,0:T(8,128)(2,1)S(1)}, u32[]{:S(2)}, u32[]{:S(2)}) collective-permute-start(bf16[128,1024]{1,0:T(8,128)(2,1)S(1)} %get-tuple-element.129), channel_id=1, source_target_pairs={{0,0},{2,1},{4,2},{6,3},{8,4},{10,5},{12,6},{14,7},{16,8},{18,9},{... | collective-permute-start | bytes 786440 | tf_op jit(solution)/shard_map/ppermute | solution.py:810
  (12 other events, 231.2 us)
Sparse Core Ops, SparseCore 0:
  10.2 70.9 all-gather.2
  83.4 65.0 all-gather.4
  213.5 102.2 reduce-scatter.1

commit v4 on v3

--- a/solution.py
+++ b/solution.py
@@ -803,9 +803,8 @@
     grad_gain, out_half = gate([grad_gain, out_half], [gnormed.third_of[0]])
     out_share = lax.all_to_all(out_half, "seq", split_axis=0, concat_axis=0, tiled=True)
     grad_gain = grad_gain + cross(grad_gain, 2)
-    *gnormed.third_of, grad_gain = gate([*gnormed.third_of, grad_gain], [])
+    *gnormed.third_of, grad_gain, in_half = gate([*gnormed.third_of, grad_gain, in_half], [])
     gnormed = gnormed.third([])
-    in_half, grad_gain = gate([in_half, grad_gain], [gnormed])
     to_owner = [(b, a) for a, b in to_shard]
     in_share = lax.ppermute(in_half, both, to_owner).astype(F32)
     grad_gain = grad_gain + sum(cross_z([grad_gain] * 3))

time: 377 us -> 375 us (level)
  transfers between devices with their start and end apart: 52 -> 52, of which waited for: 29 -> 28; matrix products, arithmetic and copies ran while one was open for 9% -> 9% of each run, Pallas kernels for 12% -> 12%
where the time goes in v4:
time: 375 us; the launch traced here: 374 us
  waiting for transfers between devices  156 us (42%)
  Pallas kernels  83.5 us (22%)
  starting transfers between devices  82.7 us (22%)
  other arithmetic  27.5 us (7%)
  between operations  14.3 us (4%)
  local copies, waits for them, and re-layouts  5.33 us (1%)
  matrix products  4.22 us (1%)
    ppermute x38, waiting for transfers between devices, cross(): return lax.ppermute(v, 'seq', [(s, s ^ bits) for s in range(16)])  92.7 us
    ppermute x38, starting transfers between devices, cross(): return lax.ppermute(v, 'seq', [(s, s ^ bits) for s in range(16)])  58.5 us
    pallas_call x1, Pallas kernels, backward_scan(): pl.pallas_call(partial(backward_kernel, top=top), grid_spec=pltpu.Prefetc...  39.1 us
    all_gather x2, waiting for transfers between devices, gather_tokens(): return lax.all_gather(v, 'seq', axis=1, tiled=True)  35.2 us
    pallas_call x1, Pallas kernels, forward_scan(): pl.pallas_call(forward_kernel, grid_spec=pltpu.PrefetchScalarGridSpec(num...  21.7 us
    ppermute x1, waiting for transfers between devices, channel_plan(): in_share = lax.ppermute(in_half, both, to_owner).astype(F32)  14 us
    ppermute x7, waiting for transfers between devices, swap_row(): return lax.ppermute(v, 'row', [(0, 1), (1, 0)])  12.9 us
    pallas_call x1, Pallas kernels, tail(): pl.pallas_call(tail_kernel, grid_spec=pltpu.PrefetchScalarGridSpec(num_sc...  12.4 us
  transfers between devices with their start and end apart: 52, of which 28 were waited for; matrix products, arithmetic and copies ran while one was open for 9% of the time, Pallas kernels for 12%

profile of v4, /device:TPU:18, one launch (start us, length us, event | category | flops | bytes accessed | tf_op | source)
XLA Modules:
  0.0 373.9 jit_solution(13296230231261739446)
XLA Ops:
  10.9 2.2 collective-permute-done.2
  15.5 2.3 collective-permute-start
  18.7 3.7 collective-permute-done.4
  22.4 7.1 %collective-permute-start.5 = (f32[32,32]{1,0:T(8,128)S(1)}, f32[32,32]{1,0:T(8,128)S(1)}, u32[]{:S(2)}, u32[]{:S(2)}) collective-permute-start(f32[32,32]{1,0:T(8,128)S(1)} %add.320), channel_id=1, source_target_pairs={{0,8},{2,10},{4,12},{6,14},{8,0},{10,2},{12,4},{14,6},{16,24},{18,... | collective-permute-start | bytes 12296 | tf_op jit(solution)/shard_map/ppermute | solution.py:653
  31.2 6.2 %all-to-all-start = ((bf16[64,16,128]{2,0,1:T(8,128)(2,1)}), bf16[64,16,128]{2,0,1:T(8,128)(2,1)S(1)}, u32[]{:S(2)}, u32[]{:S(2)}) async-start(bf16[64,16,128]{2,0,1:T(8,128)(2,1)} %copy_bitcast_fusion.1), calls=%async_computation | async-start | bytes 524288 | tf_op jit(solution)/shard_map/all_to_all | solution.py:747
  42.0 2.5 collective-permute-done.6
  46.0 35.2 %all-gather.3.cloned.1.call-done.hid = bf16[3,1024,1024]{2,1,0:T(8,128)(2,1)} async-done(((bf16[3,64,1024]{2,1,0:T(8,128)(2,1)}), bf16[3,1024,1024]{2,1,0:T(8,128)(2,1)}) %all-gather.3.cloned.1.call-update) | async-done | bytes 6291472 | tf_op jit(solution)/shard_map/all_gather | solution.py:683
  81.2 10.4 %front.1 = (bf16[3,1024,1024]{2,1,0:T(8,128)(2,1)}, bf16[3,1024,128]{2,1,0:T(8,128)(2,1)}, f32[3,1024,128]{2,1,0:T(8,128)}, bf16[3,1024,128]{2,1,0:T(8,128)(2,1)...) custom-call(s32[3,8]{1,0:T(4,128)S(1)} %copy-done.2, s32[3]{0:T(128)S(1)} %pad_add_fusion.own, ...), custom_call_target="tpu_custom_call" | custom-call | flops 1 | bytes 1 | tf_op jit(solution)/shard_map/front/pallas_call | solution.py:165
  91.8 2.0 collective-permute-done.8
  95.5 10.3 %collective-permute-done.9 = f32[4,3,64,96]{3,2,1,0:T(8,128)S(1)} collective-permute-done((f32[4,3,64,96]{3,2,1,0:T(8,128)S(1)}, f32[4,3,64,96]{3,2,1,0:T(8,128)S(1)}, u32[]{:S(2)}, u32[]{:S(2)}) %collective-permute-start.9) | collective-permute-done | bytes 294944 | tf_op jit(solution)/shard_map/ppermute | solution.py:653
  107.5 2.9 collective-permute-start.11
  111.7 11.6 %collective-permute-done.12 = f32[3,64,96]{2,1,0:T(8,128)S(1)} collective-permute-done((f32[3,64,96]{2,1,0:T(8,128)S(1)}, f32[3,64,96]{2,1,0:T(8,128)S(1)}, u32[]{:S(2)}, u32[]{:S(2)}) %collective-permute-start.12) | collective-permute-done | bytes 73760 | tf_op jit(solution)/shard_map/ppermute | solution.py:653
  123.3 6.7 %collective-permute-start.15 = (bf16[3,64,96]{2,1,0:T(8,128)(2,1)S(1)}, bf16[3,64,96]{2,1,0:T(8,128)(2,1)S(1)}, u32[]{:S(2)}, u32[]{:S(2)}) collective-permute-start(bf16[3,64,96]{2,1,0:T(8,128)(2,1)S(1)} %fusion.29), channel_id=1, source_target_pairs={{0,24},{2,26},{4,28},{6,30},{8,16},{10,18},{12,20},{14,22},{16,8},... | collective-permute-start | bytes 110600 | tf_op jit(solution)/shard_map/ppermute | solution.py:653
  130.1 5.2 %collective-permute-start.14 = (bf16[3,64,96]{2,1,0:T(8,128)(2,1)S(1)}, bf16[3,64,96]{2,1,0:T(8,128)(2,1)S(1)}, u32[]{:S(2)}, u32[]{:S(2)}) collective-permute-start(bf16[3,64,96]{2,1,0:T(8,128)(2,1)S(1)} %fusion.29), channel_id=1, source_target_pairs={{0,16},{2,18},{4,20},{6,22},{8,24},{10,26},{12,28},{14,30},{16,0},... | collective-permute-start | bytes 110600 | tf_op jit(solution)/shard_map/ppermute | solution.py:653
  135.3 4.7 %collective-permute-done.14 = bf16[3,64,96]{2,1,0:T(8,128)(2,1)S(1)} collective-permute-done((bf16[3,64,96]{2,1,0:T(8,128)(2,1)S(1)}, bf16[3,64,96]{2,1,0:T(8,128)(2,1)S(1)}, u32[]{:S(2)}, u32[]{:S(2)}) %collective-permute-start.14) | collective-permute-done | bytes 36896 | tf_op jit(solution)/shard_map/ppermute | solution.py:653
  140.0 2.4 collective-permute-start.16
  142.4 3.6 collective-permute-done.16
  146.2 2.0 collective-permute-done.17.far
  148.2 21.7 %forward_scan.1 = (bf16[3,1024,128]{2,1,0:T(8,128)(2,1)}, bf16[3,1024,128]{2,1,0:T(8,128)(2,1)}, f32[3,1024,16,128]{3,2,1,0:T(8,128)}, bf16[3,1024,1024]{2,1,0:T...) custom-call(s32[3,8]{1,0:T(4,128)S(1)} %copy-done.2, s32[3]{0:T(128)S(1)} %pad_add_fusion.own, ...), custom_call_target="tpu_custom_call" | custom-call | flops 1 | bytes 1 | tf_op jit(solution)/shard_map/forward_scan/pallas_call | solution.py:324
  170.0 39.1 %backward_scan.1 = (bf16[3,1024,128]{2,1,0:T(8,128)(2,1)}, f32[3,1024,128]{2,1,0:T(8,128)}, f32[2,4,3,64,96]{4,3,2,1,0:T(8,128)S(1)}, f32[2,4,3,64,96]{4,3,2,1,0...) custom-call(s32[3,8]{1,0:T(4,128)S(1)} %copy-done.2, ...), custom_call_target="tpu_custom_call" | custom-call | flops 1 | bytes 1 | tf_op jit(solution)/shard_map/backward_scan/pallas_call | solution.py:492
  209.3 2.1 collective-permute-done.18
  211.6 1.8 collective-permute-start.19
  213.4 5.3 %collective-permute-done.19 = bf16[4,3,64,96]{3,2,1,0:T(8,128)(2,1)S(1)} collective-permute-done((bf16[4,3,64,96]{3,2,1,0:T(8,128)(2,1)S(1)}, bf16[4,3,64,96]{3,2,1,0:T(8,128)(2,1)S(1)}, u32[]{:S(2)}, u32[]{:S(2)}) %collective-permute-start.19) | collective-permute-done | bytes 147488 | tf_op jit(solution)/shard_map/ppermute | solution.py:653
  223.3 2.5 collective-permute-done.22
  227.8 3.3 collective-permute-start.24
  231.1 4.2 %convolution_bitcast_fusion = f32[1024,128]{0,1:T(8,128)S(1)} fusion(bf16[3,1024,128]{2,1,0:T(8,128)(2,1)S(1)} %get-tuple-element.98, bf16[3,1024,1024]{2,1,0:T(8,128)(2,1)} %all-gather.5.cloned.1.call-done.gout), kind=kOutput, calls=%fused_computation.1 | convolution fusion | flops 805306368 | bytes 7602176 | tf_op jit(solution)/shard_map/rtd,rtc->dc/dot_general | solution.py:779
  235.6 1.9 collective-permute-start.26
  238.9 2.5 collective-permute-done.26
  241.5 2.4 collective-permute-done.28
  244.7 12.4 %tail.1 = (bf16[2,4,3,64,1024]{4,3,2,1,0:T(8,128)(2,1)}, bf16[2,4,3,64,1024]{4,3,2,1,0:T(8,128)(2,1)}, f32[256,1024]{1,0:T(8,128)S(1)}, f32[128,96]{1,0:T(8,128)S(1)}, f32[8,128]{1,0:T(8,128)S(1)}) custom-call(s32[3,8]{1,0:T(4,128)S(1)} %copy-done.2, s32[3]{0:T(128)S(1)} %pad_add_fusion.own, bf16[2,4,3,64,96]{4,3,2,1,0:T(8,128)(2,1)S(1)} %pad_maximum_fusion.2.near, ...), custom_call_target="tpu_custom_call" | custom-call | flops 1 | bytes 1 | tf_op jit(solution)/shard_map/tail/pallas_call | solution.py:605
  258.4 4.6 %collective-permute-done.29.refs_0_ = bf16[2,4,3,64,1024]{4,3,2,1,0:T(8,128)(2,1)} collective-permute-done((bf16[2,4,3,64,1024]{4,3,2,1,0:T(8,128)(2,1)}, bf16[2,4,3,64,1024]{4,3,2,1,0:T(8,128)(2,1)}, u32[]{:S(2)}, u32[]{:S(2)}) %collective-permute-start.29) | collective-permute-done | bytes 3145760 | tf_op jit(solution)/shard_map/ppermute | solution.py:653
  263.0 2.2 fusion.17
  266.2 3.2 collective-permute-start.32
  269.4 2.6 fusion
  272.4 20.8 %collective-permute-done.31.refs_6_.refs_1_ = bf16[2,1,64,1024]{3,2,1,0:T(8,128)(2,1)S(1)} collective-permute-done((bf16[2,1,64,1024]{3,2,1,0:T(8,128)(2,1)S(1)}, bf16[2,1,64,1024]{3,2,1,0:T(8,128)(2,1)S(1)}, u32[]{:S(2)}, u32[]{:S(2)}) %collective-permute-start.31) | collective-permute-done | bytes 262176 | tf_op jit(solution)/shard_map/ppermute | solution.py:653
  301.4 5.4 %collective-permute-done.34 = bf16[128,1024]{1,0:T(8,128)(2,1)S(1)} collective-permute-done((bf16[128,1024]{1,0:T(8,128)(2,1)S(1)}, bf16[128,1024]{1,0:T(8,128)(2,1)S(1)}, u32[]{:S(2)}, u32[]{:S(2)}) %collective-permute-start.34) | collective-permute-done | bytes 262176 | tf_op jit(solution)/shard_map/ppermute | solution.py:657
  306.9 2.6 fusion.9
  309.5 1.7 fusion.19
  312.7 4.4 %collective-permute-start.39 = (bf16[2,64,1024]{2,1,0:T(8,128)(2,1)}, bf16[2,64,1024]{2,1,0:T(8,128)(2,1)S(1)}, u32[]{:S(2)}, u32[]{:S(2)}) collective-permute-start(bf16[2,64,1024]{2,1,0:T(8,128)(2,1)} %get-tuple-element.132), channel_id=1, source_target_pairs={{0,16},{2,18},{4,20},{6,22},{8,24},{10,26},{12,28},{14,30},{16,0},... | collective-permute-start | bytes 786440 | tf_op jit(solution)/shard_map/ppermute | solution.py:653
  317.6 1.9 collective-permute-done.38.refs_2_.refs_0_
  322.6 5.4 %all-to-all-start.1 = ((bf16[16,32,128]{2,1,0:T(8,128)(2,1)}), bf16[16,32,128]{2,1,0:T(8,128)(2,1)}, u32[]{:S(2)}, u32[]{:S(2)}) async-start(bf16[16,32,128]{2,1,0:T(8,128)(2,1)} %get-tuple-element.128), calls=%async_computation.2 | async-start | bytes 262144 | tf_op jit(solution)/shard_map/all_to_all | solution.py:804
  328.0 6.8 %collective-permute-done.40.refs_2_ = bf16[2,64,1024]{2,1,0:T(8,128)(2,1)S(1)} collective-permute-done((bf16[2,64,1024]{2,1,0:T(8,128)(2,1)}, bf16[2,64,1024]{2,1,0:T(8,128)(2,1)S(1)}, u32[]{:S(2)}, u32[]{:S(2)}) %collective-permute-start.40) | collective-permute-done | bytes 262176 | tf_op jit(solution)/shard_map/ppermute | solution.py:653
  334.8 2.5 collective-permute-done.39.refs_1_
  337.4 1.7 collective-permute-start.45
  339.0 4.2 %collective-permute-start.44 = (f32[32,32]{1,0:T(8,128)S(1)}, f32[32,32]{1,0:T(8,128)S(1)}, u32[]{:S(2)}, u32[]{:S(2)}) collective-permute-start(f32[32,32]{1,0:T(8,128)S(1)} %get-tuple-element.126), channel_id=1, source_target_pairs={{0,16},{2,18},{4,20},{6,22},{8,24},{10,26},{12,28},{14,30},{16,0},... | collective-permute-start | bytes 12296 | tf_op jit(solution)/shard_map/ppermute | solution.py:653
  345.9 1.9 collective-permute-start.46
  350.0 14.0 %collective-permute-done.46 = bf16[128,1024]{1,0:T(8,128)(2,1)S(1)} collective-permute-done((bf16[128,1024]{1,0:T(8,128)(2,1)S(1)}, bf16[128,1024]{1,0:T(8,128)(2,1)S(1)}, u32[]{:S(2)}, u32[]{:S(2)}) %collective-permute-start.46) | collective-permute-done | bytes 262176 | tf_op jit(solution)/shard_map/ppermute | solution.py:809
  364.9 2.5 fusion.6
  (169 shorter events, 51.4 us)
Async XLA Ops:
  7.2 74.0 %all-gather.3.cloned.1.call-start = ((), (), s32[]{:S(2)}) async-start(), calls=%async_computation.3 | async-start | bytes 6684672 | tf_op jit(solution)/shard_map/all_gather | solution.py:683
  7.9 162.0 %all-gather.5.cloned.1.call-start = ((), (), s32[]{:S(2)}) async-start(), calls=%async_computation.5 | async-start | bytes 6684672 | tf_op jit(solution)/shard_map/all_gather | solution.py:683
  9.4 3.8 %collective-permute-start.2 = (f32[32,32]{1,0:T(8,128)S(1)}, f32[32,32]{1,0:T(8,128)S(1)}, u32[]{:S(2)}, u32[]{:S(2)}) collective-permute-start(f32[32,32]{1,0:T(8,128)S(1)} %dynamic_update_slice.5), channel_id=1, source_target_pairs={{0,1},{1,0},{2,3},{3,2},{4,5},{5,4},{6,7},{7,6},{8,9},{9,8},{10,11... | collective-permute-start | bytes 12296 | tf_op jit(solution)/shard_map/ppermute | solution.py:657
  13.9 3.9 %collective-permute-start.3 = (f32[32,32]{1,0:T(8,128)S(1)}, f32[32,32]{1,0:T(8,128)S(1)}, u32[]{:S(2)}, u32[]{:S(2)}) collective-permute-start(f32[32,32]{1,0:T(8,128)S(1)} %add.318), channel_id=1, source_target_pairs={{0,2},{2,0},{4,6},{6,4},{8,10},{10,8},{12,14},{14,12},{16,18},{18,... | collective-permute-start | bytes 12296 | tf_op jit(solution)/shard_map/ppermute | solution.py:653
  13.9 15.6 %collective-permute-start.7 = (bf16[32,2048]{1,0:T(8,128)(2,1)}, bf16[32,2048]{1,0:T(8,128)(2,1)S(1)}, u32[]{:S(2)}, u32[]{:S(2)}) collective-permute-start(bf16[32,2048]{1,0:T(8,128)(2,1)} %param.18), channel_id=1, source_target_pairs={{0,1},{1,0},{2,3},{3,2},{4,5},{5,4},{6,7},{7,6},{8,9},{9,8},{10,11... | collective-permute-start | bytes 393224 | tf_op jit(solution)/shard_map/ppermute | solution.py:657
  15.5 21.9 %collective-permute-start = (bf16[128,1024]{1,0:T(8,128)(2,1)}, bf16[128,1024]{1,0:T(8,128)(2,1)S(1)}, u32[]{:S(2)}, u32[]{:S(2)}) collective-permute-start(bf16[128,1024]{1,0:T(8,128)(2,1)} %param.17), channel_id=1, source_target_pairs={{0,0},{1,2},{2,4},{3,6},{4,8},{5,10},{6,12},{7,14},{8,16},{9,18},{... | collective-permute-start | bytes 786440 | tf_op jit(solution)/shard_map/ppermute | solution.py:742
  17.8 4.6 %collective-permute-start.4 = (f32[32,32]{1,0:T(8,128)S(1)}, f32[32,32]{1,0:T(8,128)S(1)}, u32[]{:S(2)}, u32[]{:S(2)}) collective-permute-start(f32[32,32]{1,0:T(8,128)S(1)} %add.319), channel_id=1, source_target_pairs={{0,4},{2,6},{4,0},{6,2},{8,12},{10,14},{12,8},{14,10},{16,20},{18,... | collective-permute-start | bytes 12296 | tf_op jit(solution)/shard_map/ppermute | solution.py:653
  22.4 15.8 %collective-permute-start.5 = (f32[32,32]{1,0:T(8,128)S(1)}, f32[32,32]{1,0:T(8,128)S(1)}, u32[]{:S(2)}, u32[]{:S(2)}) collective-permute-start(f32[32,32]{1,0:T(8,128)S(1)} %add.320), channel_id=1, source_target_pairs={{0,8},{2,10},{4,12},{6,14},{8,0},{10,2},{12,4},{14,6},{16,24},{18,... | collective-permute-start | bytes 12296 | tf_op jit(solution)/shard_map/ppermute | solution.py:653
  31.2 14.7 %all-to-all-start = ((bf16[64,16,128]{2,0,1:T(8,128)(2,1)}), bf16[64,16,128]{2,0,1:T(8,128)(2,1)S(1)}, u32[]{:S(2)}, u32[]{:S(2)}) async-start(bf16[64,16,128]{2,0,1:T(8,128)(2,1)} %copy_bitcast_fusion.1), calls=%async_computation | async-start | bytes 524288 | tf_op jit(solution)/shard_map/all_to_all | solution.py:747
  37.4 327.5 %reduce-scatter.2.cloned.1.call-start = ((), (), s32[]{:S(2)}) async-start(), calls=%async_computation.4 | async-start | bytes 6684672 | tf_op jit(solution)/shard_map/reduce_scatter | solution.py:771
  37.4 8.4 %collective-permute-start.1 = (bf16[128,1024]{1,0:T(8,128)(2,1)S(1)}, bf16[128,1024]{1,0:T(8,128)(2,1)S(1)}, u32[]{:S(2)}, u32[]{:S(2)}) collective-permute-start(bf16[128,1024]{1,0:T(8,128)(2,1)S(1)} %collective-permute-done), channel_id=1, source_target_pairs={{0,1},{1,0},{2,3},{3,2},{4,5},{5,4},{6,7},{7,6},{8,9},{9,8},{10,11... | collective-permute-start | bytes 786440 | tf_op jit(solution)/shard_map/ppermute | solution.py:657
  38.2 6.2 %collective-permute-start.6 = (f32[32,32]{1,0:T(8,128)S(1)}, f32[32,32]{1,0:T(8,128)S(1)}, u32[]{:S(2)}, u32[]{:S(2)}) collective-permute-start(f32[32,32]{1,0:T(8,128)S(1)} %add.321), channel_id=1, source_target_pairs={{0,16},{2,18},{4,20},{6,22},{8,24},{10,26},{12,28},{14,30},{16,0},... | collective-permute-start | bytes 12296 | tf_op jit(solution)/shard_map/ppermute | solution.py:653
  94.0 11.8 %collective-permute-start.9 = (f32[4,3,64,96]{3,2,1,0:T(8,128)S(1)}, f32[4,3,64,96]{3,2,1,0:T(8,128)S(1)}, u32[]{:S(2)}, u32[]{:S(2)}) collective-permute-start(f32[4,3,64,96]{3,2,1,0:T(8,128)S(1)} %slice_bitcast_fusion.1), channel_id=1, source_target_pairs={{0,4},{2,6},{4,0},{6,2},{8,12},{10,14},{12,8},{14,10},{16,20},{18,... | collective-permute-start | bytes 884744 | tf_op jit(solution)/shard_map/ppermute | solution.py:653
  105.9 5.7 %collective-permute-start.10 = (f32[3,64,96]{2,1,0:T(8,128)S(1)}, f32[3,64,96]{2,1,0:T(8,128)S(1)}, u32[]{:S(2)}, u32[]{:S(2)}) collective-permute-start(f32[3,64,96]{2,1,0:T(8,128)S(1)} %get-tuple-element.141), channel_id=1, source_target_pairs={{0,8},{2,10},{4,12},{6,14},{8,0},{10,2},{12,4},{14,6},{16,24},{18,... | collective-permute-start | bytes 221192 | tf_op jit(solution)/shard_map/ppermute | solution.py:653
  107.5 15.8 %collective-permute-start.12 = (f32[3,64,96]{2,1,0:T(8,128)S(1)}, f32[3,64,96]{2,1,0:T(8,128)S(1)}, u32[]{:S(2)}, u32[]{:S(2)}) collective-permute-start(f32[3,64,96]{2,1,0:T(8,128)S(1)} %get-tuple-element.142), channel_id=1, source_target_pairs={{0,24},{2,26},{4,28},{6,30},{8,16},{10,18},{12,20},{14,22},{16,8},... | collective-permute-start | bytes 221192 | tf_op jit(solution)/shard_map/ppermute | solution.py:653
  107.5 15.8 %collective-permute-start.11 = (f32[3,64,96]{2,1,0:T(8,128)S(1)}, f32[3,64,96]{2,1,0:T(8,128)S(1)}, u32[]{:S(2)}, u32[]{:S(2)}) collective-permute-start(f32[3,64,96]{2,1,0:T(8,128)S(1)} %get-tuple-element.143), channel_id=1, source_target_pairs={{0,16},{2,18},{4,20},{6,22},{8,24},{10,26},{12,28},{14,30},{16,0},... | collective-permute-start | bytes 221192 | tf_op jit(solution)/shard_map/ppermute | solution.py:653
  123.3 11.9 %collective-permute-start.15 = (bf16[3,64,96]{2,1,0:T(8,128)(2,1)S(1)}, bf16[3,64,96]{2,1,0:T(8,128)(2,1)S(1)}, u32[]{:S(2)}, u32[]{:S(2)}) collective-permute-start(bf16[3,64,96]{2,1,0:T(8,128)(2,1)S(1)} %fusion.29), channel_id=1, source_target_pairs={{0,24},{2,26},{4,28},{6,30},{8,16},{10,18},{12,20},{14,22},{16,8},... | collective-permute-start | bytes 110600 | tf_op jit(solution)/shard_map/ppermute | solution.py:653
  130.1 9.9 %collective-permute-start.14 = (bf16[3,64,96]{2,1,0:T(8,128)(2,1)S(1)}, bf16[3,64,96]{2,1,0:T(8,128)(2,1)S(1)}, u32[]{:S(2)}, u32[]{:S(2)}) collective-permute-start(bf16[3,64,96]{2,1,0:T(8,128)(2,1)S(1)} %fusion.29), channel_id=1, source_target_pairs={{0,16},{2,18},{4,20},{6,22},{8,24},{10,26},{12,28},{14,30},{16,0},... | collective-permute-start | bytes 110600 | tf_op jit(solution)/shard_map/ppermute | solution.py:653
  135.3 4.7 %collective-permute-start.13 = (bf16[3,64,96]{2,1,0:T(8,128)(2,1)S(1)}, bf16[3,64,96]{2,1,0:T(8,128)(2,1)S(1)}, u32[]{:S(2)}, u32[]{:S(2)}) collective-permute-start(bf16[3,64,96]{2,1,0:T(8,128)(2,1)S(1)} %fusion.29), channel_id=1, source_target_pairs={{0,8},{2,10},{4,12},{6,14},{8,0},{10,2},{12,4},{14,6},{16,24},{18,... | collective-permute-start | bytes 110600 | tf_op jit(solution)/shard_map/ppermute | solution.py:653
  140.0 6.0 %collective-permute-start.16 = (bf16[4,3,64,96]{3,2,1,0:T(8,128)(2,1)S(1)}, bf16[4,3,64,96]{3,2,1,0:T(8,128)(2,1)S(1)}, u32[]{:S(2)}, u32[]{:S(2)}) collective-permute-start(bf16[4,3,64,96]{3,2,1,0:T(8,128)(2,1)S(1)} %get-tuple-element.152), channel_id=1, source_target_pairs={{0,4},{2,6},{4,0},{6,2},{8,12},{10,14},{12,8},{14,10},{16,20},{18,... | collective-permute-start | bytes 442376 | tf_op jit(solution)/shard_map/ppermute | solution.py:653
  211.6 7.1 %collective-permute-start.19 = (bf16[4,3,64,96]{3,2,1,0:T(8,128)(2,1)S(1)}, bf16[4,3,64,96]{3,2,1,0:T(8,128)(2,1)S(1)}, u32[]{:S(2)}, u32[]{:S(2)}) collective-permute-start(bf16[4,3,64,96]{3,2,1,0:T(8,128)(2,1)S(1)} %fusion.21), channel_id=1, source_target_pairs={{0,4},{2,6},{4,0},{6,2},{8,12},{10,14},{12,8},{14,10},{16,20},{18,... | collective-permute-start | bytes 442376 | tf_op jit(solution)/shard_map/ppermute | solution.py:653
  218.8 4.5 %collective-permute-start.20 = (bf16[3,64,96]{2,1,0:T(8,128)(2,1)S(1)}, bf16[3,64,96]{2,1,0:T(8,128)(2,1)S(1)}, u32[]{:S(2)}, u32[]{:S(2)}) collective-permute-start(bf16[3,64,96]{2,1,0:T(8,128)(2,1)S(1)} %get-tuple-element.148), channel_id=1, source_target_pairs={{0,8},{2,10},{4,12},{6,14},{8,0},{10,2},{12,4},{14,6},{16,24},{18,... | collective-permute-start | bytes 110600 | tf_op jit(solution)/shard_map/ppermute | solution.py:653
  220.3 5.4 %collective-permute-start.22 = (bf16[3,64,96]{2,1,0:T(8,128)(2,1)S(1)}, bf16[3,64,96]{2,1,0:T(8,128)(2,1)S(1)}, u32[]{:S(2)}, u32[]{:S(2)}) collective-permute-start(bf16[3,64,96]{2,1,0:T(8,128)(2,1)S(1)} %get-tuple-element.149), channel_id=1, source_target_pairs={{0,24},{2,26},{4,28},{6,30},{8,16},{10,18},{12,20},{14,22},{16,8},... | collective-permute-start | bytes 110600 | tf_op jit(solution)/shard_map/ppermute | solution.py:653
  221.6 5.0 %collective-permute-start.21 = (bf16[3,64,96]{2,1,0:T(8,128)(2,1)S(1)}, bf16[3,64,96]{2,1,0:T(8,128)(2,1)S(1)}, u32[]{:S(2)}, u32[]{:S(2)}) collective-permute-start(bf16[3,64,96]{2,1,0:T(8,128)(2,1)S(1)} %get-tuple-element.150), channel_id=1, source_target_pairs={{0,16},{2,18},{4,20},{6,22},{8,24},{10,26},{12,28},{14,30},{16,0},... | collective-permute-start | bytes 110600 | tf_op jit(solution)/shard_map/ppermute | solution.py:653
  226.7 8.8 %collective-permute-start.25 = (bf16[3,64,96]{2,1,0:T(8,128)(2,1)S(1)}, bf16[3,64,96]{2,1,0:T(8,128)(2,1)S(1)}, u32[]{:S(2)}, u32[]{:S(2)}) collective-permute-start(bf16[3,64,96]{2,1,0:T(8,128)(2,1)S(1)} %fusion.25), channel_id=1, source_target_pairs={{0,24},{2,26},{4,28},{6,30},{8,16},{10,18},{12,20},{14,22},{16,8},... | collective-permute-start | bytes 110600 | tf_op jit(solution)/shard_map/ppermute | solution.py:653
  227.8 7.7 %collective-permute-start.24 = (bf16[3,64,96]{2,1,0:T(8,128)(2,1)S(1)}, bf16[3,64,96]{2,1,0:T(8,128)(2,1)S(1)}, u32[]{:S(2)}, u32[]{:S(2)}) collective-permute-start(bf16[3,64,96]{2,1,0:T(8,128)(2,1)S(1)} %fusion.25), channel_id=1, source_target_pairs={{0,16},{2,18},{4,20},{6,22},{8,24},{10,26},{12,28},{14,30},{16,0},... | collective-permute-start | bytes 110600 | tf_op jit(solution)/shard_map/ppermute | solution.py:653
  231.1 4.5 %collective-permute-start.23 = (bf16[3,64,96]{2,1,0:T(8,128)(2,1)S(1)}, bf16[3,64,96]{2,1,0:T(8,128)(2,1)S(1)}, u32[]{:S(2)}, u32[]{:S(2)}) collective-permute-start(bf16[3,64,96]{2,1,0:T(8,128)(2,1)S(1)} %fusion.25), channel_id=1, source_target_pairs={{0,8},{2,10},{4,12},{6,14},{8,0},{10,2},{12,4},{14,6},{16,24},{18,... | collective-permute-start | bytes 110600 | tf_op jit(solution)/shard_map/ppermute | solution.py:653
  235.6 5.7 %collective-permute-start.26 = (bf16[4,3,64,96]{3,2,1,0:T(8,128)(2,1)S(1)}, bf16[4,3,64,96]{3,2,1,0:T(8,128)(2,1)S(1)}, u32[]{:S(2)}, u32[]{:S(2)}) collective-permute-start(bf16[4,3,64,96]{3,2,1,0:T(8,128)(2,1)S(1)} %get-tuple-element.147), channel_id=1, source_target_pairs={{0,4},{2,6},{4,0},{6,2},{8,12},{10,14},{12,8},{14,10},{16,20},{18,... | collective-permute-start | bytes 442376 | tf_op jit(solution)/shard_map/ppermute | solution.py:653
  237.5 6.4 %collective-permute-start.28 = (f32[16,32,128]{2,1,0:T(8,128)S(1)}, f32[16,32,128]{2,1,0:T(8,128)S(1)}, u32[]{:S(2)}, u32[]{:S(2)}) collective-permute-start(f32[16,32,128]{2,1,0:T(8,128)S(1)} %select_bitcast_fusion), channel_id=1, source_target_pairs={{0,1},{1,0},{2,3},{3,2},{4,5},{5,4},{6,7},{7,6},{8,9},{9,8},{10,11... | collective-permute-start | bytes 786440 | tf_op jit(solution)/shard_map/ppermute | solution.py:657
  241.4 3.2 collective-permute-start.27
  257.0 6.0 %collective-permute-start.29 = (bf16[2,4,3,64,1024]{4,3,2,1,0:T(8,128)(2,1)}, bf16[2,4,3,64,1024]{4,3,2,1,0:T(8,128)(2,1)}, u32[]{:S(2)}, u32[]{:S(2)}) collective-permute-start(bf16[2,4,3,64,1024]{4,3,2,1,0:T(8,128)(2,1)} %get-tuple-element.100), channel_id=1, source_target_pairs={{0,2},{2,0},{4,6},{6,4},{8,10},{10,8},{12,14},{14,12},{16,18},{18,... | collective-permute-start | bytes 9437192 | tf_op jit(solution)/shard_map/ppermute | solution.py:653
  265.2 41.7 %collective-permute-start.33 = (bf16[2,1,64,1024]{3,2,1,0:T(8,128)(2,1)}, bf16[2,1,64,1024]{3,2,1,0:T(8,128)(2,1)S(1)}, u32[]{:S(2)}, u32[]{:S(2)}) collective-permute-start(bf16[2,1,64,1024]{3,2,1,0:T(8,128)(2,1)} %get-tuple-element.134), channel_id=1, source_target_pairs={{0,24},{2,26},{4,28},{6,30},{8,16},{10,18},{12,20},{14,22},{16,8},... | collective-permute-start | bytes 786440 | tf_op jit(solution)/shard_map/ppermute | solution.py:653
  266.2 40.7 %collective-permute-start.32 = (bf16[2,1,64,1024]{3,2,1,0:T(8,128)(2,1)}, bf16[2,1,64,1024]{3,2,1,0:T(8,128)(2,1)S(1)}, u32[]{:S(2)}, u32[]{:S(2)}) collective-permute-start(bf16[2,1,64,1024]{3,2,1,0:T(8,128)(2,1)} %get-tuple-element.135), channel_id=1, source_target_pairs={{0,16},{2,18},{4,20},{6,22},{8,24},{10,26},{12,28},{14,30},{16,0},... | collective-permute-start | bytes 786440 | tf_op jit(solution)/shard_map/ppermute | solution.py:653
  269.4 23.8 %collective-permute-start.31 = (bf16[2,1,64,1024]{3,2,1,0:T(8,128)(2,1)S(1)}, bf16[2,1,64,1024]{3,2,1,0:T(8,128)(2,1)S(1)}, u32[]{:S(2)}, u32[]{:S(2)}) collective-permute-start(bf16[2,1,64,1024]{3,2,1,0:T(8,128)(2,1)S(1)} %get-tuple-element.136), channel_id=1, source_target_pairs={{0,8},{2,10},{4,12},{6,14},{8,0},{10,2},{12,4},{14,6},{16,24},{18,... | collective-permute-start | bytes 786440 | tf_op jit(solution)/shard_map/ppermute | solution.py:653
  272.0 34.9 %collective-permute-start.30 = (bf16[4,2,64,1024]{3,2,1,0:T(8,128)(2,1)}, bf16[4,2,64,1024]{3,2,1,0:T(8,128)(2,1)S(1)}, u32[]{:S(2)}, u32[]{:S(2)}) collective-permute-start(bf16[4,2,64,1024]{3,2,1,0:T(8,128)(2,1)} %fusion), channel_id=1, source_target_pairs={{0,4},{2,6},{4,0},{6,2},{8,12},{10,14},{12,8},{14,10},{16,20},{18,... | collective-permute-start | bytes 3145736 | tf_op jit(solution)/shard_map/ppermute | solution.py:653
  293.4 3.8 %collective-permute-start.36 = (f32[32,32]{1,0:T(8,128)S(1)}, f32[32,32]{1,0:T(8,128)S(1)}, u32[]{:S(2)}, u32[]{:S(2)}) collective-permute-start(f32[32,32]{1,0:T(8,128)S(1)} %div.40), channel_id=1, source_target_pairs={{0,1},{1,0},{2,3},{3,2},{4,5},{5,4},{6,7},{7,6},{8,9},{9,8},{10,11... | collective-permute-start | bytes 12296 | tf_op jit(solution)/shard_map/ppermute | solution.py:657
  295.1 4.9 %collective-permute-start.35 = (f32[200,128]{1,0:T(8,128)S(1)}, f32[200,128]{1,0:T(8,128)S(1)}, u32[]{:S(2)}, u32[]{:S(2)}) collective-permute-start(f32[200,128]{1,0:T(8,128)S(1)} %bitcast_dynamic-update-slice_fusion), channel_id=1, source_target_pairs={{0,1},{1,0},{2,3},{3,2},{4,5},{5,4},{6,7},{7,6},{8,9},{9,8},{10,11... | collective-permute-start | bytes 307208 | tf_op jit(solution)/shard_map/ppermute | solution.py:657
  298.4 8.4 %collective-permute-start.34 = (bf16[128,1024]{1,0:T(8,128)(2,1)S(1)}, bf16[128,1024]{1,0:T(8,128)(2,1)S(1)}, u32[]{:S(2)}, u32[]{:S(2)}) collective-permute-start(bf16[128,1024]{1,0:T(8,128)(2,1)S(1)} %select_convert_fusion), channel_id=1, source_target_pairs={{0,1},{1,0},{2,3},{3,2},{4,5},{5,4},{6,7},{7,6},{8,9},{9,8},{10,11... | collective-permute-start | bytes 786440 | tf_op jit(solution)/shard_map/ppermute | solution.py:657
  309.5 10.0 %collective-permute-start.38 = (bf16[2,64,1024]{2,1,0:T(8,128)(2,1)S(1)}, bf16[2,64,1024]{2,1,0:T(8,128)(2,1)S(1)}, u32[]{:S(2)}, u32[]{:S(2)}) collective-permute-start(bf16[2,64,1024]{2,1,0:T(8,128)(2,1)S(1)} %get-tuple-element.133), channel_id=1, source_target_pairs={{0,8},{2,10},{4,12},{6,14},{8,0},{10,2},{12,4},{14,6},{16,24},{18,... | collective-permute-start | bytes 786440 | tf_op jit(solution)/shard_map/ppermute | solution.py:653
  311.2 16.8 %collective-permute-start.41 = (bf16[1,64,1024]{2,1,0:T(8,128)(2,1)}, bf16[1,64,1024]{2,1,0:T(8,128)(2,1)S(1)}, u32[]{:S(2)}, u32[]{:S(2)}) collective-permute-start(bf16[1,64,1024]{2,1,0:T(8,128)(2,1)} %fusion.19), channel_id=1, source_target_pairs={{0,4},{2,6},{4,0},{6,2},{8,12},{10,14},{12,8},{14,10},{16,20},{18,... | collective-permute-start | bytes 393224 | tf_op jit(solution)/shard_map/ppermute | solution.py:653
  312.7 22.1 %collective-permute-start.40 = (bf16[2,64,1024]{2,1,0:T(8,128)(2,1)}, bf16[2,64,1024]{2,1,0:T(8,128)(2,1)S(1)}, u32[]{:S(2)}, u32[]{:S(2)}) collective-permute-start(bf16[2,64,1024]{2,1,0:T(8,128)(2,1)} %get-tuple-element.131), channel_id=1, source_target_pairs={{0,24},{2,26},{4,28},{6,30},{8,16},{10,18},{12,20},{14,22},{16,8},... | collective-permute-start | bytes 786440 | tf_op jit(solution)/shard_map/ppermute | solution.py:653
  312.7 24.6 %collective-permute-start.39 = (bf16[2,64,1024]{2,1,0:T(8,128)(2,1)}, bf16[2,64,1024]{2,1,0:T(8,128)(2,1)S(1)}, u32[]{:S(2)}, u32[]{:S(2)}) collective-permute-start(bf16[2,64,1024]{2,1,0:T(8,128)(2,1)} %get-tuple-element.132), channel_id=1, source_target_pairs={{0,16},{2,18},{4,20},{6,22},{8,24},{10,26},{12,28},{14,30},{16,0},... | collective-permute-start | bytes 786440 | tf_op jit(solution)/shard_map/ppermute | solution.py:653
  319.5 8.5 %collective-permute-start.42 = (f32[32,32]{1,0:T(8,128)S(1)}, f32[32,32]{1,0:T(8,128)S(1)}, u32[]{:S(2)}, u32[]{:S(2)}) collective-permute-start(f32[32,32]{1,0:T(8,128)S(1)} %get-tuple-element.117), channel_id=1, source_target_pairs={{0,4},{2,6},{4,0},{6,2},{8,12},{10,14},{12,8},{14,10},{16,20},{18,... | collective-permute-start | bytes 12296 | tf_op jit(solution)/shard_map/ppermute | solution.py:653
  322.6 25.8 %all-to-all-start.1 = ((bf16[16,32,128]{2,1,0:T(8,128)(2,1)}), bf16[16,32,128]{2,1,0:T(8,128)(2,1)}, u32[]{:S(2)}, u32[]{:S(2)}) async-start(bf16[16,32,128]{2,1,0:T(8,128)(2,1)} %get-tuple-element.128), calls=%async_computation.2 | async-start | bytes 262144 | tf_op jit(solution)/shard_map/all_to_all | solution.py:804
  337.4 10.5 %collective-permute-start.45 = (f32[32,32]{1,0:T(8,128)S(1)}, f32[32,32]{1,0:T(8,128)S(1)}, u32[]{:S(2)}, u32[]{:S(2)}) collective-permute-start(f32[32,32]{1,0:T(8,128)S(1)} %get-tuple-element.126), channel_id=1, source_target_pairs={{0,24},{2,26},{4,28},{6,30},{8,16},{10,18},{12,20},{14,22},{16,8},... | collective-permute-start | bytes 12296 | tf_op jit(solution)/shard_map/ppermute | solution.py:653
  339.0 8.8 %collective-permute-start.44 = (f32[32,32]{1,0:T(8,128)S(1)}, f32[32,32]{1,0:T(8,128)S(1)}, u32[]{:S(2)}, u32[]{:S(2)}) collective-permute-start(f32[32,32]{1,0:T(8,128)S(1)} %get-tuple-element.126), channel_id=1, source_target_pairs={{0,16},{2,18},{4,20},{6,22},{8,24},{10,26},{12,28},{14,30},{16,0},... | collective-permute-start | bytes 12296 | tf_op jit(solution)/shard_map/ppermute | solution.py:653
  343.2 4.7 %collective-permute-start.43 = (f32[32,32]{1,0:T(8,128)S(1)}, f32[32,32]{1,0:T(8,128)S(1)}, u32[]{:S(2)}, u32[]{:S(2)}) collective-permute-start(f32[32,32]{1,0:T(8,128)S(1)} %get-tuple-element.126), channel_id=1, source_target_pairs={{0,8},{2,10},{4,12},{6,14},{8,0},{10,2},{12,4},{14,6},{16,24},{18,... | collective-permute-start | bytes 12296 | tf_op jit(solution)/shard_map/ppermute | solution.py:653
  345.9 18.1 %collective-permute-start.46 = (bf16[128,1024]{1,0:T(8,128)(2,1)S(1)}, bf16[128,1024]{1,0:T(8,128)(2,1)S(1)}, u32[]{:S(2)}, u32[]{:S(2)}) collective-permute-start(bf16[128,1024]{1,0:T(8,128)(2,1)S(1)} %get-tuple-element.127), channel_id=1, source_target_pairs={{0,0},{2,1},{4,2},{6,3},{8,4},{10,5},{12,6},{14,7},{16,8},{18,9},{... | collective-permute-start | bytes 786440 | tf_op jit(solution)/shard_map/ppermute | solution.py:809
  (11 other events, 230.2 us)
Sparse Core Ops, SparseCore 0:
  10.2 70.9 all-gather.2
  83.4 65.0 all-gather.4
  213.5 102.1 reduce-scatter.1

commit v5 on v4

--- a/solution.py
+++ b/solution.py
@@ -737,7 +737,6 @@
     gain_len = norm_gain.shape[0]
 
     hid = gather_tokens(hidden_in)
-    gout = gather_tokens(grad_out)
     to_shard = [(i, 2 * (i % shards) + i // shards) for i in range(2 * shards)]
     mine = lax.ppermute(in_proj, both, to_shard)
     other = swap_row(mine)
@@ -763,6 +762,7 @@
     normed, x, z, conv, keep, send = front(
         doc_starts, own, hid, gain_whole, weight, conv_w, conv_b, x_proj
     )
+    gout = gather_tokens(gate([grad_out], [keep])[0])
     low = sum_pieces(keep, send, F32, []).astype(BF)
     near, far = spread_pieces(low)
     gated, y, states, mixed, last, stats = forward_scan(

time: 375 us -> 371 us (0.989)
  starting transfers between devices: 82.7 us -> 76.3 us
    ppermute x38, starting transfers between devices: 58.5 us -> 50.4 us  [cross(): return lax.ppermute(v, 'seq', [(s, s ^ bits) for s in range(16)])]
    ppermute x1, waiting for transfers between devices: 14 us -> 8.63 us  [channel_plan(): in_share = lax.ppermute(in_half, both, to_owner).astype(F32)]
  transfers between devices with their start and end apart: 52 -> 52, of which waited for: 28 -> 29; matrix products, arithmetic and copies ran while one was open for 9% -> 10% of each run, Pallas kernels for 12% -> 9%
where the time goes in v5:
time: 371 us; the launch traced here: 370 us
  waiting for transfers between devices  155 us (42%)
  Pallas kernels  83.8 us (23%)
  starting transfers between devices  76.3 us (21%)
  other arithmetic  28.5 us (8%)
  between operations  14.3 us (4%)
  local copies, waits for them, and re-layouts  6.91 us (2%)
  matrix products  5.07 us (1%)
    ppermute x38, waiting for transfers between devices, cross(): return lax.ppermute(v, 'seq', [(s, s ^ bits) for s in range(16)])  96.3 us
    ppermute x38, starting transfers between devices, cross(): return lax.ppermute(v, 'seq', [(s, s ^ bits) for s in range(16)])  50.4 us
    pallas_call x1, Pallas kernels, backward_scan(): pl.pallas_call(partial(backward_kernel, top=top), grid_spec=pltpu.Prefetc...  39.1 us
    all_gather x2, waiting for transfers between devices, gather_tokens(): return lax.all_gather(v, 'seq', axis=1, tiled=True)  36.6 us
    pallas_call x1, Pallas kernels, forward_scan(): pl.pallas_call(forward_kernel, grid_spec=pltpu.PrefetchScalarGridSpec(num...  21.9 us
    ppermute x7, waiting for transfers between devices, swap_row(): return lax.ppermute(v, 'row', [(0, 1), (1, 0)])  12.7 us
    pallas_call x1, Pallas kernels, tail(): pl.pallas_call(tail_kernel, grid_spec=pltpu.PrefetchScalarGridSpec(num_sc...  12.5 us
    pallas_call x1, Pallas kernels, front(): pl.pallas_call(front_kernel, grid_spec=pltpu.PrefetchScalarGridSpec(num_s...  10.4 us
  transfers between devices with their start and end apart: 52, of which 29 were waited for; matrix products, arithmetic and copies ran while one was open for 10% of the time, Pallas kernels for 9%

profile of v5, /device:TPU:18, one launch (start us, length us, event | category | flops | bytes accessed | tf_op | source)
XLA Modules:
  0.0 369.8 jit_solution(6539196017345779990)
XLA Ops:
  10.2 2.2 collective-permute-done.2
  14.8 2.3 collective-permute-start
  18.0 4.1 %collective-permute-done.4 = f32[32,32]{1,0:T(8,128)S(1)} collective-permute-done((f32[32,32]{1,0:T(8,128)S(1)}, f32[32,32]{1,0:T(8,128)S(1)}, u32[]{:S(2)}, u32[]{:S(2)}) %collective-permute-start.4) | collective-permute-done | bytes 4128 | tf_op jit(solution)/shard_map/ppermute | solution.py:653
  22.1 4.7 %collective-permute-start.5 = (f32[32,32]{1,0:T(8,128)S(1)}, f32[32,32]{1,0:T(8,128)S(1)}, u32[]{:S(2)}, u32[]{:S(2)}) collective-permute-start(f32[32,32]{1,0:T(8,128)S(1)} %add.320), channel_id=1, source_target_pairs={{0,8},{2,10},{4,12},{6,14},{8,0},{10,2},{12,4},{14,6},{16,24},{18,... | collective-permute-start | bytes 12296 | tf_op jit(solution)/shard_map/ppermute | solution.py:653
  28.4 6.5 %all-to-all-start = ((bf16[64,16,128]{2,0,1:T(8,128)(2,1)}), bf16[64,16,128]{2,0,1:T(8,128)(2,1)S(1)}, u32[]{:S(2)}, u32[]{:S(2)}) async-start(bf16[64,16,128]{2,0,1:T(8,128)(2,1)} %copy_bitcast_fusion.1), calls=%async_computation | async-start | bytes 524288 | tf_op jit(solution)/shard_map/all_to_all | solution.py:746
  40.7 1.8 copy.112.refs_0_
  44.3 36.6 %all-gather.3.cloned.1.call-done.hid = bf16[3,1024,1024]{2,1,0:T(8,128)(2,1)} async-done(((bf16[3,64,1024]{2,1,0:T(8,128)(2,1)}), bf16[3,1024,1024]{2,1,0:T(8,128)(2,1)}) %all-gather.3.cloned.1.call-update) | async-done | bytes 6291472 | tf_op jit(solution)/shard_map/all_gather | solution.py:683
  80.9 10.4 %front.1 = (bf16[3,1024,1024]{2,1,0:T(8,128)(2,1)}, bf16[3,1024,128]{2,1,0:T(8,128)(2,1)}, f32[3,1024,128]{2,1,0:T(8,128)}, bf16[3,1024,128]{2,1,0:T(8,128)(2,1)...) custom-call(s32[3,8]{1,0:T(4,128)S(1)} %copy-done.2, s32[3]{0:T(128)S(1)} %pad_add_fusion.own, ...), custom_call_target="tpu_custom_call" | custom-call | flops 1 | bytes 1 | tf_op jit(solution)/shard_map/front/pallas_call | solution.py:165
  91.6 2.0 collective-permute-done.8
  95.4 14.0 %collective-permute-done.9 = f32[4,3,64,96]{3,2,1,0:T(8,128)S(1)} collective-permute-done((f32[4,3,64,96]{3,2,1,0:T(8,128)S(1)}, f32[4,3,64,96]{3,2,1,0:T(8,128)S(1)}, u32[]{:S(2)}, u32[]{:S(2)}) %collective-permute-start.9) | collective-permute-done | bytes 294944 | tf_op jit(solution)/shard_map/ppermute | solution.py:653
  111.1 2.8 collective-permute-start.11
  113.9 3.3 collective-permute-done.10
  117.3 5.9 %collective-permute-done.12 = f32[3,64,96]{2,1,0:T(8,128)S(1)} collective-permute-done((f32[3,64,96]{2,1,0:T(8,128)S(1)}, f32[3,64,96]{2,1,0:T(8,128)S(1)}, u32[]{:S(2)}, u32[]{:S(2)}) %collective-permute-start.12) | collective-permute-done | bytes 73760 | tf_op jit(solution)/shard_map/ppermute | solution.py:653
  124.7 3.8 %collective-permute-start.14 = (bf16[3,64,96]{2,1,0:T(8,128)(2,1)S(1)}, bf16[3,64,96]{2,1,0:T(8,128)(2,1)S(1)}, u32[]{:S(2)}, u32[]{:S(2)}) collective-permute-start(bf16[3,64,96]{2,1,0:T(8,128)(2,1)S(1)} %fusion.29), channel_id=1, source_target_pairs={{0,16},{2,18},{4,20},{6,22},{8,24},{10,26},{12,28},{14,30},{16,0},... | collective-permute-start | bytes 110600 | tf_op jit(solution)/shard_map/ppermute | solution.py:653
  128.8 3.7 collective-permute-done.14
  133.5 2.3 collective-permute-start.16
  135.7 8.8 %collective-permute-done.16 = bf16[4,3,64,96]{3,2,1,0:T(8,128)(2,1)S(1)} collective-permute-done((bf16[4,3,64,96]{3,2,1,0:T(8,128)(2,1)S(1)}, bf16[4,3,64,96]{3,2,1,0:T(8,128)(2,1)S(1)}, u32[]{:S(2)}, u32[]{:S(2)}) %collective-permute-start.16) | collective-permute-done | bytes 147488 | tf_op jit(solution)/shard_map/ppermute | solution.py:653
  146.4 21.9 %forward_scan.1 = (bf16[3,1024,128]{2,1,0:T(8,128)(2,1)}, bf16[3,1024,128]{2,1,0:T(8,128)(2,1)}, f32[3,1024,16,128]{3,2,1,0:T(8,128)}, bf16[3,1024,1024]{2,1,0:T...) custom-call(s32[3,8]{1,0:T(4,128)S(1)} %copy-done.2, s32[3]{0:T(128)S(1)} %pad_add_fusion.own, ...), custom_call_target="tpu_custom_call" | custom-call | flops 1 | bytes 1 | tf_op jit(solution)/shard_map/forward_scan/pallas_call | solution.py:324
  168.3 39.1 %backward_scan.1 = (bf16[3,1024,128]{2,1,0:T(8,128)(2,1)}, f32[3,1024,128]{2,1,0:T(8,128)}, f32[2,4,3,64,96]{4,3,2,1,0:T(8,128)S(1)}, f32[2,4,3,64,96]{4,3,2,1,0...) custom-call(s32[3,8]{1,0:T(4,128)S(1)} %copy-done.2, ...), custom_call_target="tpu_custom_call" | custom-call | flops 1 | bytes 1 | tf_op jit(solution)/shard_map/backward_scan/pallas_call | solution.py:492
  207.6 2.2 collective-permute-done.18
  209.9 1.8 collective-permute-start.19
  211.7 5.2 %collective-permute-done.19 = bf16[4,3,64,96]{3,2,1,0:T(8,128)(2,1)S(1)} collective-permute-done((bf16[4,3,64,96]{3,2,1,0:T(8,128)(2,1)S(1)}, bf16[4,3,64,96]{3,2,1,0:T(8,128)(2,1)S(1)}, u32[]{:S(2)}, u32[]{:S(2)}) %collective-permute-start.19) | collective-permute-done | bytes 147488 | tf_op jit(solution)/shard_map/ppermute | solution.py:653
  217.0 3.6 collective-permute-start.20
  220.8 2.1 collective-permute-start.21
  223.1 2.9 collective-permute-done.22
  227.7 2.8 collective-permute-start.24
  230.5 5.1 %fusion.43 = f32[1024,128,1]{1,0,2:T(8,128)S(1)} fusion(bf16[3,1024,1024]{2,1,0:T(8,128)(2,1)} %all-gather.5.cloned.1.call-done.gout, bf16[3,1024,128]{2,1,0:T(8,128)(2,1)S(1)} %get-tuple-element.98), kind=kOutput, calls=%fused_computation.117 | convolution fusion | flops 805306368 | bytes 7602176 | tf_op jit(solution)/shard_map/rtd,rtc->dc/dot_general | solution.py:779
  235.6 1.8 collective-permute-start.26
  239.0 2.3 collective-permute-done.26
  241.5 2.3 collective-permute-done.28
  244.6 12.5 %tail.1 = (bf16[2,4,3,64,1024]{4,3,2,1,0:T(8,128)(2,1)}, bf16[2,4,3,64,1024]{4,3,2,1,0:T(8,128)(2,1)}, f32[256,1024]{1,0:T(8,128)S(1)}, f32[128,96]{1,0:T(8,128)S(1)}, f32[8,128]{1,0:T(8,128)S(1)}) custom-call(s32[3,8]{1,0:T(4,128)S(1)} %copy-done.2, s32[3]{0:T(128)S(1)} %pad_add_fusion.own, bf16[2,4,3,64,96]{4,3,2,1,0:T(8,128)(2,1)S(1)} %pad_maximum_fusion.2.near, ...), custom_call_target="tpu_custom_call" | custom-call | flops 1 | bytes 1 | tf_op jit(solution)/shard_map/tail/pallas_call | solution.py:605
  258.5 4.6 %collective-permute-done.29.refs_0_ = bf16[2,4,3,64,1024]{4,3,2,1,0:T(8,128)(2,1)} collective-permute-done((bf16[2,4,3,64,1024]{4,3,2,1,0:T(8,128)(2,1)}, bf16[2,4,3,64,1024]{4,3,2,1,0:T(8,128)(2,1)}, u32[]{:S(2)}, u32[]{:S(2)}) %collective-permute-start.29) | collective-permute-done | bytes 3145760 | tf_op jit(solution)/shard_map/ppermute | solution.py:653
  263.1 2.2 fusion.17
  265.9 3.4 collective-permute-start.32
  269.3 2.6 fusion
  272.4 21.1 %collective-permute-done.31.refs_6_.refs_1_ = bf16[2,1,64,1024]{3,2,1,0:T(8,128)(2,1)S(1)} collective-permute-done((bf16[2,1,64,1024]{3,2,1,0:T(8,128)(2,1)S(1)}, bf16[2,1,64,1024]{3,2,1,0:T(8,128)(2,1)S(1)}, u32[]{:S(2)}, u32[]{:S(2)}) %collective-permute-start.31) | collective-permute-done | bytes 262176 | tf_op jit(solution)/shard_map/ppermute | solution.py:653
  301.6 5.4 %collective-permute-done.34 = bf16[128,1024]{1,0:T(8,128)(2,1)S(1)} collective-permute-done((bf16[128,1024]{1,0:T(8,128)(2,1)S(1)}, bf16[128,1024]{1,0:T(8,128)(2,1)S(1)}, u32[]{:S(2)}, u32[]{:S(2)}) %collective-permute-start.34) | collective-permute-done | bytes 262176 | tf_op jit(solution)/shard_map/ppermute | solution.py:657
  307.2 2.6 fusion.9
  313.0 4.4 %collective-permute-start.39 = (bf16[2,64,1024]{2,1,0:T(8,128)(2,1)}, bf16[2,64,1024]{2,1,0:T(8,128)(2,1)S(1)}, u32[]{:S(2)}, u32[]{:S(2)}) collective-permute-start(bf16[2,64,1024]{2,1,0:T(8,128)(2,1)} %get-tuple-element.132), channel_id=1, source_target_pairs={{0,16},{2,18},{4,20},{6,22},{8,24},{10,26},{12,28},{14,30},{16,0},... | collective-permute-start | bytes 786440 | tf_op jit(solution)/shard_map/ppermute | solution.py:653
  317.9 1.9 collective-permute-done.38.refs_2_.refs_0_
  322.9 5.4 %all-to-all-start.1 = ((bf16[16,32,128]{2,1,0:T(8,128)(2,1)}), bf16[16,32,128]{2,1,0:T(8,128)(2,1)}, u32[]{:S(2)}, u32[]{:S(2)}) async-start(bf16[16,32,128]{2,1,0:T(8,128)(2,1)} %get-tuple-element.128), calls=%async_computation.2 | async-start | bytes 262144 | tf_op jit(solution)/shard_map/all_to_all | solution.py:804
  328.3 6.7 %collective-permute-done.40.refs_2_ = bf16[2,64,1024]{2,1,0:T(8,128)(2,1)S(1)} collective-permute-done((bf16[2,64,1024]{2,1,0:T(8,128)(2,1)}, bf16[2,64,1024]{2,1,0:T(8,128)(2,1)S(1)}, u32[]{:S(2)}, u32[]{:S(2)}) %collective-permute-start.40) | collective-permute-done | bytes 262176 | tf_op jit(solution)/shard_map/ppermute | solution.py:653
  335.1 2.5 collective-permute-done.39.refs_1_
  339.3 4.2 %collective-permute-start.44 = (f32[32,32]{1,0:T(8,128)S(1)}, f32[32,32]{1,0:T(8,128)S(1)}, u32[]{:S(2)}, u32[]{:S(2)}) collective-permute-start(f32[32,32]{1,0:T(8,128)S(1)} %get-tuple-element.126), channel_id=1, source_target_pairs={{0,16},{2,18},{4,20},{6,22},{8,24},{10,26},{12,28},{14,30},{16,0},... | collective-permute-start | bytes 12296 | tf_op jit(solution)/shard_map/ppermute | solution.py:653
  343.5 1.9 collective-permute-start.46
  348.2 2.5 fusion.6
  352.9 8.6 %collective-permute-done.46 = bf16[128,1024]{1,0:T(8,128)(2,1)} collective-permute-done((bf16[128,1024]{1,0:T(8,128)(2,1)S(1)}, bf16[128,1024]{1,0:T(8,128)(2,1)}, u32[]{:S(2)}, u32[]{:S(2)}) %collective-permute-start.46) | collective-permute-done | bytes 262176 | tf_op jit(solution)/shard_map/ppermute | solution.py:809
  361.5 1.8 convert_element_type.488
  (170 shorter events, 53.2 us)
Async XLA Ops:
  7.2 73.7 %all-gather.3.cloned.1.call-start = ((), (), s32[]{:S(2)}) async-start(), calls=%async_computation.3 | async-start | bytes 6684672 | tf_op jit(solution)/shard_map/all_gather | solution.py:683
  8.6 3.8 %collective-permute-start.2 = (f32[32,32]{1,0:T(8,128)S(1)}, f32[32,32]{1,0:T(8,128)S(1)}, u32[]{:S(2)}, u32[]{:S(2)}) collective-permute-start(f32[32,32]{1,0:T(8,128)S(1)} %dynamic_update_slice.5), channel_id=1, source_target_pairs={{0,1},{1,0},{2,3},{3,2},{4,5},{5,4},{6,7},{7,6},{8,9},{9,8},{10,11... | collective-permute-start | bytes 12296 | tf_op jit(solution)/shard_map/ppermute | solution.py:657
  13.1 3.9 %collective-permute-start.3 = (f32[32,32]{1,0:T(8,128)S(1)}, f32[32,32]{1,0:T(8,128)S(1)}, u32[]{:S(2)}, u32[]{:S(2)}) collective-permute-start(f32[32,32]{1,0:T(8,128)S(1)} %add.318), channel_id=1, source_target_pairs={{0,2},{2,0},{4,6},{6,4},{8,10},{10,8},{12,14},{14,12},{16,18},{18,... | collective-permute-start | bytes 12296 | tf_op jit(solution)/shard_map/ppermute | solution.py:653
  13.2 13.5 %collective-permute-start.7 = (bf16[32,2048]{1,0:T(8,128)(2,1)}, bf16[32,2048]{1,0:T(8,128)(2,1)S(1)}, u32[]{:S(2)}, u32[]{:S(2)}) collective-permute-start(bf16[32,2048]{1,0:T(8,128)(2,1)} %param.18), channel_id=1, source_target_pairs={{0,1},{1,0},{2,3},{3,2},{4,5},{5,4},{6,7},{7,6},{8,9},{9,8},{10,11... | collective-permute-start | bytes 393224 | tf_op jit(solution)/shard_map/ppermute | solution.py:657
  14.8 20.3 %collective-permute-start = (bf16[128,1024]{1,0:T(8,128)(2,1)}, bf16[128,1024]{1,0:T(8,128)(2,1)S(1)}, u32[]{:S(2)}, u32[]{:S(2)}) collective-permute-start(bf16[128,1024]{1,0:T(8,128)(2,1)} %param.17), channel_id=1, source_target_pairs={{0,0},{1,2},{2,4},{3,6},{4,8},{5,10},{6,12},{7,14},{8,16},{9,18},{... | collective-permute-start | bytes 786440 | tf_op jit(solution)/shard_map/ppermute | solution.py:741
  17.1 5.0 %collective-permute-start.4 = (f32[32,32]{1,0:T(8,128)S(1)}, f32[32,32]{1,0:T(8,128)S(1)}, u32[]{:S(2)}, u32[]{:S(2)}) collective-permute-start(f32[32,32]{1,0:T(8,128)S(1)} %add.319), channel_id=1, source_target_pairs={{0,4},{2,6},{4,0},{6,2},{8,12},{10,14},{12,8},{14,10},{16,20},{18,... | collective-permute-start | bytes 12296 | tf_op jit(solution)/shard_map/ppermute | solution.py:653
  22.1 14.8 %collective-permute-start.5 = (f32[32,32]{1,0:T(8,128)S(1)}, f32[32,32]{1,0:T(8,128)S(1)}, u32[]{:S(2)}, u32[]{:S(2)}) collective-permute-start(f32[32,32]{1,0:T(8,128)S(1)} %add.320), channel_id=1, source_target_pairs={{0,8},{2,10},{4,12},{6,14},{8,0},{10,2},{12,4},{14,6},{16,24},{18,... | collective-permute-start | bytes 12296 | tf_op jit(solution)/shard_map/ppermute | solution.py:653
  28.4 15.8 %all-to-all-start = ((bf16[64,16,128]{2,0,1:T(8,128)(2,1)}), bf16[64,16,128]{2,0,1:T(8,128)(2,1)S(1)}, u32[]{:S(2)}, u32[]{:S(2)}) async-start(bf16[64,16,128]{2,0,1:T(8,128)(2,1)} %copy_bitcast_fusion.1), calls=%async_computation | async-start | bytes 524288 | tf_op jit(solution)/shard_map/all_to_all | solution.py:746
  35.0 133.3 %all-gather.5.cloned.1.call-start = ((), (), s32[]{:S(2)}) async-start(), calls=%async_computation.5 | async-start | bytes 6684672 | tf_op jit(solution)/shard_map/all_gather | solution.py:683
  35.0 9.1 %collective-permute-start.1 = (bf16[128,1024]{1,0:T(8,128)(2,1)S(1)}, bf16[128,1024]{1,0:T(8,128)(2,1)S(1)}, u32[]{:S(2)}, u32[]{:S(2)}) collective-permute-start(bf16[128,1024]{1,0:T(8,128)(2,1)S(1)} %collective-permute-done), channel_id=1, source_target_pairs={{0,1},{1,0},{2,3},{3,2},{4,5},{5,4},{6,7},{7,6},{8,9},{9,8},{10,11... | collective-permute-start | bytes 786440 | tf_op jit(solution)/shard_map/ppermute | solution.py:657
  36.9 6.0 %collective-permute-start.6 = (f32[32,32]{1,0:T(8,128)S(1)}, f32[32,32]{1,0:T(8,128)S(1)}, u32[]{:S(2)}, u32[]{:S(2)}) collective-permute-start(f32[32,32]{1,0:T(8,128)S(1)} %add.321), channel_id=1, source_target_pairs={{0,16},{2,18},{4,20},{6,22},{8,24},{10,26},{12,28},{14,30},{16,0},... | collective-permute-start | bytes 12296 | tf_op jit(solution)/shard_map/ppermute | solution.py:653
  91.3 256.9 %reduce-scatter.2.cloned.1.call-start = ((), (), s32[]{:S(2)}) async-start(), calls=%async_computation.4 | async-start | bytes 6684672 | tf_op jit(solution)/shard_map/reduce_scatter | solution.py:771
  93.8 15.6 %collective-permute-start.9 = (f32[4,3,64,96]{3,2,1,0:T(8,128)S(1)}, f32[4,3,64,96]{3,2,1,0:T(8,128)S(1)}, u32[]{:S(2)}, u32[]{:S(2)}) collective-permute-start(f32[4,3,64,96]{3,2,1,0:T(8,128)S(1)} %slice_bitcast_fusion.1), channel_id=1, source_target_pairs={{0,4},{2,6},{4,0},{6,2},{8,12},{10,14},{12,8},{14,10},{16,20},{18,... | collective-permute-start | bytes 884744 | tf_op jit(solution)/shard_map/ppermute | solution.py:653
  109.5 7.8 %collective-permute-start.10 = (f32[3,64,96]{2,1,0:T(8,128)S(1)}, f32[3,64,96]{2,1,0:T(8,128)S(1)}, u32[]{:S(2)}, u32[]{:S(2)}) collective-permute-start(f32[3,64,96]{2,1,0:T(8,128)S(1)} %get-tuple-element.141), channel_id=1, source_target_pairs={{0,8},{2,10},{4,12},{6,14},{8,0},{10,2},{12,4},{14,6},{16,24},{18,... | collective-permute-start | bytes 221192 | tf_op jit(solution)/shard_map/ppermute | solution.py:653
  109.6 13.6 %collective-permute-start.12 = (f32[3,64,96]{2,1,0:T(8,128)S(1)}, f32[3,64,96]{2,1,0:T(8,128)S(1)}, u32[]{:S(2)}, u32[]{:S(2)}) collective-permute-start(f32[3,64,96]{2,1,0:T(8,128)S(1)} %get-tuple-element.142), channel_id=1, source_target_pairs={{0,24},{2,26},{4,28},{6,30},{8,16},{10,18},{12,20},{14,22},{16,8},... | collective-permute-start | bytes 221192 | tf_op jit(solution)/shard_map/ppermute | solution.py:653
  111.1 12.7 %collective-permute-start.11 = (f32[3,64,96]{2,1,0:T(8,128)S(1)}, f32[3,64,96]{2,1,0:T(8,128)S(1)}, u32[]{:S(2)}, u32[]{:S(2)}) collective-permute-start(f32[3,64,96]{2,1,0:T(8,128)S(1)} %get-tuple-element.143), channel_id=1, source_target_pairs={{0,16},{2,18},{4,20},{6,22},{8,24},{10,26},{12,28},{14,30},{16,0},... | collective-permute-start | bytes 221192 | tf_op jit(solution)/shard_map/ppermute | solution.py:653
  123.9 4.9 %collective-permute-start.15 = (bf16[3,64,96]{2,1,0:T(8,128)(2,1)S(1)}, bf16[3,64,96]{2,1,0:T(8,128)(2,1)S(1)}, u32[]{:S(2)}, u32[]{:S(2)}) collective-permute-start(bf16[3,64,96]{2,1,0:T(8,128)(2,1)S(1)} %fusion.29), channel_id=1, source_target_pairs={{0,24},{2,26},{4,28},{6,30},{8,16},{10,18},{12,20},{14,22},{16,8},... | collective-permute-start | bytes 110600 | tf_op jit(solution)/shard_map/ppermute | solution.py:653
  124.7 7.7 %collective-permute-start.14 = (bf16[3,64,96]{2,1,0:T(8,128)(2,1)S(1)}, bf16[3,64,96]{2,1,0:T(8,128)(2,1)S(1)}, u32[]{:S(2)}, u32[]{:S(2)}) collective-permute-start(bf16[3,64,96]{2,1,0:T(8,128)(2,1)S(1)} %fusion.29), channel_id=1, source_target_pairs={{0,16},{2,18},{4,20},{6,22},{8,24},{10,26},{12,28},{14,30},{16,0},... | collective-permute-start | bytes 110600 | tf_op jit(solution)/shard_map/ppermute | solution.py:653
  128.5 4.9 %collective-permute-start.13 = (bf16[3,64,96]{2,1,0:T(8,128)(2,1)S(1)}, bf16[3,64,96]{2,1,0:T(8,128)(2,1)S(1)}, u32[]{:S(2)}, u32[]{:S(2)}) collective-permute-start(bf16[3,64,96]{2,1,0:T(8,128)(2,1)S(1)} %fusion.29), channel_id=1, source_target_pairs={{0,8},{2,10},{4,12},{6,14},{8,0},{10,2},{12,4},{14,6},{16,24},{18,... | collective-permute-start | bytes 110600 | tf_op jit(solution)/shard_map/ppermute | solution.py:653
  133.5 11.0 %collective-permute-start.16 = (bf16[4,3,64,96]{3,2,1,0:T(8,128)(2,1)S(1)}, bf16[4,3,64,96]{3,2,1,0:T(8,128)(2,1)S(1)}, u32[]{:S(2)}, u32[]{:S(2)}) collective-permute-start(bf16[4,3,64,96]{3,2,1,0:T(8,128)(2,1)S(1)} %get-tuple-element.152), channel_id=1, source_target_pairs={{0,4},{2,6},{4,0},{6,2},{8,12},{10,14},{12,8},{14,10},{16,20},{18,... | collective-permute-start | bytes 442376 | tf_op jit(solution)/shard_map/ppermute | solution.py:653
  209.9 7.0 %collective-permute-start.19 = (bf16[4,3,64,96]{3,2,1,0:T(8,128)(2,1)S(1)}, bf16[4,3,64,96]{3,2,1,0:T(8,128)(2,1)S(1)}, u32[]{:S(2)}, u32[]{:S(2)}) collective-permute-start(bf16[4,3,64,96]{3,2,1,0:T(8,128)(2,1)S(1)} %fusion.21), channel_id=1, source_target_pairs={{0,4},{2,6},{4,0},{6,2},{8,12},{10,14},{12,8},{14,10},{16,20},{18,... | collective-permute-start | bytes 442376 | tf_op jit(solution)/shard_map/ppermute | solution.py:653
  217.0 6.1 %collective-permute-start.20 = (bf16[3,64,96]{2,1,0:T(8,128)(2,1)S(1)}, bf16[3,64,96]{2,1,0:T(8,128)(2,1)S(1)}, u32[]{:S(2)}, u32[]{:S(2)}) collective-permute-start(bf16[3,64,96]{2,1,0:T(8,128)(2,1)S(1)} %get-tuple-element.148), channel_id=1, source_target_pairs={{0,8},{2,10},{4,12},{6,14},{8,0},{10,2},{12,4},{14,6},{16,24},{18,... | collective-permute-start | bytes 110600 | tf_op jit(solution)/shard_map/ppermute | solution.py:653
  220.5 5.5 %collective-permute-start.22 = (bf16[3,64,96]{2,1,0:T(8,128)(2,1)S(1)}, bf16[3,64,96]{2,1,0:T(8,128)(2,1)S(1)}, u32[]{:S(2)}, u32[]{:S(2)}) collective-permute-start(bf16[3,64,96]{2,1,0:T(8,128)(2,1)S(1)} %get-tuple-element.149), channel_id=1, source_target_pairs={{0,24},{2,26},{4,28},{6,30},{8,16},{10,18},{12,20},{14,22},{16,8},... | collective-permute-start | bytes 110600 | tf_op jit(solution)/shard_map/ppermute | solution.py:653
  220.8 5.2 %collective-permute-start.21 = (bf16[3,64,96]{2,1,0:T(8,128)(2,1)S(1)}, bf16[3,64,96]{2,1,0:T(8,128)(2,1)S(1)}, u32[]{:S(2)}, u32[]{:S(2)}) collective-permute-start(bf16[3,64,96]{2,1,0:T(8,128)(2,1)S(1)} %get-tuple-element.150), channel_id=1, source_target_pairs={{0,16},{2,18},{4,20},{6,22},{8,24},{10,26},{12,28},{14,30},{16,0},... | collective-permute-start | bytes 110600 | tf_op jit(solution)/shard_map/ppermute | solution.py:653
  226.0 9.5 %collective-permute-start.25 = (bf16[3,64,96]{2,1,0:T(8,128)(2,1)S(1)}, bf16[3,64,96]{2,1,0:T(8,128)(2,1)S(1)}, u32[]{:S(2)}, u32[]{:S(2)}) collective-permute-start(bf16[3,64,96]{2,1,0:T(8,128)(2,1)S(1)} %fusion.25), channel_id=1, source_target_pairs={{0,24},{2,26},{4,28},{6,30},{8,16},{10,18},{12,20},{14,22},{16,8},... | collective-permute-start | bytes 110600 | tf_op jit(solution)/shard_map/ppermute | solution.py:653
  227.7 7.8 %collective-permute-start.24 = (bf16[3,64,96]{2,1,0:T(8,128)(2,1)S(1)}, bf16[3,64,96]{2,1,0:T(8,128)(2,1)S(1)}, u32[]{:S(2)}, u32[]{:S(2)}) collective-permute-start(bf16[3,64,96]{2,1,0:T(8,128)(2,1)S(1)} %fusion.25), channel_id=1, source_target_pairs={{0,16},{2,18},{4,20},{6,22},{8,24},{10,26},{12,28},{14,30},{16,0},... | collective-permute-start | bytes 110600 | tf_op jit(solution)/shard_map/ppermute | solution.py:653
  230.4 5.1 %collective-permute-start.23 = (bf16[3,64,96]{2,1,0:T(8,128)(2,1)S(1)}, bf16[3,64,96]{2,1,0:T(8,128)(2,1)S(1)}, u32[]{:S(2)}, u32[]{:S(2)}) collective-permute-start(bf16[3,64,96]{2,1,0:T(8,128)(2,1)S(1)} %fusion.25), channel_id=1, source_target_pairs={{0,8},{2,10},{4,12},{6,14},{8,0},{10,2},{12,4},{14,6},{16,24},{18,... | collective-permute-start | bytes 110600 | tf_op jit(solution)/shard_map/ppermute | solution.py:653
  235.6 5.7 %collective-permute-start.26 = (bf16[4,3,64,96]{3,2,1,0:T(8,128)(2,1)S(1)}, bf16[4,3,64,96]{3,2,1,0:T(8,128)(2,1)S(1)}, u32[]{:S(2)}, u32[]{:S(2)}) collective-permute-start(bf16[4,3,64,96]{3,2,1,0:T(8,128)(2,1)S(1)} %get-tuple-element.147), channel_id=1, source_target_pairs={{0,4},{2,6},{4,0},{6,2},{8,12},{10,14},{12,8},{14,10},{16,20},{18,... | collective-permute-start | bytes 442376 | tf_op jit(solution)/shard_map/ppermute | solution.py:653
  237.4 6.4 %collective-permute-start.28 = (f32[16,32,128]{2,1,0:T(8,128)S(1)}, f32[16,32,128]{2,1,0:T(8,128)S(1)}, u32[]{:S(2)}, u32[]{:S(2)}) collective-permute-start(f32[16,32,128]{2,1,0:T(8,128)S(1)} %select_bitcast_fusion), channel_id=1, source_target_pairs={{0,1},{1,0},{2,3},{3,2},{4,5},{5,4},{6,7},{7,6},{8,9},{9,8},{10,11... | collective-permute-start | bytes 786440 | tf_op jit(solution)/shard_map/ppermute | solution.py:657
  241.4 3.1 collective-permute-start.27
  257.1 6.0 %collective-permute-start.29 = (bf16[2,4,3,64,1024]{4,3,2,1,0:T(8,128)(2,1)}, bf16[2,4,3,64,1024]{4,3,2,1,0:T(8,128)(2,1)}, u32[]{:S(2)}, u32[]{:S(2)}) collective-permute-start(bf16[2,4,3,64,1024]{4,3,2,1,0:T(8,128)(2,1)} %get-tuple-element.100), channel_id=1, source_target_pairs={{0,2},{2,0},{4,6},{6,4},{8,10},{10,8},{12,14},{14,12},{16,18},{18,... | collective-permute-start | bytes 9437192 | tf_op jit(solution)/shard_map/ppermute | solution.py:653
  265.2 41.9 %collective-permute-start.33 = (bf16[2,1,64,1024]{3,2,1,0:T(8,128)(2,1)}, bf16[2,1,64,1024]{3,2,1,0:T(8,128)(2,1)S(1)}, u32[]{:S(2)}, u32[]{:S(2)}) collective-permute-start(bf16[2,1,64,1024]{3,2,1,0:T(8,128)(2,1)} %get-tuple-element.134), channel_id=1, source_target_pairs={{0,24},{2,26},{4,28},{6,30},{8,16},{10,18},{12,20},{14,22},{16,8},... | collective-permute-start | bytes 786440 | tf_op jit(solution)/shard_map/ppermute | solution.py:653
  265.9 41.3 %collective-permute-start.32 = (bf16[2,1,64,1024]{3,2,1,0:T(8,128)(2,1)}, bf16[2,1,64,1024]{3,2,1,0:T(8,128)(2,1)S(1)}, u32[]{:S(2)}, u32[]{:S(2)}) collective-permute-start(bf16[2,1,64,1024]{3,2,1,0:T(8,128)(2,1)} %get-tuple-element.135), channel_id=1, source_target_pairs={{0,16},{2,18},{4,20},{6,22},{8,24},{10,26},{12,28},{14,30},{16,0},... | collective-permute-start | bytes 786440 | tf_op jit(solution)/shard_map/ppermute | solution.py:653
  269.3 24.2 %collective-permute-start.31 = (bf16[2,1,64,1024]{3,2,1,0:T(8,128)(2,1)S(1)}, bf16[2,1,64,1024]{3,2,1,0:T(8,128)(2,1)S(1)}, u32[]{:S(2)}, u32[]{:S(2)}) collective-permute-start(bf16[2,1,64,1024]{3,2,1,0:T(8,128)(2,1)S(1)} %get-tuple-element.136), channel_id=1, source_target_pairs={{0,8},{2,10},{4,12},{6,14},{8,0},{10,2},{12,4},{14,6},{16,24},{18,... | collective-permute-start | bytes 786440 | tf_op jit(solution)/shard_map/ppermute | solution.py:653
  271.9 35.2 %collective-permute-start.30 = (bf16[4,2,64,1024]{3,2,1,0:T(8,128)(2,1)}, bf16[4,2,64,1024]{3,2,1,0:T(8,128)(2,1)S(1)}, u32[]{:S(2)}, u32[]{:S(2)}) collective-permute-start(bf16[4,2,64,1024]{3,2,1,0:T(8,128)(2,1)} %fusion), channel_id=1, source_target_pairs={{0,4},{2,6},{4,0},{6,2},{8,12},{10,14},{12,8},{14,10},{16,20},{18,... | collective-permute-start | bytes 3145736 | tf_op jit(solution)/shard_map/ppermute | solution.py:653
  293.7 3.8 %collective-permute-start.36 = (f32[32,32]{1,0:T(8,128)S(1)}, f32[32,32]{1,0:T(8,128)S(1)}, u32[]{:S(2)}, u32[]{:S(2)}) collective-permute-start(f32[32,32]{1,0:T(8,128)S(1)} %div.40), channel_id=1, source_target_pairs={{0,1},{1,0},{2,3},{3,2},{4,5},{5,4},{6,7},{7,6},{8,9},{9,8},{10,11... | collective-permute-start | bytes 12296 | tf_op jit(solution)/shard_map/ppermute | solution.py:657
  295.4 4.9 %collective-permute-start.35 = (f32[200,128]{1,0:T(8,128)S(1)}, f32[200,128]{1,0:T(8,128)S(1)}, u32[]{:S(2)}, u32[]{:S(2)}) collective-permute-start(f32[200,128]{1,0:T(8,128)S(1)} %bitcast_dynamic-update-slice_fusion), channel_id=1, source_target_pairs={{0,1},{1,0},{2,3},{3,2},{4,5},{5,4},{6,7},{7,6},{8,9},{9,8},{10,11... | collective-permute-start | bytes 307208 | tf_op jit(solution)/shard_map/ppermute | solution.py:657
  298.7 8.4 %collective-permute-start.34 = (bf16[128,1024]{1,0:T(8,128)(2,1)S(1)}, bf16[128,1024]{1,0:T(8,128)(2,1)S(1)}, u32[]{:S(2)}, u32[]{:S(2)}) collective-permute-start(bf16[128,1024]{1,0:T(8,128)(2,1)S(1)} %select_convert_fusion), channel_id=1, source_target_pairs={{0,1},{1,0},{2,3},{3,2},{4,5},{5,4},{6,7},{7,6},{8,9},{9,8},{10,11... | collective-permute-start | bytes 786440 | tf_op jit(solution)/shard_map/ppermute | solution.py:657
  309.8 10.0 %collective-permute-start.38 = (bf16[2,64,1024]{2,1,0:T(8,128)(2,1)S(1)}, bf16[2,64,1024]{2,1,0:T(8,128)(2,1)S(1)}, u32[]{:S(2)}, u32[]{:S(2)}) collective-permute-start(bf16[2,64,1024]{2,1,0:T(8,128)(2,1)S(1)} %get-tuple-element.133), channel_id=1, source_target_pairs={{0,8},{2,10},{4,12},{6,14},{8,0},{10,2},{12,4},{14,6},{16,24},{18,... | collective-permute-start | bytes 786440 | tf_op jit(solution)/shard_map/ppermute | solution.py:653
  311.5 16.8 %collective-permute-start.41 = (bf16[1,64,1024]{2,1,0:T(8,128)(2,1)}, bf16[1,64,1024]{2,1,0:T(8,128)(2,1)S(1)}, u32[]{:S(2)}, u32[]{:S(2)}) collective-permute-start(bf16[1,64,1024]{2,1,0:T(8,128)(2,1)} %fusion.19), channel_id=1, source_target_pairs={{0,4},{2,6},{4,0},{6,2},{8,12},{10,14},{12,8},{14,10},{16,20},{18,... | collective-permute-start | bytes 393224 | tf_op jit(solution)/shard_map/ppermute | solution.py:653
  313.0 22.1 %collective-permute-start.40 = (bf16[2,64,1024]{2,1,0:T(8,128)(2,1)}, bf16[2,64,1024]{2,1,0:T(8,128)(2,1)S(1)}, u32[]{:S(2)}, u32[]{:S(2)}) collective-permute-start(bf16[2,64,1024]{2,1,0:T(8,128)(2,1)} %get-tuple-element.131), channel_id=1, source_target_pairs={{0,24},{2,26},{4,28},{6,30},{8,16},{10,18},{12,20},{14,22},{16,8},... | collective-permute-start | bytes 786440 | tf_op jit(solution)/shard_map/ppermute | solution.py:653
  313.0 24.6 %collective-permute-start.39 = (bf16[2,64,1024]{2,1,0:T(8,128)(2,1)}, bf16[2,64,1024]{2,1,0:T(8,128)(2,1)S(1)}, u32[]{:S(2)}, u32[]{:S(2)}) collective-permute-start(bf16[2,64,1024]{2,1,0:T(8,128)(2,1)} %get-tuple-element.132), channel_id=1, source_target_pairs={{0,16},{2,18},{4,20},{6,22},{8,24},{10,26},{12,28},{14,30},{16,0},... | collective-permute-start | bytes 786440 | tf_op jit(solution)/shard_map/ppermute | solution.py:653
  319.8 8.5 %collective-permute-start.42 = (f32[32,32]{1,0:T(8,128)S(1)}, f32[32,32]{1,0:T(8,128)S(1)}, u32[]{:S(2)}, u32[]{:S(2)}) collective-permute-start(f32[32,32]{1,0:T(8,128)S(1)} %get-tuple-element.117), channel_id=1, source_target_pairs={{0,4},{2,6},{4,0},{6,2},{8,12},{10,14},{12,8},{14,10},{16,20},{18,... | collective-permute-start | bytes 12296 | tf_op jit(solution)/shard_map/ppermute | solution.py:653
  322.9 28.4 %all-to-all-start.1 = ((bf16[16,32,128]{2,1,0:T(8,128)(2,1)}), bf16[16,32,128]{2,1,0:T(8,128)(2,1)}, u32[]{:S(2)}, u32[]{:S(2)}) async-start(bf16[16,32,128]{2,1,0:T(8,128)(2,1)} %get-tuple-element.128), calls=%async_computation.2 | async-start | bytes 262144 | tf_op jit(solution)/shard_map/all_to_all | solution.py:804
  337.6 13.1 %collective-permute-start.45 = (f32[32,32]{1,0:T(8,128)S(1)}, f32[32,32]{1,0:T(8,128)S(1)}, u32[]{:S(2)}, u32[]{:S(2)}) collective-permute-start(f32[32,32]{1,0:T(8,128)S(1)} %get-tuple-element.126), channel_id=1, source_target_pairs={{0,24},{2,26},{4,28},{6,30},{8,16},{10,18},{12,20},{14,22},{16,8},... | collective-permute-start | bytes 12296 | tf_op jit(solution)/shard_map/ppermute | solution.py:653
  339.3 11.4 %collective-permute-start.44 = (f32[32,32]{1,0:T(8,128)S(1)}, f32[32,32]{1,0:T(8,128)S(1)}, u32[]{:S(2)}, u32[]{:S(2)}) collective-permute-start(f32[32,32]{1,0:T(8,128)S(1)} %get-tuple-element.126), channel_id=1, source_target_pairs={{0,16},{2,18},{4,20},{6,22},{8,24},{10,26},{12,28},{14,30},{16,0},... | collective-permute-start | bytes 12296 | tf_op jit(solution)/shard_map/ppermute | solution.py:653
  343.5 7.2 %collective-permute-start.43 = (f32[32,32]{1,0:T(8,128)S(1)}, f32[32,32]{1,0:T(8,128)S(1)}, u32[]{:S(2)}, u32[]{:S(2)}) collective-permute-start(f32[32,32]{1,0:T(8,128)S(1)} %get-tuple-element.126), channel_id=1, source_target_pairs={{0,8},{2,10},{4,12},{6,14},{8,0},{10,2},{12,4},{14,6},{16,24},{18,... | collective-permute-start | bytes 12296 | tf_op jit(solution)/shard_map/ppermute | solution.py:653
  343.5 18.0 %collective-permute-start.46 = (bf16[128,1024]{1,0:T(8,128)(2,1)S(1)}, bf16[128,1024]{1,0:T(8,128)(2,1)}, u32[]{:S(2)}, u32[]{:S(2)}) collective-permute-start(bf16[128,1024]{1,0:T(8,128)(2,1)S(1)} %get-tuple-element.127), channel_id=1, source_target_pairs={{0,0},{2,1},{4,2},{6,3},{8,4},{10,5},{12,6},{14,7},{16,8},{18,9},{... | collective-permute-start | bytes 786440 | tf_op jit(solution)/shard_map/ppermute | solution.py:809
  (11 other events, 227.9 us)
Sparse Core Ops, SparseCore 0:
  10.2 70.5 all-gather.2
  91.4 73.4 all-gather.4
  211.8 104.3 reduce-scatter.1

commit v6 on v5

--- a/solution.py
+++ b/solution.py
@@ -664,13 +664,17 @@
     return v
 
 
-def sum_pieces(keep, send, sent, others):
-    (acc,) = gate([keep.astype(F32) + cross(send, 1).astype(F32)], others)
-    acc = acc[0] + cross(acc[1].astype(sent), 2).astype(F32)
+def sum_pieces(keep, send, sent, held):
+    near = cross(send, 1)
+    acc = keep.astype(F32) + near.astype(F32)
+    far = cross(acc[1].astype(sent), 2)
+    if held is not None:
+        (held,) = gate([held], [near])
+    acc = acc[0] + far.astype(F32)
     total = acc[0]
     for k in (1, 2, 3):
         total = total + cross(acc[k].astype(sent), 4 * k).astype(F32)
-    return total
+    return total, held
 
 
 def spread_pieces(own_piece):
@@ -762,8 +766,8 @@
     normed, x, z, conv, keep, send = front(
         doc_starts, own, hid, gain_whole, weight, conv_w, conv_b, x_proj
     )
-    gout = gather_tokens(gate([grad_out], [keep])[0])
-    low = sum_pieces(keep, send, F32, []).astype(BF)
+    low, gout = sum_pieces(keep, send, F32, grad_out)
+    low, gout = low.astype(BF), gather_tokens(gout)
     near, far = spread_pieces(low)
     gated, y, states, mixed, last, stats = forward_scan(
         [], doc_starts, own, near, far, dt_proj, dtb, decay, skip, conv, z, out_cols
@@ -775,7 +779,7 @@
         gout, out_cols, states, wide,
     )
     keep, send, gated = gate([keep, send, gated], [])
-    low = sum_pieces(keep, send, BF, []).astype(BF)
+    low = sum_pieces(keep, send, BF, None)[0].astype(BF)
     gout_cols = jnp.einsum("rtd,rtc->dc", gout, gated, preferred_element_type=F32)
     parts = gout_cols.reshape(shards, 2, width // (2 * shards), ch)
     keep = jnp.where(first, parts[:, 0], parts[:, 1])

time: 371 us -> 369 us (level)
  no operation moved by 1% of the time
where the time goes in v6:
time: 369 us; the launch traced here: 368 us
  waiting for transfers between devices  155 us (42%)
  Pallas kernels  83.5 us (23%)
  starting transfers between devices  76.3 us (21%)
  other arithmetic  28.5 us (8%)
  between operations  14.3 us (4%)
  local copies, waits for them, and re-layouts  5.89 us (2%)
  matrix products  5.07 us (1%)
    ppermute x38, waiting for transfers between devices, cross(): return lax.ppermute(v, 'seq', [(s, s ^ bits) for s in range(16)])  96.8 us
    ppermute x38, starting transfers between devices, cross(): return lax.ppermute(v, 'seq', [(s, s ^ bits) for s in range(16)])  51 us
    pallas_call x1, Pallas kernels, backward_scan(): pl.pallas_call(partial(backward_kernel, top=top), grid_spec=pltpu.Prefetc...  39.1 us
    all_gather x2, waiting for transfers between devices, gather_tokens(): return lax.all_gather(v, 'seq', axis=1, tiled=True)  36.6 us
    pallas_call x1, Pallas kernels, forward_scan(): pl.pallas_call(forward_kernel, grid_spec=pltpu.PrefetchScalarGridSpec(num...  21.8 us
    pallas_call x1, Pallas kernels, tail(): pl.pallas_call(tail_kernel, grid_spec=pltpu.PrefetchScalarGridSpec(num_sc...  12.1 us
    ppermute x7, waiting for transfers between devices, swap_row(): return lax.ppermute(v, 'row', [(0, 1), (1, 0)])  11.7 us
    pallas_call x1, Pallas kernels, front(): pl.pallas_call(front_kernel, grid_spec=pltpu.PrefetchScalarGridSpec(num_s...  10.4 us
  transfers between devices with their start and end apart: 52, of which 29 were waited for; matrix products, arithmetic and copies ran while one was open for 10% of the time, Pallas kernels for 9%

profile of v6, /device:TPU:18, one launch (start us, length us, event | category | flops | bytes accessed | tf_op | source)
XLA Modules:
  0.0 368.1 jit_solution(13141940589444609131)
XLA Ops:
  10.2 2.2 collective-permute-done.2
  14.8 2.3 collective-permute-start
  18.0 4.1 %collective-permute-done.4 = f32[32,32]{1,0:T(8,128)S(1)} collective-permute-done((f32[32,32]{1,0:T(8,128)S(1)}, f32[32,32]{1,0:T(8,128)S(1)}, u32[]{:S(2)}, u32[]{:S(2)}) %collective-permute-start.4) | collective-permute-done | bytes 4128 | tf_op jit(solution)/shard_map/ppermute | solution.py:653
  22.1 4.7 %collective-permute-start.5 = (f32[32,32]{1,0:T(8,128)S(1)}, f32[32,32]{1,0:T(8,128)S(1)}, u32[]{:S(2)}, u32[]{:S(2)}) collective-permute-start(f32[32,32]{1,0:T(8,128)S(1)} %add.320), channel_id=1, source_target_pairs={{0,8},{2,10},{4,12},{6,14},{8,0},{10,2},{12,4},{14,6},{16,24},{18,... | collective-permute-start | bytes 12296 | tf_op jit(solution)/shard_map/ppermute | solution.py:653
  28.4 6.5 %all-to-all-start = ((bf16[64,16,128]{2,0,1:T(8,128)(2,1)}), bf16[64,16,128]{2,0,1:T(8,128)(2,1)S(1)}, u32[]{:S(2)}, u32[]{:S(2)}) async-start(bf16[64,16,128]{2,0,1:T(8,128)(2,1)} %copy_bitcast_fusion.1), calls=%async_computation | async-start | bytes 524288 | tf_op jit(solution)/shard_map/all_to_all | solution.py:750
  40.7 2.2 collective-permute-done.6
  44.3 36.6 %all-gather.3.cloned.1.call-done.hid = bf16[3,1024,1024]{2,1,0:T(8,128)(2,1)} async-done(((bf16[3,64,1024]{2,1,0:T(8,128)(2,1)}), bf16[3,1024,1024]{2,1,0:T(8,128)(2,1)}) %all-gather.3.cloned.1.call-update) | async-done | bytes 6291472 | tf_op jit(solution)/shard_map/all_gather | solution.py:687
  80.9 10.4 %front.1 = (bf16[3,1024,1024]{2,1,0:T(8,128)(2,1)}, bf16[3,1024,128]{2,1,0:T(8,128)(2,1)}, f32[3,1024,128]{2,1,0:T(8,128)}, bf16[3,1024,128]{2,1,0:T(8,128)(2,1)...) custom-call(s32[3,8]{1,0:T(4,128)S(1)} %copy-done.2, s32[3]{0:T(128)S(1)} %pad_add_fusion.own, ...), custom_call_target="tpu_custom_call" | custom-call | flops 1 | bytes 1 | tf_op jit(solution)/shard_map/front/pallas_call | solution.py:165
  95.3 11.9 %collective-permute-done.9 = f32[4,3,64,96]{3,2,1,0:T(8,128)S(1)} collective-permute-done((f32[4,3,64,96]{3,2,1,0:T(8,128)S(1)}, f32[4,3,64,96]{3,2,1,0:T(8,128)S(1)}, u32[]{:S(2)}, u32[]{:S(2)}) %collective-permute-start.9) | collective-permute-done | bytes 294944 | tf_op jit(solution)/shard_map/ppermute | solution.py:653
  107.4 2.3 collective-permute-start.12
  109.7 2.1 collective-permute-start.11
  111.8 3.3 collective-permute-done.10
  115.1 6.1 %collective-permute-done.12 = f32[3,64,96]{2,1,0:T(8,128)S(1)} collective-permute-done((f32[3,64,96]{2,1,0:T(8,128)S(1)}, f32[3,64,96]{2,1,0:T(8,128)S(1)}, u32[]{:S(2)}, u32[]{:S(2)}) %collective-permute-start.12) | collective-permute-done | bytes 73760 | tf_op jit(solution)/shard_map/ppermute | solution.py:653
  121.2 3.4 collective-permute-done.11
  124.7 4.0 %collective-permute-start.14 = (bf16[3,64,96]{2,1,0:T(8,128)(2,1)S(1)}, bf16[3,64,96]{2,1,0:T(8,128)(2,1)S(1)}, u32[]{:S(2)}, u32[]{:S(2)}) collective-permute-start(bf16[3,64,96]{2,1,0:T(8,128)(2,1)S(1)} %fusion.29), channel_id=1, source_target_pairs={{0,16},{2,18},{4,20},{6,22},{8,24},{10,26},{12,28},{14,30},{16,0},... | collective-permute-start | bytes 110600 | tf_op jit(solution)/shard_map/ppermute | solution.py:653
  132.8 2.1 collective-permute-start.16
  134.9 8.7 %collective-permute-done.16 = bf16[4,3,64,96]{3,2,1,0:T(8,128)(2,1)S(1)} collective-permute-done((bf16[4,3,64,96]{3,2,1,0:T(8,128)(2,1)S(1)}, bf16[4,3,64,96]{3,2,1,0:T(8,128)(2,1)S(1)}, u32[]{:S(2)}, u32[]{:S(2)}) %collective-permute-start.16) | collective-permute-done | bytes 147488 | tf_op jit(solution)/shard_map/ppermute | solution.py:653
  143.7 1.7 collective-permute-done.17.far
  145.4 21.8 %forward_scan.1 = (bf16[3,1024,128]{2,1,0:T(8,128)(2,1)}, bf16[3,1024,128]{2,1,0:T(8,128)(2,1)}, f32[3,1024,16,128]{3,2,1,0:T(8,128)}, bf16[3,1024,1024]{2,1,0:T...) custom-call(s32[3,8]{1,0:T(4,128)S(1)} %copy-done.2, s32[3]{0:T(128)S(1)} %pad_add_fusion.own, ...), custom_call_target="tpu_custom_call" | custom-call | flops 1 | bytes 1 | tf_op jit(solution)/shard_map/forward_scan/pallas_call | solution.py:324
  167.3 39.1 %backward_scan.1 = (bf16[3,1024,128]{2,1,0:T(8,128)(2,1)}, f32[3,1024,128]{2,1,0:T(8,128)}, f32[2,4,3,64,96]{4,3,2,1,0:T(8,128)S(1)}, f32[2,4,3,64,96]{4,3,2,1,0...) custom-call(s32[3,8]{1,0:T(4,128)S(1)} %copy-done.2, ...), custom_call_target="tpu_custom_call" | custom-call | flops 1 | bytes 1 | tf_op jit(solution)/shard_map/backward_scan/pallas_call | solution.py:492
  206.6 2.2 collective-permute-done.18
  208.9 1.7 collective-permute-start.19
  210.6 5.3 %collective-permute-done.19 = bf16[4,3,64,96]{3,2,1,0:T(8,128)(2,1)S(1)} collective-permute-done((bf16[4,3,64,96]{3,2,1,0:T(8,128)(2,1)S(1)}, bf16[4,3,64,96]{3,2,1,0:T(8,128)(2,1)S(1)}, u32[]{:S(2)}, u32[]{:S(2)}) %collective-permute-start.19) | collective-permute-done | bytes 147488 | tf_op jit(solution)/shard_map/ppermute | solution.py:653
  216.0 3.8 %collective-permute-start.20 = (bf16[3,64,96]{2,1,0:T(8,128)(2,1)S(1)}, bf16[3,64,96]{2,1,0:T(8,128)(2,1)S(1)}, u32[]{:S(2)}, u32[]{:S(2)}) collective-permute-start(bf16[3,64,96]{2,1,0:T(8,128)(2,1)S(1)} %get-tuple-element.148), channel_id=1, source_target_pairs={{0,8},{2,10},{4,12},{6,14},{8,0},{10,2},{12,4},{14,6},{16,24},{18,... | collective-permute-start | bytes 110600 | tf_op jit(solution)/shard_map/ppermute | solution.py:653
  220.0 2.2 collective-permute-start.21
  222.3 3.4 collective-permute-done.22
  227.1 3.1 collective-permute-start.24
  230.1 5.1 %fusion.43 = f32[1024,128,1]{1,0,2:T(8,128)S(1)} fusion(bf16[3,1024,1024]{2,1,0:T(8,128)(2,1)} %all-gather.5.cloned.1.call-done.gout, bf16[3,1024,128]{2,1,0:T(8,128)(2,1)S(1)} %get-tuple-element.98), kind=kOutput, calls=%fused_computation.117 | convolution fusion | flops 805306368 | bytes 7602176 | tf_op jit(solution)/shard_map/rtd,rtc->dc/dot_general | solution.py:783
  237.4 3.6 collective-permute-done.26
  243.3 12.1 %tail.1 = (bf16[2,4,3,64,1024]{4,3,2,1,0:T(8,128)(2,1)}, bf16[2,4,3,64,1024]{4,3,2,1,0:T(8,128)(2,1)}, f32[256,1024]{1,0:T(8,128)S(1)}, f32[128,96]{1,0:T(8,128)S(1)}, f32[8,128]{1,0:T(8,128)S(1)}) custom-call(s32[3,8]{1,0:T(4,128)S(1)} %copy-done.2, s32[3]{0:T(128)S(1)} %pad_add_fusion.own, bf16[2,4,3,64,96]{4,3,2,1,0:T(8,128)(2,1)S(1)} %pad_maximum_fusion.2.near, ...), custom_call_target="tpu_custom_call" | custom-call | flops 1 | bytes 1 | tf_op jit(solution)/shard_map/tail/pallas_call | solution.py:605
  256.9 4.6 %collective-permute-done.29.refs_0_ = bf16[2,4,3,64,1024]{4,3,2,1,0:T(8,128)(2,1)} collective-permute-done((bf16[2,4,3,64,1024]{4,3,2,1,0:T(8,128)(2,1)}, bf16[2,4,3,64,1024]{4,3,2,1,0:T(8,128)(2,1)}, u32[]{:S(2)}, u32[]{:S(2)}) %collective-permute-start.29) | collective-permute-done | bytes 3145760 | tf_op jit(solution)/shard_map/ppermute | solution.py:653
  261.5 2.2 fusion.17
  264.5 3.4 collective-permute-start.32
  267.9 2.6 fusion
  271.8 19.7 %collective-permute-done.31.refs_6_.refs_1_ = bf16[2,1,64,1024]{3,2,1,0:T(8,128)(2,1)S(1)} collective-permute-done((bf16[2,1,64,1024]{3,2,1,0:T(8,128)(2,1)S(1)}, bf16[2,1,64,1024]{3,2,1,0:T(8,128)(2,1)S(1)}, u32[]{:S(2)}, u32[]{:S(2)}) %collective-permute-start.31) | collective-permute-done | bytes 262176 | tf_op jit(solution)/shard_map/ppermute | solution.py:653
  299.7 5.4 %collective-permute-done.34 = bf16[128,1024]{1,0:T(8,128)(2,1)S(1)} collective-permute-done((bf16[128,1024]{1,0:T(8,128)(2,1)S(1)}, bf16[128,1024]{1,0:T(8,128)(2,1)S(1)}, u32[]{:S(2)}, u32[]{:S(2)}) %collective-permute-start.34) | collective-permute-done | bytes 262176 | tf_op jit(solution)/shard_map/ppermute | solution.py:657
  305.3 2.6 fusion.9
  307.9 1.7 fusion.19
  311.1 4.4 %collective-permute-start.39 = (bf16[2,64,1024]{2,1,0:T(8,128)(2,1)}, bf16[2,64,1024]{2,1,0:T(8,128)(2,1)S(1)}, u32[]{:S(2)}, u32[]{:S(2)}) collective-permute-start(bf16[2,64,1024]{2,1,0:T(8,128)(2,1)} %get-tuple-element.132), channel_id=1, source_target_pairs={{0,16},{2,18},{4,20},{6,22},{8,24},{10,26},{12,28},{14,30},{16,0},... | collective-permute-start | bytes 786440 | tf_op jit(solution)/shard_map/ppermute | solution.py:653
  321.0 5.1 %all-to-all-start.1 = ((bf16[16,32,128]{2,1,0:T(8,128)(2,1)}), bf16[16,32,128]{2,1,0:T(8,128)(2,1)}, u32[]{:S(2)}, u32[]{:S(2)}) async-start(bf16[16,32,128]{2,1,0:T(8,128)(2,1)} %get-tuple-element.128), calls=%async_computation.2 | async-start | bytes 262144 | tf_op jit(solution)/shard_map/all_to_all | solution.py:808
  326.1 7.1 %collective-permute-done.40.refs_2_ = bf16[2,64,1024]{2,1,0:T(8,128)(2,1)S(1)} collective-permute-done((bf16[2,64,1024]{2,1,0:T(8,128)(2,1)}, bf16[2,64,1024]{2,1,0:T(8,128)(2,1)S(1)}, u32[]{:S(2)}, u32[]{:S(2)}) %collective-permute-start.40) | collective-permute-done | bytes 262176 | tf_op jit(solution)/shard_map/ppermute | solution.py:653
  333.2 2.5 collective-permute-done.39.refs_1_
  335.7 1.7 collective-permute-start.45
  337.5 4.2 %collective-permute-start.44 = (f32[32,32]{1,0:T(8,128)S(1)}, f32[32,32]{1,0:T(8,128)S(1)}, u32[]{:S(2)}, u32[]{:S(2)}) collective-permute-start(f32[32,32]{1,0:T(8,128)S(1)} %get-tuple-element.126), channel_id=1, source_target_pairs={{0,16},{2,18},{4,20},{6,22},{8,24},{10,26},{12,28},{14,30},{16,0},... | collective-permute-start | bytes 12296 | tf_op jit(solution)/shard_map/ppermute | solution.py:653
  341.6 1.9 collective-permute-start.46
  346.3 2.5 fusion.6
  351.0 8.8 %collective-permute-done.46 = bf16[128,1024]{1,0:T(8,128)(2,1)} collective-permute-done((bf16[128,1024]{1,0:T(8,128)(2,1)S(1)}, bf16[128,1024]{1,0:T(8,128)(2,1)}, u32[]{:S(2)}, u32[]{:S(2)}) %collective-permute-start.46) | collective-permute-done | bytes 262176 | tf_op jit(solution)/shard_map/ppermute | solution.py:813
  359.8 1.8 convert_element_type.488
  (170 shorter events, 53.6 us)
Async XLA Ops:
  7.2 73.7 %all-gather.3.cloned.1.call-start = ((), (), s32[]{:S(2)}) async-start(), calls=%async_computation.3 | async-start | bytes 6684672 | tf_op jit(solution)/shard_map/all_gather | solution.py:687
  8.6 3.8 %collective-permute-start.2 = (f32[32,32]{1,0:T(8,128)S(1)}, f32[32,32]{1,0:T(8,128)S(1)}, u32[]{:S(2)}, u32[]{:S(2)}) collective-permute-start(f32[32,32]{1,0:T(8,128)S(1)} %dynamic_update_slice.5), channel_id=1, source_target_pairs={{0,1},{1,0},{2,3},{3,2},{4,5},{5,4},{6,7},{7,6},{8,9},{9,8},{10,11... | collective-permute-start | bytes 12296 | tf_op jit(solution)/shard_map/ppermute | solution.py:657
  13.1 3.9 %collective-permute-start.3 = (f32[32,32]{1,0:T(8,128)S(1)}, f32[32,32]{1,0:T(8,128)S(1)}, u32[]{:S(2)}, u32[]{:S(2)}) collective-permute-start(f32[32,32]{1,0:T(8,128)S(1)} %add.318), channel_id=1, source_target_pairs={{0,2},{2,0},{4,6},{6,4},{8,10},{10,8},{12,14},{14,12},{16,18},{18,... | collective-permute-start | bytes 12296 | tf_op jit(solution)/shard_map/ppermute | solution.py:653
  13.2 13.5 %collective-permute-start.7 = (bf16[32,2048]{1,0:T(8,128)(2,1)}, bf16[32,2048]{1,0:T(8,128)(2,1)S(1)}, u32[]{:S(2)}, u32[]{:S(2)}) collective-permute-start(bf16[32,2048]{1,0:T(8,128)(2,1)} %param.18), channel_id=1, source_target_pairs={{0,1},{1,0},{2,3},{3,2},{4,5},{5,4},{6,7},{7,6},{8,9},{9,8},{10,11... | collective-permute-start | bytes 393224 | tf_op jit(solution)/shard_map/ppermute | solution.py:657
  14.8 20.3 %collective-permute-start = (bf16[128,1024]{1,0:T(8,128)(2,1)}, bf16[128,1024]{1,0:T(8,128)(2,1)S(1)}, u32[]{:S(2)}, u32[]{:S(2)}) collective-permute-start(bf16[128,1024]{1,0:T(8,128)(2,1)} %param.17), channel_id=1, source_target_pairs={{0,0},{1,2},{2,4},{3,6},{4,8},{5,10},{6,12},{7,14},{8,16},{9,18},{... | collective-permute-start | bytes 786440 | tf_op jit(solution)/shard_map/ppermute | solution.py:745
  17.1 5.0 %collective-permute-start.4 = (f32[32,32]{1,0:T(8,128)S(1)}, f32[32,32]{1,0:T(8,128)S(1)}, u32[]{:S(2)}, u32[]{:S(2)}) collective-permute-start(f32[32,32]{1,0:T(8,128)S(1)} %add.319), channel_id=1, source_target_pairs={{0,4},{2,6},{4,0},{6,2},{8,12},{10,14},{12,8},{14,10},{16,20},{18,... | collective-permute-start | bytes 12296 | tf_op jit(solution)/shard_map/ppermute | solution.py:653
  22.1 14.8 %collective-permute-start.5 = (f32[32,32]{1,0:T(8,128)S(1)}, f32[32,32]{1,0:T(8,128)S(1)}, u32[]{:S(2)}, u32[]{:S(2)}) collective-permute-start(f32[32,32]{1,0:T(8,128)S(1)} %add.320), channel_id=1, source_target_pairs={{0,8},{2,10},{4,12},{6,14},{8,0},{10,2},{12,4},{14,6},{16,24},{18,... | collective-permute-start | bytes 12296 | tf_op jit(solution)/shard_map/ppermute | solution.py:653
  28.4 15.8 %all-to-all-start = ((bf16[64,16,128]{2,0,1:T(8,128)(2,1)}), bf16[64,16,128]{2,0,1:T(8,128)(2,1)S(1)}, u32[]{:S(2)}, u32[]{:S(2)}) async-start(bf16[64,16,128]{2,0,1:T(8,128)(2,1)} %copy_bitcast_fusion.1), calls=%async_computation | async-start | bytes 524288 | tf_op jit(solution)/shard_map/all_to_all | solution.py:750
  35.0 132.3 %all-gather.5.cloned.1.call-start = ((), (), s32[]{:S(2)}) async-start(), calls=%async_computation.5 | async-start | bytes 6684672 | tf_op jit(solution)/shard_map/all_gather | solution.py:687
  35.0 9.1 %collective-permute-start.1 = (bf16[128,1024]{1,0:T(8,128)(2,1)S(1)}, bf16[128,1024]{1,0:T(8,128)(2,1)S(1)}, u32[]{:S(2)}, u32[]{:S(2)}) collective-permute-start(bf16[128,1024]{1,0:T(8,128)(2,1)S(1)} %collective-permute-done), channel_id=1, source_target_pairs={{0,1},{1,0},{2,3},{3,2},{4,5},{5,4},{6,7},{7,6},{8,9},{9,8},{10,11... | collective-permute-start | bytes 786440 | tf_op jit(solution)/shard_map/ppermute | solution.py:657
  36.9 6.0 %collective-permute-start.6 = (f32[32,32]{1,0:T(8,128)S(1)}, f32[32,32]{1,0:T(8,128)S(1)}, u32[]{:S(2)}, u32[]{:S(2)}) collective-permute-start(f32[32,32]{1,0:T(8,128)S(1)} %add.321), channel_id=1, source_target_pairs={{0,16},{2,18},{4,20},{6,22},{8,24},{10,26},{12,28},{14,30},{16,0},... | collective-permute-start | bytes 12296 | tf_op jit(solution)/shard_map/ppermute | solution.py:653
  93.6 252.8 %reduce-scatter.2.cloned.1.call-start = ((), (), s32[]{:S(2)}) async-start(), calls=%async_computation.4 | async-start | bytes 6684672 | tf_op jit(solution)/shard_map/reduce_scatter | solution.py:775
  93.8 13.5 %collective-permute-start.9 = (f32[4,3,64,96]{3,2,1,0:T(8,128)S(1)}, f32[4,3,64,96]{3,2,1,0:T(8,128)S(1)}, u32[]{:S(2)}, u32[]{:S(2)}) collective-permute-start(f32[4,3,64,96]{3,2,1,0:T(8,128)S(1)} %slice_bitcast_fusion.1), channel_id=1, source_target_pairs={{0,4},{2,6},{4,0},{6,2},{8,12},{10,14},{12,8},{14,10},{16,20},{18,... | collective-permute-start | bytes 884744 | tf_op jit(solution)/shard_map/ppermute | solution.py:653
  107.3 7.8 %collective-permute-start.10 = (f32[3,64,96]{2,1,0:T(8,128)S(1)}, f32[3,64,96]{2,1,0:T(8,128)S(1)}, u32[]{:S(2)}, u32[]{:S(2)}) collective-permute-start(f32[3,64,96]{2,1,0:T(8,128)S(1)} %get-tuple-element.141), channel_id=1, source_target_pairs={{0,8},{2,10},{4,12},{6,14},{8,0},{10,2},{12,4},{14,6},{16,24},{18,... | collective-permute-start | bytes 221192 | tf_op jit(solution)/shard_map/ppermute | solution.py:653
  107.4 13.8 %collective-permute-start.12 = (f32[3,64,96]{2,1,0:T(8,128)S(1)}, f32[3,64,96]{2,1,0:T(8,128)S(1)}, u32[]{:S(2)}, u32[]{:S(2)}) collective-permute-start(f32[3,64,96]{2,1,0:T(8,128)S(1)} %get-tuple-element.142), channel_id=1, source_target_pairs={{0,24},{2,26},{4,28},{6,30},{8,16},{10,18},{12,20},{14,22},{16,8},... | collective-permute-start | bytes 221192 | tf_op jit(solution)/shard_map/ppermute | solution.py:653
  109.7 14.9 %collective-permute-start.11 = (f32[3,64,96]{2,1,0:T(8,128)S(1)}, f32[3,64,96]{2,1,0:T(8,128)S(1)}, u32[]{:S(2)}, u32[]{:S(2)}) collective-permute-start(f32[3,64,96]{2,1,0:T(8,128)S(1)} %get-tuple-element.143), channel_id=1, source_target_pairs={{0,16},{2,18},{4,20},{6,22},{8,24},{10,26},{12,28},{14,30},{16,0},... | collective-permute-start | bytes 221192 | tf_op jit(solution)/shard_map/ppermute | solution.py:653
  124.6 5.2 %collective-permute-start.15 = (bf16[3,64,96]{2,1,0:T(8,128)(2,1)S(1)}, bf16[3,64,96]{2,1,0:T(8,128)(2,1)S(1)}, u32[]{:S(2)}, u32[]{:S(2)}) collective-permute-start(bf16[3,64,96]{2,1,0:T(8,128)(2,1)S(1)} %fusion.29), channel_id=1, source_target_pairs={{0,24},{2,26},{4,28},{6,30},{8,16},{10,18},{12,20},{14,22},{16,8},... | collective-permute-start | bytes 110600 | tf_op jit(solution)/shard_map/ppermute | solution.py:653
  124.7 6.7 %collective-permute-start.14 = (bf16[3,64,96]{2,1,0:T(8,128)(2,1)S(1)}, bf16[3,64,96]{2,1,0:T(8,128)(2,1)S(1)}, u32[]{:S(2)}, u32[]{:S(2)}) collective-permute-start(bf16[3,64,96]{2,1,0:T(8,128)(2,1)S(1)} %fusion.29), channel_id=1, source_target_pairs={{0,16},{2,18},{4,20},{6,22},{8,24},{10,26},{12,28},{14,30},{16,0},... | collective-permute-start | bytes 110600 | tf_op jit(solution)/shard_map/ppermute | solution.py:653
  128.7 4.1 %collective-permute-start.13 = (bf16[3,64,96]{2,1,0:T(8,128)(2,1)S(1)}, bf16[3,64,96]{2,1,0:T(8,128)(2,1)S(1)}, u32[]{:S(2)}, u32[]{:S(2)}) collective-permute-start(bf16[3,64,96]{2,1,0:T(8,128)(2,1)S(1)} %fusion.29), channel_id=1, source_target_pairs={{0,8},{2,10},{4,12},{6,14},{8,0},{10,2},{12,4},{14,6},{16,24},{18,... | collective-permute-start | bytes 110600 | tf_op jit(solution)/shard_map/ppermute | solution.py:653
  132.8 10.7 %collective-permute-start.16 = (bf16[4,3,64,96]{3,2,1,0:T(8,128)(2,1)S(1)}, bf16[4,3,64,96]{3,2,1,0:T(8,128)(2,1)S(1)}, u32[]{:S(2)}, u32[]{:S(2)}) collective-permute-start(bf16[4,3,64,96]{3,2,1,0:T(8,128)(2,1)S(1)} %get-tuple-element.152), channel_id=1, source_target_pairs={{0,4},{2,6},{4,0},{6,2},{8,12},{10,14},{12,8},{14,10},{16,20},{18,... | collective-permute-start | bytes 442376 | tf_op jit(solution)/shard_map/ppermute | solution.py:653
  206.4 2.4 collective-permute-start.18
  208.9 7.0 %collective-permute-start.19 = (bf16[4,3,64,96]{3,2,1,0:T(8,128)(2,1)S(1)}, bf16[4,3,64,96]{3,2,1,0:T(8,128)(2,1)S(1)}, u32[]{:S(2)}, u32[]{:S(2)}) collective-permute-start(bf16[4,3,64,96]{3,2,1,0:T(8,128)(2,1)S(1)} %fusion.21), channel_id=1, source_target_pairs={{0,4},{2,6},{4,0},{6,2},{8,12},{10,14},{12,8},{14,10},{16,20},{18,... | collective-permute-start | bytes 442376 | tf_op jit(solution)/shard_map/ppermute | solution.py:653
  216.0 6.3 %collective-permute-start.20 = (bf16[3,64,96]{2,1,0:T(8,128)(2,1)S(1)}, bf16[3,64,96]{2,1,0:T(8,128)(2,1)S(1)}, u32[]{:S(2)}, u32[]{:S(2)}) collective-permute-start(bf16[3,64,96]{2,1,0:T(8,128)(2,1)S(1)} %get-tuple-element.148), channel_id=1, source_target_pairs={{0,8},{2,10},{4,12},{6,14},{8,0},{10,2},{12,4},{14,6},{16,24},{18,... | collective-permute-start | bytes 110600 | tf_op jit(solution)/shard_map/ppermute | solution.py:653
  219.8 5.8 %collective-permute-start.22 = (bf16[3,64,96]{2,1,0:T(8,128)(2,1)S(1)}, bf16[3,64,96]{2,1,0:T(8,128)(2,1)S(1)}, u32[]{:S(2)}, u32[]{:S(2)}) collective-permute-start(bf16[3,64,96]{2,1,0:T(8,128)(2,1)S(1)} %get-tuple-element.149), channel_id=1, source_target_pairs={{0,24},{2,26},{4,28},{6,30},{8,16},{10,18},{12,20},{14,22},{16,8},... | collective-permute-start | bytes 110600 | tf_op jit(solution)/shard_map/ppermute | solution.py:653
  220.0 5.7 %collective-permute-start.21 = (bf16[3,64,96]{2,1,0:T(8,128)(2,1)S(1)}, bf16[3,64,96]{2,1,0:T(8,128)(2,1)S(1)}, u32[]{:S(2)}, u32[]{:S(2)}) collective-permute-start(bf16[3,64,96]{2,1,0:T(8,128)(2,1)S(1)} %get-tuple-element.150), channel_id=1, source_target_pairs={{0,16},{2,18},{4,20},{6,22},{8,24},{10,26},{12,28},{14,30},{16,0},... | collective-permute-start | bytes 110600 | tf_op jit(solution)/shard_map/ppermute | solution.py:653
  225.7 9.5 %collective-permute-start.25 = (bf16[3,64,96]{2,1,0:T(8,128)(2,1)S(1)}, bf16[3,64,96]{2,1,0:T(8,128)(2,1)S(1)}, u32[]{:S(2)}, u32[]{:S(2)}) collective-permute-start(bf16[3,64,96]{2,1,0:T(8,128)(2,1)S(1)} %fusion.25), channel_id=1, source_target_pairs={{0,24},{2,26},{4,28},{6,30},{8,16},{10,18},{12,20},{14,22},{16,8},... | collective-permute-start | bytes 110600 | tf_op jit(solution)/shard_map/ppermute | solution.py:653
  227.1 8.2 %collective-permute-start.24 = (bf16[3,64,96]{2,1,0:T(8,128)(2,1)S(1)}, bf16[3,64,96]{2,1,0:T(8,128)(2,1)S(1)}, u32[]{:S(2)}, u32[]{:S(2)}) collective-permute-start(bf16[3,64,96]{2,1,0:T(8,128)(2,1)S(1)} %fusion.25), channel_id=1, source_target_pairs={{0,16},{2,18},{4,20},{6,22},{8,24},{10,26},{12,28},{14,30},{16,0},... | collective-permute-start | bytes 110600 | tf_op jit(solution)/shard_map/ppermute | solution.py:653
  230.1 5.1 %collective-permute-start.23 = (bf16[3,64,96]{2,1,0:T(8,128)(2,1)S(1)}, bf16[3,64,96]{2,1,0:T(8,128)(2,1)S(1)}, u32[]{:S(2)}, u32[]{:S(2)}) collective-permute-start(bf16[3,64,96]{2,1,0:T(8,128)(2,1)S(1)} %fusion.25), channel_id=1, source_target_pairs={{0,8},{2,10},{4,12},{6,14},{8,0},{10,2},{12,4},{14,6},{16,24},{18,... | collective-permute-start | bytes 110600 | tf_op jit(solution)/shard_map/ppermute | solution.py:653
  235.3 5.7 %collective-permute-start.26 = (bf16[4,3,64,96]{3,2,1,0:T(8,128)(2,1)S(1)}, bf16[4,3,64,96]{3,2,1,0:T(8,128)(2,1)S(1)}, u32[]{:S(2)}, u32[]{:S(2)}) collective-permute-start(bf16[4,3,64,96]{3,2,1,0:T(8,128)(2,1)S(1)} %get-tuple-element.147), channel_id=1, source_target_pairs={{0,4},{2,6},{4,0},{6,2},{8,12},{10,14},{12,8},{14,10},{16,20},{18,... | collective-permute-start | bytes 442376 | tf_op jit(solution)/shard_map/ppermute | solution.py:653
  236.1 6.5 %collective-permute-start.28 = (f32[16,32,128]{2,1,0:T(8,128)S(1)}, f32[16,32,128]{2,1,0:T(8,128)S(1)}, u32[]{:S(2)}, u32[]{:S(2)}) collective-permute-start(f32[16,32,128]{2,1,0:T(8,128)S(1)} %select_bitcast_fusion), channel_id=1, source_target_pairs={{0,1},{1,0},{2,3},{3,2},{4,5},{5,4},{6,7},{7,6},{8,9},{9,8},{10,11... | collective-permute-start | bytes 786440 | tf_op jit(solution)/shard_map/ppermute | solution.py:657
  255.5 6.0 %collective-permute-start.29 = (bf16[2,4,3,64,1024]{4,3,2,1,0:T(8,128)(2,1)}, bf16[2,4,3,64,1024]{4,3,2,1,0:T(8,128)(2,1)}, u32[]{:S(2)}, u32[]{:S(2)}) collective-permute-start(bf16[2,4,3,64,1024]{4,3,2,1,0:T(8,128)(2,1)} %get-tuple-element.100), channel_id=1, source_target_pairs={{0,2},{2,0},{4,6},{6,4},{8,10},{10,8},{12,14},{14,12},{16,18},{18,... | collective-permute-start | bytes 9437192 | tf_op jit(solution)/shard_map/ppermute | solution.py:653
  263.7 41.6 %collective-permute-start.33 = (bf16[2,1,64,1024]{3,2,1,0:T(8,128)(2,1)}, bf16[2,1,64,1024]{3,2,1,0:T(8,128)(2,1)S(1)}, u32[]{:S(2)}, u32[]{:S(2)}) collective-permute-start(bf16[2,1,64,1024]{3,2,1,0:T(8,128)(2,1)} %get-tuple-element.134), channel_id=1, source_target_pairs={{0,24},{2,26},{4,28},{6,30},{8,16},{10,18},{12,20},{14,22},{16,8},... | collective-permute-start | bytes 786440 | tf_op jit(solution)/shard_map/ppermute | solution.py:653
  264.5 40.8 %collective-permute-start.32 = (bf16[2,1,64,1024]{3,2,1,0:T(8,128)(2,1)}, bf16[2,1,64,1024]{3,2,1,0:T(8,128)(2,1)S(1)}, u32[]{:S(2)}, u32[]{:S(2)}) collective-permute-start(bf16[2,1,64,1024]{3,2,1,0:T(8,128)(2,1)} %get-tuple-element.135), channel_id=1, source_target_pairs={{0,16},{2,18},{4,20},{6,22},{8,24},{10,26},{12,28},{14,30},{16,0},... | collective-permute-start | bytes 786440 | tf_op jit(solution)/shard_map/ppermute | solution.py:653
  267.9 23.6 %collective-permute-start.31 = (bf16[2,1,64,1024]{3,2,1,0:T(8,128)(2,1)S(1)}, bf16[2,1,64,1024]{3,2,1,0:T(8,128)(2,1)S(1)}, u32[]{:S(2)}, u32[]{:S(2)}) collective-permute-start(bf16[2,1,64,1024]{3,2,1,0:T(8,128)(2,1)S(1)} %get-tuple-element.136), channel_id=1, source_target_pairs={{0,8},{2,10},{4,12},{6,14},{8,0},{10,2},{12,4},{14,6},{16,24},{18,... | collective-permute-start | bytes 786440 | tf_op jit(solution)/shard_map/ppermute | solution.py:653
  270.5 34.8 %collective-permute-start.30 = (bf16[4,2,64,1024]{3,2,1,0:T(8,128)(2,1)}, bf16[4,2,64,1024]{3,2,1,0:T(8,128)(2,1)S(1)}, u32[]{:S(2)}, u32[]{:S(2)}) collective-permute-start(bf16[4,2,64,1024]{3,2,1,0:T(8,128)(2,1)} %fusion), channel_id=1, source_target_pairs={{0,4},{2,6},{4,0},{6,2},{8,12},{10,14},{12,8},{14,10},{16,20},{18,... | collective-permute-start | bytes 3145736 | tf_op jit(solution)/shard_map/ppermute | solution.py:653
  291.8 3.8 %collective-permute-start.36 = (f32[32,32]{1,0:T(8,128)S(1)}, f32[32,32]{1,0:T(8,128)S(1)}, u32[]{:S(2)}, u32[]{:S(2)}) collective-permute-start(f32[32,32]{1,0:T(8,128)S(1)} %div.40), channel_id=1, source_target_pairs={{0,1},{1,0},{2,3},{3,2},{4,5},{5,4},{6,7},{7,6},{8,9},{9,8},{10,11... | collective-permute-start | bytes 12296 | tf_op jit(solution)/shard_map/ppermute | solution.py:657
  293.5 4.9 %collective-permute-start.35 = (f32[200,128]{1,0:T(8,128)S(1)}, f32[200,128]{1,0:T(8,128)S(1)}, u32[]{:S(2)}, u32[]{:S(2)}) collective-permute-start(f32[200,128]{1,0:T(8,128)S(1)} %bitcast_dynamic-update-slice_fusion), channel_id=1, source_target_pairs={{0,1},{1,0},{2,3},{3,2},{4,5},{5,4},{6,7},{7,6},{8,9},{9,8},{10,11... | collective-permute-start | bytes 307208 | tf_op jit(solution)/shard_map/ppermute | solution.py:657
  296.8 8.4 %collective-permute-start.34 = (bf16[128,1024]{1,0:T(8,128)(2,1)S(1)}, bf16[128,1024]{1,0:T(8,128)(2,1)S(1)}, u32[]{:S(2)}, u32[]{:S(2)}) collective-permute-start(bf16[128,1024]{1,0:T(8,128)(2,1)S(1)} %select_convert_fusion), channel_id=1, source_target_pairs={{0,1},{1,0},{2,3},{3,2},{4,5},{5,4},{6,7},{7,6},{8,9},{9,8},{10,11... | collective-permute-start | bytes 786440 | tf_op jit(solution)/shard_map/ppermute | solution.py:657
  307.9 9.4 %collective-permute-start.38 = (bf16[2,64,1024]{2,1,0:T(8,128)(2,1)S(1)}, bf16[2,64,1024]{2,1,0:T(8,128)(2,1)S(1)}, u32[]{:S(2)}, u32[]{:S(2)}) collective-permute-start(bf16[2,64,1024]{2,1,0:T(8,128)(2,1)S(1)} %get-tuple-element.133), channel_id=1, source_target_pairs={{0,8},{2,10},{4,12},{6,14},{8,0},{10,2},{12,4},{14,6},{16,24},{18,... | collective-permute-start | bytes 786440 | tf_op jit(solution)/shard_map/ppermute | solution.py:653
  309.6 16.5 %collective-permute-start.41 = (bf16[1,64,1024]{2,1,0:T(8,128)(2,1)}, bf16[1,64,1024]{2,1,0:T(8,128)(2,1)S(1)}, u32[]{:S(2)}, u32[]{:S(2)}) collective-permute-start(bf16[1,64,1024]{2,1,0:T(8,128)(2,1)} %fusion.19), channel_id=1, source_target_pairs={{0,4},{2,6},{4,0},{6,2},{8,12},{10,14},{12,8},{14,10},{16,20},{18,... | collective-permute-start | bytes 393224 | tf_op jit(solution)/shard_map/ppermute | solution.py:653
  311.1 22.1 %collective-permute-start.40 = (bf16[2,64,1024]{2,1,0:T(8,128)(2,1)}, bf16[2,64,1024]{2,1,0:T(8,128)(2,1)S(1)}, u32[]{:S(2)}, u32[]{:S(2)}) collective-permute-start(bf16[2,64,1024]{2,1,0:T(8,128)(2,1)} %get-tuple-element.131), channel_id=1, source_target_pairs={{0,24},{2,26},{4,28},{6,30},{8,16},{10,18},{12,20},{14,22},{16,8},... | collective-permute-start | bytes 786440 | tf_op jit(solution)/shard_map/ppermute | solution.py:653
  311.1 24.6 %collective-permute-start.39 = (bf16[2,64,1024]{2,1,0:T(8,128)(2,1)}, bf16[2,64,1024]{2,1,0:T(8,128)(2,1)S(1)}, u32[]{:S(2)}, u32[]{:S(2)}) collective-permute-start(bf16[2,64,1024]{2,1,0:T(8,128)(2,1)} %get-tuple-element.132), channel_id=1, source_target_pairs={{0,16},{2,18},{4,20},{6,22},{8,24},{10,26},{12,28},{14,30},{16,0},... | collective-permute-start | bytes 786440 | tf_op jit(solution)/shard_map/ppermute | solution.py:653
  317.3 8.8 %collective-permute-start.42 = (f32[32,32]{1,0:T(8,128)S(1)}, f32[32,32]{1,0:T(8,128)S(1)}, u32[]{:S(2)}, u32[]{:S(2)}) collective-permute-start(f32[32,32]{1,0:T(8,128)S(1)} %get-tuple-element.117), channel_id=1, source_target_pairs={{0,4},{2,6},{4,0},{6,2},{8,12},{10,14},{12,8},{14,10},{16,20},{18,... | collective-permute-start | bytes 12296 | tf_op jit(solution)/shard_map/ppermute | solution.py:653
  321.0 28.4 %all-to-all-start.1 = ((bf16[16,32,128]{2,1,0:T(8,128)(2,1)}), bf16[16,32,128]{2,1,0:T(8,128)(2,1)}, u32[]{:S(2)}, u32[]{:S(2)}) async-start(bf16[16,32,128]{2,1,0:T(8,128)(2,1)} %get-tuple-element.128), calls=%async_computation.2 | async-start | bytes 262144 | tf_op jit(solution)/shard_map/all_to_all | solution.py:808
  335.7 13.1 %collective-permute-start.45 = (f32[32,32]{1,0:T(8,128)S(1)}, f32[32,32]{1,0:T(8,128)S(1)}, u32[]{:S(2)}, u32[]{:S(2)}) collective-permute-start(f32[32,32]{1,0:T(8,128)S(1)} %get-tuple-element.126), channel_id=1, source_target_pairs={{0,24},{2,26},{4,28},{6,30},{8,16},{10,18},{12,20},{14,22},{16,8},... | collective-permute-start | bytes 12296 | tf_op jit(solution)/shard_map/ppermute | solution.py:653
  337.5 11.4 %collective-permute-start.44 = (f32[32,32]{1,0:T(8,128)S(1)}, f32[32,32]{1,0:T(8,128)S(1)}, u32[]{:S(2)}, u32[]{:S(2)}) collective-permute-start(f32[32,32]{1,0:T(8,128)S(1)} %get-tuple-element.126), channel_id=1, source_target_pairs={{0,16},{2,18},{4,20},{6,22},{8,24},{10,26},{12,28},{14,30},{16,0},... | collective-permute-start | bytes 12296 | tf_op jit(solution)/shard_map/ppermute | solution.py:653
  341.6 7.2 %collective-permute-start.43 = (f32[32,32]{1,0:T(8,128)S(1)}, f32[32,32]{1,0:T(8,128)S(1)}, u32[]{:S(2)}, u32[]{:S(2)}) collective-permute-start(f32[32,32]{1,0:T(8,128)S(1)} %get-tuple-element.126), channel_id=1, source_target_pairs={{0,8},{2,10},{4,12},{6,14},{8,0},{10,2},{12,4},{14,6},{16,24},{18,... | collective-permute-start | bytes 12296 | tf_op jit(solution)/shard_map/ppermute | solution.py:653
  341.6 18.1 %collective-permute-start.46 = (bf16[128,1024]{1,0:T(8,128)(2,1)S(1)}, bf16[128,1024]{1,0:T(8,128)(2,1)}, u32[]{:S(2)}, u32[]{:S(2)}) collective-permute-start(bf16[128,1024]{1,0:T(8,128)(2,1)S(1)} %get-tuple-element.127), channel_id=1, source_target_pairs={{0,0},{2,1},{4,2},{6,3},{8,4},{10,5},{12,6},{14,7},{16,8},{18,9},{... | collective-permute-start | bytes 786440 | tf_op jit(solution)/shard_map/ppermute | solution.py:813
  (12 other events, 237.3 us)
Sparse Core Ops, SparseCore 0:
  10.2 70.5 all-gather.2
  93.7 72.3 all-gather.4
  210.8 101.9 reduce-scatter.1
